TPU v7x, 512 devices: a whole 4x8x8 slice. The times are simulated.
512 devices in a mesh: dp: 16 (over x_hi, z), expert: 32 (over y, x_lo, core).
Axes of the slice: x: 4 (x_hi: 2, x_lo: 2; x = x_hi * 2 + x_lo), y: 8, z: 8, core: 2. Of those that a mesh axis runs over, the one named last changes fastest.
Arguments:
- tokens: bfloat16 [32, 128, 2560], P('expert', 'dp'), may hold values from -6 to 6
- teacher_ids: int32 [32, 128, 6], P('expert', 'dp'), may hold values from 0 to 127, all different within a row; in each aligned block of 128 rows (0 to 127, 128 to 255, ..., all dimensions but the last counted through in order) at most 8 rows name the same one
- route_weight: bfloat16 [32, 128, 6], P('expert', 'dp'), may hold values from 0.049804688 to 0.5
- teacher_gate: bfloat16 [128, 768, 2560], P('expert', 'dp'), may hold values from -0.125 to 0.125
- teacher_up: bfloat16 [128, 768, 2560], P('expert', 'dp'), may hold values from -0.125 to 0.125
- teacher_down: bfloat16 [128, 768, 2560], P('expert', 'dp'), may hold values from -0.21875 to 0.21875
- merged_gate: bfloat16 [32, 768, 2560], P('expert', 'dp'), may hold values from -0.125 to 0.125
- merged_up: bfloat16 [32, 768, 2560], P('expert', 'dp'), may hold values from -0.125 to 0.125
- merged_down: bfloat16 [32, 768, 2560], P('expert', 'dp'), may hold values from -0.21875 to 0.21875
Outputs:
- grad_gate: float32 [32, 768, 2560], P('expert', 'dp')
- grad_up: float32 [32, 768, 2560], P('expert', 'dp')
- grad_down: float32 [32, 768, 2560], P('expert', 'dp')
Inputs may be any that keep to these rules, and one draw needn't show every extreme that they name: `teacher_ids`: A token's 6 teacher ids differ. Within one group (the 128 tokens of one index of dimension 0) no teacher is named by more than 8 tokens, and in some groups one teacher is named by exactly 8.
All inputs are finite; a program needn't handle non-finite values.
Results may differ from a plain program's by a relative error of at most 0.02.
Values may be sent and summed in bfloat16 or wider, within the bound.
No kernel may reach another device: no remote copies, remote signals or barrier semaphores. Data moves between devices by JAX's collectives and lax.ppermute only.
A program may use at most 128 MiB of HBM per device.

v0:
```python
import jax
import jax.numpy as jnp
from jax import lax
from jax.sharding import PartitionSpec as P


def silu_split(value):
    logistic = jax.nn.sigmoid(value)
    return (value * logistic, logistic * (1.0 + value * (1.0 - logistic)))


def slot_layout(group_ids, teachers, capacity, ranks):
    flat_ids = group_ids.reshape(-1)
    count_all = flat_ids.shape[0]
    hits = (flat_ids[:, None] == jnp.arange(teachers, dtype=jnp.int32)[None, :]).astype(jnp.int32)
    before = jnp.cumsum(hits, axis=0) - hits
    target = flat_ids * capacity + jnp.sum(before * hits, axis=1)
    matches = target[:, None] == jnp.arange(teachers * capacity, dtype=jnp.int32)[None, :]
    source = jnp.sum(jnp.where(matches, jnp.arange(count_all, dtype=jnp.int32)[:, None], 0), axis=0)
    filled = jnp.any(matches, axis=0)
    return (source // ranks, source, filled)


def body(
    tokens,
    teacher_ids,
    route_weight,
    teacher_gate,
    teacher_up,
    teacher_down,
    merged_gate,
    merged_up,
    merged_down,
):
    expert_count = lax.axis_size("expert")
    merge_count = teacher_gate.shape[0]
    capacity = tokens.shape[1]
    features = tokens.shape[2]
    group_ids = lax.all_gather(teacher_ids, "dp", axis=1, tiled=True)
    gathered_tokens, gathered_weight = (
        lax.all_gather(tokens, "dp", axis=1, tiled=True),
        lax.all_gather(route_weight, "dp", axis=1, tiled=True),
    )
    token_index, slot_index, filled = slot_layout(
        group_ids[0], merge_count * expert_count, capacity, group_ids.shape[2]
    )
    slot_rows = jnp.where(
        filled[:, None],
        jnp.take(gathered_tokens[0], token_index, axis=0),
        jnp.zeros((), jnp.bfloat16),
    )
    slot_weight = jnp.where(
        filled, jnp.take(gathered_weight[0].reshape(-1), slot_index), jnp.zeros((), jnp.bfloat16)
    )
    slot_rows = slot_rows.reshape(expert_count, merge_count, capacity, features)
    slot_weight = slot_weight.reshape(expert_count, merge_count, capacity)
    row_block = lax.all_to_all(slot_rows, "expert", split_axis=0, concat_axis=0, tiled=True)
    weight_block = lax.all_to_all(slot_weight, "expert", split_axis=0, concat_axis=0, tiled=True)
    t_gate_value = jnp.einsum(
        "emkd,mfd->emkf", row_block, teacher_gate, preferred_element_type=jnp.float32
    )
    t_up_value = jnp.einsum(
        "emkd,mfd->emkf", row_block, teacher_up, preferred_element_type=jnp.float32
    )
    t_silu, t_slope = silu_split(t_gate_value)
    teacher_hidden = (t_silu * t_up_value).astype(jnp.bfloat16)
    t_part = jnp.einsum(
        "emkf,mfd->emkd", teacher_hidden, teacher_down, preferred_element_type=jnp.float32
    )
    gate_value = jnp.einsum(
        "emkd,fd->emkf", row_block, merged_gate[0], preferred_element_type=jnp.float32
    )
    up_value = jnp.einsum(
        "emkd,fd->emkf", row_block, merged_up[0], preferred_element_type=jnp.float32
    )
    gate_silu, gate_slope = silu_split(gate_value)
    hidden = (gate_silu * up_value).astype(jnp.bfloat16)
    s_part = jnp.einsum("emkf,fd->emkd", hidden, merged_down[0], preferred_element_type=jnp.float32)
    results = (row_block, weight_block, gate_silu, gate_slope, up_value, hidden, s_part - t_part)
    row_block, weight_block, gate_silu, gate_slope, up_value, hidden, gap_term = results
    output_gap = lax.psum(gap_term.astype(jnp.bfloat16), "dp").astype(jnp.float32)
    slot_grad = (weight_block.astype(jnp.float32)[..., None] * output_gap).astype(jnp.bfloat16)
    grad_down = jnp.einsum("emkf,emkd->fd", hidden, slot_grad, preferred_element_type=jnp.float32)
    hidden_grad = jnp.einsum(
        "emkd,fd->emkf", slot_grad, merged_down[0], preferred_element_type=jnp.float32
    )
    gate_grad = (hidden_grad * up_value * gate_slope).astype(jnp.bfloat16)
    up_grad = (hidden_grad * gate_silu).astype(jnp.bfloat16)
    grad_gate = jnp.einsum(
        "emkf,emkd->fd", gate_grad, row_block, preferred_element_type=jnp.float32
    )
    grad_up = jnp.einsum("emkf,emkd->fd", up_grad, row_block, preferred_element_type=jnp.float32)
    return (grad_gate[None], grad_up[None], grad_down[None])


def solution(mesh):
    placed = (
        P("expert", "dp", None),
        P("expert", "dp", None),
        P("expert", "dp", None),
        P("expert", "dp", None),
        P("expert", "dp", None),
        P("expert", "dp", None),
        P("expert", "dp", None),
        P("expert", "dp", None),
        P("expert", "dp", None),
    )
    return jax.shard_map(
        body,
        mesh=mesh,
        in_specs=placed,
        out_specs=(P("expert", "dp", None), P("expert", "dp", None), P("expert", "dp", None)),
        check_vma=False,
    )
```

profile of v0, /device:TPU:6, one launch (start us, length us, event | category | flops | bytes accessed | tf_op | source)
XLA Modules:
  0.0 453.5 jit_solution(6737765582952456654)
XLA Ops:
  7.2 0.8 copy.41
  8.1 45.7 %all_gather.9 = s32[1,128,6]{2,0,1:T(1,128)S(1)} all-gather(s32[1,8,6]{2,0,1:T(1,128)S(1)} %copy.41), channel_id=1, replica_groups=mesh['dp'=16,'expert'=32] {'dp'}, dimensions={1}, use_global_device_ids=true | all-gather | bytes 3264 | tf_op jit(solution)/shard_map/all_gather | solution.py:39
  53.8 0.1 eq.39
  54.0 0.5 broadcast.169
  54.5 0.8 reduce.5
  55.4 0.1 reshape_squeeze.6
  55.5 0.2 fusion.18
  55.9 0.3 fusion.21
  56.2 0.5 fusion.4
  56.7 0.4 select_reduce_fusion
  57.1 0.1 reduce_sum.24
  57.3 0.1 compare_and_fusion
  57.5 39.5 %all_gather.11 = bf16[1,128,2560]{2,1,0:T(8,128)(2,1)S(1)} all-gather(bf16[1,8,2560]{2,1,0:T(8,128)(2,1)} %param.9), channel_id=1, replica_groups=mesh['dp'=16,'expert'=32] {'dp'}, dimensions={1}, use_global_device_ids=true | all-gather | bytes 696320 | tf_op jit(solution)/shard_map/all_gather | solution.py:41
  97.0 6.3 %gather_fusion.1 = bf16[1024,2560]{1,0:T(8,128)(2,1)} fusion(bf16[128,2560]{1,0:T(8,128)(2,1)S(1)} %bitcast.93, s32[1024]{0:T(1024)S(1)} %broadcast_clamp_fusion), kind=kCustom, calls=%fused_computation.1 | custom fusion | bytes 10489856 | tf_op jit(solution)/shard_map/jit(_take)/gather | solution.py:49
  103.3 3.2 select_select_fusion
  106.5 127.5 %all_to_all.10 = bf16[32,4,8,2560]{3,2,1,0:T(8,128)(2,1)S(1)} all-to-all(bf16[32,4,8,2560]{3,2,1,0:T(8,128)(2,1)S(1)} %select_select_fusion), channel_id=1, replica_groups=mesh['dp'=16,'expert'=32] {'expert'}, dimensions={0} | all-to-all | bytes 10485760 | tf_op jit(solution)/shard_map/all_to_all | solution.py:57
  234.0 1.5 fusion.29
  235.5 0.4 copy-done.6
  235.9 2.3 convolution_bitcast_fusion.3
  238.2 1.5 multiply_convert_fusion.7
  239.7 9.4 %fusion.7 = f32[4,32,8,2560]{3,2,0,1:T(8,128)} fusion(bf16[32,4,8,2560]{3,2,1,0:T(8,128)(2,1)} %copy-done.1, bf16[4,48,2560]{2,1,0:T(8,128)(2,1)S(1)} %copy-done, bf16[4,48,2560]{2,1,0:T(8,128)(2,1)S(1)} %copy-done.2, f32[32,4,8,48]{3,2,1,0:T(8,128)} %convolution_bitcast_fusion.3), kind=kOutput, calls=%fused_computation.18 | convolution fusion | flops 503611392 | bytes 17891328 | tf_op jit(solution)/shard_map/emkf,mfd->emkd/dot_general | solution.py:67
  249.2 7.9 %fusion = bf16[32,4,8,2560]{3,2,1,0:T(8,128)(2,1)} fusion(f32[4,32,8,2560]{3,2,0,1:T(8,128)} %fusion.7, bf16[32,4,8,48]{3,2,1,0:T(8,128)(2,1)S(1)} %get-tuple-element.5, bf16[1,48,2560]{2,1,0:T(8,128)(2,1)} %param.17), kind=kOutput, calls=%fused_computation.3 | convolution fusion | flops 256901120 | bytes 16072704 | tf_op jit(solution)/shard_map/emkf,fd->emkd/dot_general | solution.py:78
  257.0 0.7 copy-done.5
  257.7 37.9 %all_gather.10 = bf16[1,128,6]{2,1,0:T(8,128)(2,1)S(1)} all-gather(bf16[1,8,6]{2,1,0:T(8,128)(2,1)S(1)} %copy-done.5), channel_id=1, replica_groups=mesh['dp'=16,'expert'=32] {'dp'}, dimensions={1}, use_global_device_ids=true | all-gather | bytes 1632 | tf_op jit(solution)/shard_map/all_gather | solution.py:42
  295.6 0.1 reshape_squeeze.7
  295.7 6.8 %gather_fusion = bf16[1024]{0:T(1024)(128)(2,1)S(1)} fusion(bf16[768]{0:T(1024)(128)(2,1)S(1)} %reshape_squeeze.7, s32[1024]{0:T(1024)S(1)} %broadcast_clamp_fusion.1), kind=kCustom, calls=%fused_computation | custom fusion | bytes 8192 | tf_op jit(solution)/shard_map/jit(_take)/gather | solution.py:53
  302.7 10.8 %all_to_all.11 = bf16[32,4,8]{2,1,0:T(4,128)(2,1)S(1)} all-to-all(bf16[32,4,8]{2,1,0:T(4,128)(2,1)S(1)} %fusion.33), channel_id=1, replica_groups=mesh['dp'=16,'expert'=32] {'expert'}, dimensions={0} | all-to-all | bytes 4096 | tf_op jit(solution)/shard_map/all_to_all | solution.py:58
  313.5 120.5 %all-reduce.2.cloned.1.call-done = bf16[32,4,8,2560]{3,2,1,0:T(8,128)(2,1)} async-done(((bf16[32,4,8,2560]{3,2,1,0:T(8,128)(2,1)}), bf16[32,4,8,2560]{3,2,1,0:T(8,128)(2,1)}) %all-reduce.2.cloned.1.call-update) | async-done | bytes 5242896 | tf_op jit(solution)/shard_map/psum | solution.py:81
  434.0 4.7 %fusion.3 = f32[1,48,2560]{2,1,0:T(8,128)} fusion(bf16[32,4,8,48]{3,2,1,0:T(8,128)(2,1)S(1)} %get-tuple-element.5, bf16[32,4,8,2560]{3,2,1,0:T(8,128)(2,1)} %all-reduce.2.cloned.1.call-done, f32[32,4,8]{2,1,0:T(4,128)S(1)} %convert_element_type.33), kind=kOutput, calls=%fused_computation.8 | convolution fusion | flops 259522560 | bytes 5836800 | tf_op jit(solution)/shard_map/emkf,emkd->fd/dot_general | solution.py:83
  438.7 4.1 fusion.2
  442.9 1.9 convolution_bitcast_fusion
  444.8 1.9 convolution_bitcast_fusion.1
  (34 shorter events, 0.6 us)
Async XLA Ops:
  7.2 232.5 %copy-start = (bf16[4,48,2560]{2,1,0:T(8,128)(2,1)S(1)}, bf16[4,48,2560]{2,1,0:T(8,128)(2,1)}, u32[]{:S(2)}) copy-start(bf16[4,48,2560]{2,1,0:T(8,128)(2,1)} %param.14) | copy-start | bytes 2949124
  7.2 426.8 %all-reduce.2.cloned.1.call-start = ((), (), s32[]{:S(2)}) async-start(), calls=%async_computation.2 | async-start | bytes 10485760 | tf_op jit(solution)/shard_map/psum | solution.py:81
  106.5 127.5 %copy-start.4 = (bf16[1,48,2560]{2,1,0:T(8,128)(2,1)S(1)}, bf16[1,48,2560]{2,1,0:T(8,128)(2,1)}, u32[]{:S(2)}) copy-start(bf16[1,48,2560]{2,1,0:T(8,128)(2,1)} %param.15) | copy-start | bytes 737284
  234.0 4.2 copy-start.1
  234.0 1.9 copy-start.6
  234.0 4.2 copy-start.7
  238.2 1.5 copy-start.2
  257.0 0.7 copy-start.5
  257.7 181.0 %copy-start.3 = (bf16[1,48,2560]{2,1,0:T(8,128)(2,1)S(1)}, bf16[1,48,2560]{2,1,0:T(8,128)(2,1)}, u32[]{:S(2)}) copy-start(bf16[1,48,2560]{2,1,0:T(8,128)(2,1)} %param.17) | copy-start | bytes 737284
  434.0 8.8 %slice-start = ((s8[5242880]{0:T(1024)(128)(4,1)}), s8[4194304]{0:T(1024)(128)(4,1)S(1)}, s32[]{:S(2)}) async-start(s8[5242880]{0:T(1024)(128)(4,1)} %bitcast.94), calls=%async_computation.3 | async-start | bytes 8388608
  438.7 4.2 slice-start.1
Sparse Core Ops, SparseCore 0:
  257.2 176.8 all-reduce.1
where the time goes:
time: 455 us; the launch traced here: 453 us
  blocking collectives  261 us (57%)
  waiting for transfers between devices  121 us (27%)
  matrix products  35.1 us (8%)
  local copies, waits for them, and re-layouts  16.4 us (4%)
  between operations  14.3 us (3%)
  other arithmetic  5.69 us (1%)
    all_to_all x1, blocking collectives, body(): lax.all_to_all(slot_rows, 'expert', split_axis=0, concat_axis=0, tiled=True)  127 us
    psum x1, waiting for transfers between devices, body(): lax.psum(gap_term.astype(jnp.bfloat16), 'dp').astype(jnp.float32)  121 us
    all_gather x1, blocking collectives, body(): group_ids = lax.all_gather(teacher_ids, 'dp', axis=1, tiled=True)  45.7 us
    all_gather x1, blocking collectives, body(): lax.all_gather(tokens, 'dp', axis=1, tiled=True)  39.5 us
    all_gather x1, blocking collectives, body(): lax.all_gather(route_weight, 'dp', axis=1, tiled=True)  37.9 us
    all_to_all x1, blocking collectives, body(): lax.all_to_all(slot_weight, 'expert', split_axis=0, concat_axis=0, tiled=...  10.8 us
    dot_general x1, matrix products, body(): jnp.einsum('emkf,mfd->emkd', teacher_hidden, teacher_down, preferred_elem...  9.44 us
  transfers between devices with their start and end apart: 1, of which 1 were waited for; matrix products, arithmetic and copies ran while one was open for 2% of the time, Pallas kernels for 0%

commit v1 on v0

v1 whole, which is shorter than its diff:
```python
import jax
import jax.numpy as jnp
from jax import lax
from jax.experimental import pallas as pl
from jax.experimental.pallas import tpu as pltpu
from jax.sharding import PartitionSpec as P

HALVES = 2
SIDE = 128
BF16 = jnp.bfloat16
F32 = jnp.float32
NT_DIMS = (((1,), (1,)), ((), ()))
TN_DIMS = (((0,), (0,)), ((), ()))


def dot_nt(a, b):
    return lax.dot_general(a, b, NT_DIMS, preferred_element_type=F32)


def dot_tn(a, b):
    return lax.dot_general(a, b, TN_DIMS, preferred_element_type=F32)


def dot_nn(a, b):
    return jnp.dot(a, b, preferred_element_type=F32)


def call(kernel, outs, args, scalars=0, flops=0):
    specs = [pl.BlockSpec(memory_space=pltpu.SMEM)] * scalars
    specs += [pl.BlockSpec(memory_space=pltpu.VMEM)] * (len(args) - scalars)
    return pl.pallas_call(
        kernel,
        out_shape=outs,
        in_specs=specs,
        out_specs=jax.tree.map(lambda _: pl.BlockSpec(memory_space=pltpu.VMEM), outs),
        compiler_params=pltpu.CompilerParams(vmem_limit_bytes=48 * 1024 * 1024),
        cost_estimate=pl.CostEstimate(
            flops=flops,
            bytes_accessed=sum(a.size * a.dtype.itemsize for a in args),
            transcendentals=0,
        ),
    )(*args)


def slots_kernel(ranks, place_ref, group_ref, out_ref):
    place = place_ref[0]
    features = out_ref.shape[1] - SIDE
    slots = out_ref.shape[0]
    count = group_ref.shape[0]
    side = group_ref[:, features:].astype(F32)
    slot = lax.broadcasted_iota(jnp.int32, (count, SIDE), 1)
    teacher = ((slot // 2) * 4 + place // 4).astype(F32)
    position = (2 * (place % 4) + slot % 2).astype(F32)
    hits = jnp.zeros((count, SIDE), F32)
    weight = jnp.zeros((count, SIDE), F32)
    for k in range(ranks):
        same = side[:, k : k + 1] == teacher
        hits = jnp.where(same, 1.0, hits)
        weight = jnp.where(same, side[:, ranks + k : ranks + k + 1], weight)
    later = lax.broadcasted_iota(jnp.int32, (count, count), 0)
    earlier = lax.broadcasted_iota(jnp.int32, (count, count), 1)
    below = jnp.where(earlier < later, 1.0, 0.0).astype(BF16)
    before = dot_nn(below, hits.astype(BF16))
    chosen = jnp.where((hits > 0.0) & (before == position), 1.0, 0.0)
    rows = dot_tn(chosen.astype(BF16), group_ref[:, :features])
    weights = dot_tn((chosen * weight).astype(BF16), jnp.ones((count, SIDE), BF16))
    out_ref[:, :features] = rows[:slots].astype(BF16)
    out_ref[:, features:] = weights[:slots].astype(BF16)


def silu_split(value):
    logistic = jax.nn.sigmoid(value)
    return value * logistic, logistic * (1.0 + value * (1.0 - logistic))


def hidden_kernel(rows_ref, weights_ref, hidden_ref, silu_ref, slope_ref):
    units = weights_ref.shape[1]
    features = weights_ref.shape[2]
    half = rows_ref.shape[0] // 2
    for m in range(2):
        span = slice(m * half, (m + 1) * half)
        rows = rows_ref[span, :features]
        stack = jnp.concatenate(
            [weights_ref[m], weights_ref[2 + m], weights_ref[4], weights_ref[5]], axis=0
        )
        value = dot_nt(stack, rows)
        t_silu, _ = silu_split(value[:units])
        teacher = t_silu * value[units : 2 * units]
        s_silu, s_slope = silu_split(value[2 * units : 3 * units])
        up = value[3 * units :]
        hidden_ref[:units, span] = (s_silu * up).astype(BF16)
        hidden_ref[units:, span] = teacher.astype(BF16)
        silu_ref[:, span] = s_silu
        slope_ref[:, span] = up * s_slope


def gap_kernel(hidden_ref, side_ref, down_ref, down_t_ref, grad_ref, down_grad_ref):
    ring = hidden_ref.shape[0]
    units = hidden_ref.shape[1] // 2
    rows = hidden_ref.shape[2]
    half = rows // 2
    student = jnp.concatenate([hidden_ref[i, :units] for i in range(ring)], axis=0)
    teacher = jnp.concatenate([hidden_ref[i, units:] for i in range(ring)], axis=0)
    lane = lax.broadcasted_iota(jnp.int32, (8, SIDE), 1)
    first = jnp.where(lane == 0, 1.0, 0.0).astype(BF16)
    weight = dot_nt(first, side_ref[...])[:1]
    gap = dot_nn(down_t_ref[2], student)
    t_gap = jnp.concatenate(
        [dot_nn(down_t_ref[m], teacher[:, m * half : (m + 1) * half]) for m in range(2)], axis=1
    )
    slot_grad = (weight * (gap - t_gap)).astype(BF16)
    grad_ref[...] = dot_nn(down_ref[...], slot_grad).astype(BF16)
    down_grad_ref[...] = dot_nt(student, slot_grad).astype(BF16)


def grads_kernel(parts_ref, silu_ref, slope_ref, rows_ref, own_ref, other_ref):
    features = own_ref.shape[2]
    block = own_ref.shape[1]
    total = parts_ref[0].astype(F32)
    for i in range(1, parts_ref.shape[0]):
        total += parts_ref[i].astype(F32)
    gate = (total * slope_ref[...]).astype(BF16)
    up = (total * silu_ref[...]).astype(BF16)
    stack = jnp.concatenate([gate[:block], up[:block], gate[block:], up[block:]], axis=0)
    grads = dot_nn(stack, rows_ref[:, :features])
    own_ref[0] = grads[:block]
    own_ref[1] = grads[block : 2 * block]
    other_ref[0] = grads[2 * block : 3 * block].astype(BF16)
    other_ref[1] = grads[3 * block :].astype(BF16)


def body(
    tokens,
    teacher_ids,
    route_weight,
    teacher_gate,
    teacher_up,
    teacher_down,
    merged_gate,
    merged_up,
    merged_down,
):
    n_dp = lax.axis_size("dp")
    experts = lax.axis_size("expert")
    ring = n_dp // HALVES
    local, features = tokens.shape[1], tokens.shape[2]
    ranks = teacher_ids.shape[2]
    block = merged_gate.shape[1]
    piece = features // ring
    place = lax.axis_index("dp")
    half = place // ring
    rings = [[a * ring + i for i in range(ring)] for a in range(HALVES)]
    swap = [(a * ring + i, (1 - a) * ring + i) for a in range(HALVES) for i in range(ring)]

    side = jnp.concatenate([teacher_ids[0].astype(BF16), route_weight[0]], axis=1)
    side = jnp.pad(side, ((0, 0), (0, SIDE - 2 * ranks)))
    packet = jnp.concatenate([tokens[0], side], axis=1)
    packets = jnp.broadcast_to(packet[None], (n_dp, *packet.shape))
    group = lax.all_to_all(packets, "dp", split_axis=0, concat_axis=0, tiled=True)
    group = group.reshape(n_dp * local, features + SIDE)

    def take(array, which):
        return lax.dynamic_slice_in_dim(array, 2 * which, 2, axis=0)

    sent = [take(teacher_gate, 1 - half), take(teacher_up, 1 - half), merged_gate, merged_up]
    kept = [take(teacher_gate, half), take(teacher_up, half), merged_gate, merged_up]
    come = lax.ppermute(jnp.concatenate(sent, axis=0), "dp", swap)
    weights = jnp.concatenate([jnp.concatenate(kept, axis=0), come], axis=1)

    pairs = teacher_down.reshape(HALVES, 2, block, ring, piece)
    shared = jnp.broadcast_to(
        merged_down.reshape(1, 1, block, ring, piece), (HALVES, 1, block, ring, piece)
    )
    down = jnp.concatenate([pairs, shared], axis=1).transpose(0, 3, 1, 2, 4)
    down = down.reshape(n_dp, 3, block, piece)
    down = lax.all_to_all(down, "dp", split_axis=0, concat_axis=0, tiled=True)
    down = down.reshape(HALVES, ring, 3, block, piece)
    down = jnp.where(half == 0, down, down[::-1])
    down = down.transpose(2, 1, 0, 3, 4).reshape(3, n_dp * block, piece)
    down_t = down.transpose(0, 2, 1)

    slots = call(
        lambda *refs: slots_kernel(ranks, *refs),
        jax.ShapeDtypeStruct((2 * experts, features + SIDE), BF16),
        (place[None].astype(jnp.int32), group),
        scalars=1,
    )
    slots = slots.reshape(experts, 2, features + SIDE)
    slots = lax.all_to_all(slots, "expert", split_axis=0, concat_axis=0, tiled=True)
    slots = slots.reshape(2 * experts, features + SIDE)
    rows = lax.all_gather(slots, "dp", axis=0, tiled=True, axis_index_groups=rings)
    count = rows.shape[0]

    hidden, silu, slope = call(
        hidden_kernel,
        (
            jax.ShapeDtypeStruct((4 * block, count), BF16),
            jax.ShapeDtypeStruct((2 * block, count), F32),
            jax.ShapeDtypeStruct((2 * block, count), F32),
        ),
        (rows, weights),
    )
    hidden = lax.all_gather(hidden, "dp", axis=0, axis_index_groups=rings)
    hidden_grad, down_grad = call(
        gap_kernel,
        (
            jax.ShapeDtypeStruct((n_dp * block, count), BF16),
            jax.ShapeDtypeStruct((n_dp * block, piece), BF16),
        ),
        (hidden, rows[:, features:], down[2], down_t),
    )
    parts = hidden_grad.reshape(ring, 2 * block, count)
    parts = lax.all_to_all(
        parts, "dp", split_axis=0, concat_axis=0, tiled=True, axis_index_groups=rings
    )
    own, other = call(
        grads_kernel,
        (
            jax.ShapeDtypeStruct((2, block, features), F32),
            jax.ShapeDtypeStruct((2, block, features), BF16),
        ),
        (parts, silu, slope, rows),
    )
    other = lax.ppermute(other, "dp", swap)
    grads = own + other.astype(F32)

    down_grad = down_grad.reshape(ring, HALVES, block, piece)
    down_grad = jnp.where(half == 0, down_grad, down_grad[:, ::-1])
    down_grad = down_grad.transpose(1, 0, 2, 3).reshape(n_dp, block, piece)
    down_grad = lax.all_to_all(down_grad, "dp", split_axis=0, concat_axis=0, tiled=True)
    down_grad = down_grad.reshape(HALVES, ring, block, piece).astype(F32).sum(axis=0)
    down_grad = down_grad.transpose(1, 0, 2).reshape(block, features)
    return grads[:1], grads[1:], down_grad[None]


def solution(mesh):
    placed = (P("expert", "dp", None),) * 9
    return jax.shard_map(
        body,
        mesh=mesh,
        in_specs=placed,
        out_specs=(P("expert", "dp", None),) * 3,
        check_vma=False,
    )
```

time: 455 us -> 254 us (0.56)
  blocking collectives: 261 us -> 22.4 us
  starting transfers between devices: 0.04 us -> 36.1 us
  matrix products: 35.1 us -> 0 us
  waiting for transfers between devices: 121 us -> 136 us
  local copies, waits for them, and re-layouts: 16.4 us -> 27.2 us
  Pallas kernels: 0 us -> 7.54 us
    all_gather x3 -> x0, blocking collectives: 123 us -> none  [the longest x1 45.7 us: body(): group_ids = lax.all_gather(teacher_ids, 'dp', axis=1, tiled=True)]
    psum x1 -> x0, waiting for transfers between devices: 121 us -> none  [body(): lax.psum(gap_term.astype(jnp.bfloat16), 'dp').astype(jnp.float32)]
    all_to_all x2 -> x1, blocking collectives: 138 us -> 22.4 us  [body(): lax.all_to_all(slots, 'expert', split_axis=0, concat_axis=0, tiled=True)]
    all_gather x0 -> x2, waiting for transfers between devices: none -> 59.5 us  [the longest x1 35.5 us: body(): hidden = lax.all_gather(hidden, 'dp', axis=0, axis_index_groups=rings)]
    all_to_all x0 -> x4, waiting for transfers between devices: none -> 40 us  [the longest x1 18 us: body(): lax.all_to_all(packets, 'dp', split_axis=0, concat_axis=0, tiled=True)]
    ppermute x0 -> x2, waiting for transfers between devices: none -> 36.6 us  [the longest x1 32.4 us: body(): come = lax.ppermute(jnp.concatenate(sent, axis=0), 'dp', swap)]
    dot_general x9 -> x0, matrix products: 35.1 us -> none  [the longest x1 9.44 us: body(): jnp.einsum('emkf,mfd->emkd', teacher_hidden, teacher_down, preferred_elem...]
    all_to_all x0 -> x4, starting transfers between devices: none -> 29.4 us  [the longest x1 13.3 us: body(): lax.all_to_all(packets, 'dp', split_axis=0, concat_axis=0, tiled=True)]
  transfers between devices with their start and end apart: 1 -> 8, of which waited for: 1 -> 7; matrix products, arithmetic and copies ran while one was open for 2% -> 8% of each run, Pallas kernels for 0% -> 2%
where the time goes in v1:
time: 254 us; the launch traced here: 252 us
  waiting for transfers between devices  136 us (54%)
  starting transfers between devices  36.1 us (14%)
  local copies, waits for them, and re-layouts  27.2 us (11%)
  blocking collectives  22.4 us (9%)
  between operations  14.3 us (6%)
  other arithmetic  8.66 us (3%)
  Pallas kernels  7.54 us (3%)
    all_gather x1, waiting for transfers between devices, body(): hidden = lax.all_gather(hidden, 'dp', axis=0, axis_index_groups=rings)  35.5 us
    ppermute x1, waiting for transfers between devices, body(): come = lax.ppermute(jnp.concatenate(sent, axis=0), 'dp', swap)  32.4 us
    all_gather x1, waiting for transfers between devices, body(): lax.all_gather(slots, 'dp', axis=0, tiled=True, axis_index_groups=rings)  24 us
    all_to_all x1, blocking collectives, body(): lax.all_to_all(slots, 'expert', split_axis=0, concat_axis=0, tiled=True)  22.4 us
    all_to_all x1, waiting for transfers between devices, body(): lax.all_to_all(packets, 'dp', split_axis=0, concat_axis=0, tiled=True)  18 us
    all_to_all x1, waiting for transfers between devices, body(): lax.all_to_all(parts, 'dp', split_axis=0, concat_axis=0, tiled=True, axis...  16.7 us
    all_to_all x1, starting transfers between devices, body(): lax.all_to_all(packets, 'dp', split_axis=0, concat_axis=0, tiled=True)  13.3 us
    unnamed x31, local copies, waits for them, and re-layouts  11.2 us
  transfers between devices with their start and end apart: 8, of which 7 were waited for; matrix products, arithmetic and copies ran while one was open for 8% of the time, Pallas kernels for 2%

profile of v1, /device:TPU:6, one launch (start us, length us, event | category | flops | bytes accessed | tf_op | source)
XLA Modules:
  0.0 252.3 jit_solution(9460975680682173175)
XLA Ops:
  10.4 13.3 %all-to-all-start = ((bf16[16,8,2688]{2,1,0:T(8,128)(2,1)}), bf16[16,8,2688]{2,1,0:T(8,128)(2,1)S(1)}, u32[]{:S(2)}, u32[]{:S(2)}) async-start(bf16[16,8,2688]{2,1,0:T(8,128)(2,1)} %broadcast_in_dim.17), calls=%async_computation | async-start | bytes 1376256 | tf_op jit(solution)/shard_map/all_to_all | solution.py:159
  23.7 18.0 %all-to-all-done = bf16[16,8,2688]{2,1,0:T(8,128)(2,1)S(1)} async-done(((bf16[16,8,2688]{2,1,0:T(8,128)(2,1)}), bf16[16,8,2688]{2,1,0:T(8,128)(2,1)S(1)}, u32[]{:S(2)}, u32[]{:S(2)}) %all-to-all-start) | async-done | bytes 688160 | tf_op jit(solution)/shard_map/all_to_all | solution.py:159
  42.5 22.4 %all_to_all.25 = bf16[32,2,2688]{2,1,0:T(2,128)(2,1)S(1)} all-to-all(bf16[32,2,2688]{2,1,0:T(2,128)(2,1)S(1)} %reshape.48), channel_id=1, replica_groups=mesh['dp'=16,'expert'=32] {'expert'}, dimensions={0} | all-to-all | bytes 688128 | tf_op jit(solution)/shard_map/all_to_all | solution.py:189
  65.8 1.7 constant_dynamic-slice_fusion.2
  67.5 1.4 pad_maximum_fusion.1
  68.8 4.4 %collective-permute-start = (bf16[6,48,2560]{2,1,0:T(8,128)(2,1)}, bf16[6,48,2560]{2,1,0:T(8,128)(2,1)}, u32[]{:S(2)}, u32[]{:S(2)}) collective-permute-start(bf16[6,48,2560]{2,1,0:T(8,128)(2,1)} %pad_maximum_fusion.1), channel_id=1, source_target_pairs={{0,256},{32,288},{64,320},{96,352},{128,384},{160,416},{192,448},{... | collective-permute-start | bytes 4423688 | tf_op jit(solution)/shard_map/ppermute | solution.py:167
  73.5 2.0 reshape.50
  75.9 1.4 copy.36
  77.4 6.4 %all-to-all-start.2 = ((bf16[16,3,48,320]{3,2,1,0:T(8,128)(2,1)}), bf16[16,3,48,320]{3,2,1,0:T(8,128)(2,1)S(1)}, u32[]{:S(2)}, u32[]{:S(2)}) async-start(bf16[16,3,48,320]{3,2,1,0:T(8,128)(2,1)} %bitcast.7), calls=%async_computation.2 | async-start | bytes 3538944 | tf_op jit(solution)/shard_map/all_to_all | solution.py:176
  83.8 32.4 %collective-permute-done = bf16[6,48,2560]{2,1,0:T(8,128)(2,1)} collective-permute-done((bf16[6,48,2560]{2,1,0:T(8,128)(2,1)}, bf16[6,48,2560]{2,1,0:T(8,128)(2,1)}, u32[]{:S(2)}, u32[]{:S(2)}) %collective-permute-start) | collective-permute-done | bytes 1474592 | tf_op jit(solution)/shard_map/ppermute | solution.py:167
  116.2 2.9 %pad_maximum_fusion.weights_ref = bf16[6,96,2560]{2,1,0:T(8,128)(2,1)} fusion(bf16[6,48,2560]{2,1,0:T(8,128)(2,1)} %collective-permute-done, bf16[1,48,2560]{2,1,0:T(8,128)(2,1)S(1)} %copy-done.12, bf16[1,48,2560]{2,1,0:T(8,128)(2,1)S(1)} %copy-done.13, bf16[2,48,2560]{2,1,0:T(8,128)(2,1)S(1)} %get-tuple-element.21, bf16[2,48,2560]{2,1,0:T(8,128)(2,1)S(1)} %get-tuple-element.24), kind=kLoop, calls=%fused_computation | loop fusion | flops 14745600 | bytes 5898240 | tf_op jit(solution)/shard_map/concatenate | solution.py:168
  119.1 24.0 %all-gather.4.cloned.1.call-done.rows_ref = bf16[512,2688]{1,0:T(8,128)(2,1)} async-done(((bf16[64,2688]{1,0:T(8,128)(2,1)}), bf16[512,2688]{1,0:T(8,128)(2,1)}) %all-gather.4.cloned.1.call-update) | async-done | bytes 2752528 | tf_op jit(solution)/shard_map/all_gather | solution.py:191
  143.0 1.8 copy-done
  144.8 3.8 %shard_map.113 = (bf16[192,512]{1,0:T(8,128)(2,1)}, f32[96,512]{1,0:T(8,128)S(1)}, f32[96,512]{1,0:T(8,128)S(1)}) custom-call(bf16[512,2688]{1,0:T(8,128)(2,1)S(1)} %copy-done, bf16[6,96,2560]{2,1,0:T(8,128)(2,1)} %pad_maximum_fusion.weights_ref), custom_call_target="tpu_custom_call" | custom-call | bytes 5701632 | tf_op jit(solution)/shard_map/pallas_call | solution.py:31
  150.4 1.4 copy.38
  151.9 3.9 %copy.39 = bf16[3,768,320]{1,2,0:T(8,128)(2,1)} copy(bf16[3,768,320]{2,1,0:T(8,128)(2,1)} %bitcast.30) | data formatting | bytes 2949120 | tf_op jit(solution)/shard_map/reshape | solution.py:179
  155.8 35.5 %all-gather.6.cloned.1.call-done = bf16[1536,512]{1,0:T(8,128)(2,1)} async-done(((bf16[192,512]{1,0:T(8,128)(2,1)}), bf16[1536,512]{1,0:T(8,128)(2,1)}) %all-gather.6.cloned.1.call-update) | async-done | bytes 1572880 | tf_op jit(solution)/shard_map/all_gather | solution.py:203
  191.3 1.4 copy-done.2
  192.7 1.4 copy-done.3
  194.1 1.6 shard_map.114
  197.4 4.2 %all-to-all-start.3 = ((bf16[8,96,512]{2,1,0:T(8,128)(2,1)}), bf16[8,96,512]{2,1,0:T(8,128)(2,1)S(1)}, u32[]{:S(2)}, u32[]{:S(2)}) async-start(bf16[8,96,512]{2,1,0:T(8,128)(2,1)} %bitcast.28), calls=%async_computation.3 | async-start | bytes 1572864 | tf_op jit(solution)/shard_map/all_to_all | solution.py:213
  201.6 1.1 copy.41
  203.7 16.7 %all-to-all-done.3.parts_ref = bf16[8,96,512]{2,1,0:T(8,128)(2,1)S(1)} async-done(((bf16[8,96,512]{2,1,0:T(8,128)(2,1)}), bf16[8,96,512]{2,1,0:T(8,128)(2,1)S(1)}, u32[]{:S(2)}, u32[]{:S(2)}) %all-to-all-start.3) | async-done | bytes 786464 | tf_op jit(solution)/shard_map/all_to_all | solution.py:213
  220.5 5.5 %all-to-all-start.4 = ((bf16[16,48,320]{2,1,0:T(8,128)(2,1)}), bf16[16,48,320]{2,1,0:T(8,128)(2,1)}, u32[]{:S(2)}, u32[]{:S(2)}) async-start(bf16[16,48,320]{2,1,0:T(8,128)(2,1)} %bitcast.32), calls=%async_computation.4 | async-start | bytes 1179648 | tf_op jit(solution)/shard_map/all_to_all | solution.py:230
  227.8 1.5 shard_map.115
  229.3 1.0 copy-done.4
  230.3 2.2 collective-permute-start.1
  232.5 5.3 %all-to-all-done.4 = bf16[16,48,320]{2,1,0:T(8,128)(2,1)} async-done(((bf16[16,48,320]{2,1,0:T(8,128)(2,1)}), bf16[16,48,320]{2,1,0:T(8,128)(2,1)}, u32[]{:S(2)}, u32[]{:S(2)}) %all-to-all-start.4) | async-done | bytes 491552 | tf_op jit(solution)/shard_map/all_to_all | solution.py:230
  237.8 1.2 convert_reduce_fusion
  239.3 0.9 broadcast_in_dim_reshape.3
  240.2 4.2 %collective-permute-done.1 = bf16[2,48,2560]{2,1,0:T(8,128)(2,1)S(1)} collective-permute-done((bf16[2,48,2560]{2,1,0:T(8,128)(2,1)}, bf16[2,48,2560]{2,1,0:T(8,128)(2,1)S(1)}, u32[]{:S(2)}, u32[]{:S(2)}) %collective-permute-start.1) | collective-permute-done | bytes 491552 | tf_op jit(solution)/shard_map/ppermute | solution.py:224
  244.5 1.0 fusion.4
  (49 shorter events, 12.2 us)
Async XLA Ops:
  10.4 31.3 %all-to-all-start = ((bf16[16,8,2688]{2,1,0:T(8,128)(2,1)}), bf16[16,8,2688]{2,1,0:T(8,128)(2,1)S(1)}, u32[]{:S(2)}, u32[]{:S(2)}) async-start(bf16[16,8,2688]{2,1,0:T(8,128)(2,1)} %broadcast_in_dim.17), calls=%async_computation | async-start | bytes 1376256 | tf_op jit(solution)/shard_map/all_to_all | solution.py:159
  23.7 119.4 %all-gather.4.cloned.1.call-start = ((), (), s32[]{:S(2)}) async-start(), calls=%async_computation.5 | async-start | bytes 3096576 | tf_op jit(solution)/shard_map/all_gather | solution.py:191
  65.7 1.7 copy-start.12
  65.7 1.7 copy-start.13
  67.5 5.8 %copy-start.14 = (bf16[1,48,2560]{2,1,0:T(8,128)(2,1)S(1)}, bf16[1,48,2560]{2,1,0:T(8,128)(2,1)}, u32[]{:S(2)}) copy-start(bf16[1,48,2560]{2,1,0:T(8,128)(2,1)} %param.17) | copy-start | bytes 737284
  68.8 47.4 %collective-permute-start = (bf16[6,48,2560]{2,1,0:T(8,128)(2,1)}, bf16[6,48,2560]{2,1,0:T(8,128)(2,1)}, u32[]{:S(2)}, u32[]{:S(2)}) collective-permute-start(bf16[6,48,2560]{2,1,0:T(8,128)(2,1)} %pad_maximum_fusion.1), channel_id=1, source_target_pairs={{0,256},{32,288},{64,320},{96,352},{128,384},{160,416},{192,448},{... | collective-permute-start | bytes 4423688 | tf_op jit(solution)/shard_map/ppermute | solution.py:167
  77.4 72.6 %all-to-all-start.2 = ((bf16[16,3,48,320]{3,2,1,0:T(8,128)(2,1)}), bf16[16,3,48,320]{3,2,1,0:T(8,128)(2,1)S(1)}, u32[]{:S(2)}, u32[]{:S(2)}) async-start(bf16[16,3,48,320]{3,2,1,0:T(8,128)(2,1)} %bitcast.7), calls=%async_computation.2 | async-start | bytes 3538944 | tf_op jit(solution)/shard_map/all_to_all | solution.py:176
  83.8 107.5 %all-gather.6.cloned.1.call-start = ((), (), s32[]{:S(2)}) async-start(), calls=%async_computation.6 | async-start | bytes 1769472 | tf_op jit(solution)/shard_map/all_gather | solution.py:203
  143.0 1.8 copy-start
  148.6 0.7 copy-start.8
  149.3 0.7 copy-start.10
  151.9 3.9 %copy-start.1 = (bf16[512,2688]{1,0:T(8,128)(2,1)S(1)}, bf16[512,2688]{1,0:T(8,128)(2,1)}, u32[]{:S(2)}) copy-start(bf16[512,2688]{1,0:T(8,128)(2,1)} %all-gather.4.cloned.1.call-done.rows_ref) | copy-start | bytes 8257540
  191.3 1.4 copy-start.2
  192.6 1.4 copy-start.3
  195.7 0.9 copy-start.6
  196.6 0.8 copy-start.7
  197.4 23.0 %all-to-all-start.3 = ((bf16[8,96,512]{2,1,0:T(8,128)(2,1)}), bf16[8,96,512]{2,1,0:T(8,128)(2,1)S(1)}, u32[]{:S(2)}, u32[]{:S(2)}) async-start(bf16[8,96,512]{2,1,0:T(8,128)(2,1)} %bitcast.28), calls=%async_computation.3 | async-start | bytes 1572864 | tf_op jit(solution)/shard_map/all_to_all | solution.py:213
  220.5 17.4 %all-to-all-start.4 = ((bf16[16,48,320]{2,1,0:T(8,128)(2,1)}), bf16[16,48,320]{2,1,0:T(8,128)(2,1)}, u32[]{:S(2)}, u32[]{:S(2)}) async-start(bf16[16,48,320]{2,1,0:T(8,128)(2,1)} %bitcast.32), calls=%async_computation.4 | async-start | bytes 1179648 | tf_op jit(solution)/shard_map/all_to_all | solution.py:230
  225.9 0.9 copy-start.9
  226.9 0.9 copy-start.11
  229.3 1.0 copy-start.4
  230.3 14.1 %copy-start.5 = (f32[2,48,2560]{2,1,0:T(8,128)S(1)}, f32[2,48,2560]{2,1,0:T(8,128)}, u32[]{:S(2)}) copy-start(f32[2,48,2560]{2,1,0:T(8,128)} %copy-done.4) | copy-start | bytes 2949124
  230.3 14.1 %collective-permute-start.1 = (bf16[2,48,2560]{2,1,0:T(8,128)(2,1)}, bf16[2,48,2560]{2,1,0:T(8,128)(2,1)S(1)}, u32[]{:S(2)}, u32[]{:S(2)}) collective-permute-start(bf16[2,48,2560]{2,1,0:T(8,128)(2,1)} %get-tuple-element.15), channel_id=1, source_target_pairs={{0,256},{32,288},{64,320},{96,352},{128,384},{160,416},{192,448},{... | collective-permute-start | bytes 1474568 | tf_op jit(solution)/shard_map/ppermute | solution.py:224
Sparse Core Ops, SparseCore 0:
  65.8 77.1 all-gather.3
  150.1 41.1 all-gather.5

commit v2 on v1

v2 whole, which is shorter than its diff:
```python
import jax
import jax.numpy as jnp
from jax import lax
from jax.experimental import pallas as pl
from jax.experimental.pallas import tpu as pltpu
from jax.sharding import PartitionSpec as P

HALVES = 2
PAIR = 2
SIDE = 128
BF16 = jnp.bfloat16
F32 = jnp.float32


def dot_nn(a, b):
    return jnp.dot(a, b, preferred_element_type=F32)


def dot_nt(a, b):
    return lax.dot_general(a, b, (((1,), (1,)), ((), ())), preferred_element_type=F32)


def dot_tn(a, b):
    return lax.dot_general(a, b, (((0,), (0,)), ((), ())), preferred_element_type=F32)


def call(kernel, outs, args, scalars=0, flops=0):
    specs = [pl.BlockSpec(memory_space=pltpu.SMEM)] * scalars
    specs += [pl.BlockSpec(memory_space=pltpu.VMEM)] * (len(args) - scalars)
    return pl.pallas_call(
        kernel,
        out_shape=outs,
        in_specs=specs,
        out_specs=jax.tree.map(lambda _: pl.BlockSpec(memory_space=pltpu.VMEM), outs),
        compiler_params=pltpu.CompilerParams(vmem_limit_bytes=40 * 1024 * 1024),
        cost_estimate=pl.CostEstimate(
            flops=flops,
            bytes_accessed=sum(a.size * a.dtype.itemsize for a in args),
            transcendentals=0,
        ),
    )(*args)


def columns(total):
    return -(-total // SIDE) * SIDE


def pack_kernel(token_ref, ids_ref, weight_ref, out_ref):
    ring = out_ref.shape[0] // HALVES
    count, ranks = ids_ref.shape
    piece = token_ref.shape[1] // ring
    wide = columns(piece)
    lane = lax.broadcasted_iota(jnp.int32, (count, SIDE), 1)
    ids = ids_ref[...].astype(F32)
    weight = weight_ref[...].astype(F32)
    side = jnp.zeros((count, SIDE), F32)
    for k in range(ranks):
        side = jnp.where(lane == k, ids[:, k : k + 1], side)
        side = jnp.where(lane == ranks + k, weight[:, k : k + 1], side)
    side = side.astype(BF16)
    blank = jnp.zeros((count, wide - piece), BF16)
    for i in range(ring):
        part = token_ref[:, i * piece : (i + 1) * piece]
        row = jnp.concatenate([part, blank, side], axis=1)
        for a in range(HALVES):
            out_ref[a * ring + i] = row


def slots_kernel(ranks, piece, capacity, place_ref, group_ref, out_ref):
    ring = place_ref[1]
    half = place_ref[0] // ring
    wide = columns(piece)
    count = group_ref.shape[0]
    slots = out_ref.shape[0]
    side = group_ref[:, wide:].astype(F32)
    slot = lax.broadcasted_iota(jnp.int32, (count, slots), 1)
    column, inner = slot // (PAIR * capacity), slot % (PAIR * capacity)
    teacher = (column * HALVES * PAIR + half * PAIR + inner // capacity).astype(F32)
    position = (inner % capacity).astype(F32)
    hits = jnp.zeros((count, slots), F32)
    weight = jnp.zeros((count, slots), F32)
    for k in range(ranks):
        same = side[:, k : k + 1] == teacher
        hits = jnp.where(same, 1.0, hits)
        weight = jnp.where(same, side[:, ranks + k : ranks + k + 1], weight)
    later = lax.broadcasted_iota(jnp.int32, (count, count), 0)
    earlier = lax.broadcasted_iota(jnp.int32, (count, count), 1)
    below = jnp.where(earlier < later, 1.0, 0.0).astype(BF16)
    before = dot_nn(below, hits.astype(BF16))
    chosen = jnp.where((hits > 0.0) & (before == position), 1.0, 0.0)
    lane = lax.broadcasted_iota(jnp.int32, (count, wide), 1)
    mark = jnp.where(lane >= piece, 1.0, 0.0).astype(BF16)
    pick = jnp.concatenate([chosen, chosen * weight], axis=0).astype(BF16)
    value = jnp.concatenate([group_ref[:, :wide], mark], axis=0)
    out_ref[...] = dot_tn(pick, value).astype(BF16)


def turn_kernel(piece, capacity, rows_ref, turned_ref, weight_ref):
    count, wide = rows_ref.shape
    source = lax.broadcasted_iota(jnp.int32, (count, count), 0)
    target = lax.broadcasted_iota(jnp.int32, (count, count), 1)
    group, inner = source // (PAIR * capacity), source % (PAIR * capacity)
    goes = (inner // capacity) * (count // PAIR) + group * capacity + inner % capacity
    move = jnp.where(goes == target, 1.0, 0.0).astype(BF16)
    rows = rows_ref[...]
    turned_ref[...] = dot_tn(rows, move)[:piece].astype(BF16)
    weight_ref[...] = dot_tn(move, rows[:, wide - SIDE :]).astype(BF16)


def silu_split(value):
    logistic = jax.nn.sigmoid(value)
    return value * logistic, logistic * (1.0 + value * (1.0 - logistic))


def hidden_kernel(
    place_ref, rows_ref, t_gate_ref, t_up_ref, m_gate_ref, m_up_ref, come_ref, out_ref, silu_ref, slope_ref
):
    ring = place_ref[1]
    half = place_ref[0] // ring
    block = m_gate_ref.shape[1]
    units = 2 * block
    span = rows_ref.shape[1] // PAIR
    places = out_ref.shape[0] // PAIR
    for m in range(PAIR):
        lanes = slice(m * span, (m + 1) * span)
        own = PAIR * half + m
        stack = jnp.concatenate(
            [
                t_gate_ref[own],
                come_ref[m],
                t_up_ref[own],
                come_ref[PAIR + m],
                m_gate_ref[0],
                come_ref[2 * PAIR],
                m_up_ref[0],
                come_ref[2 * PAIR + 1],
            ],
            axis=0,
        )
        value = dot_nn(stack, rows_ref[:, lanes])
        t_silu, _ = silu_split(value[:units])
        teacher = (t_silu * value[units : 2 * units]).astype(BF16)
        s_silu, s_slope = silu_split(value[2 * units : 3 * units])
        up = value[3 * units :]
        student = (s_silu * up).astype(BF16)
        for i in range(places):
            at = m * places + i
            out_ref[at, 0] = student[:block]
            out_ref[at, 1] = student[block:]
            out_ref[at, 2] = teacher[:block]
            out_ref[at, 3] = teacher[block:]
        silu_ref[:, lanes] = s_silu
        slope_ref[:, lanes] = up * s_slope


def gap_kernel(place_ref, hidden_ref, down_ref, weight_ref, grad_ref, down_grad_ref):
    ring = hidden_ref.shape[0]
    block = hidden_ref.shape[2]
    span = hidden_ref.shape[3]
    half = place_ref[0] // ring
    second = (place_ref[0] % ring) // (ring // PAIR)
    piece = down_ref.shape[3]
    order = [(a, i) for a in range(HALVES) for i in range(ring)]
    student = jnp.concatenate([hidden_ref[i, half ^ a] for a, i in order], axis=0)
    teacher = jnp.concatenate([hidden_ref[i, 2 + (half ^ a)] for a, i in order], axis=0)
    t_down = down_ref[:, 0].reshape(HALVES * ring * block, piece)
    m_down = down_ref[:, 1].reshape(HALVES * ring * block, piece)
    gap = dot_tn(student, m_down) - dot_tn(teacher, t_down)
    start = pl.multiple_of(second * span, span)
    weight = weight_ref[pl.ds(start, span), SIDE - 1 : SIDE].astype(F32)
    slot_grad = (weight * gap).astype(BF16)
    grad = dot_nt(m_down, slot_grad).astype(BF16)
    for k, (a, i) in enumerate(order):
        grad_ref[i, half ^ a] = grad[k * block : (k + 1) * block]
    down_grad = dot_nn(student, slot_grad).astype(BF16)
    down_grad_ref[...] = down_grad.reshape(down_grad_ref.shape)


def grads_kernel(parts_ref, silu_ref, slope_ref, rows_ref, own_ref, other_ref):
    block = own_ref.shape[1]
    places = parts_ref.shape[0] // PAIR
    sums = []
    for m in range(PAIR):
        total = parts_ref[m * places].astype(F32)
        for i in range(1, places):
            total += parts_ref[m * places + i].astype(F32)
        sums.append(total)
    total = jnp.concatenate(sums, axis=1)
    gate = (total * slope_ref[...]).astype(BF16)
    up = (total * silu_ref[...]).astype(BF16)
    stack = jnp.concatenate([gate[:block], up[:block], gate[block:], up[block:]], axis=0)
    grads = dot_nt(stack, rows_ref[...])
    own_ref[0] = grads[:block]
    own_ref[1] = grads[block : 2 * block]
    other_ref[0] = grads[2 * block : 3 * block].astype(BF16)
    other_ref[1] = grads[3 * block :].astype(BF16)


def down_sum_kernel(parts_ref, out_ref):
    count, _, piece = parts_ref.shape
    quarters = out_ref.shape[1] // piece
    for q in range(quarters):
        total = parts_ref[q].astype(F32)
        for i in range(q + quarters, count, quarters):
            total += parts_ref[i].astype(F32)
        out_ref[:, q * piece : (q + 1) * piece] = total


def body(
    tokens,
    teacher_ids,
    route_weight,
    teacher_gate,
    teacher_up,
    teacher_down,
    merged_gate,
    merged_up,
    merged_down,
):
    n_dp = lax.axis_size("dp")
    experts = lax.axis_size("expert")
    ring = n_dp // HALVES
    features = tokens.shape[2]
    capacity = tokens.shape[1]
    ranks = teacher_ids.shape[2]
    block = merged_gate.shape[1]
    piece = features // ring
    quarter = features * PAIR // ring
    rows = experts * PAIR * capacity
    axis = lax.axis_index("dp").astype(jnp.int32)
    half = axis // ring
    place = jnp.stack([axis, jnp.int32(ring)])
    rings = [[a * ring + i for i in range(ring)] for a in range(HALVES)]
    swap = [(a * ring + i, (1 - a) * ring + i) for a in range(HALVES) for i in range(ring)]

    def exchange(array, axis_name, groups=None):
        return lax.all_to_all(
            array, axis_name, split_axis=0, concat_axis=0, tiled=True, axis_index_groups=groups
        )

    sent = [
        lax.dynamic_slice_in_dim(a, PAIR * (1 - half), PAIR, axis=0)
        for a in (teacher_gate, teacher_up)
    ]
    come = lax.ppermute(jnp.concatenate([*sent, merged_gate, merged_up], axis=0), "dp", swap)

    packets = call(
        pack_kernel,
        jax.ShapeDtypeStruct((n_dp, capacity, columns(piece) + SIDE), BF16),
        (tokens[0], teacher_ids[0], route_weight[0]),
    )
    group = exchange(packets, "dp").reshape(n_dp * capacity, columns(piece) + SIDE)

    pairs = teacher_down.reshape(HALVES * PAIR, block, ring // PAIR, quarter).transpose(0, 2, 1, 3)
    shared = merged_down.reshape(1, block, ring // PAIR, quarter).transpose(0, 2, 1, 3)
    shared = jnp.broadcast_to(shared, pairs.shape)
    down = jnp.stack([pairs, shared], axis=2).reshape(n_dp, 2, block, quarter)
    down, group = lax.optimization_barrier((down, group))
    down = exchange(down, "dp")

    slots = call(
        lambda *refs: slots_kernel(ranks, piece, capacity, *refs),
        jax.ShapeDtypeStruct((rows, columns(piece)), BF16),
        (place, group),
        scalars=1,
    )
    slots = exchange(slots.reshape(experts, PAIR * capacity, columns(piece)), "expert")
    turned, weight = call(
        lambda *refs: turn_kernel(piece, capacity, *refs),
        (jax.ShapeDtypeStruct((piece, rows), BF16), jax.ShapeDtypeStruct((rows, SIDE), BF16)),
        (slots.reshape(rows, columns(piece)),),
    )
    turned = lax.all_gather(turned, "dp", axis=0, tiled=True, axis_index_groups=rings)

    hidden, silu, slope = call(
        hidden_kernel,
        (
            jax.ShapeDtypeStruct((ring, 4, block, rows // PAIR), BF16),
            jax.ShapeDtypeStruct((2 * block, rows), F32),
            jax.ShapeDtypeStruct((2 * block, rows), F32),
        ),
        (place, turned, teacher_gate, teacher_up, merged_gate, merged_up, come),
        scalars=1,
    )
    hidden = exchange(hidden, "dp", rings)
    hidden_grad, down_grad = call(
        gap_kernel,
        (
            jax.ShapeDtypeStruct((ring, 2, block, rows // PAIR), BF16),
            jax.ShapeDtypeStruct((n_dp, block, quarter), BF16),
        ),
        (place, hidden, down, weight),
        scalars=1,
    )
    parts = exchange(hidden_grad.reshape(ring, 2 * block, rows // PAIR), "dp", rings)
    down_grad = exchange(down_grad, "dp")
    own, other = call(
        grads_kernel,
        (
            jax.ShapeDtypeStruct((2, block, features), F32),
            jax.ShapeDtypeStruct((2, block, features), BF16),
        ),
        (parts, silu, slope, turned),
    )
    other = lax.ppermute(other, "dp", swap)
    grad_down = call(
        down_sum_kernel, jax.ShapeDtypeStruct((block, features), F32), (down_grad,)
    )
    grad_gate = own[:1] + other[:1].astype(F32)
    grad_up = own[1:] + other[1:].astype(F32)
    return grad_gate, grad_up, grad_down[None]


def solution(mesh):
    placed = (P("expert", "dp", None),) * 9
    return jax.shard_map(
        body,
        mesh=mesh,
        in_specs=placed,
        out_specs=(P("expert", "dp", None),) * 3,
        check_vma=False,
    )
```

time: 254 us -> 228 us (0.90)
  waiting for transfers between devices: 136 us -> 88.4 us
  blocking collectives: 22.4 us -> 67.1 us
  local copies, waits for them, and re-layouts: 27.2 us -> 15.1 us
  starting transfers between devices: 36.1 us -> 28.6 us
  other arithmetic: 8.66 us -> 2.86 us
  Pallas kernels: 7.54 us -> 10.1 us
    all_to_all x1 -> x3, blocking collectives: 22.4 us -> 67.1 us  [exchange(): lax.all_to_all(array, axis_name, split_axis=0, concat_axis=0, tiled=True,...]
    all_gather x2 -> x1, waiting for transfers between devices: 59.5 us -> 17.3 us  [body(): lax.all_gather(turned, 'dp', axis=0, tiled=True, axis_index_groups=rings)]
    all_to_all x4 -> x3, waiting for transfers between devices: 40 us -> 3.56 us  [exchange(): lax.all_to_all(array, axis_name, split_axis=0, concat_axis=0, tiled=True,...]
    ppermute x1, waiting for transfers between devices: 32.4 us -> 48.4 us  [body(): lax.ppermute(jnp.concatenate([*sent, merged_gate, merged_up], axis=0), 'd...]
    ppermute x1, waiting for transfers between devices: 4.17 us -> 19.1 us  [body(): other = lax.ppermute(other, 'dp', swap)]
    reshape x5 -> x1, local copies, waits for them, and re-layouts: 7.96 us -> 1.29 us  [body(): teacher_down.reshape(HALVES * PAIR, block, ring // PAIR, quarter)]
    concatenate x4 -> x1, other arithmetic: 5.75 us -> 0.21 us  [body(): jnp.concatenate([*sent, merged_gate, merged_up], axis=0)]
    all_to_all x4 -> x3, starting transfers between devices: 29.4 us -> 24.4 us  [exchange(): lax.all_to_all(array, axis_name, split_axis=0, concat_axis=0, tiled=True,...]
  transfers between devices with their start and end apart: 8 -> 6, of which waited for: 7 -> 4; matrix products, arithmetic and copies ran while one was open for 8% -> 3% of each run, Pallas kernels for 2% -> 1%
where the time goes in v2:
time: 228 us; the launch traced here: 226 us
  waiting for transfers between devices  88.4 us (39%)
  blocking collectives  67.1 us (29%)
  starting transfers between devices  28.6 us (13%)
  local copies, waits for them, and re-layouts  15.1 us (7%)
  between operations  14.2 us (6%)
  Pallas kernels  10.1 us (4%)
  other arithmetic  2.86 us (1%)
    all_to_all x3, blocking collectives, exchange(): lax.all_to_all(array, axis_name, split_axis=0, concat_axis=0, tiled=True,...  67.1 us
    ppermute x1, waiting for transfers between devices, body(): lax.ppermute(jnp.concatenate([*sent, merged_gate, merged_up], axis=0), 'd...  48.4 us
    all_to_all x3, starting transfers between devices, exchange(): lax.all_to_all(array, axis_name, split_axis=0, concat_axis=0, tiled=True,...  24.4 us
    ppermute x1, waiting for transfers between devices, body(): other = lax.ppermute(other, 'dp', swap)  19.1 us
    all_gather x1, waiting for transfers between devices, body(): lax.all_gather(turned, 'dp', axis=0, tiled=True, axis_index_groups=rings)  17.3 us
    unnamed x37, local copies, waits for them, and re-layouts  11.6 us
    pallas_call x7, Pallas kernels, call(): pl.pallas_call(kernel, out_shape=outs, in_specs=specs, out_specs=jax.tree...  10.1 us
  transfers between devices with their start and end apart: 6, of which 4 were waited for; matrix products, arithmetic and copies ran while one was open for 3% of the time, Pallas kernels for 1%

profile of v2, /device:TPU:6, one launch (start us, length us, event | category | flops | bytes accessed | tf_op | source)
XLA Modules:
  0.0 226.3 jit_solution(5021647229993570092)
XLA Ops:
  7.2 0.8 copy.13
  7.9 0.8 copy-done.16
  9.4 0.7 shard_map.112
  10.1 13.3 %all-to-all-start = ((bf16[16,8,512]{2,1,0:T(8,128)(2,1)}), bf16[16,8,512]{2,1,0:T(8,128)(2,1)S(1)}, u32[]{:S(2)}, u32[]{:S(2)}) async-start(bf16[16,8,512]{2,1,0:T(8,128)(2,1)} %shard_map.112), calls=%async_computation | async-start | bytes 262144 | tf_op jit(solution)/shard_map/all_to_all | solution.py:237
  23.5 0.9 fusion
  24.4 1.3 copy.16
  25.9 1.5 pad_maximum_fusion
  27.4 3.6 %all-to-all-done = bf16[16,8,512]{2,1,0:T(8,128)(2,1)S(1)} async-done(((bf16[16,8,512]{2,1,0:T(8,128)(2,1)}), bf16[16,8,512]{2,1,0:T(8,128)(2,1)S(1)}, u32[]{:S(2)}, u32[]{:S(2)}) %all-to-all-start) | async-done | bytes 131104 | tf_op jit(solution)/shard_map/all_to_all | solution.py:237
  31.0 1.2 shard_map.113
  32.2 23.4 %all_to_all.30 = bf16[32,16,384]{2,1,0:T(8,128)(2,1)S(1)} all-to-all(bf16[32,16,384]{2,1,0:T(8,128)(2,1)S(1)} %bitcast.19), channel_id=1, replica_groups=mesh['dp'=16,'expert'=32] {'expert'}, dimensions={0} | all-to-all | bytes 786432 | tf_op jit(solution)/shard_map/all_to_all | solution.py:237
  55.6 1.2 shard_map.114
  57.6 6.3 %all-to-all-start.3 = ((bf16[16,2,48,640]{3,2,1,0:T(8,128)(2,1)}), bf16[16,2,48,640]{3,2,1,0:T(8,128)(2,1)S(1)}, u32[]{:S(2)}, u32[]{:S(2)}) async-start(bf16[16,2,48,640]{3,2,1,0:T(8,128)(2,1)} %pad_maximum_fusion), calls=%async_computation.3 | async-start | bytes 3932160 | tf_op jit(solution)/shard_map/all_to_all | solution.py:237
  63.9 1.2 constant_dynamic-slice_fusion
  65.3 2.1 collective-permute-start
  67.4 48.4 %collective-permute-done.come_ref = bf16[6,48,2560]{2,1,0:T(8,128)(2,1)S(1)} collective-permute-done((bf16[6,48,2560]{2,1,0:T(8,128)(2,1)S(1)}, bf16[6,48,2560]{2,1,0:T(8,128)(2,1)S(1)}, u32[]{:S(2)}, u32[]{:S(2)}) %collective-permute-start) | collective-permute-done | bytes 1474592 | tf_op jit(solution)/shard_map/ppermute | solution.py:245
  115.8 1.2 copy-done.4
  116.9 17.3 %all-gather.2.cloned.1.call-done.rows_ref = bf16[2560,512]{1,0:T(8,128)(2,1)} async-done(((bf16[320,512]{1,0:T(8,128)(2,1)}), bf16[2560,512]{1,0:T(8,128)(2,1)}) %all-gather.2.cloned.1.call-update) | async-done | bytes 2621456 | tf_op jit(solution)/shard_map/all_gather | solution.py:273
  134.3 1.7 copy-done
  136.0 1.2 copy-done.3
  137.2 1.4 copy-done.5
  138.6 1.8 shard_map.115
  140.4 0.9 copy-done.9
  142.6 27.7 %all_to_all.31.hidden_ref = bf16[8,4,48,256]{3,2,1,0:T(8,128)(2,1)S(1)} all-to-all(bf16[8,4,48,256]{3,2,1,0:T(8,128)(2,1)} %copy-done.9), channel_id=1, replica_groups={{0,32,64,96,128,160,192,224},{256,288,320,352,384,416,448,480},{1,33,65..., dimensions={0} | all-to-all | bytes 1572864 | tf_op jit(solution)/shard_map/all_to_all | solution.py:237
  170.4 2.0 shard_map.116
  172.4 0.9 copy-done.6
  173.3 15.9 %all_to_all.32.parts_ref = bf16[8,96,256]{2,1,0:T(8,128)(2,1)S(1)} all-to-all(bf16[8,96,256]{2,1,0:T(8,128)(2,1)S(1)} %bitcast.21), channel_id=1, replica_groups={{0,32,64,96,128,160,192,224},{256,288,320,352,384,416,448,480},{1,33,65..., dimensions={0} | all-to-all | bytes 786432 | tf_op jit(solution)/shard_map/all_to_all | solution.py:237
  189.2 4.8 %all-to-all-start.5 = ((bf16[16,48,640]{2,1,0:T(8,128)(2,1)}), bf16[16,48,640]{2,1,0:T(8,128)(2,1)}, u32[]{:S(2)}, u32[]{:S(2)}) async-start(bf16[16,48,640]{2,1,0:T(8,128)(2,1)} %copy-done.6), calls=%async_computation.5 | async-start | bytes 1966080 | tf_op jit(solution)/shard_map/all_to_all | solution.py:237
  194.1 1.0 shard_map.117
  195.1 2.0 collective-permute-start.1
  197.1 19.1 %collective-permute-done.1 = bf16[2,48,2560]{2,1,0:T(8,128)(2,1)S(1)} collective-permute-done((bf16[2,48,2560]{2,1,0:T(8,128)(2,1)S(1)}, bf16[2,48,2560]{2,1,0:T(8,128)(2,1)S(1)}, u32[]{:S(2)}, u32[]{:S(2)}) %collective-permute-start.1) | collective-permute-done | bytes 491552 | tf_op jit(solution)/shard_map/ppermute | solution.py:305
  216.3 1.0 convert_add_fusion
  217.3 2.1 shard_map.118
  (37 shorter events, 3.2 us)
Async XLA Ops:
  7.9 0.8 copy-start.16
  8.7 0.7 copy-start.17
  10.1 20.9 %all-to-all-start = ((bf16[16,8,512]{2,1,0:T(8,128)(2,1)}), bf16[16,8,512]{2,1,0:T(8,128)(2,1)S(1)}, u32[]{:S(2)}, u32[]{:S(2)}) async-start(bf16[16,8,512]{2,1,0:T(8,128)(2,1)} %shard_map.112), calls=%async_computation | async-start | bytes 262144 | tf_op jit(solution)/shard_map/all_to_all | solution.py:237
  23.4 110.8 %all-gather.2.cloned.1.call-start = ((), (), s32[]{:S(2)}) async-start(), calls=%async_computation.6 | async-start | bytes 2949120 | tf_op jit(solution)/shard_map/all_gather | solution.py:273
  56.9 0.7 copy-start.14
  57.5 6.3 %copy-start.2 = (bf16[4,48,2560]{2,1,0:T(8,128)(2,1)S(1)}, bf16[4,48,2560]{2,1,0:T(8,128)(2,1)}, u32[]{:S(2)}) copy-start(bf16[4,48,2560]{2,1,0:T(8,128)(2,1)} %t_gate_ref.1) | copy-start | bytes 2949124
  57.6 85.1 %all-to-all-start.3 = ((bf16[16,2,48,640]{3,2,1,0:T(8,128)(2,1)}), bf16[16,2,48,640]{3,2,1,0:T(8,128)(2,1)S(1)}, u32[]{:S(2)}, u32[]{:S(2)}) async-start(bf16[16,2,48,640]{3,2,1,0:T(8,128)(2,1)} %pad_maximum_fusion), calls=%async_computation.3 | async-start | bytes 3932160 | tf_op jit(solution)/shard_map/all_to_all | solution.py:237
  63.8 1.2 copy-start.7
  63.9 1.2 copy-start.8
  65.3 50.4 %collective-permute-start = (bf16[6,48,2560]{2,1,0:T(8,128)(2,1)S(1)}, bf16[6,48,2560]{2,1,0:T(8,128)(2,1)S(1)}, u32[]{:S(2)}, u32[]{:S(2)}) collective-permute-start(bf16[6,48,2560]{2,1,0:T(8,128)(2,1)S(1)} %pad_maximum_fusion.1), channel_id=1, source_target_pairs={{0,256},{32,288},{64,320},{96,352},{128,384},{160,416},{192,448},{... | collective-permute-start | bytes 4423688 | tf_op jit(solution)/shard_map/ppermute | solution.py:245
  115.8 1.2 copy-start.4
  134.3 1.7 copy-start
  136.0 1.2 copy-start.3
  137.2 1.4 copy-start.5
  140.4 0.9 copy-start.9
  141.3 0.7 copy-start.10
  141.9 0.7 copy-start.12
  142.6 27.8 %copy-start.15 = (bf16[512,128]{1,0:T(8,128)(2,1)S(1)}, bf16[512,128]{1,0:T(8,128)(2,1)}, u32[]{:S(2)}) copy-start(bf16[512,128]{1,0:T(8,128)(2,1)} %copy-done.14) | copy-start | bytes 393220
  170.4 23.7 %copy-start.11 = (f32[96,512]{1,0:T(8,128)S(1)}, f32[96,512]{1,0:T(8,128)}, u32[]{:S(2)}) copy-start(f32[96,512]{1,0:T(8,128)} %copy-done.10) | copy-start | bytes 589828
  170.4 23.7 %copy-start.13 = (f32[96,512]{1,0:T(8,128)S(1)}, f32[96,512]{1,0:T(8,128)}, u32[]{:S(2)}) copy-start(f32[96,512]{1,0:T(8,128)} %copy-done.12) | copy-start | bytes 589828
  172.4 0.9 copy-start.6
  173.3 20.7 %copy-start.1 = (bf16[2560,512]{1,0:T(8,128)(2,1)S(1)}, bf16[2560,512]{1,0:T(8,128)(2,1)}, u32[]{:S(2)}) copy-start(bf16[2560,512]{1,0:T(8,128)(2,1)} %all-gather.2.cloned.1.call-done.rows_ref) | copy-start | bytes 7864324
  189.2 28.1 %all-to-all-start.5 = ((bf16[16,48,640]{2,1,0:T(8,128)(2,1)}), bf16[16,48,640]{2,1,0:T(8,128)(2,1)}, u32[]{:S(2)}, u32[]{:S(2)}) async-start(bf16[16,48,640]{2,1,0:T(8,128)(2,1)} %copy-done.6), calls=%async_computation.5 | async-start | bytes 1966080 | tf_op jit(solution)/shard_map/all_to_all | solution.py:237
  195.1 21.2 %collective-permute-start.1 = (bf16[2,48,2560]{2,1,0:T(8,128)(2,1)S(1)}, bf16[2,48,2560]{2,1,0:T(8,128)(2,1)S(1)}, u32[]{:S(2)}, u32[]{:S(2)}) collective-permute-start(bf16[2,48,2560]{2,1,0:T(8,128)(2,1)S(1)} %get-tuple-element.23), channel_id=1, source_target_pairs={{0,256},{32,288},{64,320},{96,352},{128,384},{160,416},{192,448},{... | collective-permute-start | bytes 1474568 | tf_op jit(solution)/shard_map/ppermute | solution.py:305
Sparse Core Ops, SparseCore 0:
  57.7 76.5 all-gather.1

commit v3 on v2

v3 whole, which is shorter than its diff:
```python
import jax
import jax.numpy as jnp
from jax import lax
from jax.experimental import pallas as pl
from jax.experimental.pallas import tpu as pltpu
from jax.sharding import PartitionSpec as P

HALVES = 2
PAIR = 2
EARLY = (1, 7, 3, 5)
SIDE = 128
BF16 = jnp.bfloat16
F32 = jnp.float32


def dot_nn(a, b):
    return jnp.dot(a, b, preferred_element_type=F32)


def dot_nt(a, b):
    return lax.dot_general(a, b, (((1,), (1,)), ((), ())), preferred_element_type=F32)


def dot_tn(a, b):
    return lax.dot_general(a, b, (((0,), (0,)), ((), ())), preferred_element_type=F32)


def call(kernel, outs, args, scalars=0, far=(), far_outs=(), scratch=(), mib=60):
    def space(i):
        if i < scalars:
            return pl.BlockSpec(memory_space=pltpu.SMEM)
        return pl.BlockSpec(memory_space=pltpu.HBM if i in far else pltpu.VMEM)

    return pl.pallas_call(
        kernel,
        out_shape=outs,
        in_specs=[space(i) for i in range(len(args))],
        out_specs=[
            pl.BlockSpec(memory_space=pltpu.HBM if i in far_outs else pltpu.VMEM)
            for i in range(len(outs))
        ],
        scratch_shapes=scratch,
        compiler_params=pltpu.CompilerParams(vmem_limit_bytes=mib * 1024 * 1024),
        cost_estimate=pl.CostEstimate(
            flops=0,
            bytes_accessed=sum(a.size * a.dtype.itemsize for a in args),
            transcendentals=0,
        ),
    )(*args)


def start_copies(pairs, sems, first=0):
    copies = [
        pltpu.make_async_copy(source, target, sems.at[first + i])
        for i, (source, target) in enumerate(pairs)
    ]
    for copy in copies:
        copy.start()
    return copies


def wait_copies(copies):
    for copy in copies:
        copy.wait()


def columns(total):
    return -(-total // SIDE) * SIDE


def pack_kernel(
    place_ref, ids_ref, token_hbm, weight_hbm, down_ref, merged_ref, out_ref, sent_ref, token_ref, weight_ref, sems
):
    half = place_ref[0] // place_ref[1]
    pairs = [(down_ref.at[PAIR * (1 - half) + m], sent_ref.at[m]) for m in range(PAIR)]
    inputs = start_copies([(token_hbm, token_ref), (weight_hbm, weight_ref)], sems, PAIR + 1)
    copies = start_copies([*pairs, (merged_ref.at[0], sent_ref.at[PAIR])], sems)
    wait_copies(inputs)
    ring = out_ref.shape[0] // HALVES
    count, ranks = ids_ref.shape
    piece = token_ref.shape[1] // ring
    wide = columns(piece)
    lane = lax.broadcasted_iota(jnp.int32, (count, SIDE), 1)
    ids = ids_ref[...].astype(F32)
    weight = weight_ref[...].astype(F32)
    side = jnp.zeros((count, SIDE), F32)
    for k in range(ranks):
        side = jnp.where(lane == k, ids[:, k : k + 1], side)
        side = jnp.where(lane == ranks + k, weight[:, k : k + 1], side)
    side = side.astype(BF16)
    blank = jnp.zeros((count, wide - piece), BF16)
    for i in range(ring):
        part = token_ref[:, i * piece : (i + 1) * piece]
        row = jnp.concatenate([part, blank, side], axis=1)
        for a in range(HALVES):
            out_ref[a * ring + i] = row
    wait_copies(copies)


def slots_kernel(ranks, piece, capacity, place_ref, group_ref, out_ref):
    ring = place_ref[1]
    half = place_ref[0] // ring
    wide = columns(piece)
    count = group_ref.shape[0]
    slots = out_ref.shape[0]
    side = group_ref[:, wide:].astype(F32)
    slot = lax.broadcasted_iota(jnp.int32, (count, slots), 1)
    column, inner = slot // (PAIR * capacity), slot % (PAIR * capacity)
    teacher = (column * HALVES * PAIR + half * PAIR + inner // capacity).astype(F32)
    position = (inner % capacity).astype(F32)
    hits = jnp.zeros((count, slots), F32)
    weight = jnp.zeros((count, slots), F32)
    for k in range(ranks):
        same = side[:, k : k + 1] == teacher
        hits = jnp.where(same, 1.0, hits)
        weight = jnp.where(same, side[:, ranks + k : ranks + k + 1], weight)
    later = lax.broadcasted_iota(jnp.int32, (count, count), 0)
    earlier = lax.broadcasted_iota(jnp.int32, (count, count), 1)
    below = jnp.where(earlier < later, 1.0, 0.0).astype(BF16)
    before = dot_nn(below, hits.astype(BF16))
    chosen = jnp.where((hits > 0.0) & (before == position), 1.0, 0.0)
    lane = lax.broadcasted_iota(jnp.int32, (count, wide), 1)
    mark = jnp.where(lane >= piece, 1.0, 0.0).astype(BF16)
    pick = jnp.concatenate([chosen, chosen * weight], axis=0).astype(BF16)
    value = jnp.concatenate([group_ref[:, :wide], mark], axis=0)
    out_ref[...] = dot_tn(pick, value).astype(BF16)


def turn_kernel(piece, capacity, rows_ref, turned_hbm, weight_hbm, turned_ref, weight_ref, sems):
    count, wide = rows_ref.shape
    source = lax.broadcasted_iota(jnp.int32, (count, count), 0)
    target = lax.broadcasted_iota(jnp.int32, (count, count), 1)
    group, inner = source // (PAIR * capacity), source % (PAIR * capacity)
    goes = (inner // capacity) * (count // PAIR) + group * capacity + inner % capacity
    move = jnp.where(goes == target, 1.0, 0.0).astype(BF16)
    rows = rows_ref[...]
    turned_ref[...] = dot_tn(rows, move)[:piece].astype(BF16)
    copies = start_copies([(turned_ref, turned_hbm)], sems)
    weight_ref[...] = dot_tn(move, rows[:, wide - SIDE :]).astype(BF16)
    copies += start_copies([(weight_ref, weight_hbm)], sems, 1)
    wait_copies(copies)


def silu_split(value):
    logistic = jax.nn.sigmoid(value)
    return value * logistic, logistic * (1.0 + value * (1.0 - logistic))


def hidden_kernel(
    place_ref,
    rows_ref,
    t_gate_ref,
    t_up_ref,
    m_gate_ref,
    m_up_ref,
    come_ref,
    out_ref,
    silu_ref,
    slope_ref,
    row_buf,
    weight_buf,
    sems,
):
    ring = place_ref[1]
    half = place_ref[0] // ring
    block = m_gate_ref.shape[1]
    units = 2 * block
    span = rows_ref.shape[1] // PAIR
    places = out_ref.shape[0] // PAIR

    def weights(at, own_gate, come_gate, own_up, come_up):
        parts = (own_gate, come_gate, own_up, come_up)
        return [
            (part, weight_buf.at[at, pl.ds(i * block, block)]) for i, part in enumerate(parts)
        ]

    copies = []
    for m in range(PAIR):
        lanes = pl.ds(m * span, span)
        own = PAIR * half + m
        pairs = [(rows_ref.at[:, lanes], row_buf.at[m])]
        pairs += weights(
            m, t_gate_ref.at[own], come_ref.at[m], t_up_ref.at[own], come_ref.at[PAIR + m]
        )
        copies.append(start_copies(pairs, sems, 5 * m))
        if m == 0:
            pairs = weights(
                PAIR,
                m_gate_ref.at[0],
                come_ref.at[2 * PAIR],
                m_up_ref.at[0],
                come_ref.at[2 * PAIR + 1],
            )
            student_copies = start_copies(pairs, sems, 5 * PAIR)
    for m in range(PAIR):
        lanes = slice(m * span, (m + 1) * span)
        wait_copies(copies[m])
        rows = row_buf[m]
        value = dot_nn(weight_buf[m], rows)
        t_silu, _ = silu_split(value[:units])
        teacher = (t_silu * value[units:]).astype(BF16)
        if m == 0:
            wait_copies(student_copies)
        value = dot_nn(weight_buf[PAIR], rows)
        s_silu, s_slope = silu_split(value[:units])
        up = value[units:]
        student = (s_silu * up).astype(BF16)
        for i in range(places):
            at = m * places + i
            out_ref[at, 0] = student[:block]
            out_ref[at, 1] = student[block:]
            out_ref[at, 2] = teacher[:block]
            out_ref[at, 3] = teacher[block:]
        silu_ref[:, lanes] = s_silu
        slope_ref[:, lanes] = up * s_slope


def share_kernel(ring, place_ref, down_ref, merged_ref, came_ref, *refs):
    out_refs, sems = refs[:ring], refs[ring]
    half, at = place_ref[0] // ring, place_ref[0] % ring
    block = merged_ref.shape[1]
    quarter = out_refs[0].shape[2]
    pairs = []
    for k, out_ref in enumerate(out_refs):
        there = (at + k) % ring
        teacher = there // (ring // PAIR)
        start = pl.multiple_of(there % (ring // PAIR) * quarter, SIDE)
        span = pl.ds(start, quarter)
        pairs += [
            (down_ref.at[PAIR * half + teacher, :, span], out_ref.at[0, pl.ds(0, block)]),
            (came_ref.at[teacher, :, span], out_ref.at[0, pl.ds(block, block)]),
            (merged_ref.at[0, :, span], out_ref.at[1, pl.ds(0, block)]),
            (came_ref.at[PAIR, :, span], out_ref.at[1, pl.ds(block, block)]),
        ]
    wait_copies(start_copies(pairs, sems))


def gap_kernel(ring, place_ref, hidden_ref, weight_ref, *refs):
    down_refs = refs[:ring]
    grad_hbm, kept_ref, other_hbm, t_buf, m_buf, grad_ref, other_ref, sems = refs[ring:]
    block = hidden_ref.shape[2]
    units = 2 * block
    copies = []
    for i, buf in enumerate((t_buf, m_buf)):
        pairs = [
            (down_ref.at[i], buf.at[pl.ds(k * units, units)])
            for k, down_ref in enumerate(down_refs)
        ]
        copies.append(start_copies(pairs, sems, ring * i))
    span = hidden_ref.shape[3]
    at = place_ref[0] % ring
    second = at // (ring // PAIR)
    back = [(at + ring - k) % ring for k in range(ring)]
    student = jnp.concatenate([hidden_ref[i, a] for i in back for a in (0, 1)], axis=0)
    teacher = jnp.concatenate([hidden_ref[i, a] for i in back for a in (2, 3)], axis=0)
    wait_copies(copies[0])
    gap = -dot_tn(teacher, t_buf[...])
    wait_copies(copies[1])
    m_down = m_buf[...]
    gap += dot_tn(student, m_down)
    start = pl.multiple_of(second * span, span)
    weight = weight_ref[pl.ds(start, span), SIDE - 1 : SIDE].astype(F32)
    slot_grad = (weight * gap).astype(BF16)
    grad = dot_nt(m_down, slot_grad).astype(BF16)
    for k, i in enumerate(back):
        grad_ref[i] = grad[k * units : (k + 1) * units]
    copies = start_copies([(grad_ref, grad_hbm)], sems, 2 * ring)
    down_grad = dot_nn(student, slot_grad).astype(BF16)
    for k, i in enumerate(back):
        own, other = 2 * k * block, (2 * k + 1) * block
        kept_ref[i] = down_grad[own:other]
        other_ref[i] = down_grad[other : other + block]
    copies += start_copies([(other_ref, other_hbm)], sems, 2 * ring + 1)
    wait_copies(copies)


def grads_kernel(
    parts_ref,
    rows_ref,
    silu_hbm,
    slope_hbm,
    own_hbm,
    other_hbm,
    silu_ref,
    slope_ref,
    own_ref,
    other_ref,
    sems,
):
    block = own_ref.shape[1]
    places = parts_ref.shape[0] // PAIR
    inputs = start_copies([(silu_hbm, silu_ref), (slope_hbm, slope_ref)], sems)
    sums = []
    for m in range(PAIR):
        total = parts_ref[m * places].astype(F32)
        for i in range(1, places):
            total += parts_ref[m * places + i].astype(F32)
        sums.append(total)
    total = jnp.concatenate(sums, axis=1)
    wait_copies(inputs)
    gate = (total * slope_ref[...]).astype(BF16)
    up = (total * silu_ref[...]).astype(BF16)
    rows = rows_ref[...]
    grads = dot_nt(jnp.concatenate([gate[block:], up[block:]], axis=0), rows)
    other_ref[0] = grads[:block].astype(BF16)
    other_ref[1] = grads[block:].astype(BF16)
    copies = start_copies([(other_ref, other_hbm)], sems, 2)
    grads = dot_nt(jnp.concatenate([gate[:block], up[:block]], axis=0), rows)
    own_ref[0] = grads[:block]
    own_ref[1] = grads[block:]
    copies += start_copies([(own_ref, own_hbm)], sems, 3)
    wait_copies(copies)


def down_sum_kernel(parts_ref, out_ref):
    count, _, piece = parts_ref.shape
    quarters = out_ref.shape[1] // piece
    for q in range(quarters):
        total = parts_ref[q].astype(F32)
        for i in range(q + quarters, count, quarters):
            total += parts_ref[i].astype(F32)
        out_ref[:, q * piece : (q + 1) * piece] = total


def body(
    tokens,
    teacher_ids,
    route_weight,
    teacher_gate,
    teacher_up,
    teacher_down,
    merged_gate,
    merged_up,
    merged_down,
):
    n_dp = lax.axis_size("dp")
    experts = lax.axis_size("expert")
    ring = n_dp // HALVES
    features = tokens.shape[2]
    capacity = tokens.shape[1]
    ranks = teacher_ids.shape[2]
    block = merged_gate.shape[1]
    piece = features // ring
    quarter = features * PAIR // ring
    rows = experts * PAIR * capacity
    axis = lax.axis_index("dp").astype(jnp.int32)
    half = axis // ring
    place = jnp.stack([axis, jnp.int32(ring)])
    rings = [[a * ring + i for i in range(ring)] for a in range(HALVES)]
    swap = [(a * ring + i, (1 - a) * ring + i) for a in range(HALVES) for i in range(ring)]

    turns = [
        [(a * ring + i, a * ring + (i + k) % ring) for a in range(HALVES) for i in range(ring)]
        for k in range(ring)
    ]

    def exchange(array, axis_name, groups=None):
        return lax.all_to_all(
            array, axis_name, split_axis=0, concat_axis=0, tiled=True, axis_index_groups=groups
        )

    def halves(array, which):
        return lax.dynamic_slice_in_dim(array, PAIR * which, PAIR, axis=0)

    packets, sent = call(
        pack_kernel,
        (
            jax.ShapeDtypeStruct((n_dp, capacity, columns(piece) + SIDE), BF16),
            jax.ShapeDtypeStruct((PAIR + 1, block, features), BF16),
        ),
        (place, teacher_ids[0], tokens[0], route_weight[0], teacher_down, merged_down),
        scalars=1,
        far=range(2, 6),
        far_outs=(1,),
        scratch=[
            pltpu.VMEM((capacity, features), BF16),
            pltpu.VMEM((capacity, ranks), BF16),
            pltpu.SemaphoreType.DMA((PAIR + 3,)),
        ],
    )
    came = lax.ppermute(sent, "dp", swap)
    group = exchange(packets, "dp").reshape(n_dp * capacity, columns(piece) + SIDE)

    group, came = lax.optimization_barrier((group, came))
    (slots,) = call(
        lambda *refs: slots_kernel(ranks, piece, capacity, *refs),
        (jax.ShapeDtypeStruct((rows, columns(piece)), BF16),),
        (place, group),
        scalars=1,
    )
    slots = exchange(slots.reshape(experts, PAIR * capacity, columns(piece)), "expert")

    shares = call(
        lambda *refs: share_kernel(ring, *refs),
        tuple(jax.ShapeDtypeStruct((2, 2 * block, quarter), BF16) for _ in range(ring)),
        (place, teacher_down, merged_down, came),
        scalars=1,
        far=(1, 2, 3),
        far_outs=range(ring),
        scratch=[pltpu.SemaphoreType.DMA((4 * ring,))],
    )
    down = [
        shares[k] if k == 0 else lax.ppermute(shares[k], "dp", turns[k]) for k in range(ring)
    ]
    early = [down[k] for k in EARLY]
    slots, early = lax.optimization_barrier((slots, early))
    for k, array in zip(EARLY, early):
        down[k] = array

    come = lax.ppermute(
        jnp.concatenate(
            [halves(teacher_gate, 1 - half), halves(teacher_up, 1 - half), merged_gate, merged_up],
            axis=0,
        ),
        "dp",
        swap,
    )
    turned, weight = call(
        lambda *refs: turn_kernel(piece, capacity, *refs),
        (jax.ShapeDtypeStruct((piece, rows), BF16), jax.ShapeDtypeStruct((rows, SIDE), BF16)),
        (slots.reshape(rows, columns(piece)),),
        far_outs=(0, 1),
        scratch=[
            pltpu.VMEM((piece, rows), BF16),
            pltpu.VMEM((rows, SIDE), BF16),
            pltpu.SemaphoreType.DMA((2,)),
        ],
        mib=16,
    )
    turned = lax.all_gather(turned, "dp", axis=0, tiled=True, axis_index_groups=rings)
    late = [k for k in range(1, ring) if k not in EARLY]
    turned, arrays = lax.optimization_barrier((turned, [down[k] for k in late]))
    for k, array in zip(late, arrays):
        down[k] = array

    hidden, silu, slope = call(
        hidden_kernel,
        (
            jax.ShapeDtypeStruct((ring, 4, block, rows // PAIR), BF16),
            jax.ShapeDtypeStruct((2 * block, rows), F32),
            jax.ShapeDtypeStruct((2 * block, rows), F32),
        ),
        (place, turned, teacher_gate, teacher_up, merged_gate, merged_up, come),
        scalars=1,
        far=range(1, 7),
        scratch=[
            pltpu.VMEM((PAIR, features, rows // PAIR), BF16),
            pltpu.VMEM((PAIR + 1, 4 * block, features), BF16),
            pltpu.SemaphoreType.DMA((5 * PAIR + 4,)),
        ],
    )
    hidden = exchange(hidden, "dp", rings)
    hidden_grad, kept_down, other_down = call(
        lambda *refs: gap_kernel(ring, *refs),
        (
            jax.ShapeDtypeStruct((ring, 2 * block, rows // PAIR), BF16),
            jax.ShapeDtypeStruct((ring, block, quarter), BF16),
            jax.ShapeDtypeStruct((ring, block, quarter), BF16),
        ),
        (place, hidden, weight, *down),
        scalars=1,
        far=range(3, 3 + ring),
        far_outs=(0, 2),
        scratch=[
            pltpu.VMEM((n_dp * block, quarter), BF16),
            pltpu.VMEM((n_dp * block, quarter), BF16),
            pltpu.VMEM((ring, 2 * block, rows // PAIR), BF16),
            pltpu.VMEM((ring, block, quarter), BF16),
            pltpu.SemaphoreType.DMA((2 * ring + 2,)),
        ],
    )
    other_down = lax.ppermute(other_down, "dp", swap)
    parts = exchange(hidden_grad, "dp", rings)
    down_grad = exchange((kept_down.astype(F32) + other_down.astype(F32)).astype(BF16), "dp", rings)
    own, other = call(
        grads_kernel,
        (
            jax.ShapeDtypeStruct((2, block, features), F32),
            jax.ShapeDtypeStruct((2, block, features), BF16),
        ),
        (parts, turned, silu, slope),
        far=(2, 3),
        far_outs=(0, 1),
        scratch=[
            pltpu.VMEM((2 * block, rows), F32),
            pltpu.VMEM((2 * block, rows), F32),
            pltpu.VMEM((2, block, features), F32),
            pltpu.VMEM((2, block, features), BF16),
            pltpu.SemaphoreType.DMA((4,)),
        ],
    )
    other = lax.ppermute(other, "dp", swap)
    (grad_down,) = call(
        down_sum_kernel, (jax.ShapeDtypeStruct((block, features), F32),), (down_grad,), mib=16
    )
    grad_gate = own[:1] + other[:1].astype(F32)
    grad_up = own[1:] + other[1:].astype(F32)
    return grad_gate, grad_up, grad_down[None]


def solution(mesh):
    placed = (P("expert", "dp", None),) * 9
    return jax.shard_map(
        body,
        mesh=mesh,
        in_specs=placed,
        out_specs=(P("expert", "dp", None),) * 3,
        check_vma=False,
    )
```

time: 228 us -> 322 us (1.41)
  Pallas kernels: 10.1 us -> 108 us
  starting transfers between devices: 28.6 us -> 65.5 us
  blocking collectives: 67.1 us -> 47.3 us
  local copies, waits for them, and re-layouts: 15.1 us -> 4.71 us
  waiting for transfers between devices: 88.4 us -> 78.2 us
    pallas_call x7 -> x8, Pallas kernels: 10.1 us -> 108 us  [call(): pl.pallas_call(kernel, out_shape=outs, in_specs=[space(i) for i in range(...]
    ppermute x1 -> x10, starting transfers between devices: 2.08 us -> 45.6 us  [the longest x7 34.9 us: body(): lax.ppermute(shares[k], 'dp', turns[k])]
    all_to_all x3 -> x2, blocking collectives: 67.1 us -> 47.3 us  [exchange(): lax.all_to_all(array, axis_name, split_axis=0, concat_axis=0, tiled=True,...]
    ppermute x1, waiting for transfers between devices: 19.1 us -> 4.01 us  [body(): other = lax.ppermute(other, 'dp', swap)]
    ppermute x1 -> x10, waiting for transfers between devices: 48.4 us -> 35 us  [the longest x7 35 us: body(): lax.ppermute(shares[k], 'dp', turns[k])]
    all_to_all x3, waiting for transfers between devices: 3.56 us -> 15.8 us  [exchange(): lax.all_to_all(array, axis_name, split_axis=0, concat_axis=0, tiled=True,...]
    all_to_all x3, starting transfers between devices: 24.4 us -> 15.7 us  [exchange(): lax.all_to_all(array, axis_name, split_axis=0, concat_axis=0, tiled=True,...]
    unnamed x37, local copies, waits for them, and re-layouts: 11.6 us -> 4.64 us
  transfers between devices with their start and end apart: 6 -> 15, of which waited for: 4 -> 8; matrix products, arithmetic and copies ran while one was open for 3% -> 1% of each run, Pallas kernels for 1% -> 21%
where the time goes in v3:
time: 322 us; the launch traced here: 321 us
  Pallas kernels  108 us (34%)
  waiting for transfers between devices  78.2 us (24%)
  starting transfers between devices  65.5 us (20%)
  blocking collectives  47.3 us (15%)
  between operations  14.4 us (4%)
  local copies, waits for them, and re-layouts  4.71 us (1%)
    pallas_call x8, Pallas kernels, call(): pl.pallas_call(kernel, out_shape=outs, in_specs=[space(i) for i in range(...  108 us
    all_to_all x2, blocking collectives, exchange(): lax.all_to_all(array, axis_name, split_axis=0, concat_axis=0, tiled=True,...  47.3 us
    ppermute x7, waiting for transfers between devices, body(): lax.ppermute(shares[k], 'dp', turns[k])  35 us
    ppermute x7, starting transfers between devices, body(): lax.ppermute(shares[k], 'dp', turns[k])  34.9 us
    all_gather x1, waiting for transfers between devices, body(): lax.all_gather(turned, 'dp', axis=0, tiled=True, axis_index_groups=rings)  23.4 us
    all_to_all x3, waiting for transfers between devices, exchange(): lax.all_to_all(array, axis_name, split_axis=0, concat_axis=0, tiled=True,...  15.8 us
    all_to_all x3, starting transfers between devices, exchange(): lax.all_to_all(array, axis_name, split_axis=0, concat_axis=0, tiled=True,...  15.7 us
  transfers between devices with their start and end apart: 15, of which 8 were waited for; matrix products, arithmetic and copies ran while one was open for 1% of the time, Pallas kernels for 21%

profile of v3, /device:TPU:6, one launch (start us, length us, event | category | flops | bytes accessed | tf_op | source)
XLA Modules:
  0.0 321.1 jit_solution(17849007134387214636)
XLA Ops:
  7.2 1.4 copy.12
  9.2 24.8 %shard_map.112 = (bf16[16,8,512]{2,1,0:T(8,128)(2,1)}, bf16[3,48,2560]{2,1,0:T(8,128)(2,1)}) custom-call(s32[2]{0:T(128)} %pad_add_fusion.place_ref.refs_0_, s32[8,6]{1,0:T(8,128)} %bitcast.13, bf16[8,2560]{1,0:T(8,128)(2,1)} %bitcast.12, bf16[8,6]{1,0:T(8,128)(2,1)} %bitcast.14, bf16[4,48,2560]{2,1,0:T(8,128)(2,1)} %refs_1_.1, bf16[1,48,2560]{2,1,0:T(8,128)(2,1)} %refs_2_.1), custom_call_target="tpu_custom_call" | custom-call | bytes 1270056 | tf_op jit(solution)/shard_map/pallas_call | solution.py:34
  34.0 3.3 %collective-permute-start = (bf16[3,48,2560]{2,1,0:T(8,128)(2,1)}, bf16[3,48,2560]{2,1,0:T(8,128)(2,1)S(1)}, u32[]{:S(2)}, u32[]{:S(2)}) collective-permute-start(bf16[3,48,2560]{2,1,0:T(8,128)(2,1)} %get-tuple-element.35), channel_id=1, source_target_pairs={{0,256},{32,288},{64,320},{96,352},{128,384},{160,416},{192,448},{... | collective-permute-start | bytes 2211848 | tf_op jit(solution)/shard_map/ppermute | solution.py:381
  37.3 21.0 %all_to_all.25 = bf16[16,8,512]{2,1,0:T(8,128)(2,1)} all-to-all(bf16[16,8,512]{2,1,0:T(8,128)(2,1)} %get-tuple-element.34), channel_id=1, replica_groups=mesh['dp'=16,'expert'=32] {'dp'}, dimensions={0} | all-to-all | bytes 262144 | tf_op jit(solution)/shard_map/all_to_all | solution.py:358
  58.3 2.5 shard_map.113
  60.8 8.7 %all-to-all-start.1 = ((bf16[32,16,384]{2,1,0:T(8,128)(2,1)}), bf16[32,16,384]{2,1,0:T(8,128)(2,1)S(1)}, u32[]{:S(2)}, u32[]{:S(2)}) async-start(bf16[32,16,384]{2,1,0:T(8,128)(2,1)} %bitcast.9), calls=%async_computation.1 | async-start | bytes 786432 | tf_op jit(solution)/shard_map/all_to_all | solution.py:358
  69.6 61.8 %shard_map.114 = (bf16[2,96,640]{2,1,0:T(8,128)(2,1)}, bf16[2,96,640]{2,1,0:T(8,128)(2,1)}, bf16[2,96,640]{2,1,0:T(8,128)(2,1)}, bf16[2,96,640]{2,1,0:T(8,128)(2...) custom-call(s32[2]{0:T(128)} %pad_add_fusion.place_ref.refs_0_, ...), custom_call_target="tpu_custom_call" | custom-call | bytes 1966088 | tf_op jit(solution)/shard_map/pallas_call | solution.py:34
  131.4 3.5 %collective-permute-start.1 = (bf16[2,96,640]{2,1,0:T(8,128)(2,1)}, bf16[2,96,640]{2,1,0:T(8,128)(2,1)S(1)}, u32[]{:S(2)}, u32[]{:S(2)}) collective-permute-start(bf16[2,96,640]{2,1,0:T(8,128)(2,1)} %get-tuple-element.38), channel_id=1, source_target_pairs={{0,32},{32,64},{64,96},{96,128},{128,160},{160,192},{192,224},{224... | collective-permute-start | bytes 737288 | tf_op jit(solution)/shard_map/ppermute | solution.py:403
  134.9 8.6 %collective-permute-start.2 = (bf16[2,96,640]{2,1,0:T(8,128)(2,1)}, bf16[2,96,640]{2,1,0:T(8,128)(2,1)S(1)}, u32[]{:S(2)}, u32[]{:S(2)}) collective-permute-start(bf16[2,96,640]{2,1,0:T(8,128)(2,1)} %get-tuple-element.39), channel_id=1, source_target_pairs={{0,224},{32,0},{64,32},{96,64},{128,96},{160,128},{192,160},{224,1... | collective-permute-start | bytes 737288 | tf_op jit(solution)/shard_map/ppermute | solution.py:403
  143.5 2.4 collective-permute-start.3
  145.9 6.4 %collective-permute-start.4 = (bf16[2,96,640]{2,1,0:T(8,128)(2,1)}, bf16[2,96,640]{2,1,0:T(8,128)(2,1)}, u32[]{:S(2)}, u32[]{:S(2)}) collective-permute-start(bf16[2,96,640]{2,1,0:T(8,128)(2,1)} %get-tuple-element.41), channel_id=1, source_target_pairs={{0,160},{32,192},{64,224},{96,0},{128,32},{160,64},{192,96},{224,1... | collective-permute-start | bytes 737288 | tf_op jit(solution)/shard_map/ppermute | solution.py:403
  152.4 11.2 %collective-permute-done.3.refs_6_ = bf16[2,96,640]{2,1,0:T(8,128)(2,1)S(1)} collective-permute-done((bf16[2,96,640]{2,1,0:T(8,128)(2,1)}, bf16[2,96,640]{2,1,0:T(8,128)(2,1)S(1)}, u32[]{:S(2)}, u32[]{:S(2)}) %collective-permute-start.3) | collective-permute-done | bytes 245792 | tf_op jit(solution)/shard_map/ppermute | solution.py:403
  164.3 3.1 collective-permute-done.4.refs_8_
  167.4 1.2 shard_map.115
  169.7 3.4 %collective-permute-start.8 = (bf16[6,48,2560]{2,1,0:T(8,128)(2,1)S(1)}, bf16[6,48,2560]{2,1,0:T(8,128)(2,1)S(1)}, u32[]{:S(2)}, u32[]{:S(2)}) collective-permute-start(bf16[6,48,2560]{2,1,0:T(8,128)(2,1)S(1)} %pad_maximum_fusion), channel_id=1, source_target_pairs={{0,256},{32,288},{64,320},{96,352},{128,384},{160,416},{192,448},{... | collective-permute-start | bytes 4423688 | tf_op jit(solution)/shard_map/ppermute | solution.py:410
  173.2 6.3 %collective-permute-start.5 = (bf16[2,96,640]{2,1,0:T(8,128)(2,1)S(1)}, bf16[2,96,640]{2,1,0:T(8,128)(2,1)S(1)}, u32[]{:S(2)}, u32[]{:S(2)}) collective-permute-start(bf16[2,96,640]{2,1,0:T(8,128)(2,1)S(1)} %copy-done.17), channel_id=1, source_target_pairs={{0,64},{32,96},{64,128},{96,160},{128,192},{160,224},{192,0},{224,... | collective-permute-start | bytes 737288 | tf_op jit(solution)/shard_map/ppermute | solution.py:403
  179.5 2.9 collective-permute-start.6
  182.4 4.8 %collective-permute-start.7 = (bf16[2,96,640]{2,1,0:T(8,128)(2,1)S(1)}, bf16[2,96,640]{2,1,0:T(8,128)(2,1)}, u32[]{:S(2)}, u32[]{:S(2)}) collective-permute-start(bf16[2,96,640]{2,1,0:T(8,128)(2,1)S(1)} %copy-done.15), channel_id=1, source_target_pairs={{0,192},{32,224},{64,0},{96,32},{128,64},{160,96},{192,128},{224,1... | collective-permute-start | bytes 737288 | tf_op jit(solution)/shard_map/ppermute | solution.py:403
  187.2 9.9 %collective-permute-done.5.refs_5_ = bf16[2,96,640]{2,1,0:T(8,128)(2,1)S(1)} collective-permute-done((bf16[2,96,640]{2,1,0:T(8,128)(2,1)S(1)}, bf16[2,96,640]{2,1,0:T(8,128)(2,1)S(1)}, u32[]{:S(2)}, u32[]{:S(2)}) %collective-permute-start.5) | collective-permute-done | bytes 245792 | tf_op jit(solution)/shard_map/ppermute | solution.py:403
  197.1 10.7 %collective-permute-done.6.refs_7_ = bf16[2,96,640]{2,1,0:T(8,128)(2,1)S(1)} collective-permute-done((bf16[2,96,640]{2,1,0:T(8,128)(2,1)S(1)}, bf16[2,96,640]{2,1,0:T(8,128)(2,1)S(1)}, u32[]{:S(2)}, u32[]{:S(2)}) %collective-permute-start.6) | collective-permute-done | bytes 245792 | tf_op jit(solution)/shard_map/ppermute | solution.py:403
  207.8 23.4 %all-gather.2.cloned.1.call-done.rows_ref = bf16[2560,512]{1,0:T(8,128)(2,1)} async-done(((bf16[320,512]{1,0:T(8,128)(2,1)}), bf16[2560,512]{1,0:T(8,128)(2,1)}) %all-gather.2.cloned.1.call-update) | async-done | bytes 2621456 | tf_op jit(solution)/shard_map/all_gather | solution.py:430
  232.3 5.4 %shard_map.116 = (bf16[8,4,48,256]{3,2,1,0:T(8,128)(2,1)}, f32[96,512]{1,0:T(8,128)}, f32[96,512]{1,0:T(8,128)}) custom-call(s32[2]{0:T(128)} %pad_add_fusion.place_ref.refs_0_, bf16[2560,512]{1,0:T(8,128)(2,1)} %all-gather.2.cloned.1.call-done.rows_ref, bf16[4,48,2560]{2,1,0:T(8,128)(2,1)} %t_gate_ref.1, bf16[4,48,2560]{2,1,0:T(8,128)(2,1)} %t_up_ref.1, ...), custom_call_target="tpu_custom_call" | custom-call | bytes 6553608 | tf_op jit(solution)/shard_map/pallas_call | solution.py:34
  237.8 26.3 %all_to_all.26.refs_1_ = bf16[8,4,48,256]{3,2,1,0:T(8,128)(2,1)} all-to-all(bf16[8,4,48,256]{3,2,1,0:T(8,128)(2,1)} %get-tuple-element.48), channel_id=1, replica_groups={{0,32,64,96,128,160,192,224},{256,288,320,352,384,416,448,480},{1,33,65..., dimensions={0} | all-to-all | bytes 1572864 | tf_op jit(solution)/shard_map/all_to_all | solution.py:358
  264.1 6.0 %shard_map.117 = (bf16[8,96,256]{2,1,0:T(8,128)(2,1)}, bf16[8,48,640]{2,1,0:T(8,128)(2,1)}, bf16[8,48,640]{2,1,0:T(8,128)(2,1)}) custom-call(s32[2]{0:T(128)} %pad_add_fusion.place_ref.refs_0_, bf16[8,4,48,256]{3,2,1,0:T(8,128)(2,1)} %all_to_all.26.refs_1_, bf16[512,128]{1,0:T(8,128)(2,1)} %copy-done, bf16[2,96,640]{2,1,0:T(8,128)(2,1)} %get-tuple-element.50.refs_3_, ...), custom_call_target="tpu_custom_call" | custom-call | bytes 2883592 | tf_op jit(solution)/shard_map/pallas_call | solution.py:34
  270.1 3.5 %all-to-all-start.3 = ((bf16[8,96,256]{2,1,0:T(8,128)(2,1)}), bf16[8,96,256]{2,1,0:T(8,128)(2,1)S(1)}, u32[]{:S(2)}, u32[]{:S(2)}) async-start(bf16[8,96,256]{2,1,0:T(8,128)(2,1)} %get-tuple-element.58), calls=%async_computation.3 | async-start | bytes 786432 | tf_op jit(solution)/shard_map/all_to_all | solution.py:358
  273.5 4.0 %collective-permute-start.10 = (bf16[8,48,640]{2,1,0:T(8,128)(2,1)}, bf16[8,48,640]{2,1,0:T(8,128)(2,1)S(1)}, u32[]{:S(2)}, u32[]{:S(2)}) collective-permute-start(bf16[8,48,640]{2,1,0:T(8,128)(2,1)} %get-tuple-element.64), channel_id=1, source_target_pairs={{0,256},{32,288},{64,320},{96,352},{128,384},{160,416},{192,448},{... | collective-permute-start | bytes 1474568 | tf_op jit(solution)/shard_map/ppermute | solution.py:472
  277.6 8.0 %all-to-all-done.3.parts_ref = bf16[8,96,256]{2,1,0:T(8,128)(2,1)S(1)} async-done(((bf16[8,96,256]{2,1,0:T(8,128)(2,1)}), bf16[8,96,256]{2,1,0:T(8,128)(2,1)S(1)}, u32[]{:S(2)}, u32[]{:S(2)}) %all-to-all-start.3) | async-done | bytes 393248 | tf_op jit(solution)/shard_map/all_to_all | solution.py:358
  286.3 5.7 %shard_map.118 = (f32[2,48,2560]{2,1,0:T(8,128)}, bf16[2,48,2560]{2,1,0:T(8,128)(2,1)}) custom-call(bf16[8,96,256]{2,1,0:T(8,128)(2,1)} %copy-done.3, bf16[2560,512]{1,0:T(8,128)(2,1)} %all-gather.2.cloned.1.call-done.rows_ref, f32[96,512]{1,0:T(8,128)} %get-tuple-element.59.silu_hbm, f32[96,512]{1,0:T(8,128)} %get-tuple-element.60.slope_hbm), custom_call_target="tpu_custom_call" | custom-call | bytes 3407872 | tf_op jit(solution)/shard_map/pallas_call | solution.py:34
  292.0 4.1 %collective-permute-start.9 = (bf16[2,48,2560]{2,1,0:T(8,128)(2,1)}, bf16[2,48,2560]{2,1,0:T(8,128)(2,1)S(1)}, u32[]{:S(2)}, u32[]{:S(2)}) collective-permute-start(bf16[2,48,2560]{2,1,0:T(8,128)(2,1)} %get-tuple-element.62), channel_id=1, source_target_pairs={{0,256},{32,288},{64,320},{96,352},{128,384},{160,416},{192,448},{... | collective-permute-start | bytes 1474568 | tf_op jit(solution)/shard_map/ppermute | solution.py:492
  297.0 3.5 %all-to-all-start.4 = ((bf16[8,48,640]{2,1,0:T(8,128)(2,1)}), bf16[8,48,640]{2,1,0:T(8,128)(2,1)S(1)}, u32[]{:S(2)}, u32[]{:S(2)}) async-start(bf16[8,48,640]{2,1,0:T(8,128)(2,1)} %add_convert_fusion), calls=%async_computation.4 | async-start | bytes 983040 | tf_op jit(solution)/shard_map/all_to_all | solution.py:358
  300.5 4.0 %collective-permute-done.9 = bf16[2,48,2560]{2,1,0:T(8,128)(2,1)S(1)} collective-permute-done((bf16[2,48,2560]{2,1,0:T(8,128)(2,1)}, bf16[2,48,2560]{2,1,0:T(8,128)(2,1)S(1)}, u32[]{:S(2)}, u32[]{:S(2)}) %collective-permute-start.9) | collective-permute-done | bytes 491552 | tf_op jit(solution)/shard_map/ppermute | solution.py:492
  305.6 7.8 %all-to-all-done.4.parts_ref = bf16[8,48,640]{2,1,0:T(8,128)(2,1)S(1)} async-done(((bf16[8,48,640]{2,1,0:T(8,128)(2,1)}), bf16[8,48,640]{2,1,0:T(8,128)(2,1)S(1)}, u32[]{:S(2)}, u32[]{:S(2)}) %all-to-all-start.4) | async-done | bytes 491552 | tf_op jit(solution)/shard_map/all_to_all | solution.py:358
  (51 shorter events, 7.0 us)
Async XLA Ops:
  34.0 24.3 %collective-permute-start = (bf16[3,48,2560]{2,1,0:T(8,128)(2,1)}, bf16[3,48,2560]{2,1,0:T(8,128)(2,1)S(1)}, u32[]{:S(2)}, u32[]{:S(2)}) collective-permute-start(bf16[3,48,2560]{2,1,0:T(8,128)(2,1)} %get-tuple-element.35), channel_id=1, source_target_pairs={{0,256},{32,288},{64,320},{96,352},{128,384},{160,416},{192,448},{... | collective-permute-start | bytes 2211848 | tf_op jit(solution)/shard_map/ppermute | solution.py:381
  58.3 11.3 %copy-start.8 = (bf16[3,48,2560]{2,1,0:T(8,128)(2,1)}, bf16[3,48,2560]{2,1,0:T(8,128)(2,1)S(1)}, u32[]{:S(2)}) copy-start(bf16[3,48,2560]{2,1,0:T(8,128)(2,1)S(1)} %collective-permute-done.refs_3_) | copy-start | bytes 2211844
  60.8 106.6 %all-to-all-start.1 = ((bf16[32,16,384]{2,1,0:T(8,128)(2,1)}), bf16[32,16,384]{2,1,0:T(8,128)(2,1)S(1)}, u32[]{:S(2)}, u32[]{:S(2)}) async-start(bf16[32,16,384]{2,1,0:T(8,128)(2,1)} %bitcast.9), calls=%async_computation.1 | async-start | bytes 786432 | tf_op jit(solution)/shard_map/all_to_all | solution.py:358
  69.5 99.8 %copy-start.1 = (bf16[4,48,2560]{2,1,0:T(8,128)(2,1)S(1)}, bf16[4,48,2560]{2,1,0:T(8,128)(2,1)}, u32[]{:S(2)}) copy-start(bf16[4,48,2560]{2,1,0:T(8,128)(2,1)} %t_gate_ref.1) | copy-start | bytes 2949124
  69.5 99.8 %copy-start.2 = (bf16[4,48,2560]{2,1,0:T(8,128)(2,1)S(1)}, bf16[4,48,2560]{2,1,0:T(8,128)(2,1)}, u32[]{:S(2)}) copy-start(bf16[4,48,2560]{2,1,0:T(8,128)(2,1)} %t_up_ref.1) | copy-start | bytes 2949124
  69.5 161.7 %all-gather.2.cloned.1.call-start = ((), (), s32[]{:S(2)}) async-start(), calls=%async_computation.5 | async-start | bytes 2949120 | tf_op jit(solution)/shard_map/all_gather | solution.py:430
  131.4 38.1 %copy-start.6 = (bf16[1,48,2560]{2,1,0:T(8,128)(2,1)S(1)}, bf16[1,48,2560]{2,1,0:T(8,128)(2,1)}, u32[]{:S(2)}) copy-start(bf16[1,48,2560]{2,1,0:T(8,128)(2,1)} %m_gate_ref.1) | copy-start | bytes 737284
  131.4 38.1 %copy-start.7 = (bf16[1,48,2560]{2,1,0:T(8,128)(2,1)S(1)}, bf16[1,48,2560]{2,1,0:T(8,128)(2,1)}, u32[]{:S(2)}) copy-start(bf16[1,48,2560]{2,1,0:T(8,128)(2,1)} %m_up_ref.1) | copy-start | bytes 737284
  131.4 20.9 %collective-permute-start.1 = (bf16[2,96,640]{2,1,0:T(8,128)(2,1)}, bf16[2,96,640]{2,1,0:T(8,128)(2,1)S(1)}, u32[]{:S(2)}, u32[]{:S(2)}) collective-permute-start(bf16[2,96,640]{2,1,0:T(8,128)(2,1)} %get-tuple-element.38), channel_id=1, source_target_pairs={{0,32},{32,64},{64,96},{96,128},{128,160},{160,192},{192,224},{224... | collective-permute-start | bytes 737288 | tf_op jit(solution)/shard_map/ppermute | solution.py:403
  134.9 17.5 %collective-permute-start.2 = (bf16[2,96,640]{2,1,0:T(8,128)(2,1)}, bf16[2,96,640]{2,1,0:T(8,128)(2,1)S(1)}, u32[]{:S(2)}, u32[]{:S(2)}) collective-permute-start(bf16[2,96,640]{2,1,0:T(8,128)(2,1)} %get-tuple-element.39), channel_id=1, source_target_pairs={{0,224},{32,0},{64,32},{96,64},{128,96},{160,128},{192,160},{224,1... | collective-permute-start | bytes 737288 | tf_op jit(solution)/shard_map/ppermute | solution.py:403
  143.5 20.1 %collective-permute-start.3 = (bf16[2,96,640]{2,1,0:T(8,128)(2,1)}, bf16[2,96,640]{2,1,0:T(8,128)(2,1)S(1)}, u32[]{:S(2)}, u32[]{:S(2)}) collective-permute-start(bf16[2,96,640]{2,1,0:T(8,128)(2,1)} %get-tuple-element.40), channel_id=1, source_target_pairs={{0,96},{32,128},{64,160},{96,192},{128,224},{160,0},{192,32},{224,... | collective-permute-start | bytes 737288 | tf_op jit(solution)/shard_map/ppermute | solution.py:403
  145.9 21.5 %collective-permute-start.4 = (bf16[2,96,640]{2,1,0:T(8,128)(2,1)}, bf16[2,96,640]{2,1,0:T(8,128)(2,1)}, u32[]{:S(2)}, u32[]{:S(2)}) collective-permute-start(bf16[2,96,640]{2,1,0:T(8,128)(2,1)} %get-tuple-element.41), channel_id=1, source_target_pairs={{0,160},{32,192},{64,224},{96,0},{128,32},{160,64},{192,96},{224,1... | collective-permute-start | bytes 737288 | tf_op jit(solution)/shard_map/ppermute | solution.py:403
  152.4 17.1 %copy-start.10 = (bf16[2,96,640]{2,1,0:T(8,128)(2,1)}, bf16[2,96,640]{2,1,0:T(8,128)(2,1)S(1)}, u32[]{:S(2)}) copy-start(bf16[2,96,640]{2,1,0:T(8,128)(2,1)S(1)} %collective-permute-done.1.refs_4_) | copy-start | bytes 737284
  152.4 17.1 %copy-start.11 = (bf16[2,96,640]{2,1,0:T(8,128)(2,1)}, bf16[2,96,640]{2,1,0:T(8,128)(2,1)S(1)}, u32[]{:S(2)}) copy-start(bf16[2,96,640]{2,1,0:T(8,128)(2,1)S(1)} %collective-permute-done.2.refs_10_) | copy-start | bytes 737284
  163.6 0.7 copy-start.12
  169.5 3.7 %copy-start.17 = (bf16[2,96,640]{2,1,0:T(8,128)(2,1)S(1)}, bf16[2,96,640]{2,1,0:T(8,128)(2,1)}, u32[]{:S(2)}) copy-start(bf16[2,96,640]{2,1,0:T(8,128)(2,1)} %get-tuple-element.44) | copy-start | bytes 737284
  169.5 10.0 %copy-start.16 = (bf16[2,96,640]{2,1,0:T(8,128)(2,1)S(1)}, bf16[2,96,640]{2,1,0:T(8,128)(2,1)}, u32[]{:S(2)}) copy-start(bf16[2,96,640]{2,1,0:T(8,128)(2,1)} %get-tuple-element.45) | copy-start | bytes 737284
  169.5 12.9 %copy-start.15 = (bf16[2,96,640]{2,1,0:T(8,128)(2,1)S(1)}, bf16[2,96,640]{2,1,0:T(8,128)(2,1)}, u32[]{:S(2)}) copy-start(bf16[2,96,640]{2,1,0:T(8,128)(2,1)} %get-tuple-element.46) | copy-start | bytes 737284
  169.7 61.5 %collective-permute-start.8 = (bf16[6,48,2560]{2,1,0:T(8,128)(2,1)S(1)}, bf16[6,48,2560]{2,1,0:T(8,128)(2,1)S(1)}, u32[]{:S(2)}, u32[]{:S(2)}) collective-permute-start(bf16[6,48,2560]{2,1,0:T(8,128)(2,1)S(1)} %pad_maximum_fusion), channel_id=1, source_target_pairs={{0,256},{32,288},{64,320},{96,352},{128,384},{160,416},{192,448},{... | collective-permute-start | bytes 4423688 | tf_op jit(solution)/shard_map/ppermute | solution.py:410
  173.2 23.9 %collective-permute-start.5 = (bf16[2,96,640]{2,1,0:T(8,128)(2,1)S(1)}, bf16[2,96,640]{2,1,0:T(8,128)(2,1)S(1)}, u32[]{:S(2)}, u32[]{:S(2)}) collective-permute-start(bf16[2,96,640]{2,1,0:T(8,128)(2,1)S(1)} %copy-done.17), channel_id=1, source_target_pairs={{0,64},{32,96},{64,128},{96,160},{128,192},{160,224},{192,0},{224,... | collective-permute-start | bytes 737288 | tf_op jit(solution)/shard_map/ppermute | solution.py:403
  179.5 28.3 %collective-permute-start.6 = (bf16[2,96,640]{2,1,0:T(8,128)(2,1)S(1)}, bf16[2,96,640]{2,1,0:T(8,128)(2,1)S(1)}, u32[]{:S(2)}, u32[]{:S(2)}) collective-permute-start(bf16[2,96,640]{2,1,0:T(8,128)(2,1)S(1)} %copy-done.16), channel_id=1, source_target_pairs={{0,128},{32,160},{64,192},{96,224},{128,0},{160,32},{192,64},{224,... | collective-permute-start | bytes 737288 | tf_op jit(solution)/shard_map/ppermute | solution.py:403
  182.4 25.5 %collective-permute-start.7 = (bf16[2,96,640]{2,1,0:T(8,128)(2,1)S(1)}, bf16[2,96,640]{2,1,0:T(8,128)(2,1)}, u32[]{:S(2)}, u32[]{:S(2)}) collective-permute-start(bf16[2,96,640]{2,1,0:T(8,128)(2,1)S(1)} %copy-done.15), channel_id=1, source_target_pairs={{0,192},{32,224},{64,0},{96,32},{128,64},{160,96},{192,128},{224,1... | collective-permute-start | bytes 737288 | tf_op jit(solution)/shard_map/ppermute | solution.py:403
  197.1 67.0 %copy-start.13 = (bf16[2,96,640]{2,1,0:T(8,128)(2,1)}, bf16[2,96,640]{2,1,0:T(8,128)(2,1)S(1)}, u32[]{:S(2)}) copy-start(bf16[2,96,640]{2,1,0:T(8,128)(2,1)S(1)} %collective-permute-done.5.refs_5_) | copy-start | bytes 737284
  207.8 56.3 %copy-start.14 = (bf16[2,96,640]{2,1,0:T(8,128)(2,1)}, bf16[2,96,640]{2,1,0:T(8,128)(2,1)S(1)}, u32[]{:S(2)}) copy-start(bf16[2,96,640]{2,1,0:T(8,128)(2,1)S(1)} %collective-permute-done.6.refs_7_) | copy-start | bytes 737284
  231.2 1.1 copy-start.4
  270.1 15.5 %all-to-all-start.3 = ((bf16[8,96,256]{2,1,0:T(8,128)(2,1)}), bf16[8,96,256]{2,1,0:T(8,128)(2,1)S(1)}, u32[]{:S(2)}, u32[]{:S(2)}) async-start(bf16[8,96,256]{2,1,0:T(8,128)(2,1)} %get-tuple-element.58), calls=%async_computation.3 | async-start | bytes 786432 | tf_op jit(solution)/shard_map/all_to_all | solution.py:358
  273.5 22.6 %collective-permute-start.10 = (bf16[8,48,640]{2,1,0:T(8,128)(2,1)}, bf16[8,48,640]{2,1,0:T(8,128)(2,1)S(1)}, u32[]{:S(2)}, u32[]{:S(2)}) collective-permute-start(bf16[8,48,640]{2,1,0:T(8,128)(2,1)} %get-tuple-element.64), channel_id=1, source_target_pairs={{0,256},{32,288},{64,320},{96,352},{128,384},{160,416},{192,448},{... | collective-permute-start | bytes 1474568 | tf_op jit(solution)/shard_map/ppermute | solution.py:472
  285.5 0.8 copy-start.3
  286.3 9.8 %copy-start.9 = (bf16[8,48,640]{2,1,0:T(8,128)(2,1)S(1)}, bf16[8,48,640]{2,1,0:T(8,128)(2,1)}, u32[]{:S(2)}) copy-start(bf16[8,48,640]{2,1,0:T(8,128)(2,1)} %get-tuple-element.63) | copy-start | bytes 1474564
  292.0 12.6 %copy-start.5 = (f32[2,48,2560]{2,1,0:T(8,128)S(1)}, f32[2,48,2560]{2,1,0:T(8,128)}, u32[]{:S(2)}) copy-start(f32[2,48,2560]{2,1,0:T(8,128)} %get-tuple-element.61) | copy-start | bytes 2949124
  292.0 12.6 %collective-permute-start.9 = (bf16[2,48,2560]{2,1,0:T(8,128)(2,1)}, bf16[2,48,2560]{2,1,0:T(8,128)(2,1)S(1)}, u32[]{:S(2)}, u32[]{:S(2)}) collective-permute-start(bf16[2,48,2560]{2,1,0:T(8,128)(2,1)} %get-tuple-element.62), channel_id=1, source_target_pairs={{0,256},{32,288},{64,320},{96,352},{128,384},{160,416},{192,448},{... | collective-permute-start | bytes 1474568 | tf_op jit(solution)/shard_map/ppermute | solution.py:492
  297.0 16.3 %all-to-all-start.4 = ((bf16[8,48,640]{2,1,0:T(8,128)(2,1)}), bf16[8,48,640]{2,1,0:T(8,128)(2,1)S(1)}, u32[]{:S(2)}, u32[]{:S(2)}) async-start(bf16[8,48,640]{2,1,0:T(8,128)(2,1)} %add_convert_fusion), calls=%async_computation.4 | async-start | bytes 983040 | tf_op jit(solution)/shard_map/all_to_all | solution.py:358
  (1 other events, 0.6 us)
Sparse Core Ops, SparseCore 0:
  169.4 61.7 all-gather.1

commit v4 on v2

v4 whole, which is shorter than its diff:
```python
import jax
import jax.numpy as jnp
from jax import lax
from jax.experimental import pallas as pl
from jax.experimental.pallas import tpu as pltpu
from jax.sharding import PartitionSpec as P

HALVES = 2
PAIR = 2
RING = 8
SIDE = 128
BF16 = jnp.bfloat16
F32 = jnp.float32


def dot_nn(a, b):
    return jnp.dot(a, b, preferred_element_type=F32)


def dot_nt(a, b):
    return lax.dot_general(a, b, (((1,), (1,)), ((), ())), preferred_element_type=F32)


def dot_tn(a, b):
    return lax.dot_general(a, b, (((0,), (0,)), ((), ())), preferred_element_type=F32)


def call(kernel, outs, args, far=(), far_outs=(), scratch=(), mib=16):
    def space(i, alone):
        return pl.BlockSpec(memory_space=pltpu.HBM if i in alone else pltpu.VMEM)

    return pl.pallas_call(
        kernel,
        out_shape=outs,
        in_specs=[space(i, far) for i in range(len(args))],
        out_specs=[space(i, far_outs) for i in range(len(outs))],
        scratch_shapes=scratch,
        compiler_params=pltpu.CompilerParams(vmem_limit_bytes=mib * 1024 * 1024),
        cost_estimate=pl.CostEstimate(
            flops=0,
            bytes_accessed=sum(a.size * a.dtype.itemsize for a in args),
            transcendentals=0,
        ),
    )(*args)


def place():
    at = lax.axis_index("dp")
    return at // RING, at % RING


def start_copies(pairs, sems, first=0):
    copies = [
        pltpu.make_async_copy(source, target, sems.at[first + i])
        for i, (source, target) in enumerate(pairs)
    ]
    for copy in copies:
        copy.start()
    return copies


def wait_copies(copies):
    for copy in copies:
        copy.wait()


def columns(total):
    return -(-total // SIDE) * SIDE


def pack_kernel(ids_ref, token_hbm, weight_hbm, down_hbm, out_ref, sent_hbm, token_ref, weight_ref, sent_ref, sems):
    half, _ = place()
    pairs = [(down_hbm.at[PAIR * (1 - half) + m], sent_ref.at[m]) for m in range(PAIR)]
    inputs = start_copies([(token_hbm, token_ref), (weight_hbm, weight_ref)], sems)
    downs = start_copies(pairs, sems, 2)
    ranks, count = ids_ref.shape
    piece = token_ref.shape[1] // RING
    wide = columns(piece)
    lane = lax.broadcasted_iota(jnp.int32, (ranks, SIDE), 1)
    rank = lax.broadcasted_iota(jnp.int32, (ranks, SIDE), 0)
    spread = jnp.where(lane == rank, 1.0, 0.0).astype(BF16)
    side = dot_tn(ids_ref[...].astype(F32).astype(BF16), spread)
    lane = lax.broadcasted_iota(jnp.int32, (count, SIDE), 1)
    wait_copies(inputs)
    weight = weight_ref[...].astype(F32)
    for k in range(ranks):
        side = jnp.where(lane == ranks + k, weight[:, k : k + 1], side)
    side = side.astype(BF16)
    blank = jnp.zeros((count, wide - piece), BF16)
    wait_copies(downs)
    downs = start_copies([(sent_ref, sent_hbm)], sems, 2)
    for i in range(RING):
        part = token_ref[:, i * piece : (i + 1) * piece]
        row = jnp.concatenate([part, blank, side], axis=1)
        for a in range(HALVES):
            out_ref[a * RING + i] = row
    wait_copies(downs)


def slots_kernel(ranks, piece, capacity, group_ref, out_ref):
    half, _ = place()
    wide = columns(piece)
    count = group_ref.shape[0]
    slots = out_ref.shape[0]
    side = group_ref[:, wide:].astype(F32)
    slot = lax.broadcasted_iota(jnp.int32, (count, slots), 1)
    column, inner = slot // (PAIR * capacity), slot % (PAIR * capacity)
    teacher = (column * HALVES * PAIR + half * PAIR + inner // capacity).astype(F32)
    position = (inner % capacity).astype(F32)
    hits = jnp.zeros((count, slots), F32)
    weight = jnp.zeros((count, slots), F32)
    for k in range(ranks):
        same = side[:, k : k + 1] == teacher
        hits = jnp.where(same, 1.0, hits)
        weight = jnp.where(same, side[:, ranks + k : ranks + k + 1], weight)
    later = lax.broadcasted_iota(jnp.int32, (count, count), 0)
    earlier = lax.broadcasted_iota(jnp.int32, (count, count), 1)
    below = jnp.where(earlier < later, 1.0, 0.0).astype(BF16)
    before = dot_nn(below, hits.astype(BF16))
    chosen = jnp.where((hits > 0.0) & (before == position), 1.0, 0.0)
    lane = lax.broadcasted_iota(jnp.int32, (count, wide), 1)
    mark = jnp.where(lane >= piece, 1.0, 0.0).astype(BF16)
    pick = jnp.concatenate([chosen, chosen * weight], axis=0).astype(BF16)
    value = jnp.concatenate([group_ref[:, :wide], mark], axis=0)
    out_ref[...] = dot_tn(pick, value).astype(BF16)


def turn_kernel(piece, capacity, rows_ref, turned_ref, weight_ref):
    count, wide = rows_ref.shape
    source = lax.broadcasted_iota(jnp.int32, (count, count), 0)
    target = lax.broadcasted_iota(jnp.int32, (count, count), 1)
    group, inner = source // (PAIR * capacity), source % (PAIR * capacity)
    goes = (inner // capacity) * (count // PAIR) + group * capacity + inner % capacity
    move = jnp.where(goes == target, 1.0, 0.0).astype(BF16)
    rows = rows_ref[...]
    turned_ref[...] = dot_tn(rows, move)[:piece].astype(BF16)
    weight_ref[...] = dot_tn(move, rows[:, wide - SIDE :]).astype(BF16)


def silu_split(value):
    logistic = jax.nn.sigmoid(value)
    return value * logistic, logistic * (1.0 + value * (1.0 - logistic))


def hidden_kernel(
    rows_ref,
    t_gate_ref,
    t_up_ref,
    m_gate_ref,
    m_up_ref,
    come_ref,
    out_ref,
    silu_ref,
    slope_ref,
    row_buf,
    weight_buf,
    sems,
):
    half, _ = place()
    block = m_gate_ref.shape[1]
    units = 2 * block
    span = rows_ref.shape[1] // PAIR
    places = out_ref.shape[0] // PAIR

    def weights(at, own_gate, come_gate, own_up, come_up):
        parts = (own_gate, come_gate, own_up, come_up)
        return [
            (part, weight_buf.at[at, pl.ds(i * block, block)]) for i, part in enumerate(parts)
        ]

    copies = []
    for m in range(PAIR):
        lanes = pl.ds(m * span, span)
        own = PAIR * half + m
        pairs = [(rows_ref.at[:, lanes], row_buf.at[m])]
        pairs += weights(
            m, t_gate_ref.at[own], come_ref.at[m], t_up_ref.at[own], come_ref.at[PAIR + m]
        )
        copies.append(start_copies(pairs, sems, 5 * m))
        if m == 0:
            pairs = weights(
                PAIR,
                m_gate_ref.at[0],
                come_ref.at[2 * PAIR],
                m_up_ref.at[0],
                come_ref.at[2 * PAIR + 1],
            )
            student_copies = start_copies(pairs, sems, 5 * PAIR)
    for m in range(PAIR):
        lanes = slice(m * span, (m + 1) * span)
        wait_copies(copies[m])
        rows = row_buf[m]
        value = dot_nn(weight_buf[m], rows)
        t_silu, _ = silu_split(value[:units])
        teacher = (t_silu * value[units:]).astype(BF16)
        if m == 0:
            wait_copies(student_copies)
        value = dot_nn(weight_buf[PAIR], rows)
        s_silu, s_slope = silu_split(value[:units])
        up = value[units:]
        student = (s_silu * up).astype(BF16)
        for i in range(places):
            at = m * places + i
            out_ref[at, 0] = student[:block]
            out_ref[at, 1] = student[block:]
            out_ref[at, 2] = teacher[:block]
            out_ref[at, 3] = teacher[block:]
        silu_ref[:, lanes] = s_silu
        slope_ref[:, lanes] = up * s_slope


def share_kernel(down_ref, merged_ref, came_ref, out_ref):
    half, _ = place()
    quarter = out_ref.shape[3]
    for i in range(RING):
        m, q = i // (RING // PAIR), i % (RING // PAIR)
        span = slice(q * quarter, (q + 1) * quarter)
        out_ref[i, 0] = down_ref[PAIR * half + m, :, span]
        out_ref[i, 1] = came_ref[m, :, span]
        out_ref[i, 2] = merged_ref[0, :, span]


def gap_kernel(hidden_ref, weight_ref, down_ref, merged_ref, grad_ref, kept_ref, other_ref):
    block = hidden_ref.shape[2]
    span = hidden_ref.shape[3]
    _, at = place()
    ring = range(RING)
    student = jnp.concatenate([hidden_ref[i, a] for i in ring for a in (0, 1)], axis=0)
    teacher = jnp.concatenate([hidden_ref[i, a] for i in ring for a in (2, 3)], axis=0)
    t_down = jnp.concatenate([down_ref[i, a] for i in ring for a in (0, 1)], axis=0)
    m_down = jnp.concatenate([x for i in ring for x in (down_ref[i, 2], merged_ref[i])], axis=0)
    gap = dot_tn(student, m_down) - dot_tn(teacher, t_down)
    start = pl.multiple_of(at // (RING // PAIR) * span, span)
    weight = weight_ref[pl.ds(start, span), SIDE - 1 : SIDE].astype(F32)
    slot_grad = (weight * gap).astype(BF16)
    grad_ref[...] = dot_nt(m_down, slot_grad).astype(BF16).reshape(grad_ref.shape)
    down_grad = dot_nn(student, slot_grad).astype(BF16)
    for i in ring:
        own, other = 2 * i * block, (2 * i + 1) * block
        kept_ref[i] = down_grad[own:other]
        other_ref[i] = down_grad[other : other + block]


def grads_kernel(parts_ref, silu_ref, slope_ref, rows_ref, own_ref, other_ref):
    block = own_ref.shape[1]
    places = parts_ref.shape[0] // PAIR
    sums = []
    for m in range(PAIR):
        total = parts_ref[m * places].astype(F32)
        for i in range(1, places):
            total += parts_ref[m * places + i].astype(F32)
        sums.append(total)
    total = jnp.concatenate(sums, axis=1)
    gate = (total * slope_ref[...]).astype(BF16)
    up = (total * silu_ref[...]).astype(BF16)
    stack = jnp.concatenate([gate[:block], up[:block], gate[block:], up[block:]], axis=0)
    grads = dot_nt(stack, rows_ref[...])
    own_ref[0] = grads[:block]
    own_ref[1] = grads[block : 2 * block]
    other_ref[0] = grads[2 * block : 3 * block].astype(BF16)
    other_ref[1] = grads[3 * block :].astype(BF16)


def down_sum_kernel(parts_ref, out_ref):
    count, _, piece = parts_ref.shape
    quarters = out_ref.shape[1] // piece
    for q in range(quarters):
        total = parts_ref[q].astype(F32)
        for i in range(q + quarters, count, quarters):
            total += parts_ref[i].astype(F32)
        out_ref[:, q * piece : (q + 1) * piece] = total


def body(
    tokens,
    teacher_ids,
    route_weight,
    teacher_gate,
    teacher_up,
    teacher_down,
    merged_gate,
    merged_up,
    merged_down,
):
    n_dp = HALVES * RING
    experts = lax.axis_size("expert")
    features = tokens.shape[2]
    capacity = tokens.shape[1]
    ranks = teacher_ids.shape[2]
    block = merged_gate.shape[1]
    piece = features // RING
    quarter = features * PAIR // RING
    rows = experts * PAIR * capacity
    span = rows // PAIR
    half = lax.axis_index("dp") // RING
    rings = [[a * RING + i for i in range(RING)] for a in range(HALVES)]
    swap = [(a * RING + i, (1 - a) * RING + i) for a in range(HALVES) for i in range(RING)]

    def exchange(array, axis_name, groups=None):
        return lax.all_to_all(
            array, axis_name, split_axis=0, concat_axis=0, tiled=True, axis_index_groups=groups
        )

    def halves(array, which):
        return lax.dynamic_slice_in_dim(array, PAIR * which, PAIR, axis=0)

    packets, sent = call(
        pack_kernel,
        (
            jax.ShapeDtypeStruct((n_dp, capacity, columns(piece) + SIDE), BF16),
            jax.ShapeDtypeStruct((PAIR, block, features), BF16),
        ),
        (teacher_ids[0].T, tokens[0], route_weight[0], teacher_down),
        far=(1, 2, 3),
        far_outs=(1,),
        scratch=[
            pltpu.VMEM((capacity, features), BF16),
            pltpu.VMEM((capacity, ranks), BF16),
            pltpu.VMEM((PAIR, block, features), BF16),
            pltpu.SemaphoreType.DMA((PAIR + 2,)),
        ],
        mib=60,
    )
    came = lax.ppermute(sent, "dp", swap)
    group = exchange(packets, "dp").reshape(n_dp * capacity, columns(piece) + SIDE)
    group, came = lax.optimization_barrier((group, came))

    (slots,) = call(
        lambda *refs: slots_kernel(ranks, piece, capacity, *refs),
        (jax.ShapeDtypeStruct((rows, columns(piece)), BF16),),
        (group,),
    )
    slots = exchange(slots.reshape(experts, PAIR * capacity, columns(piece)), "expert")

    (down,) = call(
        share_kernel,
        (jax.ShapeDtypeStruct((RING, PAIR + 1, block, quarter), BF16),),
        (teacher_down, merged_down, came),
    )
    down = exchange(down, "dp", rings)
    merged = lax.ppermute(down[:, PAIR], "dp", swap)

    come = lax.ppermute(
        jnp.concatenate(
            [halves(teacher_gate, 1 - half), halves(teacher_up, 1 - half), merged_gate, merged_up],
            axis=0,
        ),
        "dp",
        swap,
    )
    turned, weight = call(
        lambda *refs: turn_kernel(piece, capacity, *refs),
        (jax.ShapeDtypeStruct((piece, rows), BF16), jax.ShapeDtypeStruct((rows, SIDE), BF16)),
        (slots.reshape(rows, columns(piece)),),
    )
    turned = lax.all_gather(turned, "dp", axis=0, tiled=True, axis_index_groups=rings)

    hidden, silu, slope = call(
        hidden_kernel,
        (
            jax.ShapeDtypeStruct((RING, 4, block, span), BF16),
            jax.ShapeDtypeStruct((2 * block, rows), F32),
            jax.ShapeDtypeStruct((2 * block, rows), F32),
        ),
        (turned, teacher_gate, teacher_up, merged_gate, merged_up, come),
        far=range(6),
        scratch=[
            pltpu.VMEM((PAIR, features, span), BF16),
            pltpu.VMEM((PAIR + 1, 4 * block, features), BF16),
            pltpu.SemaphoreType.DMA((5 * PAIR + 4,)),
        ],
        mib=60,
    )
    hidden = exchange(hidden, "dp", rings)
    hidden_grad, kept_down, other_down = call(
        gap_kernel,
        (
            jax.ShapeDtypeStruct((RING, 2 * block, span), BF16),
            jax.ShapeDtypeStruct((RING, block, quarter), BF16),
            jax.ShapeDtypeStruct((RING, block, quarter), BF16),
        ),
        (hidden, weight, down, merged),
    )
    other_down = lax.ppermute(other_down, "dp", swap)
    parts = exchange(hidden_grad, "dp", rings)
    own, other = call(
        grads_kernel,
        (
            jax.ShapeDtypeStruct((2, block, features), F32),
            jax.ShapeDtypeStruct((2, block, features), BF16),
        ),
        (parts, silu, slope, turned),
    )
    other = lax.ppermute(other, "dp", swap)
    down_grad = (kept_down.astype(F32) + other_down.astype(F32)).astype(BF16)
    down_grad = exchange(down_grad, "dp", rings)
    (grad_down,) = call(
        down_sum_kernel, (jax.ShapeDtypeStruct((block, features), F32),), (down_grad,)
    )
    grad_gate = own[:1] + other[:1].astype(F32)
    grad_up = own[1:] + other[1:].astype(F32)
    return grad_gate, grad_up, grad_down[None]


def solution(mesh):
    placed = (P("expert", "dp", None),) * 9
    return jax.shard_map(
        body,
        mesh=mesh,
        in_specs=placed,
        out_specs=(P("expert", "dp", None),) * 3,
        check_vma=False,
    )
```

time: 228 us -> 224 us (0.982)
  blocking collectives: 67.1 us -> 44.3 us
  waiting for transfers between devices: 88.4 us -> 98.7 us
  starting transfers between devices: 28.6 us -> 35.6 us
  Pallas kernels: 10.1 us -> 14.5 us
  local copies, waits for them, and re-layouts: 15.1 us -> 10.8 us
    all_to_all x3 -> x2, blocking collectives: 67.1 us -> 44.3 us  [exchange(): lax.all_to_all(array, axis_name, split_axis=0, concat_axis=0, tiled=True,...]
    all_to_all x3 -> x4, waiting for transfers between devices: 3.56 us -> 26 us  [exchange(): lax.all_to_all(array, axis_name, split_axis=0, concat_axis=0, tiled=True,...]
    ppermute x1 -> x4, starting transfers between devices: 2.08 us -> 15.7 us  [the longest x1 4.21 us: body(): other_down = lax.ppermute(other_down, 'dp', swap)]
    ppermute x1, waiting for transfers between devices: 19.1 us -> 6.9 us  [body(): other = lax.ppermute(other, 'dp', swap)]
    all_to_all x3 -> x4, starting transfers between devices: 24.4 us -> 15.5 us  [exchange(): lax.all_to_all(array, axis_name, split_axis=0, concat_axis=0, tiled=True,...]
    pallas_call x7 -> x8, Pallas kernels: 10.1 us -> 14.5 us  [call(): pl.pallas_call(kernel, out_shape=outs, in_specs=[space(i, far) for i in r...]
    all_gather x1, waiting for transfers between devices: 17.3 us -> 21.7 us  [body(): lax.all_gather(turned, 'dp', axis=0, tiled=True, axis_index_groups=rings)]
    ppermute x1 -> x4, waiting for transfers between devices: 48.4 us -> 44.1 us  [the longest x1 32.5 us: body(): lax.ppermute(jnp.concatenate([halves(teacher_gate, 1 - half), halves(teac...]
  transfers between devices with their start and end apart: 6 -> 10, of which waited for: 4 -> 7; matrix products, arithmetic and copies ran while one was open for 3% -> 2% of each run, Pallas kernels for 1% -> 3%
where the time goes in v4:
time: 224 us; the launch traced here: 222 us
  waiting for transfers between devices  98.7 us (44%)
  blocking collectives  44.3 us (20%)
  starting transfers between devices  35.6 us (16%)
  Pallas kernels  14.5 us (6%)
  between operations  14.3 us (6%)
  local copies, waits for them, and re-layouts  10.8 us (5%)
  other arithmetic  4.11 us (2%)
    all_to_all x2, blocking collectives, exchange(): lax.all_to_all(array, axis_name, split_axis=0, concat_axis=0, tiled=True,...  44.3 us
    ppermute x1, waiting for transfers between devices, body(): lax.ppermute(jnp.concatenate([halves(teacher_gate, 1 - half), halves(teac...  32.5 us
    all_to_all x4, waiting for transfers between devices, exchange(): lax.all_to_all(array, axis_name, split_axis=0, concat_axis=0, tiled=True,...  26 us
    all_gather x1, waiting for transfers between devices, body(): lax.all_gather(turned, 'dp', axis=0, tiled=True, axis_index_groups=rings)  21.7 us
    all_to_all x4, starting transfers between devices, exchange(): lax.all_to_all(array, axis_name, split_axis=0, concat_axis=0, tiled=True,...  15.5 us
    pallas_call x8, Pallas kernels, call(): pl.pallas_call(kernel, out_shape=outs, in_specs=[space(i, far) for i in r...  14.5 us
    ppermute x1, waiting for transfers between devices, body(): merged = lax.ppermute(down[:, PAIR], 'dp', swap)  11.6 us
    unnamed x36, local copies, waits for them, and re-layouts  8.33 us
  transfers between devices with their start and end apart: 10, of which 7 were waited for; matrix products, arithmetic and copies ran while one was open for 2% of the time, Pallas kernels for 3%

profile of v4, /device:TPU:6, one launch (start us, length us, event | category | flops | bytes accessed | tf_op | source)
XLA Modules:
  0.0 222.3 jit_solution(9848942310542241852)
XLA Ops:
  7.2 1.3 copy.22
  8.5 3.4 %shard_map.112 = (bf16[16,8,512]{2,1,0:T(8,128)(2,1)}, bf16[2,48,2560]{2,1,0:T(8,128)(2,1)}) custom-call(s32[6,8]{1,0:T(8,128)} %bitcast.21, bf16[8,2560]{1,0:T(8,128)(2,1)} %bitcast.20, bf16[8,6]{1,0:T(8,128)(2,1)} %bitcast.22, bf16[4,48,2560]{2,1,0:T(8,128)(2,1)} %down_ref.1), custom_call_target="tpu_custom_call" | custom-call | bytes 1024288 | tf_op jit(solution)/shard_map/pallas_call | solution.py:32
  11.9 3.3 %collective-permute-start = (bf16[2,48,2560]{2,1,0:T(8,128)(2,1)}, bf16[2,48,2560]{2,1,0:T(8,128)(2,1)S(1)}, u32[]{:S(2)}, u32[]{:S(2)}) collective-permute-start(bf16[2,48,2560]{2,1,0:T(8,128)(2,1)} %get-tuple-element.18), channel_id=1, source_target_pairs={{0,256},{32,288},{64,320},{96,352},{128,384},{160,416},{192,448},{... | collective-permute-start | bytes 1474568 | tf_op jit(solution)/shard_map/ppermute | solution.py:324
  15.2 20.9 %all_to_all.30 = bf16[16,8,512]{2,1,0:T(8,128)(2,1)S(1)} all-to-all(bf16[16,8,512]{2,1,0:T(8,128)(2,1)} %get-tuple-element.17), channel_id=1, replica_groups=mesh['dp'=16,'expert'=32] {'dp'}, dimensions={0} | all-to-all | bytes 262144 | tf_op jit(solution)/shard_map/all_to_all | solution.py:300
  36.7 23.4 %all_to_all.31 = bf16[32,16,384]{2,1,0:T(8,128)(2,1)S(1)} all-to-all(bf16[32,16,384]{2,1,0:T(8,128)(2,1)S(1)} %bitcast.17), channel_id=1, replica_groups=mesh['dp'=16,'expert'=32] {'expert'}, dimensions={0} | all-to-all | bytes 786432 | tf_op jit(solution)/shard_map/all_to_all | solution.py:300
  60.2 1.2 shard_map.114
  61.4 1.2 shard_map.116
  62.6 4.2 %all-to-all-start.3 = ((bf16[8,3,48,640]{3,2,1,0:T(8,128)(2,1)}), bf16[8,3,48,640]{3,2,1,0:T(8,128)(2,1)S(1)}, u32[]{:S(2)}, u32[]{:S(2)}) async-start(bf16[8,3,48,640]{3,2,1,0:T(8,128)(2,1)} %shard_map.116), calls=%async_computation.3 | async-start | bytes 2949120 | tf_op jit(solution)/shard_map/all_to_all | solution.py:300
  66.9 1.2 constant_dynamic-slice_fusion
  68.1 1.2 pad_maximum_fusion
  69.2 4.0 %collective-permute-start.1 = (bf16[6,48,2560]{2,1,0:T(8,128)(2,1)S(1)}, bf16[6,48,2560]{2,1,0:T(8,128)(2,1)S(1)}, u32[]{:S(2)}, u32[]{:S(2)}) collective-permute-start(bf16[6,48,2560]{2,1,0:T(8,128)(2,1)S(1)} %pad_maximum_fusion), channel_id=1, source_target_pairs={{0,256},{32,288},{64,320},{96,352},{128,384},{160,416},{192,448},{... | collective-permute-start | bytes 4423688 | tf_op jit(solution)/shard_map/ppermute | solution.py:343
  73.3 32.5 %collective-permute-done.1.come_ref = bf16[6,48,2560]{2,1,0:T(8,128)(2,1)S(1)} collective-permute-done((bf16[6,48,2560]{2,1,0:T(8,128)(2,1)S(1)}, bf16[6,48,2560]{2,1,0:T(8,128)(2,1)S(1)}, u32[]{:S(2)}, u32[]{:S(2)}) %collective-permute-start.1) | collective-permute-done | bytes 1474592 | tf_op jit(solution)/shard_map/ppermute | solution.py:343
  105.8 21.7 %all-gather.2.cloned.1.call-done.rows_ref = bf16[2560,512]{1,0:T(8,128)(2,1)} async-done(((bf16[320,512]{1,0:T(8,128)(2,1)}), bf16[2560,512]{1,0:T(8,128)(2,1)}) %all-gather.2.cloned.1.call-update) | async-done | bytes 2621456 | tf_op jit(solution)/shard_map/all_gather | solution.py:356
  127.5 4.7 %shard_map.115 = (bf16[8,4,48,256]{3,2,1,0:T(8,128)(2,1)}, f32[96,512]{1,0:T(8,128)}, f32[96,512]{1,0:T(8,128)}) custom-call(bf16[2560,512]{1,0:T(8,128)(2,1)} %all-gather.2.cloned.1.call-done.rows_ref, bf16[4,48,2560]{2,1,0:T(8,128)(2,1)} %t_gate_ref.1, bf16[4,48,2560]{2,1,0:T(8,128)(2,1)} %t_up_ref.1, bf16[1,48,2560]{2,1,0:T(8,128)(2,1)} %m_gate_ref.1, ...), custom_call_target="tpu_custom_call" | custom-call | bytes 6553600 | tf_op jit(solution)/shard_map/pallas_call | solution.py:32
  132.3 4.4 %all-to-all-start.2 = ((bf16[8,4,48,256]{3,2,1,0:T(8,128)(2,1)}), bf16[8,4,48,256]{3,2,1,0:T(8,128)(2,1)S(1)}, u32[]{:S(2)}, u32[]{:S(2)}) async-start(bf16[8,4,48,256]{3,2,1,0:T(8,128)(2,1)} %get-tuple-element.21), calls=%async_computation.2 | async-start | bytes 1572864 | tf_op jit(solution)/shard_map/all_to_all | solution.py:300
  136.7 4.2 %collective-permute-start.2 = (bf16[8,48,640]{2,1,0:T(8,128)(2,1)S(1)}, bf16[8,48,640]{2,1,0:T(8,128)(2,1)S(1)}, u32[]{:S(2)}, u32[]{:S(2)}) collective-permute-start(bf16[8,48,640]{2,1,0:T(8,128)(2,1)S(1)} %slice_bitcast_fusion), channel_id=1, source_target_pairs={{0,256},{32,288},{64,320},{96,352},{128,384},{160,416},{192,448},{... | collective-permute-start | bytes 1474568 | tf_op jit(solution)/shard_map/ppermute | solution.py:341
  140.9 11.6 %collective-permute-done.2.merged_ref = bf16[8,48,640]{2,1,0:T(8,128)(2,1)S(1)} collective-permute-done((bf16[8,48,640]{2,1,0:T(8,128)(2,1)S(1)}, bf16[8,48,640]{2,1,0:T(8,128)(2,1)S(1)}, u32[]{:S(2)}, u32[]{:S(2)}) %collective-permute-start.2) | collective-permute-done | bytes 491552 | tf_op jit(solution)/shard_map/ppermute | solution.py:341
  153.2 6.2 %all-to-all-done.2.hidden_ref = bf16[8,4,48,256]{3,2,1,0:T(8,128)(2,1)S(1)} async-done(((bf16[8,4,48,256]{3,2,1,0:T(8,128)(2,1)}), bf16[8,4,48,256]{3,2,1,0:T(8,128)(2,1)S(1)}, u32[]{:S(2)}, u32[]{:S(2)}) %all-to-all-start.2) | async-done | bytes 786464 | tf_op jit(solution)/shard_map/all_to_all | solution.py:300
  159.4 1.4 copy-done.2
  160.8 1.0 copy-done.9
  161.8 1.4 shard_map.117
  165.6 3.5 %all-to-all-start.4 = ((bf16[8,96,256]{2,1,0:T(8,128)(2,1)}), bf16[8,96,256]{2,1,0:T(8,128)(2,1)S(1)}, u32[]{:S(2)}, u32[]{:S(2)}) async-start(bf16[8,96,256]{2,1,0:T(8,128)(2,1)} %copy-done.10), calls=%async_computation.4 | async-start | bytes 786432 | tf_op jit(solution)/shard_map/all_to_all | solution.py:300
  169.0 4.2 %collective-permute-start.4 = (bf16[8,48,640]{2,1,0:T(8,128)(2,1)}, bf16[8,48,640]{2,1,0:T(8,128)(2,1)}, u32[]{:S(2)}, u32[]{:S(2)}) collective-permute-start(bf16[8,48,640]{2,1,0:T(8,128)(2,1)} %copy-done.14), channel_id=1, source_target_pairs={{0,256},{32,288},{64,320},{96,352},{128,384},{160,416},{192,448},{... | collective-permute-start | bytes 1474568 | tf_op jit(solution)/shard_map/ppermute | solution.py:384
  173.2 10.8 %all-to-all-done.4.parts_ref = bf16[8,96,256]{2,1,0:T(8,128)(2,1)S(1)} async-done(((bf16[8,96,256]{2,1,0:T(8,128)(2,1)}), bf16[8,96,256]{2,1,0:T(8,128)(2,1)S(1)}, u32[]{:S(2)}, u32[]{:S(2)}) %all-to-all-start.4) | async-done | bytes 393248 | tf_op jit(solution)/shard_map/all_to_all | solution.py:300
  185.9 1.0 shard_map.118
  187.0 1.0 copy-done.4
  187.9 4.3 %collective-permute-start.3 = (bf16[2,48,2560]{2,1,0:T(8,128)(2,1)S(1)}, bf16[2,48,2560]{2,1,0:T(8,128)(2,1)S(1)}, u32[]{:S(2)}, u32[]{:S(2)}) collective-permute-start(bf16[2,48,2560]{2,1,0:T(8,128)(2,1)S(1)} %get-tuple-element.28), channel_id=1, source_target_pairs={{0,256},{32,288},{64,320},{96,352},{128,384},{160,416},{192,448},{... | collective-permute-start | bytes 1474568 | tf_op jit(solution)/shard_map/ppermute | solution.py:394
  192.3 1.9 add_convert_fusion
  194.2 3.5 %all-to-all-start.5 = ((bf16[8,48,640]{2,1,0:T(8,128)(2,1)}), bf16[8,48,640]{2,1,0:T(8,128)(2,1)S(1)}, u32[]{:S(2)}, u32[]{:S(2)}) async-start(bf16[8,48,640]{2,1,0:T(8,128)(2,1)} %add_convert_fusion), calls=%async_computation.5 | async-start | bytes 983040 | tf_op jit(solution)/shard_map/all_to_all | solution.py:300
  197.7 6.9 %collective-permute-done.3 = bf16[2,48,2560]{2,1,0:T(8,128)(2,1)S(1)} collective-permute-done((bf16[2,48,2560]{2,1,0:T(8,128)(2,1)S(1)}, bf16[2,48,2560]{2,1,0:T(8,128)(2,1)S(1)}, u32[]{:S(2)}, u32[]{:S(2)}) %collective-permute-start.3) | collective-permute-done | bytes 491552 | tf_op jit(solution)/shard_map/ppermute | solution.py:394
  204.6 1.0 convert_add_fusion
  205.6 9.0 %all-to-all-done.5.parts_ref = bf16[8,48,640]{2,1,0:T(8,128)(2,1)S(1)} async-done(((bf16[8,48,640]{2,1,0:T(8,128)(2,1)}), bf16[8,48,640]{2,1,0:T(8,128)(2,1)S(1)}, u32[]{:S(2)}, u32[]{:S(2)}) %all-to-all-start.5) | async-done | bytes 491552 | tf_op jit(solution)/shard_map/all_to_all | solution.py:300
  (41 shorter events, 6.6 us)
Async XLA Ops:
  7.2 120.3 %all-gather.2.cloned.1.call-start = ((), (), s32[]{:S(2)}) async-start(), calls=%async_computation.6 | async-start | bytes 2949120 | tf_op jit(solution)/shard_map/all_gather | solution.py:356
  8.5 52.9 %copy-start.3 = (bf16[4,48,2560]{2,1,0:T(8,128)(2,1)S(1)}, bf16[4,48,2560]{2,1,0:T(8,128)(2,1)}, u32[]{:S(2)}) copy-start(bf16[4,48,2560]{2,1,0:T(8,128)(2,1)} %down_ref.1) | copy-start | bytes 2949124
  8.5 52.9 %copy-start.11 = (bf16[1,48,2560]{2,1,0:T(8,128)(2,1)S(1)}, bf16[1,48,2560]{2,1,0:T(8,128)(2,1)}, u32[]{:S(2)}) copy-start(bf16[1,48,2560]{2,1,0:T(8,128)(2,1)} %merged_ref.1) | copy-start | bytes 737284
  11.9 24.2 %collective-permute-start = (bf16[2,48,2560]{2,1,0:T(8,128)(2,1)}, bf16[2,48,2560]{2,1,0:T(8,128)(2,1)S(1)}, u32[]{:S(2)}, u32[]{:S(2)}) collective-permute-start(bf16[2,48,2560]{2,1,0:T(8,128)(2,1)} %get-tuple-element.18), channel_id=1, source_target_pairs={{0,256},{32,288},{64,320},{96,352},{128,384},{160,416},{192,448},{... | collective-permute-start | bytes 1474568 | tf_op jit(solution)/shard_map/ppermute | solution.py:324
  62.6 4.3 %copy-start.15 = (bf16[4,48,2560]{2,1,0:T(8,128)(2,1)S(1)}, bf16[4,48,2560]{2,1,0:T(8,128)(2,1)}, u32[]{:S(2)}) copy-start(bf16[4,48,2560]{2,1,0:T(8,128)(2,1)} %t_gate_ref.1) | copy-start | bytes 2949124
  62.6 69.6 %all-to-all-start.3 = ((bf16[8,3,48,640]{3,2,1,0:T(8,128)(2,1)}), bf16[8,3,48,640]{3,2,1,0:T(8,128)(2,1)S(1)}, u32[]{:S(2)}, u32[]{:S(2)}) async-start(bf16[8,3,48,640]{3,2,1,0:T(8,128)(2,1)} %shard_map.116), calls=%async_computation.3 | async-start | bytes 2949120 | tf_op jit(solution)/shard_map/all_to_all | solution.py:300
  66.9 1.2 copy-start.17
  69.2 36.5 %collective-permute-start.1 = (bf16[6,48,2560]{2,1,0:T(8,128)(2,1)S(1)}, bf16[6,48,2560]{2,1,0:T(8,128)(2,1)S(1)}, u32[]{:S(2)}, u32[]{:S(2)}) collective-permute-start(bf16[6,48,2560]{2,1,0:T(8,128)(2,1)S(1)} %pad_maximum_fusion), channel_id=1, source_target_pairs={{0,256},{32,288},{64,320},{96,352},{128,384},{160,416},{192,448},{... | collective-permute-start | bytes 4423688 | tf_op jit(solution)/shard_map/ppermute | solution.py:343
  105.8 21.7 %copy-start.16 = (bf16[6,48,2560]{2,1,0:T(8,128)(2,1)}, bf16[6,48,2560]{2,1,0:T(8,128)(2,1)S(1)}, u32[]{:S(2)}) copy-start(bf16[6,48,2560]{2,1,0:T(8,128)(2,1)S(1)} %collective-permute-done.1.come_ref) | copy-start | bytes 4423684
  132.2 27.2 %copy-start.1 = (bf16[8,3,48,640]{3,2,1,0:T(8,128)(2,1)}, bf16[8,3,48,640]{3,2,1,0:T(8,128)(2,1)S(1)}, u32[]{:S(2)}) copy-start(bf16[8,3,48,640]{3,2,1,0:T(8,128)(2,1)S(1)} %all-to-all-done.3.down_ref) | copy-start | bytes 4423684
  132.3 27.2 %all-to-all-start.2 = ((bf16[8,4,48,256]{3,2,1,0:T(8,128)(2,1)}), bf16[8,4,48,256]{3,2,1,0:T(8,128)(2,1)S(1)}, u32[]{:S(2)}, u32[]{:S(2)}) async-start(bf16[8,4,48,256]{3,2,1,0:T(8,128)(2,1)} %get-tuple-element.21), calls=%async_computation.2 | async-start | bytes 1572864 | tf_op jit(solution)/shard_map/all_to_all | solution.py:300
  136.7 15.8 %collective-permute-start.2 = (bf16[8,48,640]{2,1,0:T(8,128)(2,1)S(1)}, bf16[8,48,640]{2,1,0:T(8,128)(2,1)S(1)}, u32[]{:S(2)}, u32[]{:S(2)}) collective-permute-start(bf16[8,48,640]{2,1,0:T(8,128)(2,1)S(1)} %slice_bitcast_fusion), channel_id=1, source_target_pairs={{0,256},{32,288},{64,320},{96,352},{128,384},{160,416},{192,448},{... | collective-permute-start | bytes 1474568 | tf_op jit(solution)/shard_map/ppermute | solution.py:341
  152.4 0.8 copy-start.8
  159.4 1.4 copy-start.2
  160.8 1.0 copy-start.9
  161.8 22.2 %copy-start = (bf16[2560,512]{1,0:T(8,128)(2,1)S(1)}, bf16[2560,512]{1,0:T(8,128)(2,1)}, u32[]{:S(2)}) copy-start(bf16[2560,512]{1,0:T(8,128)(2,1)} %all-gather.2.cloned.1.call-done.rows_ref) | copy-start | bytes 7864324
  163.2 0.8 copy-start.6
  164.0 0.7 copy-start.10
  164.8 0.8 copy-start.14
  165.6 18.5 %all-to-all-start.4 = ((bf16[8,96,256]{2,1,0:T(8,128)(2,1)}), bf16[8,96,256]{2,1,0:T(8,128)(2,1)S(1)}, u32[]{:S(2)}, u32[]{:S(2)}) async-start(bf16[8,96,256]{2,1,0:T(8,128)(2,1)} %copy-done.10), calls=%async_computation.4 | async-start | bytes 786432 | tf_op jit(solution)/shard_map/all_to_all | solution.py:300
  169.0 23.2 %collective-permute-start.4 = (bf16[8,48,640]{2,1,0:T(8,128)(2,1)}, bf16[8,48,640]{2,1,0:T(8,128)(2,1)}, u32[]{:S(2)}, u32[]{:S(2)}) collective-permute-start(bf16[8,48,640]{2,1,0:T(8,128)(2,1)} %copy-done.14), channel_id=1, source_target_pairs={{0,256},{32,288},{64,320},{96,352},{128,384},{160,416},{192,448},{... | collective-permute-start | bytes 1474568 | tf_op jit(solution)/shard_map/ppermute | solution.py:384
  184.1 0.9 copy-start.12
  185.0 0.9 copy-start.13
  185.9 6.3 %copy-start.7 = (bf16[8,48,640]{2,1,0:T(8,128)(2,1)S(1)}, bf16[8,48,640]{2,1,0:T(8,128)(2,1)}, u32[]{:S(2)}) copy-start(bf16[8,48,640]{2,1,0:T(8,128)(2,1)} %copy-done.6) | copy-start | bytes 1474564
  187.0 1.0 copy-start.4
  187.9 16.7 %copy-start.5 = (f32[2,48,2560]{2,1,0:T(8,128)S(1)}, f32[2,48,2560]{2,1,0:T(8,128)}, u32[]{:S(2)}) copy-start(f32[2,48,2560]{2,1,0:T(8,128)} %copy-done.4) | copy-start | bytes 2949124
  187.9 16.7 %collective-permute-start.3 = (bf16[2,48,2560]{2,1,0:T(8,128)(2,1)S(1)}, bf16[2,48,2560]{2,1,0:T(8,128)(2,1)S(1)}, u32[]{:S(2)}, u32[]{:S(2)}) collective-permute-start(bf16[2,48,2560]{2,1,0:T(8,128)(2,1)S(1)} %get-tuple-element.28), channel_id=1, source_target_pairs={{0,256},{32,288},{64,320},{96,352},{128,384},{160,416},{192,448},{... | collective-permute-start | bytes 1474568 | tf_op jit(solution)/shard_map/ppermute | solution.py:394
  194.2 20.4 %all-to-all-start.5 = ((bf16[8,48,640]{2,1,0:T(8,128)(2,1)}), bf16[8,48,640]{2,1,0:T(8,128)(2,1)S(1)}, u32[]{:S(2)}, u32[]{:S(2)}) async-start(bf16[8,48,640]{2,1,0:T(8,128)(2,1)} %add_convert_fusion), calls=%async_computation.5 | async-start | bytes 983040 | tf_op jit(solution)/shard_map/all_to_all | solution.py:300
Sparse Core Ops, SparseCore 0:
  61.5 65.9 all-gather.1

commit v5 on v4

v5 whole, which is shorter than its diff:
```python
import jax
import jax.numpy as jnp
from jax import lax
from jax.experimental import pallas as pl
from jax.experimental.pallas import tpu as pltpu
from jax.sharding import PartitionSpec as P

HALVES = 2
PAIR = 2
RING = 8
SIDE = 128
BF16 = jnp.bfloat16
F32 = jnp.float32


def dot_nn(a, b):
    return jnp.dot(a, b, preferred_element_type=F32)


def dot_nt(a, b):
    return lax.dot_general(a, b, (((1,), (1,)), ((), ())), preferred_element_type=F32)


def dot_tn(a, b):
    return lax.dot_general(a, b, (((0,), (0,)), ((), ())), preferred_element_type=F32)


def call(kernel, outs, args, far=(), far_outs=(), scratch=(), mib=16):
    def space(i, alone):
        return pl.BlockSpec(memory_space=pltpu.HBM if i in alone else pltpu.VMEM)

    return pl.pallas_call(
        kernel,
        out_shape=outs,
        in_specs=[space(i, far) for i in range(len(args))],
        out_specs=[space(i, far_outs) for i in range(len(outs))],
        scratch_shapes=scratch,
        compiler_params=pltpu.CompilerParams(vmem_limit_bytes=mib * 1024 * 1024),
        cost_estimate=pl.CostEstimate(
            flops=0,
            bytes_accessed=sum(a.size * a.dtype.itemsize for a in args),
            transcendentals=0,
        ),
    )(*args)


def place():
    at = lax.axis_index("dp")
    return at // RING, at % RING


def start_copies(pairs, sems, first=0):
    copies = [
        pltpu.make_async_copy(source, target, sems.at[first + i])
        for i, (source, target) in enumerate(pairs)
    ]
    for copy in copies:
        copy.start()
    return copies


def wait_copies(copies):
    for copy in copies:
        copy.wait()


def pack_kernel(
    ids_ref, token_hbm, weight_hbm, down_hbm, merged_hbm, out_ref, sent_hbm, token_ref, weight_ref, sent_ref, sems
):
    half, _ = place()
    inputs = start_copies([(token_hbm, token_ref), (weight_hbm, weight_ref)], sems)
    pairs = [(down_hbm.at[PAIR * (1 - half) + m], sent_ref.at[m]) for m in range(PAIR)]
    downs = start_copies([*pairs, (merged_hbm.at[0], sent_ref.at[PAIR])], sems, 2)
    ranks, count = ids_ref.shape
    features = token_ref.shape[1]
    lane = lax.broadcasted_iota(jnp.int32, (ranks, SIDE), 1)
    rank = lax.broadcasted_iota(jnp.int32, (ranks, SIDE), 0)
    spread = jnp.where(lane == rank, 1.0, 0.0).astype(BF16)
    side = dot_tn(ids_ref[...].astype(F32).astype(BF16), spread)
    lane = lax.broadcasted_iota(jnp.int32, (count, SIDE), 1)
    wait_copies(inputs)
    weight = weight_ref[...].astype(F32)
    for k in range(ranks):
        side = jnp.where(lane == ranks + k, weight[:, k : k + 1], side)
    side = side.astype(BF16)
    wait_copies(downs)
    downs = start_copies([(sent_ref, sent_hbm)], sems, 2)
    tokens = token_ref[...]
    for i in range(out_ref.shape[0]):
        out_ref[i, :, :features] = tokens
        out_ref[i, :, features:] = side
    wait_copies(downs)


def slots_kernel(ranks, capacity, group_ref, out_ref):
    half, _ = place()
    wide = group_ref.shape[1] - SIDE
    count = group_ref.shape[0]
    slots = out_ref.shape[0]
    side = group_ref[:, wide:].astype(F32)
    slot = lax.broadcasted_iota(jnp.int32, (count, slots), 1)
    column, inner = slot // (PAIR * capacity), slot % (PAIR * capacity)
    teacher = (column * HALVES * PAIR + half * PAIR + inner // capacity).astype(F32)
    position = (inner % capacity).astype(F32)
    hits = jnp.zeros((count, slots), F32)
    weight = jnp.zeros((count, slots), F32)
    for k in range(ranks):
        same = side[:, k : k + 1] == teacher
        hits = jnp.where(same, 1.0, hits)
        weight = jnp.where(same, side[:, ranks + k : ranks + k + 1], weight)
    later = lax.broadcasted_iota(jnp.int32, (count, count), 0)
    earlier = lax.broadcasted_iota(jnp.int32, (count, count), 1)
    below = jnp.where(earlier < later, 1.0, 0.0).astype(BF16)
    before = dot_nn(below, hits.astype(BF16))
    chosen = jnp.where((hits > 0.0) & (before == position), 1.0, 0.0)
    out_ref[:, :wide] = dot_tn(chosen.astype(BF16), group_ref[:, :wide]).astype(BF16)
    weights = dot_tn((chosen * weight).astype(BF16), jnp.ones((count, SIDE), BF16))
    out_ref[:, wide:] = weights.astype(BF16)


def by_teacher(count, capacity, source_axis):
    source = lax.broadcasted_iota(jnp.int32, (count, count), source_axis)
    target = lax.broadcasted_iota(jnp.int32, (count, count), 1 - source_axis)
    group, inner = source // (PAIR * capacity), source % (PAIR * capacity)
    goes = (inner // capacity) * (count // PAIR) + group * capacity + inner % capacity
    return jnp.where(goes == target, 1.0, 0.0).astype(BF16)


def silu_split(value):
    logistic = jax.nn.sigmoid(value)
    return value * logistic, logistic * (1.0 + value * (1.0 - logistic))


def hidden_kernel(
    capacity,
    rows_hbm,
    t_gate_hbm,
    t_up_hbm,
    m_gate_hbm,
    m_up_hbm,
    come_hbm,
    out_ref,
    silu_ref,
    slope_ref,
    weight_ref,
    raw_buf,
    row_buf,
    weight_buf,
    sems,
):
    half, _ = place()
    block = m_gate_hbm.shape[1]
    units = 2 * block
    count, wide = raw_buf.shape
    features = wide - SIDE
    span = count // PAIR
    places = out_ref.shape[0] // PAIR
    tile = 7 * SIDE
    tiles = [slice(i, i + tile) for i in range(0, wide, tile)]

    def weights(at, own_gate, come_gate, own_up, come_up):
        parts = (own_gate, come_gate, own_up, come_up)
        return [
            (part, weight_buf.at[at, pl.ds(i * block, block)]) for i, part in enumerate(parts)
        ]

    pairs = [(rows_hbm.at[:, pl.ds(t.start, tile)], raw_buf.at[:, pl.ds(t.start, tile)]) for t in tiles]
    row_copies = start_copies(pairs, sems)
    pairs = []
    for m in range(PAIR):
        own = PAIR * half + m
        pairs += weights(
            m, t_gate_hbm.at[own], come_hbm.at[m], t_up_hbm.at[own], come_hbm.at[PAIR + m]
        )
    pairs += weights(
        PAIR,
        m_gate_hbm.at[0],
        come_hbm.at[2 * PAIR],
        m_up_hbm.at[0],
        come_hbm.at[2 * PAIR + 1],
    )
    copies = start_copies(pairs, sems, len(tiles))
    move = by_teacher(count, capacity, 1)
    for t, copy in zip(tiles, row_copies):
        copy.wait()
        row_buf[:, t] = dot_nn(move, raw_buf[:, t]).astype(BF16)
    weight_ref[...] = row_buf[:, features:]
    wait_copies(copies)
    for m in range(PAIR):
        lanes = slice(m * span, (m + 1) * span)
        rows = row_buf[lanes, :features]
        value = dot_nt(weight_buf[m], rows)
        t_silu, _ = silu_split(value[:units])
        teacher = (t_silu * value[units:]).astype(BF16)
        value = dot_nt(weight_buf[PAIR], rows)
        s_silu, s_slope = silu_split(value[:units])
        up = value[units:]
        student = (s_silu * up).astype(BF16)
        for i in range(places):
            at = m * places + i
            out_ref[at, 0] = student[:block]
            out_ref[at, 1] = student[block:]
            out_ref[at, 2] = teacher[:block]
            out_ref[at, 3] = teacher[block:]
        silu_ref[:, lanes] = s_silu
        slope_ref[:, lanes] = up * s_slope


def share_kernel(down_ref, merged_ref, came_ref, *out_refs):
    half, at = place()
    block = merged_ref.shape[1]
    quarter = out_refs[0].shape[2]
    for k, out_ref in enumerate(out_refs):
        there = (at + k) % RING
        m = there // (RING // PAIR)
        span = pl.ds(pl.multiple_of(there % (RING // PAIR) * quarter, SIDE), quarter)
        out_ref[0, :block] = down_ref[PAIR * half + m, :, span]
        out_ref[0, block:] = came_ref[m, :, span]
        out_ref[1, :block] = merged_ref[0, :, span]
        out_ref[1, block:] = came_ref[PAIR, :, span]


def gap_kernel(hidden_ref, weight_ref, *refs):
    down_refs = refs[:RING]
    grad_ref, kept_ref, other_ref = refs[RING:]
    block = hidden_ref.shape[2]
    units = 2 * block
    span = hidden_ref.shape[3]
    _, at = place()
    back = [(at + RING - k) % RING for k in range(RING)]
    student = jnp.concatenate([hidden_ref[i, a] for i in back for a in (0, 1)], axis=0)
    teacher = jnp.concatenate([hidden_ref[i, a] for i in back for a in (2, 3)], axis=0)
    t_down = jnp.concatenate([down_ref[0] for down_ref in down_refs], axis=0)
    m_down = jnp.concatenate([down_ref[1] for down_ref in down_refs], axis=0)
    gap = dot_tn(student, m_down) - dot_tn(teacher, t_down)
    start = pl.multiple_of(at // (RING // PAIR) * span, span)
    weight = weight_ref[pl.ds(start, span), SIDE - 1 : SIDE].astype(F32)
    slot_grad = (weight * gap).astype(BF16)
    grad = dot_nt(m_down, slot_grad).astype(BF16)
    down_grad = dot_nn(student, slot_grad).astype(BF16)
    for k, i in enumerate(back):
        grad_ref[i] = grad[k * units : (k + 1) * units]
        kept_ref[i] = down_grad[k * units : k * units + block]
        other_ref[i] = down_grad[k * units + block : (k + 1) * units]


def grads_kernel(capacity, parts_ref, silu_ref, slope_ref, rows_ref, own_ref, other_ref):
    block = own_ref.shape[1]
    places = parts_ref.shape[0] // PAIR
    sums = []
    for m in range(PAIR):
        total = parts_ref[m * places].astype(F32)
        for i in range(1, places):
            total += parts_ref[m * places + i].astype(F32)
        sums.append(total)
    total = jnp.concatenate(sums, axis=1)
    gate = (total * slope_ref[...]).astype(BF16)
    up = (total * silu_ref[...]).astype(BF16)
    stack = jnp.concatenate([gate[:block], up[:block], gate[block:], up[block:]], axis=0)
    stack = dot_nn(stack, by_teacher(stack.shape[1], capacity, 1)).astype(BF16)
    grads = dot_nn(stack, rows_ref[:, : own_ref.shape[2]])
    own_ref[0] = grads[:block]
    own_ref[1] = grads[block : 2 * block]
    other_ref[0] = grads[2 * block : 3 * block].astype(BF16)
    other_ref[1] = grads[3 * block :].astype(BF16)


def down_sum_kernel(parts_ref, out_ref):
    count, _, piece = parts_ref.shape
    quarters = out_ref.shape[1] // piece
    for q in range(quarters):
        total = parts_ref[q].astype(F32)
        for i in range(q + quarters, count, quarters):
            total += parts_ref[i].astype(F32)
        out_ref[:, q * piece : (q + 1) * piece] = total


def body(
    tokens,
    teacher_ids,
    route_weight,
    teacher_gate,
    teacher_up,
    teacher_down,
    merged_gate,
    merged_up,
    merged_down,
):
    n_dp = HALVES * RING
    experts = lax.axis_size("expert")
    features = tokens.shape[2]
    capacity = tokens.shape[1]
    ranks = teacher_ids.shape[2]
    block = merged_gate.shape[1]
    wide = features + SIDE
    quarter = features * PAIR // RING
    rows = experts * PAIR * capacity
    span = rows // PAIR
    half = lax.axis_index("dp") // RING
    rings = [[a * RING + i for i in range(RING)] for a in range(HALVES)]
    swap = [(a * RING + i, (1 - a) * RING + i) for a in range(HALVES) for i in range(RING)]

    turns = [
        [(a * RING + i, a * RING + (i + k) % RING) for a in range(HALVES) for i in range(RING)]
        for k in range(RING)
    ]

    def exchange(array, axis_name, groups=None):
        return lax.all_to_all(
            array, axis_name, split_axis=0, concat_axis=0, tiled=True, axis_index_groups=groups
        )

    def halves(array, which):
        return lax.dynamic_slice_in_dim(array, PAIR * which, PAIR, axis=0)

    packets, sent = call(
        pack_kernel,
        (
            jax.ShapeDtypeStruct((n_dp, capacity, wide), BF16),
            jax.ShapeDtypeStruct((PAIR + 1, block, features), BF16),
        ),
        (teacher_ids[0].T, tokens[0], route_weight[0], teacher_down, merged_down),
        far=range(1, 5),
        far_outs=(1,),
        scratch=[
            pltpu.VMEM((capacity, features), BF16),
            pltpu.VMEM((capacity, ranks), BF16),
            pltpu.VMEM((PAIR + 1, block, features), BF16),
            pltpu.SemaphoreType.DMA((PAIR + 3,)),
        ],
        mib=60,
    )
    came = lax.ppermute(sent, "dp", swap)
    group = exchange(packets, "dp").reshape(n_dp * capacity, wide)
    group, came = lax.optimization_barrier((group, came))

    (slots,) = call(
        lambda *refs: slots_kernel(ranks, capacity, *refs),
        (jax.ShapeDtypeStruct((rows, wide), BF16),),
        (group,),
        mib=60,
    )
    slots = exchange(slots.reshape(experts, PAIR * capacity, wide), "expert").reshape(rows, wide)

    down = call(
        share_kernel,
        tuple(jax.ShapeDtypeStruct((2, 2 * block, quarter), BF16) for _ in range(RING)),
        (teacher_down, merged_down, came),
    )
    down = [down[k] if k == 0 else lax.ppermute(down[k], "dp", turns[k]) for k in range(RING)]

    come = lax.ppermute(
        jnp.concatenate(
            [halves(teacher_gate, 1 - half), halves(teacher_up, 1 - half), merged_gate, merged_up],
            axis=0,
        ),
        "dp",
        swap,
    )
    slots, come, down = lax.optimization_barrier((slots, come, down))

    hidden, silu, slope, weight = call(
        lambda *refs: hidden_kernel(capacity, *refs),
        (
            jax.ShapeDtypeStruct((RING, 4, block, span), BF16),
            jax.ShapeDtypeStruct((2 * block, rows), F32),
            jax.ShapeDtypeStruct((2 * block, rows), F32),
            jax.ShapeDtypeStruct((rows, SIDE), BF16),
        ),
        (slots, teacher_gate, teacher_up, merged_gate, merged_up, come),
        far=range(6),
        scratch=[
            pltpu.VMEM((rows, wide), BF16),
            pltpu.VMEM((rows, wide), BF16),
            pltpu.VMEM((PAIR + 1, 4 * block, features), BF16),
            pltpu.SemaphoreType.DMA((32,)),
        ],
        mib=24,
    )
    hidden = exchange(hidden, "dp", rings)
    hidden_grad, kept_down, other_down = call(
        gap_kernel,
        (
            jax.ShapeDtypeStruct((RING, 2 * block, span), BF16),
            jax.ShapeDtypeStruct((RING, block, quarter), BF16),
            jax.ShapeDtypeStruct((RING, block, quarter), BF16),
        ),
        (hidden, weight, *down),
    )
    other_down = lax.ppermute(other_down, "dp", swap)
    parts = exchange(hidden_grad, "dp", rings)
    down_grad = (kept_down.astype(F32) + other_down.astype(F32)).astype(BF16)
    parts, down_grad = lax.optimization_barrier((parts, down_grad))
    down_grad = exchange(down_grad, "dp", rings)
    own, other = call(
        lambda *refs: grads_kernel(capacity, *refs),
        (
            jax.ShapeDtypeStruct((2, block, features), F32),
            jax.ShapeDtypeStruct((2, block, features), BF16),
        ),
        (parts, silu, slope, slots),
    )
    other = lax.ppermute(other, "dp", swap)
    (grad_down,) = call(
        down_sum_kernel, (jax.ShapeDtypeStruct((block, features), F32),), (down_grad,)
    )
    grad_gate = own[:1] + other[:1].astype(F32)
    grad_up = own[1:] + other[1:].astype(F32)
    return grad_gate, grad_up, grad_down[None]


def solution(mesh):
    placed = (P("expert", "dp", None),) * 9
    return jax.shard_map(
        body,
        mesh=mesh,
        in_specs=placed,
        out_specs=(P("expert", "dp", None),) * 3,
        check_vma=False,
    )
```

time: 224 us -> 251 us (1.12)
  starting transfers between devices: 35.6 us -> 69.8 us
  blocking collectives: 44.3 us -> 27 us
  waiting for transfers between devices: 98.7 us -> 112 us
  between operations: 14.3 us -> 1.05 us
  Pallas kernels: 14.5 us -> 21.2 us
  local copies, waits for them, and re-layouts: 10.8 us -> 15.1 us
    ppermute x1, waiting for transfers between devices: 0.01 us -> 24.8 us  [body(): came = lax.ppermute(sent, 'dp', swap)]
    ppermute x1 -> x7, starting transfers between devices: 4.19 us -> 27.6 us  [body(): lax.ppermute(down[k], 'dp', turns[k])]
    all_gather x1 -> x0, waiting for transfers between devices: 21.7 us -> none  [body(): lax.all_gather(turned, 'dp', axis=0, tiled=True, axis_index_groups=rings)]
    all_to_all x2 -> x1, blocking collectives: 44.3 us -> 27 us  [exchange(): lax.all_to_all(array, axis_name, split_axis=0, concat_axis=0, tiled=True,...]
    all_to_all x4, waiting for transfers between devices: 26 us -> 9.53 us  [exchange(): lax.all_to_all(array, axis_name, split_axis=0, concat_axis=0, tiled=True,...]
    all_to_all x4, starting transfers between devices: 15.5 us -> 29 us  [exchange(): lax.all_to_all(array, axis_name, split_axis=0, concat_axis=0, tiled=True,...]
    ppermute x1, waiting for transfers between devices: 32.5 us -> 43.6 us  [body(): lax.ppermute(jnp.concatenate([halves(teacher_gate, 1 - half), halves(teac...]
    ppermute x1 -> x7, waiting for transfers between devices: 11.6 us -> 22.1 us  [body(): lax.ppermute(down[k], 'dp', turns[k])]
  transfers between devices with their start and end apart: 10 -> 15, of which waited for: 7 -> 9; matrix products, arithmetic and copies ran while one was open for 2% -> 2% of each run, Pallas kernels for 3% -> 0%
where the time goes in v5:
time: 251 us; the launch traced here: 250 us
  waiting for transfers between devices  112 us (45%)
  starting transfers between devices  69.8 us (28%)
  blocking collectives  27 us (11%)
  Pallas kernels  21.2 us (8%)
  local copies, waits for them, and re-layouts  15.1 us (6%)
  other arithmetic  3.35 us (1%)
    ppermute x1, waiting for transfers between devices, body(): lax.ppermute(jnp.concatenate([halves(teacher_gate, 1 - half), halves(teac...  43.6 us
    all_to_all x4, starting transfers between devices, exchange(): lax.all_to_all(array, axis_name, split_axis=0, concat_axis=0, tiled=True,...  29 us
    ppermute x7, starting transfers between devices, body(): lax.ppermute(down[k], 'dp', turns[k])  27.6 us
    all_to_all x1, blocking collectives, exchange(): lax.all_to_all(array, axis_name, split_axis=0, concat_axis=0, tiled=True,...  27 us
    ppermute x1, waiting for transfers between devices, body(): came = lax.ppermute(sent, 'dp', swap)  24.8 us
    ppermute x7, waiting for transfers between devices, body(): lax.ppermute(down[k], 'dp', turns[k])  22.1 us
    pallas_call x7, Pallas kernels, call(): pl.pallas_call(kernel, out_shape=outs, in_specs=[space(i, far) for i in r...  21.2 us
    unnamed x64, local copies, waits for them, and re-layouts  12.5 us
  transfers between devices with their start and end apart: 15, of which 9 were waited for; matrix products, arithmetic and copies ran while one was open for 2% of the time, Pallas kernels for 0%

profile of v5, /device:TPU:6, one launch (start us, length us, event | category | flops | bytes accessed | tf_op | source)
XLA Modules:
  0.0 249.6 jit_solution(4328190521272415407)
XLA Ops:
  1.9 3.7 %shard_map.112 = (bf16[16,8,2688]{2,1,0:T(8,128)(2,1)}, bf16[3,48,2560]{2,1,0:T(8,128)(2,1)}) custom-call(s32[6,8]{1,0:T(8,128)} %bitcast.18, bf16[8,2560]{1,0:T(8,128)(2,1)} %bitcast.17, bf16[8,6]{1,0:T(8,128)(2,1)} %bitcast.19, bf16[4,48,2560]{2,1,0:T(8,128)(2,1)} %down_ref.1, bf16[1,48,2560]{2,1,0:T(8,128)(2,1)} %merged_ref.1), custom_call_target="tpu_custom_call" | custom-call | bytes 1270048 | tf_op jit(solution)/shard_map/pallas_call | solution.py:32
  5.6 13.3 %all-to-all-start = ((bf16[16,8,2688]{2,1,0:T(8,128)(2,1)}), bf16[16,8,2688]{2,1,0:T(8,128)(2,1)S(1)}, u32[]{:S(2)}, u32[]{:S(2)}) async-start(bf16[16,8,2688]{2,1,0:T(8,128)(2,1)} %get-tuple-element.36), calls=%async_computation | async-start | bytes 1376256 | tf_op jit(solution)/shard_map/all_to_all | solution.py:309
  18.9 2.0 collective-permute-start
  20.9 24.8 %collective-permute-done.came_ref = bf16[3,48,2560]{2,1,0:T(8,128)(2,1)S(1)} collective-permute-done((bf16[3,48,2560]{2,1,0:T(8,128)(2,1)}, bf16[3,48,2560]{2,1,0:T(8,128)(2,1)S(1)}, u32[]{:S(2)}, u32[]{:S(2)}) %collective-permute-start) | collective-permute-done | bytes 737312 | tf_op jit(solution)/shard_map/ppermute | solution.py:333
  46.6 3.9 %shard_map.113 = bf16[512,2688]{1,0:T(8,128)(2,1)} custom-call(bf16[128,2688]{1,0:T(8,128)(2,1)} %bitcast.15), custom_call_target="tpu_custom_call" | custom-call | bytes 688128 | tf_op jit(solution)/shard_map/pallas_call | solution.py:32
  50.5 8.7 %all-to-all-start.1 = ((bf16[32,16,2688]{2,1,0:T(8,128)(2,1)}), bf16[32,16,2688]{2,1,0:T(8,128)(2,1)S(1)}, u32[]{:S(2)}, u32[]{:S(2)}) async-start(bf16[32,16,2688]{2,1,0:T(8,128)(2,1)} %bitcast.14), calls=%async_computation.1 | async-start | bytes 5505024 | tf_op jit(solution)/shard_map/all_to_all | solution.py:309
  60.9 3.3 %collective-permute-start.1 = (bf16[6,48,2560]{2,1,0:T(8,128)(2,1)S(1)}, bf16[6,48,2560]{2,1,0:T(8,128)(2,1)S(1)}, u32[]{:S(2)}, u32[]{:S(2)}) collective-permute-start(bf16[6,48,2560]{2,1,0:T(8,128)(2,1)S(1)} %pad_maximum_fusion), channel_id=1, source_target_pairs={{0,256},{32,288},{64,320},{96,352},{128,384},{160,416},{192,448},{... | collective-permute-start | bytes 4423688 | tf_op jit(solution)/shard_map/ppermute | solution.py:352
  64.4 3.6 %collective-permute-start.2 = (bf16[2,96,640]{2,1,0:T(8,128)(2,1)S(1)}, bf16[2,96,640]{2,1,0:T(8,128)(2,1)S(1)}, u32[]{:S(2)}, u32[]{:S(2)}) collective-permute-start(bf16[2,96,640]{2,1,0:T(8,128)(2,1)S(1)} %get-tuple-element.41), channel_id=1, source_target_pairs={{0,32},{32,64},{64,96},{96,128},{128,160},{160,192},{192,224},{224... | collective-permute-start | bytes 737288 | tf_op jit(solution)/shard_map/ppermute | solution.py:350
  68.0 3.9 %collective-permute-start.3 = (bf16[2,96,640]{2,1,0:T(8,128)(2,1)S(1)}, bf16[2,96,640]{2,1,0:T(8,128)(2,1)S(1)}, u32[]{:S(2)}, u32[]{:S(2)}) collective-permute-start(bf16[2,96,640]{2,1,0:T(8,128)(2,1)S(1)} %get-tuple-element.42), channel_id=1, source_target_pairs={{0,64},{32,96},{64,128},{96,160},{128,192},{160,224},{192,0},{224,... | collective-permute-start | bytes 737288 | tf_op jit(solution)/shard_map/ppermute | solution.py:350
  71.9 4.5 %collective-permute-start.4 = (bf16[2,96,640]{2,1,0:T(8,128)(2,1)S(1)}, bf16[2,96,640]{2,1,0:T(8,128)(2,1)S(1)}, u32[]{:S(2)}, u32[]{:S(2)}) collective-permute-start(bf16[2,96,640]{2,1,0:T(8,128)(2,1)S(1)} %get-tuple-element.43), channel_id=1, source_target_pairs={{0,96},{32,128},{64,160},{96,192},{128,224},{160,0},{192,32},{224,... | collective-permute-start | bytes 737288 | tf_op jit(solution)/shard_map/ppermute | solution.py:350
  76.4 4.3 %collective-permute-start.5 = (bf16[2,96,640]{2,1,0:T(8,128)(2,1)S(1)}, bf16[2,96,640]{2,1,0:T(8,128)(2,1)S(1)}, u32[]{:S(2)}, u32[]{:S(2)}) collective-permute-start(bf16[2,96,640]{2,1,0:T(8,128)(2,1)S(1)} %get-tuple-element.44), channel_id=1, source_target_pairs={{0,128},{32,160},{64,192},{96,224},{128,0},{160,32},{192,64},{224,... | collective-permute-start | bytes 737288 | tf_op jit(solution)/shard_map/ppermute | solution.py:350
  80.7 43.6 %collective-permute-done.1.refs_5_ = bf16[6,48,2560]{2,1,0:T(8,128)(2,1)S(1)} collective-permute-done((bf16[6,48,2560]{2,1,0:T(8,128)(2,1)S(1)}, bf16[6,48,2560]{2,1,0:T(8,128)(2,1)S(1)}, u32[]{:S(2)}, u32[]{:S(2)}) %collective-permute-start.1) | collective-permute-done | bytes 1474592 | tf_op jit(solution)/shard_map/ppermute | solution.py:352
  125.4 5.6 %collective-permute-start.6 = (bf16[2,96,640]{2,1,0:T(8,128)(2,1)S(1)}, bf16[2,96,640]{2,1,0:T(8,128)(2,1)S(1)}, u32[]{:S(2)}, u32[]{:S(2)}) collective-permute-start(bf16[2,96,640]{2,1,0:T(8,128)(2,1)S(1)} %get-tuple-element.45), channel_id=1, source_target_pairs={{0,160},{32,192},{64,224},{96,0},{128,32},{160,64},{192,96},{224,1... | collective-permute-start | bytes 737288 | tf_op jit(solution)/shard_map/ppermute | solution.py:350
  131.7 3.5 %collective-permute-start.7 = (bf16[2,96,640]{2,1,0:T(8,128)(2,1)S(1)}, bf16[2,96,640]{2,1,0:T(8,128)(2,1)S(1)}, u32[]{:S(2)}, u32[]{:S(2)}) collective-permute-start(bf16[2,96,640]{2,1,0:T(8,128)(2,1)S(1)} %get-tuple-element.46), channel_id=1, source_target_pairs={{0,192},{32,224},{64,0},{96,32},{128,64},{160,96},{192,128},{224,1... | collective-permute-start | bytes 737288 | tf_op jit(solution)/shard_map/ppermute | solution.py:350
  135.8 2.2 collective-permute-start.8
  139.5 12.4 %collective-permute-done.6.refs_5_ = bf16[2,96,640]{2,1,0:T(8,128)(2,1)S(1)} collective-permute-done((bf16[2,96,640]{2,1,0:T(8,128)(2,1)S(1)}, bf16[2,96,640]{2,1,0:T(8,128)(2,1)S(1)}, u32[]{:S(2)}, u32[]{:S(2)}) %collective-permute-start.6) | collective-permute-done | bytes 245792 | tf_op jit(solution)/shard_map/ppermute | solution.py:350
  152.7 5.8 %collective-permute-done.7.refs_6_ = bf16[2,96,640]{2,1,0:T(8,128)(2,1)S(1)} collective-permute-done((bf16[2,96,640]{2,1,0:T(8,128)(2,1)S(1)}, bf16[2,96,640]{2,1,0:T(8,128)(2,1)S(1)}, u32[]{:S(2)}, u32[]{:S(2)}) %collective-permute-start.7) | collective-permute-done | bytes 245792 | tf_op jit(solution)/shard_map/ppermute | solution.py:350
  159.1 3.9 %collective-permute-done.8.refs_7_ = bf16[2,96,640]{2,1,0:T(8,128)(2,1)S(1)} collective-permute-done((bf16[2,96,640]{2,1,0:T(8,128)(2,1)S(1)}, bf16[2,96,640]{2,1,0:T(8,128)(2,1)S(1)}, u32[]{:S(2)}, u32[]{:S(2)}) %collective-permute-start.8) | collective-permute-done | bytes 245792 | tf_op jit(solution)/shard_map/ppermute | solution.py:350
  166.1 1.4 copy-done.4
  167.5 8.5 %shard_map.115 = (bf16[8,4,48,256]{3,2,1,0:T(8,128)(2,1)S(1)}, f32[96,512]{1,0:T(8,128)S(1)}, f32[96,512]{1,0:T(8,128)S(1)}, bf16[512,128]{1,0:T(8,128)(2,1)S(1)}) custom-call(bf16[512,2688]{1,0:T(8,128)(2,1)S(1)} %bitcast.12, bf16[4,48,2560]{2,1,0:T(8,128)(2,1)S(1)} %copy-done.1, bf16[4,48,2560]{2,1,0:T(8,128)(2,1)S(1)} %copy-done.2, ...), custom_call_target="tpu_custom_call" | custom-call | bytes 6684672 | tf_op jit(solution)/shard_map/pallas_call | solution.py:32
  176.1 27.0 %all_to_all.25.hidden_ref = bf16[8,4,48,256]{3,2,1,0:T(8,128)(2,1)S(1)} all-to-all(bf16[8,4,48,256]{3,2,1,0:T(8,128)(2,1)S(1)} %get-tuple-element.50), channel_id=1, replica_groups={{0,32,64,96,128,160,192,224},{256,288,320,352,384,416,448,480},{1,33,65..., dimensions={0} | all-to-all | bytes 1572864 | tf_op jit(solution)/shard_map/all_to_all | solution.py:309
  203.1 2.4 shard_map.116
  206.3 3.7 %collective-permute-start.9 = (bf16[8,48,640]{2,1,0:T(8,128)(2,1)}, bf16[8,48,640]{2,1,0:T(8,128)(2,1)}, u32[]{:S(2)}, u32[]{:S(2)}) collective-permute-start(bf16[8,48,640]{2,1,0:T(8,128)(2,1)} %get-tuple-element.62), channel_id=1, source_target_pairs={{0,256},{32,288},{64,320},{96,352},{128,384},{160,416},{192,448},{... | collective-permute-start | bytes 1474568 | tf_op jit(solution)/shard_map/ppermute | solution.py:390
  210.0 3.5 %all-to-all-start.3 = ((bf16[8,96,256]{2,1,0:T(8,128)(2,1)}), bf16[8,96,256]{2,1,0:T(8,128)(2,1)S(1)}, u32[]{:S(2)}, u32[]{:S(2)}) async-start(bf16[8,96,256]{2,1,0:T(8,128)(2,1)} %get-tuple-element.60), calls=%async_computation.3 | async-start | bytes 786432 | tf_op jit(solution)/shard_map/all_to_all | solution.py:309
  213.5 7.4 %collective-permute-done.9 = bf16[8,48,640]{2,1,0:T(8,128)(2,1)} collective-permute-done((bf16[8,48,640]{2,1,0:T(8,128)(2,1)}, bf16[8,48,640]{2,1,0:T(8,128)(2,1)}, u32[]{:S(2)}, u32[]{:S(2)}) %collective-permute-start.9) | collective-permute-done | bytes 491552 | tf_op jit(solution)/shard_map/ppermute | solution.py:390
  220.8 2.1 add_convert_fusion
  223.0 2.4 all-to-all-done.3.refs_0_
  225.4 1.7 shard_map.117
  228.1 4.3 %collective-permute-start.10 = (bf16[2,48,2560]{2,1,0:T(8,128)(2,1)}, bf16[2,48,2560]{2,1,0:T(8,128)(2,1)S(1)}, u32[]{:S(2)}, u32[]{:S(2)}) collective-permute-start(bf16[2,48,2560]{2,1,0:T(8,128)(2,1)} %get-tuple-element.67), channel_id=1, source_target_pairs={{0,256},{32,288},{64,320},{96,352},{128,384},{160,416},{192,448},{... | collective-permute-start | bytes 1474568 | tf_op jit(solution)/shard_map/ppermute | solution.py:403
  232.4 3.5 %all-to-all-start.4 = ((bf16[8,48,640]{2,1,0:T(8,128)(2,1)}), bf16[8,48,640]{2,1,0:T(8,128)(2,1)S(1)}, u32[]{:S(2)}, u32[]{:S(2)}) async-start(bf16[8,48,640]{2,1,0:T(8,128)(2,1)} %add_convert_fusion), calls=%async_computation.4 | async-start | bytes 983040 | tf_op jit(solution)/shard_map/all_to_all | solution.py:309
  235.9 4.7 %collective-permute-done.10 = bf16[2,48,2560]{2,1,0:T(8,128)(2,1)S(1)} collective-permute-done((bf16[2,48,2560]{2,1,0:T(8,128)(2,1)}, bf16[2,48,2560]{2,1,0:T(8,128)(2,1)S(1)}, u32[]{:S(2)}, u32[]{:S(2)}) %collective-permute-start.10) | collective-permute-done | bytes 491552 | tf_op jit(solution)/shard_map/ppermute | solution.py:403
  241.6 7.1 %all-to-all-done.4.parts_ref = bf16[8,48,640]{2,1,0:T(8,128)(2,1)S(1)} async-done(((bf16[8,48,640]{2,1,0:T(8,128)(2,1)}), bf16[8,48,640]{2,1,0:T(8,128)(2,1)S(1)}, u32[]{:S(2)}, u32[]{:S(2)}) %all-to-all-start.4) | async-done | bytes 491552 | tf_op jit(solution)/shard_map/all_to_all | solution.py:309
  (75 shorter events, 16.0 us)
Async XLA Ops:
  5.6 40.1 %all-to-all-start = ((bf16[16,8,2688]{2,1,0:T(8,128)(2,1)}), bf16[16,8,2688]{2,1,0:T(8,128)(2,1)S(1)}, u32[]{:S(2)}, u32[]{:S(2)}) async-start(bf16[16,8,2688]{2,1,0:T(8,128)(2,1)} %get-tuple-element.36), calls=%async_computation | async-start | bytes 1376256 | tf_op jit(solution)/shard_map/all_to_all | solution.py:309
  18.9 26.8 %collective-permute-start = (bf16[3,48,2560]{2,1,0:T(8,128)(2,1)}, bf16[3,48,2560]{2,1,0:T(8,128)(2,1)S(1)}, u32[]{:S(2)}, u32[]{:S(2)}) collective-permute-start(bf16[3,48,2560]{2,1,0:T(8,128)(2,1)} %get-tuple-element.37), channel_id=1, source_target_pairs={{0,256},{32,288},{64,320},{96,352},{128,384},{160,416},{192,448},{... | collective-permute-start | bytes 2211848 | tf_op jit(solution)/shard_map/ppermute | solution.py:333
  45.7 4.8 %copy-start.10 = (bf16[3,48,2560]{2,1,0:T(8,128)(2,1)}, bf16[3,48,2560]{2,1,0:T(8,128)(2,1)S(1)}, u32[]{:S(2)}) copy-start(bf16[3,48,2560]{2,1,0:T(8,128)(2,1)S(1)} %collective-permute-done.came_ref) | copy-start | bytes 2211844
  50.5 113.2 %all-to-all-start.1 = ((bf16[32,16,2688]{2,1,0:T(8,128)(2,1)}), bf16[32,16,2688]{2,1,0:T(8,128)(2,1)S(1)}, u32[]{:S(2)}, u32[]{:S(2)}) async-start(bf16[32,16,2688]{2,1,0:T(8,128)(2,1)} %bitcast.14), calls=%async_computation.1 | async-start | bytes 5505024 | tf_op jit(solution)/shard_map/all_to_all | solution.py:309
  60.6 3.5 %copy-start = (bf16[4,48,2560]{2,1,0:T(8,128)(2,1)S(1)}, bf16[4,48,2560]{2,1,0:T(8,128)(2,1)}, u32[]{:S(2)}) copy-start(bf16[4,48,2560]{2,1,0:T(8,128)(2,1)} %down_ref.1) | copy-start | bytes 2949124
  60.6 3.5 %copy-start.5 = (bf16[1,48,2560]{2,1,0:T(8,128)(2,1)S(1)}, bf16[1,48,2560]{2,1,0:T(8,128)(2,1)}, u32[]{:S(2)}) copy-start(bf16[1,48,2560]{2,1,0:T(8,128)(2,1)} %merged_ref.1) | copy-start | bytes 737284
  60.6 3.5 %copy-start.11 = (bf16[3,48,2560]{2,1,0:T(8,128)(2,1)S(1)}, bf16[3,48,2560]{2,1,0:T(8,128)(2,1)}, u32[]{:S(2)}) copy-start(bf16[3,48,2560]{2,1,0:T(8,128)(2,1)} %copy-done.10) | copy-start | bytes 2211844
  60.9 63.4 %collective-permute-start.1 = (bf16[6,48,2560]{2,1,0:T(8,128)(2,1)S(1)}, bf16[6,48,2560]{2,1,0:T(8,128)(2,1)S(1)}, u32[]{:S(2)}, u32[]{:S(2)}) collective-permute-start(bf16[6,48,2560]{2,1,0:T(8,128)(2,1)S(1)} %pad_maximum_fusion), channel_id=1, source_target_pairs={{0,256},{32,288},{64,320},{96,352},{128,384},{160,416},{192,448},{... | collective-permute-start | bytes 4423688 | tf_op jit(solution)/shard_map/ppermute | solution.py:352
  64.4 66.6 %collective-permute-start.2 = (bf16[2,96,640]{2,1,0:T(8,128)(2,1)S(1)}, bf16[2,96,640]{2,1,0:T(8,128)(2,1)S(1)}, u32[]{:S(2)}, u32[]{:S(2)}) collective-permute-start(bf16[2,96,640]{2,1,0:T(8,128)(2,1)S(1)} %get-tuple-element.41), channel_id=1, source_target_pairs={{0,32},{32,64},{64,96},{96,128},{128,160},{160,192},{192,224},{224... | collective-permute-start | bytes 737288 | tf_op jit(solution)/shard_map/ppermute | solution.py:350
  68.0 67.1 %collective-permute-start.3 = (bf16[2,96,640]{2,1,0:T(8,128)(2,1)S(1)}, bf16[2,96,640]{2,1,0:T(8,128)(2,1)S(1)}, u32[]{:S(2)}, u32[]{:S(2)}) collective-permute-start(bf16[2,96,640]{2,1,0:T(8,128)(2,1)S(1)} %get-tuple-element.42), channel_id=1, source_target_pairs={{0,64},{32,96},{64,128},{96,160},{128,192},{160,224},{192,0},{224,... | collective-permute-start | bytes 737288 | tf_op jit(solution)/shard_map/ppermute | solution.py:350
  71.9 66.2 %collective-permute-start.4 = (bf16[2,96,640]{2,1,0:T(8,128)(2,1)S(1)}, bf16[2,96,640]{2,1,0:T(8,128)(2,1)S(1)}, u32[]{:S(2)}, u32[]{:S(2)}) collective-permute-start(bf16[2,96,640]{2,1,0:T(8,128)(2,1)S(1)} %get-tuple-element.43), channel_id=1, source_target_pairs={{0,96},{32,128},{64,160},{96,192},{128,224},{160,0},{192,32},{224,... | collective-permute-start | bytes 737288 | tf_op jit(solution)/shard_map/ppermute | solution.py:350
  76.4 62.4 %collective-permute-start.5 = (bf16[2,96,640]{2,1,0:T(8,128)(2,1)S(1)}, bf16[2,96,640]{2,1,0:T(8,128)(2,1)S(1)}, u32[]{:S(2)}, u32[]{:S(2)}) collective-permute-start(bf16[2,96,640]{2,1,0:T(8,128)(2,1)S(1)} %get-tuple-element.44), channel_id=1, source_target_pairs={{0,128},{32,160},{64,192},{96,224},{128,0},{160,32},{192,64},{224,... | collective-permute-start | bytes 737288 | tf_op jit(solution)/shard_map/ppermute | solution.py:350
  125.4 26.5 %collective-permute-start.6 = (bf16[2,96,640]{2,1,0:T(8,128)(2,1)S(1)}, bf16[2,96,640]{2,1,0:T(8,128)(2,1)S(1)}, u32[]{:S(2)}, u32[]{:S(2)}) collective-permute-start(bf16[2,96,640]{2,1,0:T(8,128)(2,1)S(1)} %get-tuple-element.45), channel_id=1, source_target_pairs={{0,160},{32,192},{64,224},{96,0},{128,32},{160,64},{192,96},{224,1... | collective-permute-start | bytes 737288 | tf_op jit(solution)/shard_map/ppermute | solution.py:350
  131.7 26.8 %collective-permute-start.7 = (bf16[2,96,640]{2,1,0:T(8,128)(2,1)S(1)}, bf16[2,96,640]{2,1,0:T(8,128)(2,1)S(1)}, u32[]{:S(2)}, u32[]{:S(2)}) collective-permute-start(bf16[2,96,640]{2,1,0:T(8,128)(2,1)S(1)} %get-tuple-element.46), channel_id=1, source_target_pairs={{0,192},{32,224},{64,0},{96,32},{128,64},{160,96},{192,128},{224,1... | collective-permute-start | bytes 737288 | tf_op jit(solution)/shard_map/ppermute | solution.py:350
  135.8 27.1 %collective-permute-start.8 = (bf16[2,96,640]{2,1,0:T(8,128)(2,1)S(1)}, bf16[2,96,640]{2,1,0:T(8,128)(2,1)S(1)}, u32[]{:S(2)}, u32[]{:S(2)}) collective-permute-start(bf16[2,96,640]{2,1,0:T(8,128)(2,1)S(1)} %get-tuple-element.47), channel_id=1, source_target_pairs={{0,224},{32,0},{64,32},{96,64},{128,96},{160,128},{192,160},{224,1... | collective-permute-start | bytes 737288 | tf_op jit(solution)/shard_map/ppermute | solution.py:350
  166.1 1.4 copy-start.4
  167.5 35.6 %copy-start.26 = (bf16[2,96,640]{2,1,0:T(8,128)(2,1)S(1)}, bf16[2,96,640]{2,1,0:T(8,128)(2,1)}, u32[]{:S(2)}) copy-start(bf16[2,96,640]{2,1,0:T(8,128)(2,1)} %copy-done.25) | copy-start | bytes 737284
  176.0 29.5 %copy-start.27 = (f32[96,512]{1,0:T(8,128)}, f32[96,512]{1,0:T(8,128)S(1)}, u32[]{:S(2)}) copy-start(f32[96,512]{1,0:T(8,128)S(1)} %get-tuple-element.64.refs_1_) | copy-start | bytes 589828
  176.0 29.5 %copy-start.29 = (f32[96,512]{1,0:T(8,128)}, f32[96,512]{1,0:T(8,128)S(1)}, u32[]{:S(2)}) copy-start(f32[96,512]{1,0:T(8,128)S(1)} %get-tuple-element.65.refs_2_) | copy-start | bytes 589828
  176.0 27.1 %copy-start.14 = (bf16[2,96,640]{2,1,0:T(8,128)(2,1)S(1)}, bf16[2,96,640]{2,1,0:T(8,128)(2,1)}, u32[]{:S(2)}) copy-start(bf16[2,96,640]{2,1,0:T(8,128)(2,1)} %copy-done.13) | copy-start | bytes 737284
  176.0 27.1 %copy-start.16 = (bf16[2,96,640]{2,1,0:T(8,128)(2,1)S(1)}, bf16[2,96,640]{2,1,0:T(8,128)(2,1)}, u32[]{:S(2)}) copy-start(bf16[2,96,640]{2,1,0:T(8,128)(2,1)} %copy-done.15) | copy-start | bytes 737284
  176.0 27.1 %copy-start.18 = (bf16[2,96,640]{2,1,0:T(8,128)(2,1)S(1)}, bf16[2,96,640]{2,1,0:T(8,128)(2,1)}, u32[]{:S(2)}) copy-start(bf16[2,96,640]{2,1,0:T(8,128)(2,1)} %copy-done.17) | copy-start | bytes 737284
  176.1 27.0 %copy-start.20 = (bf16[2,96,640]{2,1,0:T(8,128)(2,1)S(1)}, bf16[2,96,640]{2,1,0:T(8,128)(2,1)}, u32[]{:S(2)}) copy-start(bf16[2,96,640]{2,1,0:T(8,128)(2,1)} %copy-done.19) | copy-start | bytes 737284
  176.1 27.0 %copy-start.22 = (bf16[2,96,640]{2,1,0:T(8,128)(2,1)S(1)}, bf16[2,96,640]{2,1,0:T(8,128)(2,1)}, u32[]{:S(2)}) copy-start(bf16[2,96,640]{2,1,0:T(8,128)(2,1)} %copy-done.21) | copy-start | bytes 737284
  176.1 27.0 %copy-start.24 = (bf16[2,96,640]{2,1,0:T(8,128)(2,1)S(1)}, bf16[2,96,640]{2,1,0:T(8,128)(2,1)}, u32[]{:S(2)}) copy-start(bf16[2,96,640]{2,1,0:T(8,128)(2,1)} %copy-done.23) | copy-start | bytes 737284
  206.3 19.1 %copy-start.28 = (f32[96,512]{1,0:T(8,128)S(1)}, f32[96,512]{1,0:T(8,128)}, u32[]{:S(2)}) copy-start(f32[96,512]{1,0:T(8,128)} %copy-done.27) | copy-start | bytes 589828
  206.3 19.1 %copy-start.30 = (f32[96,512]{1,0:T(8,128)S(1)}, f32[96,512]{1,0:T(8,128)}, u32[]{:S(2)}) copy-start(f32[96,512]{1,0:T(8,128)} %copy-done.29) | copy-start | bytes 589828
  206.3 14.6 %collective-permute-start.9 = (bf16[8,48,640]{2,1,0:T(8,128)(2,1)}, bf16[8,48,640]{2,1,0:T(8,128)(2,1)}, u32[]{:S(2)}, u32[]{:S(2)}) collective-permute-start(bf16[8,48,640]{2,1,0:T(8,128)(2,1)} %get-tuple-element.62), channel_id=1, source_target_pairs={{0,256},{32,288},{64,320},{96,352},{128,384},{160,416},{192,448},{... | collective-permute-start | bytes 1474568 | tf_op jit(solution)/shard_map/ppermute | solution.py:390
  210.0 15.4 %all-to-all-start.3 = ((bf16[8,96,256]{2,1,0:T(8,128)(2,1)}), bf16[8,96,256]{2,1,0:T(8,128)(2,1)S(1)}, u32[]{:S(2)}, u32[]{:S(2)}) async-start(bf16[8,96,256]{2,1,0:T(8,128)(2,1)} %get-tuple-element.60), calls=%async_computation.3 | async-start | bytes 786432 | tf_op jit(solution)/shard_map/all_to_all | solution.py:309
  228.1 12.6 %copy-start.7 = (f32[2,48,2560]{2,1,0:T(8,128)S(1)}, f32[2,48,2560]{2,1,0:T(8,128)}, u32[]{:S(2)}) copy-start(f32[2,48,2560]{2,1,0:T(8,128)} %copy-done.6) | copy-start | bytes 2949124
  228.1 12.6 %collective-permute-start.10 = (bf16[2,48,2560]{2,1,0:T(8,128)(2,1)}, bf16[2,48,2560]{2,1,0:T(8,128)(2,1)S(1)}, u32[]{:S(2)}, u32[]{:S(2)}) collective-permute-start(bf16[2,48,2560]{2,1,0:T(8,128)(2,1)} %get-tuple-element.67), channel_id=1, source_target_pairs={{0,256},{32,288},{64,320},{96,352},{128,384},{160,416},{192,448},{... | collective-permute-start | bytes 1474568 | tf_op jit(solution)/shard_map/ppermute | solution.py:403
  232.4 16.4 %all-to-all-start.4 = ((bf16[8,48,640]{2,1,0:T(8,128)(2,1)}), bf16[8,48,640]{2,1,0:T(8,128)(2,1)S(1)}, u32[]{:S(2)}, u32[]{:S(2)}) async-start(bf16[8,48,640]{2,1,0:T(8,128)(2,1)} %add_convert_fusion), calls=%async_computation.4 | async-start | bytes 983040 | tf_op jit(solution)/shard_map/all_to_all | solution.py:309
  (15 other events, 13.8 us)

commit v6 on v5

v6 whole, which is shorter than its diff:
```python
import jax
import jax.numpy as jnp
from jax import lax
from jax.experimental import pallas as pl
from jax.experimental.pallas import tpu as pltpu
from jax.sharding import PartitionSpec as P

HALVES = 2
PAIR = 2
RING = 8
SIDE = 128
BF16 = jnp.bfloat16
F32 = jnp.float32


def dot_nn(a, b):
    return jnp.dot(a, b, preferred_element_type=F32)


def dot_nt(a, b):
    return lax.dot_general(a, b, (((1,), (1,)), ((), ())), preferred_element_type=F32)


def dot_tn(a, b):
    return lax.dot_general(a, b, (((0,), (0,)), ((), ())), preferred_element_type=F32)


def call(kernel, outs, args, mib=16, flops=0):
    space = pl.BlockSpec(memory_space=pltpu.VMEM)
    return pl.pallas_call(
        kernel,
        out_shape=outs,
        in_specs=[space] * len(args),
        out_specs=[space] * len(outs),
        compiler_params=pltpu.CompilerParams(vmem_limit_bytes=mib * 1024 * 1024),
        cost_estimate=pl.CostEstimate(
            flops=flops,
            bytes_accessed=sum(a.size * a.dtype.itemsize for a in args),
            transcendentals=0,
        ),
    )(*args)


def place():
    at = lax.axis_index("dp")
    return at // RING, at % RING


def pack_kernel(ids_ref, token_ref, weight_ref, out_ref):
    ranks, count = ids_ref.shape
    features = token_ref.shape[1]
    lane = lax.broadcasted_iota(jnp.int32, (ranks, SIDE), 1)
    rank = lax.broadcasted_iota(jnp.int32, (ranks, SIDE), 0)
    spread = jnp.where(lane == rank, 1.0, 0.0).astype(BF16)
    side = dot_tn(ids_ref[...].astype(F32).astype(BF16), spread)
    lane = lax.broadcasted_iota(jnp.int32, (count, SIDE), 1)
    weight = weight_ref[...].astype(F32)
    for k in range(ranks):
        side = jnp.where(lane == ranks + k, weight[:, k : k + 1], side)
    side = side.astype(BF16)
    tokens = token_ref[...]
    for i in range(out_ref.shape[0]):
        out_ref[i, :, :features] = tokens
        out_ref[i, :, features:] = side


def slots_kernel(ranks, capacity, group_ref, out_ref):
    half, _ = place()
    wide = group_ref.shape[1] - SIDE
    count = group_ref.shape[0]
    slots = out_ref.shape[0]
    side = group_ref[:, wide:].astype(F32)
    slot = lax.broadcasted_iota(jnp.int32, (count, slots), 1)
    column, inner = slot // (PAIR * capacity), slot % (PAIR * capacity)
    teacher = (column * HALVES * PAIR + half * PAIR + inner // capacity).astype(F32)
    position = (inner % capacity).astype(F32)
    hits = jnp.zeros((count, slots), F32)
    weight = jnp.zeros((count, slots), F32)
    for k in range(ranks):
        same = side[:, k : k + 1] == teacher
        hits = jnp.where(same, 1.0, hits)
        weight = jnp.where(same, side[:, ranks + k : ranks + k + 1], weight)
    later = lax.broadcasted_iota(jnp.int32, (count, count), 0)
    earlier = lax.broadcasted_iota(jnp.int32, (count, count), 1)
    below = jnp.where(earlier < later, 1.0, 0.0).astype(BF16)
    before = dot_nn(below, hits.astype(BF16))
    chosen = jnp.where((hits > 0.0) & (before == position), 1.0, 0.0)
    out_ref[:, :wide] = dot_tn(chosen.astype(BF16), group_ref[:, :wide]).astype(BF16)
    weights = dot_tn((chosen * weight).astype(BF16), jnp.ones((count, SIDE), BF16))
    out_ref[:, wide:] = weights.astype(BF16)


def by_teacher(count, capacity, source_axis):
    source = lax.broadcasted_iota(jnp.int32, (count, count), source_axis)
    target = lax.broadcasted_iota(jnp.int32, (count, count), 1 - source_axis)
    group, inner = source // (PAIR * capacity), source % (PAIR * capacity)
    goes = (inner // capacity) * (count // PAIR) + group * capacity + inner % capacity
    return jnp.where(goes == target, 1.0, 0.0).astype(BF16)


def silu_split(value):
    logistic = jax.nn.sigmoid(value)
    return value * logistic, logistic * (1.0 + value * (1.0 - logistic))


def hidden_kernel(
    capacity,
    rows_ref,
    t_gate_ref,
    t_up_ref,
    m_gate_ref,
    m_up_ref,
    t_come_ref,
    m_come_ref,
    out_ref,
    silu_ref,
    slope_ref,
    weight_ref,
):
    half, _ = place()
    block = m_gate_ref.shape[1]
    units = 2 * block
    count = rows_ref.shape[0]
    features = rows_ref.shape[1] - SIDE
    span = count // PAIR
    places = out_ref.shape[0] // PAIR
    rows = rows_ref[:, :features]

    def gate_up(*parts):
        value = dot_nt(jnp.concatenate(parts, axis=0), rows)
        return value[:units], value[units:]

    gate, up = gate_up(m_gate_ref[0], m_come_ref[0], m_up_ref[0], m_come_ref[1])
    silu, slope = silu_split(gate)
    silu_ref[...] = silu
    slope_ref[...] = up * slope
    hidden = [(silu * up).astype(BF16)]
    for m in range(PAIR):
        own = PAIR * half + m
        gate, up = gate_up(t_gate_ref[own], t_come_ref[m], t_up_ref[own], t_come_ref[PAIR + m])
        silu, _ = silu_split(gate)
        hidden.append((silu * up).astype(BF16))
    move = by_teacher(count, capacity, 0)
    hidden = dot_nn(jnp.concatenate(hidden, axis=0), move).astype(BF16)
    weight_ref[...] = dot_tn(move, rows_ref[:, features:]).astype(BF16)
    for m in range(PAIR):
        lanes = slice(m * span, (m + 1) * span)
        first = (1 + m) * units
        for i in range(places):
            at = m * places + i
            out_ref[at, 0] = hidden[:block, lanes]
            out_ref[at, 1] = hidden[block:units, lanes]
            out_ref[at, 2] = hidden[first : first + block, lanes]
            out_ref[at, 3] = hidden[first + block : first + units, lanes]


def share_kernel(down_ref, merged_ref, *out_refs):
    half, at = place()
    quarter = out_refs[0].shape[2]
    for k, out_ref in enumerate(out_refs):
        there = (at + k) % RING
        m = there // (RING // PAIR)
        span = pl.ds(pl.multiple_of(there % (RING // PAIR) * quarter, SIDE), quarter)
        out_ref[0] = down_ref[PAIR * half + m, :, span]
        out_ref[1] = down_ref[PAIR * (1 - half) + m, :, span]
        out_ref[2] = merged_ref[0, :, span]


def pass_kernel(*refs):
    out_ref = refs[-1]
    for k, down_ref in enumerate(refs[:-1]):
        out_ref[k] = down_ref[1:]


def gap_kernel(hidden_ref, weight_ref, came_ref, *refs):
    down_refs = refs[:RING]
    grad_ref, student_ref, slot_grad_ref = refs[RING:]
    block = hidden_ref.shape[2]
    units = 2 * block
    span = hidden_ref.shape[3]
    _, at = place()
    back = [(at + RING - k) % RING for k in range(RING)]
    student = jnp.concatenate([hidden_ref[i, a] for i in back for a in (0, 1)], axis=0)
    teacher = jnp.concatenate([hidden_ref[i, a] for i in back for a in (2, 3)], axis=0)
    t_down = jnp.concatenate([x for k in range(RING) for x in (down_refs[k][0], came_ref[k, 0])], axis=0)
    m_down = jnp.concatenate([x for k in range(RING) for x in (down_refs[k][2], came_ref[k, 1])], axis=0)
    gap = dot_tn(student, m_down) - dot_tn(teacher, t_down)
    start = pl.multiple_of(at // (RING // PAIR) * span, span)
    weight = weight_ref[pl.ds(start, span), SIDE - 1 : SIDE].astype(F32)
    slot_grad = (weight * gap).astype(BF16)
    grad = dot_nt(m_down, slot_grad).astype(BF16)
    for k, i in enumerate(back):
        grad_ref[i] = grad[k * units : (k + 1) * units]
    student_ref[...] = student
    slot_grad_ref[...] = slot_grad


def down_grad_kernel(student_ref, slot_grad_ref, kept_ref, other_ref):
    block = kept_ref.shape[1]
    units = 2 * block
    _, at = place()
    down_grad = dot_nn(student_ref[...], slot_grad_ref[...]).astype(BF16)
    for k in range(RING):
        i = (at + RING - k) % RING
        kept_ref[i] = down_grad[k * units : k * units + block]
        other_ref[i] = down_grad[k * units + block : (k + 1) * units]


def grads_kernel(capacity, parts_ref, silu_ref, slope_ref, rows_ref, own_ref, other_ref):
    block = own_ref.shape[1]
    places = parts_ref.shape[0] // PAIR
    units = parts_ref.shape[1]
    count = rows_ref.shape[0]
    parts = jnp.concatenate(
        [
            jnp.concatenate([parts_ref[m * places + i] for i in range(places)], axis=0)
            for m in range(PAIR)
        ],
        axis=1,
    )
    parts = dot_nn(parts, by_teacher(count, capacity, 1))
    total = parts[:units]
    for i in range(1, places):
        total += parts[i * units : (i + 1) * units]
    gate = (total * slope_ref[...]).astype(BF16)
    up = (total * silu_ref[...]).astype(BF16)
    stack = jnp.concatenate([gate[:block], up[:block], gate[block:], up[block:]], axis=0)
    grads = dot_nn(stack, rows_ref[:, : own_ref.shape[2]])
    own_ref[0] = grads[:block]
    own_ref[1] = grads[block : 2 * block]
    other_ref[0] = grads[2 * block : 3 * block].astype(BF16)
    other_ref[1] = grads[3 * block :].astype(BF16)


def down_sum_kernel(parts_ref, out_ref):
    count, _, piece = parts_ref.shape
    quarters = out_ref.shape[1] // piece
    for q in range(quarters):
        total = parts_ref[q].astype(F32)
        for i in range(q + quarters, count, quarters):
            total += parts_ref[i].astype(F32)
        out_ref[:, q * piece : (q + 1) * piece] = total


def body(
    tokens,
    teacher_ids,
    route_weight,
    teacher_gate,
    teacher_up,
    teacher_down,
    merged_gate,
    merged_up,
    merged_down,
):
    n_dp = HALVES * RING
    experts = lax.axis_size("expert")
    features = tokens.shape[2]
    capacity = tokens.shape[1]
    ranks = teacher_ids.shape[2]
    block = merged_gate.shape[1]
    wide = features + SIDE
    quarter = features * PAIR // RING
    rows = experts * PAIR * capacity
    span = rows // PAIR
    half = lax.axis_index("dp") // RING
    rings = [[a * RING + i for i in range(RING)] for a in range(HALVES)]
    swap = [(a * RING + i, (1 - a) * RING + i) for a in range(HALVES) for i in range(RING)]

    turns = [
        [(a * RING + i, a * RING + (i + k) % RING) for a in range(HALVES) for i in range(RING)]
        for k in range(RING)
    ]

    def exchange(array, axis_name, groups=None):
        return lax.all_to_all(
            array, axis_name, split_axis=0, concat_axis=0, tiled=True, axis_index_groups=groups
        )

    def halves(array, which):
        return lax.dynamic_slice_in_dim(array, PAIR * which, PAIR, axis=0)

    (packets,) = call(
        pack_kernel,
        (jax.ShapeDtypeStruct((n_dp, capacity, wide), BF16),),
        (teacher_ids[0].T, tokens[0], route_weight[0]),
    )
    group = exchange(packets, "dp").reshape(n_dp * capacity, wide)

    m_come = lax.ppermute(jnp.concatenate([merged_gate, merged_up], axis=0), "dp", swap)
    group, m_come = lax.optimization_barrier((group, m_come))
    (slots,) = call(
        lambda *refs: slots_kernel(ranks, capacity, *refs),
        (jax.ShapeDtypeStruct((rows, wide), BF16),),
        (group,),
        mib=60,
    )
    slots = exchange(slots.reshape(experts, PAIR * capacity, wide), "expert").reshape(rows, wide)

    down = call(
        share_kernel,
        tuple(jax.ShapeDtypeStruct((PAIR + 1, block, quarter), BF16) for _ in range(RING)),
        (teacher_down, merged_down),
    )
    down = [down[k] if k == 0 else lax.ppermute(down[k], "dp", turns[k]) for k in range(RING)]

    t_sent = jnp.concatenate([halves(teacher_gate, 1 - half), halves(teacher_up, 1 - half)], axis=0)
    t_sent, down[3], down[5] = lax.optimization_barrier((t_sent, down[3], down[5]))
    t_come = lax.ppermute(t_sent, "dp", swap)
    slots, t_come, down = lax.optimization_barrier((slots, t_come, down))

    (passed,) = call(
        pass_kernel, (jax.ShapeDtypeStruct((RING, PAIR, block, quarter), BF16),), tuple(down)
    )
    came = lax.ppermute(passed, "dp", swap)

    hidden, silu, slope, weight = call(
        lambda *refs: hidden_kernel(capacity, *refs),
        (
            jax.ShapeDtypeStruct((RING, 4, block, span), BF16),
            jax.ShapeDtypeStruct((2 * block, rows), F32),
            jax.ShapeDtypeStruct((2 * block, rows), F32),
            jax.ShapeDtypeStruct((rows, SIDE), BF16),
        ),
        (slots, teacher_gate, teacher_up, merged_gate, merged_up, t_come, m_come),
        mib=60,
    )
    hidden = exchange(hidden, "dp", rings)
    hidden_grad, student, slot_grad = call(
        gap_kernel,
        (
            jax.ShapeDtypeStruct((RING, 2 * block, span), BF16),
            jax.ShapeDtypeStruct((n_dp * block, span), BF16),
            jax.ShapeDtypeStruct((span, quarter), BF16),
        ),
        (hidden, weight, came, *down),
    )
    parts = exchange(hidden_grad, "dp", rings)
    kept_down, other_down = call(
        down_grad_kernel,
        (
            jax.ShapeDtypeStruct((RING, block, quarter), BF16),
            jax.ShapeDtypeStruct((RING, block, quarter), BF16),
        ),
        (student, slot_grad),
    )
    other_down = lax.ppermute(other_down, "dp", swap)
    down_grad = (kept_down.astype(F32) + other_down.astype(F32)).astype(BF16)
    own, other = call(
        lambda *refs: grads_kernel(capacity, *refs),
        (
            jax.ShapeDtypeStruct((2, block, features), F32),
            jax.ShapeDtypeStruct((2, block, features), BF16),
        ),
        (parts, silu, slope, slots),
        flops=0,
    )
    other, down_grad = lax.optimization_barrier((other, down_grad))
    down_grad = exchange(down_grad, "dp", rings)
    other = lax.ppermute(other, "dp", swap)
    (grad_down,) = call(
        down_sum_kernel, (jax.ShapeDtypeStruct((block, features), F32),), (down_grad,)
    )
    grad_gate = own[:1] + other[:1].astype(F32)
    grad_up = own[1:] + other[1:].astype(F32)
    return grad_gate, grad_up, grad_down[None]


def solution(mesh):
    placed = (P("expert", "dp", None),) * 9
    return jax.shard_map(
        body,
        mesh=mesh,
        in_specs=placed,
        out_specs=(P("expert", "dp", None),) * 3,
        check_vma=False,
    )
```

time: 251 us -> 232 us (0.924)
  waiting for transfers between devices: 112 us -> 83.7 us
  blocking collectives: 27 us -> 0 us
  local copies, waits for them, and re-layouts: 15.1 us -> 34.7 us
  starting transfers between devices: 69.8 us -> 87.6 us
  Pallas kernels: 21.2 us -> 17.8 us
    all_to_all x1 -> x0, blocking collectives: 27 us -> none  [exchange(): lax.all_to_all(array, axis_name, split_axis=0, concat_axis=0, tiled=True,...]
    ppermute x2 -> x3, waiting for transfers between devices: 68.4 us -> 43.3 us  [the longest x1 22.8 us: body(): came = lax.ppermute(passed, 'dp', swap)]
    unnamed x64 -> x90, local copies, waits for them, and re-layouts: 12.5 us -> 32.7 us
    all_to_all x4 -> x5, starting transfers between devices: 29 us -> 40.7 us  [exchange(): lax.all_to_all(array, axis_name, split_axis=0, concat_axis=0, tiled=True,...]
    ppermute x2 -> x3, starting transfers between devices: 5.26 us -> 11.6 us  [the longest x1 6.08 us: body(): t_come = lax.ppermute(t_sent, 'dp', swap)]
    pallas_call x7 -> x9, Pallas kernels: 21.2 us -> 17.8 us  [call(): pl.pallas_call(kernel, out_shape=outs, in_specs=[space] * len(args), out_...]
    ppermute x7, waiting for transfers between devices: 22.1 us -> 19.5 us  [body(): lax.ppermute(down[k], 'dp', turns[k])]
    all_to_all x4 -> x5, waiting for transfers between devices: 9.53 us -> 11.3 us  [exchange(): lax.all_to_all(array, axis_name, split_axis=0, concat_axis=0, tiled=True,...]
  transfers between devices with their start and end apart: 15 -> 17, of which waited for: 9 -> 12; matrix products, arithmetic and copies ran while one was open for 2% -> 3% of each run, Pallas kernels for 0% -> 0%
where the time goes in v6:
time: 232 us; the launch traced here: 230 us
  starting transfers between devices  87.6 us (38%)
  waiting for transfers between devices  83.7 us (36%)
  local copies, waits for them, and re-layouts  34.7 us (15%)
  Pallas kernels  17.8 us (8%)
  other arithmetic  5.48 us (2%)
    all_to_all x5, starting transfers between devices, exchange(): lax.all_to_all(array, axis_name, split_axis=0, concat_axis=0, tiled=True,...  40.7 us
    unnamed x90, local copies, waits for them, and re-layouts  32.7 us
    ppermute x7, starting transfers between devices, body(): lax.ppermute(down[k], 'dp', turns[k])  27.6 us
    ppermute x1, waiting for transfers between devices, body(): came = lax.ppermute(passed, 'dp', swap)  22.8 us
    ppermute x7, waiting for transfers between devices, body(): lax.ppermute(down[k], 'dp', turns[k])  19.5 us
    ppermute x1, waiting for transfers between devices, body(): lax.ppermute(jnp.concatenate([merged_gate, merged_up], axis=0), 'dp', swap)  19 us
    pallas_call x9, Pallas kernels, call(): pl.pallas_call(kernel, out_shape=outs, in_specs=[space] * len(args), out_...  17.8 us
    all_to_all x5, waiting for transfers between devices, exchange(): lax.all_to_all(array, axis_name, split_axis=0, concat_axis=0, tiled=True,...  11.3 us
  transfers between devices with their start and end apart: 17, of which 12 were waited for; matrix products, arithmetic and copies ran while one was open for 3% of the time, Pallas kernels for 0%

profile of v6, /device:TPU:6, one launch (start us, length us, event | category | flops | bytes accessed | tf_op | source)
XLA Modules:
  0.0 230.3 jit_solution(8550204071638915549)
XLA Ops:
  3.8 13.3 %all-to-all-start = ((bf16[16,8,2688]{2,1,0:T(8,128)(2,1)}), bf16[16,8,2688]{2,1,0:T(8,128)(2,1)S(1)}, u32[]{:S(2)}, u32[]{:S(2)}) async-start(bf16[16,8,2688]{2,1,0:T(8,128)(2,1)} %shard_map.112), calls=%async_computation | async-start | bytes 1376256 | tf_op jit(solution)/shard_map/all_to_all | solution.py:276
  18.2 2.0 collective-permute-start
  20.3 19.0 %collective-permute-done.refs_6_ = bf16[2,48,2560]{2,1,0:T(8,128)(2,1)} collective-permute-done((bf16[2,48,2560]{2,1,0:T(8,128)(2,1)S(1)}, bf16[2,48,2560]{2,1,0:T(8,128)(2,1)}, u32[]{:S(2)}, u32[]{:S(2)}) %collective-permute-start) | collective-permute-done | bytes 491552 | tf_op jit(solution)/shard_map/ppermute | solution.py:290
  40.1 3.9 %shard_map.113 = bf16[512,2688]{1,0:T(8,128)(2,1)} custom-call(bf16[128,2688]{1,0:T(8,128)(2,1)} %bitcast.18), custom_call_target="tpu_custom_call" | custom-call | bytes 688128 | tf_op jit(solution)/shard_map/pallas_call | solution.py:30
  44.0 8.8 %all-to-all-start.1 = ((bf16[32,16,2688]{2,1,0:T(8,128)(2,1)}), bf16[32,16,2688]{2,1,0:T(8,128)(2,1)S(1)}, u32[]{:S(2)}, u32[]{:S(2)}) async-start(bf16[32,16,2688]{2,1,0:T(8,128)(2,1)} %bitcast.17), calls=%async_computation.1 | async-start | bytes 5505024 | tf_op jit(solution)/shard_map/all_to_all | solution.py:276
  57.6 4.2 %collective-permute-start.1 = (bf16[3,48,640]{2,1,0:T(8,128)(2,1)}, bf16[3,48,640]{2,1,0:T(8,128)(2,1)S(1)}, u32[]{:S(2)}, u32[]{:S(2)}) collective-permute-start(bf16[3,48,640]{2,1,0:T(8,128)(2,1)} %get-tuple-element.40), channel_id=1, source_target_pairs={{0,96},{32,128},{64,160},{96,192},{128,224},{160,0},{192,32},{224,... | collective-permute-start | bytes 552968 | tf_op jit(solution)/shard_map/ppermute | solution.py:305
  61.8 4.7 %collective-permute-start.2 = (bf16[3,48,640]{2,1,0:T(8,128)(2,1)}, bf16[3,48,640]{2,1,0:T(8,128)(2,1)S(1)}, u32[]{:S(2)}, u32[]{:S(2)}) collective-permute-start(bf16[3,48,640]{2,1,0:T(8,128)(2,1)} %get-tuple-element.41), channel_id=1, source_target_pairs={{0,160},{32,192},{64,224},{96,0},{128,32},{160,64},{192,96},{224,1... | collective-permute-start | bytes 552968 | tf_op jit(solution)/shard_map/ppermute | solution.py:305
  67.9 5.5 %collective-permute-done.1.refs_3_ = bf16[3,48,640]{2,1,0:T(8,128)(2,1)S(1)} collective-permute-done((bf16[3,48,640]{2,1,0:T(8,128)(2,1)}, bf16[3,48,640]{2,1,0:T(8,128)(2,1)S(1)}, u32[]{:S(2)}, u32[]{:S(2)}) %collective-permute-start.1) | collective-permute-done | bytes 184352 | tf_op jit(solution)/shard_map/ppermute | solution.py:305
  74.1 3.5 %collective-permute-done.2.refs_5_ = bf16[3,48,640]{2,1,0:T(8,128)(2,1)S(1)} collective-permute-done((bf16[3,48,640]{2,1,0:T(8,128)(2,1)}, bf16[3,48,640]{2,1,0:T(8,128)(2,1)S(1)}, u32[]{:S(2)}, u32[]{:S(2)}) %collective-permute-start.2) | collective-permute-done | bytes 184352 | tf_op jit(solution)/shard_map/ppermute | solution.py:305
  78.3 6.1 %collective-permute-start.3 = (bf16[4,48,2560]{2,1,0:T(8,128)(2,1)S(1)}, bf16[4,48,2560]{2,1,0:T(8,128)(2,1)}, u32[]{:S(2)}, u32[]{:S(2)}) collective-permute-start(bf16[4,48,2560]{2,1,0:T(8,128)(2,1)S(1)} %pad_maximum_fusion), channel_id=1, source_target_pairs={{0,256},{32,288},{64,320},{96,352},{128,384},{160,416},{192,448},{... | collective-permute-start | bytes 2949128 | tf_op jit(solution)/shard_map/ppermute | solution.py:309
  84.4 5.7 %collective-permute-start.4 = (bf16[3,48,640]{2,1,0:T(8,128)(2,1)S(1)}, bf16[3,48,640]{2,1,0:T(8,128)(2,1)S(1)}, u32[]{:S(2)}, u32[]{:S(2)}) collective-permute-start(bf16[3,48,640]{2,1,0:T(8,128)(2,1)S(1)} %copy-done.43), channel_id=1, source_target_pairs={{0,32},{32,64},{64,96},{96,128},{128,160},{160,192},{192,224},{224... | collective-permute-start | bytes 552968 | tf_op jit(solution)/shard_map/ppermute | solution.py:305
  90.1 2.3 collective-permute-start.5
  92.4 3.7 %collective-permute-start.6 = (bf16[3,48,640]{2,1,0:T(8,128)(2,1)S(1)}, bf16[3,48,640]{2,1,0:T(8,128)(2,1)S(1)}, u32[]{:S(2)}, u32[]{:S(2)}) collective-permute-start(bf16[3,48,640]{2,1,0:T(8,128)(2,1)S(1)} %copy-done.39), channel_id=1, source_target_pairs={{0,128},{32,160},{64,192},{96,224},{128,0},{160,32},{192,64},{224,... | collective-permute-start | bytes 552968 | tf_op jit(solution)/shard_map/ppermute | solution.py:305
  96.2 3.9 %collective-permute-start.7 = (bf16[3,48,640]{2,1,0:T(8,128)(2,1)S(1)}, bf16[3,48,640]{2,1,0:T(8,128)(2,1)S(1)}, u32[]{:S(2)}, u32[]{:S(2)}) collective-permute-start(bf16[3,48,640]{2,1,0:T(8,128)(2,1)S(1)} %get-tuple-element.49), channel_id=1, source_target_pairs={{0,192},{32,224},{64,0},{96,32},{128,64},{160,96},{192,128},{224,1... | collective-permute-start | bytes 552968 | tf_op jit(solution)/shard_map/ppermute | solution.py:305
  100.7 3.2 %collective-permute-start.8 = (bf16[3,48,640]{2,1,0:T(8,128)(2,1)S(1)}, bf16[3,48,640]{2,1,0:T(8,128)(2,1)S(1)}, u32[]{:S(2)}, u32[]{:S(2)}) collective-permute-start(bf16[3,48,640]{2,1,0:T(8,128)(2,1)S(1)} %get-tuple-element.50), channel_id=1, source_target_pairs={{0,224},{32,0},{64,32},{96,64},{128,96},{160,128},{192,160},{224,1... | collective-permute-start | bytes 552968 | tf_op jit(solution)/shard_map/ppermute | solution.py:305
  103.9 4.0 %collective-permute-done.5.refs_2_ = bf16[3,48,640]{2,1,0:T(8,128)(2,1)S(1)} collective-permute-done((bf16[3,48,640]{2,1,0:T(8,128)(2,1)S(1)}, bf16[3,48,640]{2,1,0:T(8,128)(2,1)S(1)}, u32[]{:S(2)}, u32[]{:S(2)}) %collective-permute-start.5) | collective-permute-done | bytes 184352 | tf_op jit(solution)/shard_map/ppermute | solution.py:305
  109.3 4.0 %collective-permute-done.7.refs_6_ = bf16[3,48,640]{2,1,0:T(8,128)(2,1)S(1)} collective-permute-done((bf16[3,48,640]{2,1,0:T(8,128)(2,1)S(1)}, bf16[3,48,640]{2,1,0:T(8,128)(2,1)S(1)}, u32[]{:S(2)}, u32[]{:S(2)}) %collective-permute-start.7) | collective-permute-done | bytes 184352 | tf_op jit(solution)/shard_map/ppermute | solution.py:305
  113.9 2.5 %collective-permute-done.8.refs_7_ = bf16[3,48,640]{2,1,0:T(8,128)(2,1)S(1)} collective-permute-done((bf16[3,48,640]{2,1,0:T(8,128)(2,1)S(1)}, bf16[3,48,640]{2,1,0:T(8,128)(2,1)S(1)}, u32[]{:S(2)}, u32[]{:S(2)}) %collective-permute-start.8) | collective-permute-done | bytes 184352 | tf_op jit(solution)/shard_map/ppermute | solution.py:305
  120.1 6.8 %shard_map.115 = (bf16[8,4,48,256]{3,2,1,0:T(8,128)(2,1)}, f32[96,512]{1,0:T(8,128)}, f32[96,512]{1,0:T(8,128)}, bf16[512,128]{1,0:T(8,128)(2,1)}) custom-call(bf16[512,2688]{1,0:T(8,128)(2,1)} %bitcast.12, bf16[4,48,2560]{2,1,0:T(8,128)(2,1)} %refs_1_.1, bf16[4,48,2560]{2,1,0:T(8,128)(2,1)} %refs_2_.1, bf16[1,48,2560]{2,1,0:T(8,128)(2,1)} %refs_3_.1, ...), custom_call_target="tpu_custom_call" | custom-call | bytes 6684672 | tf_op jit(solution)/shard_map/pallas_call | solution.py:30
  126.9 8.1 %all-to-all-start.2 = ((bf16[8,4,48,256]{3,2,1,0:T(8,128)(2,1)}), bf16[8,4,48,256]{3,2,1,0:T(8,128)(2,1)S(1)}, u32[]{:S(2)}, u32[]{:S(2)}) async-start(bf16[8,4,48,256]{3,2,1,0:T(8,128)(2,1)} %get-tuple-element.54), calls=%async_computation.2 | async-start | bytes 1572864 | tf_op jit(solution)/shard_map/all_to_all | solution.py:276
  142.5 3.5 %collective-permute-start.9 = (bf16[8,2,48,640]{3,2,1,0:T(8,128)(2,1)S(1)}, bf16[8,2,48,640]{3,2,1,0:T(8,128)(2,1)S(1)}, u32[]{:S(2)}, u32[]{:S(2)}) collective-permute-start(bf16[8,2,48,640]{3,2,1,0:T(8,128)(2,1)S(1)} %shard_map.116), channel_id=1, source_target_pairs={{0,256},{32,288},{64,320},{96,352},{128,384},{160,416},{192,448},{... | collective-permute-start | bytes 2949128 | tf_op jit(solution)/shard_map/ppermute | solution.py:315
  146.0 22.8 %collective-permute-done.9.came_ref = bf16[8,2,48,640]{3,2,1,0:T(8,128)(2,1)S(1)} collective-permute-done((bf16[8,2,48,640]{3,2,1,0:T(8,128)(2,1)S(1)}, bf16[8,2,48,640]{3,2,1,0:T(8,128)(2,1)S(1)}, u32[]{:S(2)}, u32[]{:S(2)}) %collective-permute-start.9) | collective-permute-done | bytes 983072 | tf_op jit(solution)/shard_map/ppermute | solution.py:315
  183.3 3.1 %collective-permute-start.10 = (bf16[8,48,640]{2,1,0:T(8,128)(2,1)}, bf16[8,48,640]{2,1,0:T(8,128)(2,1)}, u32[]{:S(2)}, u32[]{:S(2)}) collective-permute-start(bf16[8,48,640]{2,1,0:T(8,128)(2,1)} %get-tuple-element.72), channel_id=1, source_target_pairs={{0,256},{32,288},{64,320},{96,352},{128,384},{160,416},{192,448},{... | collective-permute-start | bytes 1474568 | tf_op jit(solution)/shard_map/ppermute | solution.py:347
  186.4 6.9 %all-to-all-start.3 = ((bf16[8,96,256]{2,1,0:T(8,128)(2,1)}), bf16[8,96,256]{2,1,0:T(8,128)(2,1)S(1)}, u32[]{:S(2)}, u32[]{:S(2)}) async-start(bf16[8,96,256]{2,1,0:T(8,128)(2,1)} %copy-done.31), calls=%async_computation.3 | async-start | bytes 786432 | tf_op jit(solution)/shard_map/all_to_all | solution.py:276
  193.4 5.1 %collective-permute-done.10 = bf16[8,48,640]{2,1,0:T(8,128)(2,1)} collective-permute-done((bf16[8,48,640]{2,1,0:T(8,128)(2,1)}, bf16[8,48,640]{2,1,0:T(8,128)(2,1)}, u32[]{:S(2)}, u32[]{:S(2)}) %collective-permute-start.10) | collective-permute-done | bytes 491552 | tf_op jit(solution)/shard_map/ppermute | solution.py:347
  198.5 2.1 add_convert_fusion
  200.6 5.1 %all-to-all-done.3.refs_0_ = bf16[8,96,256]{2,1,0:T(8,128)(2,1)S(1)} async-done(((bf16[8,96,256]{2,1,0:T(8,128)(2,1)}), bf16[8,96,256]{2,1,0:T(8,128)(2,1)S(1)}, u32[]{:S(2)}, u32[]{:S(2)}) %all-to-all-start.3) | async-done | bytes 393248 | tf_op jit(solution)/shard_map/all_to_all | solution.py:276
  208.5 4.6 %collective-permute-start.11 = (bf16[2,48,2560]{2,1,0:T(8,128)(2,1)}, bf16[2,48,2560]{2,1,0:T(8,128)(2,1)S(1)}, u32[]{:S(2)}, u32[]{:S(2)}) collective-permute-start(bf16[2,48,2560]{2,1,0:T(8,128)(2,1)} %get-tuple-element.73), channel_id=1, source_target_pairs={{0,256},{32,288},{64,320},{96,352},{128,384},{160,416},{192,448},{... | collective-permute-start | bytes 1474568 | tf_op jit(solution)/shard_map/ppermute | solution.py:360
  213.1 3.5 %all-to-all-start.4 = ((bf16[8,48,640]{2,1,0:T(8,128)(2,1)}), bf16[8,48,640]{2,1,0:T(8,128)(2,1)S(1)}, u32[]{:S(2)}, u32[]{:S(2)}) async-start(bf16[8,48,640]{2,1,0:T(8,128)(2,1)} %add_convert_fusion), calls=%async_computation.4 | async-start | bytes 983040 | tf_op jit(solution)/shard_map/all_to_all | solution.py:276
  216.6 4.5 %collective-permute-done.11 = bf16[2,48,2560]{2,1,0:T(8,128)(2,1)S(1)} collective-permute-done((bf16[2,48,2560]{2,1,0:T(8,128)(2,1)}, bf16[2,48,2560]{2,1,0:T(8,128)(2,1)S(1)}, u32[]{:S(2)}, u32[]{:S(2)}) %collective-permute-start.11) | collective-permute-done | bytes 491552 | tf_op jit(solution)/shard_map/ppermute | solution.py:360
  221.1 2.2 convert_add_fusion
  223.3 6.2 %all-to-all-done.4.parts_ref = bf16[8,48,640]{2,1,0:T(8,128)(2,1)S(1)} async-done(((bf16[8,48,640]{2,1,0:T(8,128)(2,1)}), bf16[8,48,640]{2,1,0:T(8,128)(2,1)S(1)}, u32[]{:S(2)}, u32[]{:S(2)}) %all-to-all-start.4) | async-done | bytes 491552 | tf_op jit(solution)/shard_map/all_to_all | solution.py:276
  (107 shorter events, 44.4 us)
Async XLA Ops:
  3.8 35.4 %all-to-all-start = ((bf16[16,8,2688]{2,1,0:T(8,128)(2,1)}), bf16[16,8,2688]{2,1,0:T(8,128)(2,1)S(1)}, u32[]{:S(2)}, u32[]{:S(2)}) async-start(bf16[16,8,2688]{2,1,0:T(8,128)(2,1)} %shard_map.112), calls=%async_computation | async-start | bytes 1376256 | tf_op jit(solution)/shard_map/all_to_all | solution.py:276
  18.2 21.0 %collective-permute-start = (bf16[2,48,2560]{2,1,0:T(8,128)(2,1)S(1)}, bf16[2,48,2560]{2,1,0:T(8,128)(2,1)}, u32[]{:S(2)}, u32[]{:S(2)}) collective-permute-start(bf16[2,48,2560]{2,1,0:T(8,128)(2,1)S(1)} %pad_maximum_fusion.1), channel_id=1, source_target_pairs={{0,256},{32,288},{64,320},{96,352},{128,384},{160,416},{192,448},{... | collective-permute-start | bytes 1474568 | tf_op jit(solution)/shard_map/ppermute | solution.py:290
  44.0 8.9 %copy-start.32 = (bf16[1,48,2560]{2,1,0:T(8,128)(2,1)S(1)}, bf16[1,48,2560]{2,1,0:T(8,128)(2,1)}, u32[]{:S(2)}) copy-start(bf16[1,48,2560]{2,1,0:T(8,128)(2,1)} %merged_ref.1) | copy-start | bytes 737284
  44.0 74.6 %all-to-all-start.1 = ((bf16[32,16,2688]{2,1,0:T(8,128)(2,1)}), bf16[32,16,2688]{2,1,0:T(8,128)(2,1)S(1)}, u32[]{:S(2)}, u32[]{:S(2)}) async-start(bf16[32,16,2688]{2,1,0:T(8,128)(2,1)} %bitcast.17), calls=%async_computation.1 | async-start | bytes 5505024 | tf_op jit(solution)/shard_map/all_to_all | solution.py:276
  52.9 1.2 copy-start.2
  57.6 15.8 %collective-permute-start.1 = (bf16[3,48,640]{2,1,0:T(8,128)(2,1)}, bf16[3,48,640]{2,1,0:T(8,128)(2,1)S(1)}, u32[]{:S(2)}, u32[]{:S(2)}) collective-permute-start(bf16[3,48,640]{2,1,0:T(8,128)(2,1)} %get-tuple-element.40), channel_id=1, source_target_pairs={{0,96},{32,128},{64,160},{96,192},{128,224},{160,0},{192,32},{224,... | collective-permute-start | bytes 552968 | tf_op jit(solution)/shard_map/ppermute | solution.py:305
  61.8 15.8 %collective-permute-start.2 = (bf16[3,48,640]{2,1,0:T(8,128)(2,1)}, bf16[3,48,640]{2,1,0:T(8,128)(2,1)S(1)}, u32[]{:S(2)}, u32[]{:S(2)}) collective-permute-start(bf16[3,48,640]{2,1,0:T(8,128)(2,1)} %get-tuple-element.41), channel_id=1, source_target_pairs={{0,160},{32,192},{64,224},{96,0},{128,32},{160,64},{192,96},{224,1... | collective-permute-start | bytes 552968 | tf_op jit(solution)/shard_map/ppermute | solution.py:305
  66.5 17.9 %copy-start.43 = (bf16[3,48,640]{2,1,0:T(8,128)(2,1)S(1)}, bf16[3,48,640]{2,1,0:T(8,128)(2,1)}, u32[]{:S(2)}) copy-start(bf16[3,48,640]{2,1,0:T(8,128)(2,1)} %copy-done.42) | copy-start | bytes 552964
  66.5 23.7 %copy-start.41 = (bf16[3,48,640]{2,1,0:T(8,128)(2,1)S(1)}, bf16[3,48,640]{2,1,0:T(8,128)(2,1)}, u32[]{:S(2)}) copy-start(bf16[3,48,640]{2,1,0:T(8,128)(2,1)} %copy-done.40) | copy-start | bytes 552964
  66.5 25.9 %copy-start.39 = (bf16[3,48,640]{2,1,0:T(8,128)(2,1)S(1)}, bf16[3,48,640]{2,1,0:T(8,128)(2,1)}, u32[]{:S(2)}) copy-start(bf16[3,48,640]{2,1,0:T(8,128)(2,1)} %copy-done.38) | copy-start | bytes 552964
  78.3 40.3 %collective-permute-start.3 = (bf16[4,48,2560]{2,1,0:T(8,128)(2,1)S(1)}, bf16[4,48,2560]{2,1,0:T(8,128)(2,1)}, u32[]{:S(2)}, u32[]{:S(2)}) collective-permute-start(bf16[4,48,2560]{2,1,0:T(8,128)(2,1)S(1)} %pad_maximum_fusion), channel_id=1, source_target_pairs={{0,256},{32,288},{64,320},{96,352},{128,384},{160,416},{192,448},{... | collective-permute-start | bytes 2949128 | tf_op jit(solution)/shard_map/ppermute | solution.py:309
  84.4 15.7 %collective-permute-start.4 = (bf16[3,48,640]{2,1,0:T(8,128)(2,1)S(1)}, bf16[3,48,640]{2,1,0:T(8,128)(2,1)S(1)}, u32[]{:S(2)}, u32[]{:S(2)}) collective-permute-start(bf16[3,48,640]{2,1,0:T(8,128)(2,1)S(1)} %copy-done.43), channel_id=1, source_target_pairs={{0,32},{32,64},{64,96},{96,128},{128,160},{160,192},{192,224},{224... | collective-permute-start | bytes 552968 | tf_op jit(solution)/shard_map/ppermute | solution.py:305
  90.1 17.8 %collective-permute-start.5 = (bf16[3,48,640]{2,1,0:T(8,128)(2,1)S(1)}, bf16[3,48,640]{2,1,0:T(8,128)(2,1)S(1)}, u32[]{:S(2)}, u32[]{:S(2)}) collective-permute-start(bf16[3,48,640]{2,1,0:T(8,128)(2,1)S(1)} %copy-done.41), channel_id=1, source_target_pairs={{0,64},{32,96},{64,128},{96,160},{128,192},{160,224},{192,0},{224,... | collective-permute-start | bytes 552968 | tf_op jit(solution)/shard_map/ppermute | solution.py:305
  92.4 16.2 %collective-permute-start.6 = (bf16[3,48,640]{2,1,0:T(8,128)(2,1)S(1)}, bf16[3,48,640]{2,1,0:T(8,128)(2,1)S(1)}, u32[]{:S(2)}, u32[]{:S(2)}) collective-permute-start(bf16[3,48,640]{2,1,0:T(8,128)(2,1)S(1)} %copy-done.39), channel_id=1, source_target_pairs={{0,128},{32,160},{64,192},{96,224},{128,0},{160,32},{192,64},{224,... | collective-permute-start | bytes 552968 | tf_op jit(solution)/shard_map/ppermute | solution.py:305
  96.2 17.1 %collective-permute-start.7 = (bf16[3,48,640]{2,1,0:T(8,128)(2,1)S(1)}, bf16[3,48,640]{2,1,0:T(8,128)(2,1)S(1)}, u32[]{:S(2)}, u32[]{:S(2)}) collective-permute-start(bf16[3,48,640]{2,1,0:T(8,128)(2,1)S(1)} %get-tuple-element.49), channel_id=1, source_target_pairs={{0,192},{32,224},{64,0},{96,32},{128,64},{160,96},{192,128},{224,1... | collective-permute-start | bytes 552968 | tf_op jit(solution)/shard_map/ppermute | solution.py:305
  100.7 15.7 %collective-permute-start.8 = (bf16[3,48,640]{2,1,0:T(8,128)(2,1)S(1)}, bf16[3,48,640]{2,1,0:T(8,128)(2,1)S(1)}, u32[]{:S(2)}, u32[]{:S(2)}) collective-permute-start(bf16[3,48,640]{2,1,0:T(8,128)(2,1)S(1)} %get-tuple-element.50), channel_id=1, source_target_pairs={{0,224},{32,0},{64,32},{96,64},{128,96},{160,128},{192,160},{224,1... | collective-permute-start | bytes 552968 | tf_op jit(solution)/shard_map/ppermute | solution.py:305
  118.6 1.5 copy-start
  126.9 42.9 %all-to-all-start.2 = ((bf16[8,4,48,256]{3,2,1,0:T(8,128)(2,1)}), bf16[8,4,48,256]{3,2,1,0:T(8,128)(2,1)S(1)}, u32[]{:S(2)}, u32[]{:S(2)}) async-start(bf16[8,4,48,256]{3,2,1,0:T(8,128)(2,1)} %get-tuple-element.54), calls=%async_computation.2 | async-start | bytes 1572864 | tf_op jit(solution)/shard_map/all_to_all | solution.py:276
  135.0 0.9 copy-start.7
  135.9 0.9 copy-start.10
  136.9 0.9 copy-start.13
  142.5 26.4 %collective-permute-start.9 = (bf16[8,2,48,640]{3,2,1,0:T(8,128)(2,1)S(1)}, bf16[8,2,48,640]{3,2,1,0:T(8,128)(2,1)S(1)}, u32[]{:S(2)}, u32[]{:S(2)}) collective-permute-start(bf16[8,2,48,640]{3,2,1,0:T(8,128)(2,1)S(1)} %shard_map.116), channel_id=1, source_target_pairs={{0,256},{32,288},{64,320},{96,352},{128,384},{160,416},{192,448},{... | collective-permute-start | bytes 2949128 | tf_op jit(solution)/shard_map/ppermute | solution.py:315
  168.9 0.9 copy-start.3
  169.8 1.2 copy-start.4
  179.3 26.4 %copy-start.1 = (bf16[32,16,2688]{2,1,0:T(8,128)(2,1)S(1)}, bf16[32,16,2688]{2,1,0:T(8,128)(2,1)}, u32[]{:S(2)}) copy-start(bf16[32,16,2688]{2,1,0:T(8,128)(2,1)} %copy-done) | copy-start | bytes 8257540
  181.3 24.4 %copy-start.33 = (f32[96,512]{1,0:T(8,128)S(1)}, f32[96,512]{1,0:T(8,128)}, u32[]{:S(2)}) copy-start(f32[96,512]{1,0:T(8,128)} %get-tuple-element.65.refs_1_) | copy-start | bytes 589828
  181.3 24.4 %copy-start.34 = (f32[96,512]{1,0:T(8,128)S(1)}, f32[96,512]{1,0:T(8,128)}, u32[]{:S(2)}) copy-start(f32[96,512]{1,0:T(8,128)} %get-tuple-element.66.refs_2_) | copy-start | bytes 589828
  183.3 15.2 %collective-permute-start.10 = (bf16[8,48,640]{2,1,0:T(8,128)(2,1)}, bf16[8,48,640]{2,1,0:T(8,128)(2,1)}, u32[]{:S(2)}, u32[]{:S(2)}) collective-permute-start(bf16[8,48,640]{2,1,0:T(8,128)(2,1)} %get-tuple-element.72), channel_id=1, source_target_pairs={{0,256},{32,288},{64,320},{96,352},{128,384},{160,416},{192,448},{... | collective-permute-start | bytes 1474568 | tf_op jit(solution)/shard_map/ppermute | solution.py:347
  186.4 19.2 %all-to-all-start.3 = ((bf16[8,96,256]{2,1,0:T(8,128)(2,1)}), bf16[8,96,256]{2,1,0:T(8,128)(2,1)S(1)}, u32[]{:S(2)}, u32[]{:S(2)}) async-start(bf16[8,96,256]{2,1,0:T(8,128)(2,1)} %copy-done.31), calls=%async_computation.3 | async-start | bytes 786432 | tf_op jit(solution)/shard_map/all_to_all | solution.py:276
  207.5 1.0 copy-start.5
  208.5 12.5 %collective-permute-start.11 = (bf16[2,48,2560]{2,1,0:T(8,128)(2,1)}, bf16[2,48,2560]{2,1,0:T(8,128)(2,1)S(1)}, u32[]{:S(2)}, u32[]{:S(2)}) collective-permute-start(bf16[2,48,2560]{2,1,0:T(8,128)(2,1)} %get-tuple-element.73), channel_id=1, source_target_pairs={{0,256},{32,288},{64,320},{96,352},{128,384},{160,416},{192,448},{... | collective-permute-start | bytes 1474568 | tf_op jit(solution)/shard_map/ppermute | solution.py:360
  213.1 16.4 %all-to-all-start.4 = ((bf16[8,48,640]{2,1,0:T(8,128)(2,1)}), bf16[8,48,640]{2,1,0:T(8,128)(2,1)S(1)}, u32[]{:S(2)}, u32[]{:S(2)}) async-start(bf16[8,48,640]{2,1,0:T(8,128)(2,1)} %add_convert_fusion), calls=%async_computation.4 | async-start | bytes 983040 | tf_op jit(solution)/shard_map/all_to_all | solution.py:276
  (30 other events, 24.1 us)

commit v7 on v6

--- a/solution.py
+++ b/solution.py
@@ -25,7 +25,7 @@
     return lax.dot_general(a, b, (((0,), (0,)), ((), ())), preferred_element_type=F32)
 
 
-def call(kernel, outs, args, mib=16, flops=0):
+def call(kernel, outs, args, mib=16):
     space = pl.BlockSpec(memory_space=pltpu.VMEM)
     return pl.pallas_call(
         kernel,
@@ -34,7 +34,7 @@
         out_specs=[space] * len(outs),
         compiler_params=pltpu.CompilerParams(vmem_limit_bytes=mib * 1024 * 1024),
         cost_estimate=pl.CostEstimate(
-            flops=flops,
+            flops=0,
             bytes_accessed=sum(a.size * a.dtype.itemsize for a in args),
             transcendentals=0,
         ),
@@ -110,8 +110,7 @@
     t_up_ref,
     m_gate_ref,
     m_up_ref,
-    t_come_ref,
-    m_come_ref,
+    come_ref,
     out_ref,
     silu_ref,
     slope_ref,
@@ -130,14 +129,14 @@
         value = dot_nt(jnp.concatenate(parts, axis=0), rows)
         return value[:units], value[units:]
 
-    gate, up = gate_up(m_gate_ref[0], m_come_ref[0], m_up_ref[0], m_come_ref[1])
+    gate, up = gate_up(m_gate_ref[0], come_ref[2 * PAIR], m_up_ref[0], come_ref[2 * PAIR + 1])
     silu, slope = silu_split(gate)
     silu_ref[...] = silu
     slope_ref[...] = up * slope
     hidden = [(silu * up).astype(BF16)]
     for m in range(PAIR):
         own = PAIR * half + m
-        gate, up = gate_up(t_gate_ref[own], t_come_ref[m], t_up_ref[own], t_come_ref[PAIR + m])
+        gate, up = gate_up(t_gate_ref[own], come_ref[m], t_up_ref[own], come_ref[PAIR + m])
         silu, _ = silu_split(gate)
         hidden.append((silu * up).astype(BF16))
     move = by_teacher(count, capacity, 0)
@@ -154,27 +153,23 @@
             out_ref[at, 3] = hidden[first + block : first + units, lanes]
 
 
-def share_kernel(down_ref, merged_ref, *out_refs):
+def share_kernel(down_ref, merged_ref, came_ref, merged_came_ref, *out_refs):
     half, at = place()
+    block = merged_ref.shape[1]
     quarter = out_refs[0].shape[2]
     for k, out_ref in enumerate(out_refs):
         there = (at + k) % RING
         m = there // (RING // PAIR)
         span = pl.ds(pl.multiple_of(there % (RING // PAIR) * quarter, SIDE), quarter)
-        out_ref[0] = down_ref[PAIR * half + m, :, span]
-        out_ref[1] = down_ref[PAIR * (1 - half) + m, :, span]
-        out_ref[2] = merged_ref[0, :, span]
-
-
-def pass_kernel(*refs):
-    out_ref = refs[-1]
-    for k, down_ref in enumerate(refs[:-1]):
-        out_ref[k] = down_ref[1:]
-
-
-def gap_kernel(hidden_ref, weight_ref, came_ref, *refs):
+        out_ref[0, :block] = down_ref[PAIR * half + m, :, span]
+        out_ref[0, block:] = came_ref[m, :, span]
+        out_ref[1, :block] = merged_ref[0, :, span]
+        out_ref[1, block:] = merged_came_ref[0, :, span]
+
+
+def gap_kernel(hidden_ref, weight_ref, *refs):
     down_refs = refs[:RING]
-    grad_ref, student_ref, slot_grad_ref = refs[RING:]
+    grad_ref, kept_ref, other_ref = refs[RING:]
     block = hidden_ref.shape[2]
     units = 2 * block
     span = hidden_ref.shape[3]
@@ -182,26 +177,16 @@
     back = [(at + RING - k) % RING for k in range(RING)]
     student = jnp.concatenate([hidden_ref[i, a] for i in back for a in (0, 1)], axis=0)
     teacher = jnp.concatenate([hidden_ref[i, a] for i in back for a in (2, 3)], axis=0)
-    t_down = jnp.concatenate([x for k in range(RING) for x in (down_refs[k][0], came_ref[k, 0])], axis=0)
-    m_down = jnp.concatenate([x for k in range(RING) for x in (down_refs[k][2], came_ref[k, 1])], axis=0)
+    t_down = jnp.concatenate([down_ref[0] for down_ref in down_refs], axis=0)
+    m_down = jnp.concatenate([down_ref[1] for down_ref in down_refs], axis=0)
     gap = dot_tn(student, m_down) - dot_tn(teacher, t_down)
     start = pl.multiple_of(at // (RING // PAIR) * span, span)
     weight = weight_ref[pl.ds(start, span), SIDE - 1 : SIDE].astype(F32)
     slot_grad = (weight * gap).astype(BF16)
     grad = dot_nt(m_down, slot_grad).astype(BF16)
+    down_grad = dot_nn(student, slot_grad).astype(BF16)
     for k, i in enumerate(back):
         grad_ref[i] = grad[k * units : (k + 1) * units]
-    student_ref[...] = student
-    slot_grad_ref[...] = slot_grad
-
-
-def down_grad_kernel(student_ref, slot_grad_ref, kept_ref, other_ref):
-    block = kept_ref.shape[1]
-    units = 2 * block
-    _, at = place()
-    down_grad = dot_nn(student_ref[...], slot_grad_ref[...]).astype(BF16)
-    for k in range(RING):
-        i = (at + RING - k) % RING
         kept_ref[i] = down_grad[k * units : k * units + block]
         other_ref[i] = down_grad[k * units + block : (k + 1) * units]
 
@@ -287,8 +272,8 @@
     )
     group = exchange(packets, "dp").reshape(n_dp * capacity, wide)
 
-    m_come = lax.ppermute(jnp.concatenate([merged_gate, merged_up], axis=0), "dp", swap)
-    group, m_come = lax.optimization_barrier((group, m_come))
+    came = lax.ppermute(halves(teacher_down, 1 - half), "dp", swap)
+    group, came = lax.optimization_barrier((group, came))
     (slots,) = call(
         lambda *refs: slots_kernel(ranks, capacity, *refs),
         (jax.ShapeDtypeStruct((rows, wide), BF16),),
@@ -297,22 +282,19 @@
     )
     slots = exchange(slots.reshape(experts, PAIR * capacity, wide), "expert").reshape(rows, wide)
 
+    merged_came = lax.ppermute(merged_down, "dp", swap)
     down = call(
         share_kernel,
-        tuple(jax.ShapeDtypeStruct((PAIR + 1, block, quarter), BF16) for _ in range(RING)),
-        (teacher_down, merged_down),
+        tuple(jax.ShapeDtypeStruct((2, 2 * block, quarter), BF16) for _ in range(RING)),
+        (teacher_down, merged_down, came, merged_came),
     )
     down = [down[k] if k == 0 else lax.ppermute(down[k], "dp", turns[k]) for k in range(RING)]
 
-    t_sent = jnp.concatenate([halves(teacher_gate, 1 - half), halves(teacher_up, 1 - half)], axis=0)
-    t_sent, down[3], down[5] = lax.optimization_barrier((t_sent, down[3], down[5]))
-    t_come = lax.ppermute(t_sent, "dp", swap)
-    slots, t_come, down = lax.optimization_barrier((slots, t_come, down))
-
-    (passed,) = call(
-        pass_kernel, (jax.ShapeDtypeStruct((RING, PAIR, block, quarter), BF16),), tuple(down)
-    )
-    came = lax.ppermute(passed, "dp", swap)
+    parts = [halves(teacher_gate, 1 - half), halves(teacher_up, 1 - half), merged_gate, merged_up]
+    come = jnp.concatenate(parts, axis=0)
+    come, down[1] = lax.optimization_barrier((come, down[1]))
+    come = lax.ppermute(come, "dp", swap)
+    slots, come, down = lax.optimization_barrier((slots, come, down))
 
     hidden, silu, slope, weight = call(
         lambda *refs: hidden_kernel(capacity, *refs),
@@ -322,28 +304,20 @@
             jax.ShapeDtypeStruct((2 * block, rows), F32),
             jax.ShapeDtypeStruct((rows, SIDE), BF16),
         ),
-        (slots, teacher_gate, teacher_up, merged_gate, merged_up, t_come, m_come),
+        (slots, teacher_gate, teacher_up, merged_gate, merged_up, come),
         mib=60,
     )
     hidden = exchange(hidden, "dp", rings)
-    hidden_grad, student, slot_grad = call(
+    hidden_grad, kept_down, other_down = call(
         gap_kernel,
         (
             jax.ShapeDtypeStruct((RING, 2 * block, span), BF16),
-            jax.ShapeDtypeStruct((n_dp * block, span), BF16),
-            jax.ShapeDtypeStruct((span, quarter), BF16),
-        ),
-        (hidden, weight, came, *down),
-    )
-    parts = exchange(hidden_grad, "dp", rings)
-    kept_down, other_down = call(
-        down_grad_kernel,
-        (
             jax.ShapeDtypeStruct((RING, block, quarter), BF16),
             jax.ShapeDtypeStruct((RING, block, quarter), BF16),
         ),
-        (student, slot_grad),
-    )
+        (hidden, weight, *down),
+    )
+    parts = exchange(hidden_grad, "dp", rings)
     other_down = lax.ppermute(other_down, "dp", swap)
     down_grad = (kept_down.astype(F32) + other_down.astype(F32)).astype(BF16)
     own, other = call(
@@ -353,7 +327,6 @@
             jax.ShapeDtypeStruct((2, block, features), BF16),
         ),
         (parts, silu, slope, slots),
-        flops=0,
     )
     other, down_grad = lax.optimization_barrier((other, down_grad))
     down_grad = exchange(down_grad, "dp", rings)

time: 232 us -> 231 us (level)
  the two profiles are of different devices: /device:TPU:6 before, /device:TPU:32 now
where the time goes in v7:
time: 231 us; the launch traced here: 230 us
  waiting for transfers between devices  92.9 us (40%)
  starting transfers between devices  75.8 us (33%)
  blocking collectives  28.7 us (12%)
  Pallas kernels  17.1 us (7%)
  local copies, waits for them, and re-layouts  11.2 us (5%)
  other arithmetic  3.31 us (1%)
    ppermute x7, waiting for transfers between devices, body(): lax.ppermute(down[k], 'dp', turns[k])  34.9 us
    all_to_all x1, blocking collectives, exchange(): lax.all_to_all(array, axis_name, split_axis=0, concat_axis=0, tiled=True,...  28.7 us
    ppermute x7, starting transfers between devices, body(): lax.ppermute(down[k], 'dp', turns[k])  27.8 us
    all_to_all x4, starting transfers between devices, exchange(): lax.all_to_all(array, axis_name, split_axis=0, concat_axis=0, tiled=True,...  27.4 us
    ppermute x1, waiting for transfers between devices, body(): merged_came = lax.ppermute(merged_down, 'dp', swap)  17.8 us
    ppermute x1, waiting for transfers between devices, body(): came = lax.ppermute(halves(teacher_down, 1 - half), 'dp', swap)  17.2 us
    pallas_call x7, Pallas kernels, call(): pl.pallas_call(kernel, out_shape=outs, in_specs=[space] * len(args), out_...  17.1 us
    all_to_all x4, waiting for transfers between devices, exchange(): lax.all_to_all(array, axis_name, split_axis=0, concat_axis=0, tiled=True,...  10.2 us
  transfers between devices with their start and end apart: 16, of which 12 were waited for; matrix products, arithmetic and copies ran while one was open for 2% of the time, Pallas kernels for 0%

profile of v7, /device:TPU:32, one launch (start us, length us, event | category | flops | bytes accessed | tf_op | source)
XLA Modules:
  0.0 229.8 jit_solution(12645387086814269633)
XLA Ops:
  3.9 12.9 %all-to-all-start = ((bf16[16,8,2688]{2,1,0:T(8,128)(2,1)}), bf16[16,8,2688]{2,1,0:T(8,128)(2,1)S(1)}, u32[]{:S(2)}, u32[]{:S(2)}) async-start(bf16[16,8,2688]{2,1,0:T(8,128)(2,1)} %shard_map.112), calls=%async_computation | async-start | bytes 1376256 | tf_op jit(solution)/shard_map/all_to_all | solution.py:261
  16.9 5.3 %collective-permute-start = (bf16[2,48,2560]{2,1,0:T(8,128)(2,1)S(1)}, bf16[2,48,2560]{2,1,0:T(8,128)(2,1)S(1)}, u32[]{:S(2)}, u32[]{:S(2)}) collective-permute-start(bf16[2,48,2560]{2,1,0:T(8,128)(2,1)S(1)} %constant_dynamic-slice_fusion.2), channel_id=1, source_target_pairs={{0,256},{32,288},{64,320},{96,352},{128,384},{160,416},{192,448},{... | collective-permute-start | bytes 1474568 | tf_op jit(solution)/shard_map/ppermute | solution.py:275
  22.2 17.2 %collective-permute-done.came_ref = bf16[2,48,2560]{2,1,0:T(8,128)(2,1)S(1)} collective-permute-done((bf16[2,48,2560]{2,1,0:T(8,128)(2,1)S(1)}, bf16[2,48,2560]{2,1,0:T(8,128)(2,1)S(1)}, u32[]{:S(2)}, u32[]{:S(2)}) %collective-permute-start) | collective-permute-done | bytes 491552 | tf_op jit(solution)/shard_map/ppermute | solution.py:275
  40.3 3.9 %shard_map.113 = bf16[512,2688]{1,0:T(8,128)(2,1)} custom-call(bf16[128,2688]{1,0:T(8,128)(2,1)} %bitcast.18), custom_call_target="tpu_custom_call" | custom-call | bytes 688128 | tf_op jit(solution)/shard_map/pallas_call | solution.py:30
  44.2 7.5 %all-to-all-start.1 = ((bf16[32,16,2688]{2,1,0:T(8,128)(2,1)}), bf16[32,16,2688]{2,1,0:T(8,128)(2,1)S(1)}, u32[]{:S(2)}, u32[]{:S(2)}) async-start(bf16[32,16,2688]{2,1,0:T(8,128)(2,1)} %bitcast.17), calls=%async_computation.1 | async-start | bytes 5505024 | tf_op jit(solution)/shard_map/all_to_all | solution.py:261
  51.8 4.8 %collective-permute-start.1 = (bf16[1,48,2560]{2,1,0:T(8,128)(2,1)S(1)}, bf16[1,48,2560]{2,1,0:T(8,128)(2,1)S(1)}, u32[]{:S(2)}, u32[]{:S(2)}) collective-permute-start(bf16[1,48,2560]{2,1,0:T(8,128)(2,1)S(1)} %copy-done.7), channel_id=1, source_target_pairs={{0,256},{32,288},{64,320},{96,352},{128,384},{160,416},{192,448},{... | collective-permute-start | bytes 737288 | tf_op jit(solution)/shard_map/ppermute | solution.py:285
  57.9 17.8 %collective-permute-done.1.merged_came_ref = bf16[1,48,2560]{2,1,0:T(8,128)(2,1)S(1)} collective-permute-done((bf16[1,48,2560]{2,1,0:T(8,128)(2,1)S(1)}, bf16[1,48,2560]{2,1,0:T(8,128)(2,1)S(1)}, u32[]{:S(2)}, u32[]{:S(2)}) %collective-permute-start.1) | collective-permute-done | bytes 245792 | tf_op jit(solution)/shard_map/ppermute | solution.py:285
  76.5 3.7 %collective-permute-start.2 = (bf16[2,96,640]{2,1,0:T(8,128)(2,1)S(1)}, bf16[2,96,640]{2,1,0:T(8,128)(2,1)S(1)}, u32[]{:S(2)}, u32[]{:S(2)}) collective-permute-start(bf16[2,96,640]{2,1,0:T(8,128)(2,1)S(1)} %get-tuple-element.38), channel_id=1, source_target_pairs={{0,32},{32,64},{64,96},{96,128},{128,160},{160,192},{192,224},{224... | collective-permute-start | bytes 737288 | tf_op jit(solution)/shard_map/ppermute | solution.py:291
  80.5 7.0 %collective-permute-done.2.refs_1_ = bf16[2,96,640]{2,1,0:T(8,128)(2,1)S(1)} collective-permute-done((bf16[2,96,640]{2,1,0:T(8,128)(2,1)S(1)}, bf16[2,96,640]{2,1,0:T(8,128)(2,1)S(1)}, u32[]{:S(2)}, u32[]{:S(2)}) %collective-permute-start.2) | collective-permute-done | bytes 245792 | tf_op jit(solution)/shard_map/ppermute | solution.py:291
  87.5 2.6 %collective-permute-start.3 = (bf16[6,48,2560]{2,1,0:T(8,128)(2,1)S(1)}, bf16[6,48,2560]{2,1,0:T(8,128)(2,1)}, u32[]{:S(2)}, u32[]{:S(2)}) collective-permute-start(bf16[6,48,2560]{2,1,0:T(8,128)(2,1)S(1)} %pad_maximum_fusion), channel_id=1, source_target_pairs={{0,256},{32,288},{64,320},{96,352},{128,384},{160,416},{192,448},{... | collective-permute-start | bytes 4423688 | tf_op jit(solution)/shard_map/ppermute | solution.py:296
  90.1 2.7 %collective-permute-start.4 = (bf16[2,96,640]{2,1,0:T(8,128)(2,1)S(1)}, bf16[2,96,640]{2,1,0:T(8,128)(2,1)S(1)}, u32[]{:S(2)}, u32[]{:S(2)}) collective-permute-start(bf16[2,96,640]{2,1,0:T(8,128)(2,1)S(1)} %get-tuple-element.42), channel_id=1, source_target_pairs={{0,64},{32,96},{64,128},{96,160},{128,192},{160,224},{192,0},{224,... | collective-permute-start | bytes 737288 | tf_op jit(solution)/shard_map/ppermute | solution.py:291
  92.9 5.8 %collective-permute-start.5 = (bf16[2,96,640]{2,1,0:T(8,128)(2,1)S(1)}, bf16[2,96,640]{2,1,0:T(8,128)(2,1)S(1)}, u32[]{:S(2)}, u32[]{:S(2)}) collective-permute-start(bf16[2,96,640]{2,1,0:T(8,128)(2,1)S(1)} %get-tuple-element.43), channel_id=1, source_target_pairs={{0,96},{32,128},{64,160},{96,192},{128,224},{160,0},{192,32},{224,... | collective-permute-start | bytes 737288 | tf_op jit(solution)/shard_map/ppermute | solution.py:291
  98.7 3.5 %collective-permute-start.6 = (bf16[2,96,640]{2,1,0:T(8,128)(2,1)S(1)}, bf16[2,96,640]{2,1,0:T(8,128)(2,1)S(1)}, u32[]{:S(2)}, u32[]{:S(2)}) collective-permute-start(bf16[2,96,640]{2,1,0:T(8,128)(2,1)S(1)} %get-tuple-element.44), channel_id=1, source_target_pairs={{0,128},{32,160},{64,192},{96,224},{128,0},{160,32},{192,64},{224,... | collective-permute-start | bytes 737288 | tf_op jit(solution)/shard_map/ppermute | solution.py:291
  102.2 5.2 %collective-permute-start.7 = (bf16[2,96,640]{2,1,0:T(8,128)(2,1)S(1)}, bf16[2,96,640]{2,1,0:T(8,128)(2,1)S(1)}, u32[]{:S(2)}, u32[]{:S(2)}) collective-permute-start(bf16[2,96,640]{2,1,0:T(8,128)(2,1)S(1)} %get-tuple-element.45), channel_id=1, source_target_pairs={{0,160},{32,192},{64,224},{96,0},{128,32},{160,64},{192,96},{224,1... | collective-permute-start | bytes 737288 | tf_op jit(solution)/shard_map/ppermute | solution.py:291
  107.4 2.0 collective-permute-done.4.refs_2_
  109.4 4.9 %collective-permute-start.8 = (bf16[2,96,640]{2,1,0:T(8,128)(2,1)S(1)}, bf16[2,96,640]{2,1,0:T(8,128)(2,1)S(1)}, u32[]{:S(2)}, u32[]{:S(2)}) collective-permute-start(bf16[2,96,640]{2,1,0:T(8,128)(2,1)S(1)} %get-tuple-element.46), channel_id=1, source_target_pairs={{0,192},{32,224},{64,0},{96,32},{128,64},{160,96},{192,128},{224,1... | collective-permute-start | bytes 737288 | tf_op jit(solution)/shard_map/ppermute | solution.py:291
  114.3 12.7 %collective-permute-done.5.refs_3_ = bf16[2,96,640]{2,1,0:T(8,128)(2,1)S(1)} collective-permute-done((bf16[2,96,640]{2,1,0:T(8,128)(2,1)S(1)}, bf16[2,96,640]{2,1,0:T(8,128)(2,1)S(1)}, u32[]{:S(2)}, u32[]{:S(2)}) %collective-permute-start.5) | collective-permute-done | bytes 245792 | tf_op jit(solution)/shard_map/ppermute | solution.py:291
  126.9 1.9 collective-permute-start.9
  129.6 3.4 %collective-permute-done.7.refs_5_ = bf16[2,96,640]{2,1,0:T(8,128)(2,1)S(1)} collective-permute-done((bf16[2,96,640]{2,1,0:T(8,128)(2,1)S(1)}, bf16[2,96,640]{2,1,0:T(8,128)(2,1)S(1)}, u32[]{:S(2)}, u32[]{:S(2)}) %collective-permute-start.7) | collective-permute-done | bytes 245792 | tf_op jit(solution)/shard_map/ppermute | solution.py:291
  133.6 9.6 %collective-permute-done.8.refs_6_ = bf16[2,96,640]{2,1,0:T(8,128)(2,1)S(1)} collective-permute-done((bf16[2,96,640]{2,1,0:T(8,128)(2,1)S(1)}, bf16[2,96,640]{2,1,0:T(8,128)(2,1)S(1)}, u32[]{:S(2)}, u32[]{:S(2)}) %collective-permute-start.8) | collective-permute-done | bytes 245792 | tf_op jit(solution)/shard_map/ppermute | solution.py:291
  146.5 6.9 %shard_map.115 = (bf16[8,4,48,256]{3,2,1,0:T(8,128)(2,1)}, f32[96,512]{1,0:T(8,128)}, f32[96,512]{1,0:T(8,128)}, bf16[512,128]{1,0:T(8,128)(2,1)}) custom-call(bf16[512,2688]{1,0:T(8,128)(2,1)} %bitcast.12, bf16[4,48,2560]{2,1,0:T(8,128)(2,1)} %refs_1_.1, bf16[4,48,2560]{2,1,0:T(8,128)(2,1)} %refs_2_.1, bf16[1,48,2560]{2,1,0:T(8,128)(2,1)} %refs_3_.1, ...), custom_call_target="tpu_custom_call" | custom-call | bytes 6684672 | tf_op jit(solution)/shard_map/pallas_call | solution.py:30
  153.5 28.7 %all_to_all.25.hidden_ref = bf16[8,4,48,256]{3,2,1,0:T(8,128)(2,1)S(1)} all-to-all(bf16[8,4,48,256]{3,2,1,0:T(8,128)(2,1)} %get-tuple-element.50), channel_id=1, replica_groups={{0,32,64,96,128,160,192,224},{256,288,320,352,384,416,448,480},{1,33,65..., dimensions={0} | all-to-all | bytes 1572864 | tf_op jit(solution)/shard_map/all_to_all | solution.py:261
  182.2 2.4 %shard_map.116 = (bf16[8,96,256]{2,1,0:T(8,128)(2,1)}, bf16[8,48,640]{2,1,0:T(8,128)(2,1)S(1)}, bf16[8,48,640]{2,1,0:T(8,128)(2,1)}) custom-call(bf16[8,4,48,256]{3,2,1,0:T(8,128)(2,1)S(1)} %all_to_all.25.hidden_ref, bf16[512,128]{1,0:T(8,128)(2,1)S(1)} %copy-done.20, bf16[2,96,640]{2,1,0:T(8,128)(2,1)S(1)} %copy-done.9, ...), custom_call_target="tpu_custom_call" | custom-call | bytes 2883584 | tf_op jit(solution)/shard_map/pallas_call | solution.py:30
  185.3 4.6 %collective-permute-start.10 = (bf16[8,48,640]{2,1,0:T(8,128)(2,1)}, bf16[8,48,640]{2,1,0:T(8,128)(2,1)}, u32[]{:S(2)}, u32[]{:S(2)}) collective-permute-start(bf16[8,48,640]{2,1,0:T(8,128)(2,1)} %get-tuple-element.66), channel_id=1, source_target_pairs={{0,256},{32,288},{64,320},{96,352},{128,384},{160,416},{192,448},{... | collective-permute-start | bytes 1474568 | tf_op jit(solution)/shard_map/ppermute | solution.py:321
  190.0 3.5 %all-to-all-start.3 = ((bf16[8,96,256]{2,1,0:T(8,128)(2,1)}), bf16[8,96,256]{2,1,0:T(8,128)(2,1)S(1)}, u32[]{:S(2)}, u32[]{:S(2)}) async-start(bf16[8,96,256]{2,1,0:T(8,128)(2,1)} %get-tuple-element.60), calls=%async_computation.3 | async-start | bytes 786432 | tf_op jit(solution)/shard_map/all_to_all | solution.py:261
  193.4 6.9 %collective-permute-done.10 = bf16[8,48,640]{2,1,0:T(8,128)(2,1)} collective-permute-done((bf16[8,48,640]{2,1,0:T(8,128)(2,1)}, bf16[8,48,640]{2,1,0:T(8,128)(2,1)}, u32[]{:S(2)}, u32[]{:S(2)}) %collective-permute-start.10) | collective-permute-done | bytes 491552 | tf_op jit(solution)/shard_map/ppermute | solution.py:321
  200.3 2.1 add_convert_fusion
  202.4 3.6 %all-to-all-done.3.refs_0_ = bf16[8,96,256]{2,1,0:T(8,128)(2,1)S(1)} async-done(((bf16[8,96,256]{2,1,0:T(8,128)(2,1)}), bf16[8,96,256]{2,1,0:T(8,128)(2,1)S(1)}, u32[]{:S(2)}, u32[]{:S(2)}) %all-to-all-start.3) | async-done | bytes 393248 | tf_op jit(solution)/shard_map/all_to_all | solution.py:261
  208.8 3.2 %collective-permute-start.11 = (bf16[2,48,2560]{2,1,0:T(8,128)(2,1)}, bf16[2,48,2560]{2,1,0:T(8,128)(2,1)S(1)}, u32[]{:S(2)}, u32[]{:S(2)}) collective-permute-start(bf16[2,48,2560]{2,1,0:T(8,128)(2,1)} %get-tuple-element.67), channel_id=1, source_target_pairs={{0,256},{32,288},{64,320},{96,352},{128,384},{160,416},{192,448},{... | collective-permute-start | bytes 1474568 | tf_op jit(solution)/shard_map/ppermute | solution.py:333
  212.0 3.5 %all-to-all-start.4 = ((bf16[8,48,640]{2,1,0:T(8,128)(2,1)}), bf16[8,48,640]{2,1,0:T(8,128)(2,1)S(1)}, u32[]{:S(2)}, u32[]{:S(2)}) async-start(bf16[8,48,640]{2,1,0:T(8,128)(2,1)} %add_convert_fusion), calls=%async_computation.4 | async-start | bytes 983040 | tf_op jit(solution)/shard_map/all_to_all | solution.py:261
  215.5 5.9 %collective-permute-done.11 = bf16[2,48,2560]{2,1,0:T(8,128)(2,1)S(1)} collective-permute-done((bf16[2,48,2560]{2,1,0:T(8,128)(2,1)}, bf16[2,48,2560]{2,1,0:T(8,128)(2,1)S(1)}, u32[]{:S(2)}, u32[]{:S(2)}) %collective-permute-start.11) | collective-permute-done | bytes 491552 | tf_op jit(solution)/shard_map/ppermute | solution.py:333
  222.4 6.6 %all-to-all-done.4.parts_ref = bf16[8,48,640]{2,1,0:T(8,128)(2,1)S(1)} async-done(((bf16[8,48,640]{2,1,0:T(8,128)(2,1)}), bf16[8,48,640]{2,1,0:T(8,128)(2,1)S(1)}, u32[]{:S(2)}, u32[]{:S(2)}) %all-to-all-start.4) | async-done | bytes 491552 | tf_op jit(solution)/shard_map/all_to_all | solution.py:261
  (66 shorter events, 16.6 us)
Async XLA Ops:
  0.6 16.2 %copy-start.2 = (bf16[4,48,2560]{2,1,0:T(8,128)(2,1)S(1)}, bf16[4,48,2560]{2,1,0:T(8,128)(2,1)}, u32[]{:S(2)}) copy-start(bf16[4,48,2560]{2,1,0:T(8,128)(2,1)} %down_ref.1) | copy-start | bytes 2949124
  3.9 35.5 %all-to-all-start = ((bf16[16,8,2688]{2,1,0:T(8,128)(2,1)}), bf16[16,8,2688]{2,1,0:T(8,128)(2,1)S(1)}, u32[]{:S(2)}, u32[]{:S(2)}) async-start(bf16[16,8,2688]{2,1,0:T(8,128)(2,1)} %shard_map.112), calls=%async_computation | async-start | bytes 1376256 | tf_op jit(solution)/shard_map/all_to_all | solution.py:261
  16.9 22.5 %collective-permute-start = (bf16[2,48,2560]{2,1,0:T(8,128)(2,1)S(1)}, bf16[2,48,2560]{2,1,0:T(8,128)(2,1)S(1)}, u32[]{:S(2)}, u32[]{:S(2)}) collective-permute-start(bf16[2,48,2560]{2,1,0:T(8,128)(2,1)S(1)} %constant_dynamic-slice_fusion.2), channel_id=1, source_target_pairs={{0,256},{32,288},{64,320},{96,352},{128,384},{160,416},{192,448},{... | collective-permute-start | bytes 1474568 | tf_op jit(solution)/shard_map/ppermute | solution.py:275
  44.2 7.5 %copy-start.7 = (bf16[1,48,2560]{2,1,0:T(8,128)(2,1)S(1)}, bf16[1,48,2560]{2,1,0:T(8,128)(2,1)}, u32[]{:S(2)}) copy-start(bf16[1,48,2560]{2,1,0:T(8,128)(2,1)} %merged_ref.1) | copy-start | bytes 737284
  44.2 100.8 %all-to-all-start.1 = ((bf16[32,16,2688]{2,1,0:T(8,128)(2,1)}), bf16[32,16,2688]{2,1,0:T(8,128)(2,1)S(1)}, u32[]{:S(2)}, u32[]{:S(2)}) async-start(bf16[32,16,2688]{2,1,0:T(8,128)(2,1)} %bitcast.17), calls=%async_computation.1 | async-start | bytes 5505024 | tf_op jit(solution)/shard_map/all_to_all | solution.py:261
  51.8 23.9 %copy-start.3 = (bf16[4,48,2560]{2,1,0:T(8,128)(2,1)S(1)}, bf16[4,48,2560]{2,1,0:T(8,128)(2,1)}, u32[]{:S(2)}) copy-start(bf16[4,48,2560]{2,1,0:T(8,128)(2,1)} %down_ref.1) | copy-start | bytes 2949124
  51.8 23.9 %collective-permute-start.1 = (bf16[1,48,2560]{2,1,0:T(8,128)(2,1)S(1)}, bf16[1,48,2560]{2,1,0:T(8,128)(2,1)S(1)}, u32[]{:S(2)}, u32[]{:S(2)}) collective-permute-start(bf16[1,48,2560]{2,1,0:T(8,128)(2,1)S(1)} %copy-done.7), channel_id=1, source_target_pairs={{0,256},{32,288},{64,320},{96,352},{128,384},{160,416},{192,448},{... | collective-permute-start | bytes 737288 | tf_op jit(solution)/shard_map/ppermute | solution.py:285
  57.9 22.4 %copy-start.24 = (bf16[1,48,2560]{2,1,0:T(8,128)(2,1)S(1)}, bf16[1,48,2560]{2,1,0:T(8,128)(2,1)}, u32[]{:S(2)}) copy-start(bf16[1,48,2560]{2,1,0:T(8,128)(2,1)} %refs_3_.1) | copy-start | bytes 737284
  57.9 22.4 %copy-start.25 = (bf16[1,48,2560]{2,1,0:T(8,128)(2,1)S(1)}, bf16[1,48,2560]{2,1,0:T(8,128)(2,1)}, u32[]{:S(2)}) copy-start(bf16[1,48,2560]{2,1,0:T(8,128)(2,1)} %refs_4_.1) | copy-start | bytes 737284
  76.5 11.0 %collective-permute-start.2 = (bf16[2,96,640]{2,1,0:T(8,128)(2,1)S(1)}, bf16[2,96,640]{2,1,0:T(8,128)(2,1)S(1)}, u32[]{:S(2)}, u32[]{:S(2)}) collective-permute-start(bf16[2,96,640]{2,1,0:T(8,128)(2,1)S(1)} %get-tuple-element.38), channel_id=1, source_target_pairs={{0,32},{32,64},{64,96},{96,128},{128,160},{160,192},{192,224},{224... | collective-permute-start | bytes 737288 | tf_op jit(solution)/shard_map/ppermute | solution.py:291
  87.5 57.5 %collective-permute-start.3 = (bf16[6,48,2560]{2,1,0:T(8,128)(2,1)S(1)}, bf16[6,48,2560]{2,1,0:T(8,128)(2,1)}, u32[]{:S(2)}, u32[]{:S(2)}) collective-permute-start(bf16[6,48,2560]{2,1,0:T(8,128)(2,1)S(1)} %pad_maximum_fusion), channel_id=1, source_target_pairs={{0,256},{32,288},{64,320},{96,352},{128,384},{160,416},{192,448},{... | collective-permute-start | bytes 4423688 | tf_op jit(solution)/shard_map/ppermute | solution.py:296
  90.1 19.3 %collective-permute-start.4 = (bf16[2,96,640]{2,1,0:T(8,128)(2,1)S(1)}, bf16[2,96,640]{2,1,0:T(8,128)(2,1)S(1)}, u32[]{:S(2)}, u32[]{:S(2)}) collective-permute-start(bf16[2,96,640]{2,1,0:T(8,128)(2,1)S(1)} %get-tuple-element.42), channel_id=1, source_target_pairs={{0,64},{32,96},{64,128},{96,160},{128,192},{160,224},{192,0},{224,... | collective-permute-start | bytes 737288 | tf_op jit(solution)/shard_map/ppermute | solution.py:291
  92.9 34.1 %collective-permute-start.5 = (bf16[2,96,640]{2,1,0:T(8,128)(2,1)S(1)}, bf16[2,96,640]{2,1,0:T(8,128)(2,1)S(1)}, u32[]{:S(2)}, u32[]{:S(2)}) collective-permute-start(bf16[2,96,640]{2,1,0:T(8,128)(2,1)S(1)} %get-tuple-element.43), channel_id=1, source_target_pairs={{0,96},{32,128},{64,160},{96,192},{128,224},{160,0},{192,32},{224,... | collective-permute-start | bytes 737288 | tf_op jit(solution)/shard_map/ppermute | solution.py:291
  98.7 30.2 %collective-permute-start.6 = (bf16[2,96,640]{2,1,0:T(8,128)(2,1)S(1)}, bf16[2,96,640]{2,1,0:T(8,128)(2,1)S(1)}, u32[]{:S(2)}, u32[]{:S(2)}) collective-permute-start(bf16[2,96,640]{2,1,0:T(8,128)(2,1)S(1)} %get-tuple-element.44), channel_id=1, source_target_pairs={{0,128},{32,160},{64,192},{96,224},{128,0},{160,32},{192,64},{224,... | collective-permute-start | bytes 737288 | tf_op jit(solution)/shard_map/ppermute | solution.py:291
  102.2 30.7 %collective-permute-start.7 = (bf16[2,96,640]{2,1,0:T(8,128)(2,1)S(1)}, bf16[2,96,640]{2,1,0:T(8,128)(2,1)S(1)}, u32[]{:S(2)}, u32[]{:S(2)}) collective-permute-start(bf16[2,96,640]{2,1,0:T(8,128)(2,1)S(1)} %get-tuple-element.45), channel_id=1, source_target_pairs={{0,160},{32,192},{64,224},{96,0},{128,32},{160,64},{192,96},{224,1... | collective-permute-start | bytes 737288 | tf_op jit(solution)/shard_map/ppermute | solution.py:291
  109.4 33.9 %collective-permute-start.8 = (bf16[2,96,640]{2,1,0:T(8,128)(2,1)S(1)}, bf16[2,96,640]{2,1,0:T(8,128)(2,1)S(1)}, u32[]{:S(2)}, u32[]{:S(2)}) collective-permute-start(bf16[2,96,640]{2,1,0:T(8,128)(2,1)S(1)} %get-tuple-element.46), channel_id=1, source_target_pairs={{0,192},{32,224},{64,0},{96,32},{128,64},{160,96},{192,128},{224,1... | collective-permute-start | bytes 737288 | tf_op jit(solution)/shard_map/ppermute | solution.py:291
  126.9 17.3 %collective-permute-start.9 = (bf16[2,96,640]{2,1,0:T(8,128)(2,1)S(1)}, bf16[2,96,640]{2,1,0:T(8,128)(2,1)S(1)}, u32[]{:S(2)}, u32[]{:S(2)}) collective-permute-start(bf16[2,96,640]{2,1,0:T(8,128)(2,1)S(1)} %get-tuple-element.47), channel_id=1, source_target_pairs={{0,224},{32,0},{64,32},{96,64},{128,96},{160,128},{192,160},{224,1... | collective-permute-start | bytes 737288 | tf_op jit(solution)/shard_map/ppermute | solution.py:291
  145.0 1.5 copy-start
  153.4 28.7 %copy-start.9 = (bf16[2,96,640]{2,1,0:T(8,128)(2,1)S(1)}, bf16[2,96,640]{2,1,0:T(8,128)(2,1)}, u32[]{:S(2)}) copy-start(bf16[2,96,640]{2,1,0:T(8,128)(2,1)} %copy-done.8) | copy-start | bytes 737284
  153.4 28.7 %copy-start.11 = (bf16[2,96,640]{2,1,0:T(8,128)(2,1)S(1)}, bf16[2,96,640]{2,1,0:T(8,128)(2,1)}, u32[]{:S(2)}) copy-start(bf16[2,96,640]{2,1,0:T(8,128)(2,1)} %copy-done.10) | copy-start | bytes 737284
  153.4 28.7 %copy-start.13 = (bf16[2,96,640]{2,1,0:T(8,128)(2,1)S(1)}, bf16[2,96,640]{2,1,0:T(8,128)(2,1)}, u32[]{:S(2)}) copy-start(bf16[2,96,640]{2,1,0:T(8,128)(2,1)} %copy-done.12) | copy-start | bytes 737284
  153.4 28.7 %copy-start.15 = (bf16[2,96,640]{2,1,0:T(8,128)(2,1)S(1)}, bf16[2,96,640]{2,1,0:T(8,128)(2,1)}, u32[]{:S(2)}) copy-start(bf16[2,96,640]{2,1,0:T(8,128)(2,1)} %copy-done.14) | copy-start | bytes 737284
  153.4 28.7 %copy-start.17 = (bf16[2,96,640]{2,1,0:T(8,128)(2,1)S(1)}, bf16[2,96,640]{2,1,0:T(8,128)(2,1)}, u32[]{:S(2)}) copy-start(bf16[2,96,640]{2,1,0:T(8,128)(2,1)} %copy-done.16) | copy-start | bytes 737284
  153.4 28.7 %copy-start.20 = (bf16[512,128]{1,0:T(8,128)(2,1)S(1)}, bf16[512,128]{1,0:T(8,128)(2,1)}, u32[]{:S(2)}) copy-start(bf16[512,128]{1,0:T(8,128)(2,1)} %get-tuple-element.51.weight_ref) | copy-start | bytes 393220
  182.2 23.9 %copy-start.1 = (bf16[32,16,2688]{2,1,0:T(8,128)(2,1)S(1)}, bf16[32,16,2688]{2,1,0:T(8,128)(2,1)}, u32[]{:S(2)}) copy-start(bf16[32,16,2688]{2,1,0:T(8,128)(2,1)} %copy-done) | copy-start | bytes 8257540
  185.3 20.7 %copy-start.18 = (f32[96,512]{1,0:T(8,128)S(1)}, f32[96,512]{1,0:T(8,128)}, u32[]{:S(2)}) copy-start(f32[96,512]{1,0:T(8,128)} %get-tuple-element.61.refs_1_) | copy-start | bytes 589828
  185.3 20.7 %copy-start.19 = (f32[96,512]{1,0:T(8,128)S(1)}, f32[96,512]{1,0:T(8,128)}, u32[]{:S(2)}) copy-start(f32[96,512]{1,0:T(8,128)} %get-tuple-element.62.refs_2_) | copy-start | bytes 589828
  185.3 15.0 %collective-permute-start.10 = (bf16[8,48,640]{2,1,0:T(8,128)(2,1)}, bf16[8,48,640]{2,1,0:T(8,128)(2,1)}, u32[]{:S(2)}, u32[]{:S(2)}) collective-permute-start(bf16[8,48,640]{2,1,0:T(8,128)(2,1)} %get-tuple-element.66), channel_id=1, source_target_pairs={{0,256},{32,288},{64,320},{96,352},{128,384},{160,416},{192,448},{... | collective-permute-start | bytes 1474568 | tf_op jit(solution)/shard_map/ppermute | solution.py:321
  190.0 16.0 %all-to-all-start.3 = ((bf16[8,96,256]{2,1,0:T(8,128)(2,1)}), bf16[8,96,256]{2,1,0:T(8,128)(2,1)S(1)}, u32[]{:S(2)}, u32[]{:S(2)}) async-start(bf16[8,96,256]{2,1,0:T(8,128)(2,1)} %get-tuple-element.60), calls=%async_computation.3 | async-start | bytes 786432 | tf_op jit(solution)/shard_map/all_to_all | solution.py:261
  208.8 12.6 %copy-start.5 = (f32[2,48,2560]{2,1,0:T(8,128)S(1)}, f32[2,48,2560]{2,1,0:T(8,128)}, u32[]{:S(2)}) copy-start(f32[2,48,2560]{2,1,0:T(8,128)} %copy-done.4) | copy-start | bytes 2949124
  208.8 12.6 %collective-permute-start.11 = (bf16[2,48,2560]{2,1,0:T(8,128)(2,1)}, bf16[2,48,2560]{2,1,0:T(8,128)(2,1)S(1)}, u32[]{:S(2)}, u32[]{:S(2)}) collective-permute-start(bf16[2,48,2560]{2,1,0:T(8,128)(2,1)} %get-tuple-element.67), channel_id=1, source_target_pairs={{0,256},{32,288},{64,320},{96,352},{128,384},{160,416},{192,448},{... | collective-permute-start | bytes 1474568 | tf_op jit(solution)/shard_map/ppermute | solution.py:333
  212.0 17.0 %all-to-all-start.4 = ((bf16[8,48,640]{2,1,0:T(8,128)(2,1)}), bf16[8,48,640]{2,1,0:T(8,128)(2,1)S(1)}, u32[]{:S(2)}, u32[]{:S(2)}) async-start(bf16[8,48,640]{2,1,0:T(8,128)(2,1)} %add_convert_fusion), calls=%async_computation.4 | async-start | bytes 983040 | tf_op jit(solution)/shard_map/all_to_all | solution.py:261
  (10 other events, 7.6 us)

commit v8 on v7

--- a/solution.py
+++ b/solution.py
@@ -7,6 +7,7 @@
 
 HALVES = 2
 PAIR = 2
+EARLY = (1, 7, 2)
 RING = 8
 SIDE = 128
 BF16 = jnp.bfloat16
@@ -25,13 +26,16 @@
     return lax.dot_general(a, b, (((0,), (0,)), ((), ())), preferred_element_type=F32)
 
 
-def call(kernel, outs, args, mib=16):
-    space = pl.BlockSpec(memory_space=pltpu.VMEM)
+def call(kernel, outs, args, far=(), scratch=(), mib=16):
+    def space(i, alone):
+        return pl.BlockSpec(memory_space=pltpu.HBM if i in alone else pltpu.VMEM)
+
     return pl.pallas_call(
         kernel,
         out_shape=outs,
-        in_specs=[space] * len(args),
-        out_specs=[space] * len(outs),
+        in_specs=[space(i, far) for i in range(len(args))],
+        out_specs=[space(i, ()) for i in range(len(outs))],
+        scratch_shapes=scratch,
         compiler_params=pltpu.CompilerParams(vmem_limit_bytes=mib * 1024 * 1024),
         cost_estimate=pl.CostEstimate(
             flops=0,
@@ -39,6 +43,21 @@
             transcendentals=0,
         ),
     )(*args)
+
+
+def start_copies(pairs, sems, first=0):
+    copies = [
+        pltpu.make_async_copy(source, target, sems.at[first + i])
+        for i, (source, target) in enumerate(pairs)
+    ]
+    for copy in copies:
+        copy.start()
+    return copies
+
+
+def wait_copies(copies):
+    for copy in copies:
+        copy.wait()
 
 
 def place():
@@ -105,43 +124,60 @@
 
 def hidden_kernel(
     capacity,
-    rows_ref,
-    t_gate_ref,
-    t_up_ref,
-    m_gate_ref,
-    m_up_ref,
-    come_ref,
+    rows_hbm,
+    t_gate_hbm,
+    t_up_hbm,
+    m_gate_hbm,
+    m_up_hbm,
+    come_hbm,
     out_ref,
     silu_ref,
     slope_ref,
     weight_ref,
+    row_buf,
+    weight_buf,
+    sems,
 ):
     half, _ = place()
-    block = m_gate_ref.shape[1]
+    block = m_gate_hbm.shape[1]
     units = 2 * block
-    count = rows_ref.shape[0]
-    features = rows_ref.shape[1] - SIDE
+    count, wide = row_buf.shape
+    features = wide - SIDE
     span = count // PAIR
     places = out_ref.shape[0] // PAIR
-    rows = rows_ref[:, :features]
-
-    def gate_up(*parts):
-        value = dot_nt(jnp.concatenate(parts, axis=0), rows)
+
+    def weights(at, *parts):
+        pairs = [(part, weight_buf.at[at, pl.ds(i * block, block)]) for i, part in enumerate(parts)]
+        return start_copies(pairs, sems, 4 * at)
+
+    def gate_up(at):
+        value = dot_nt(weight_buf[at], row_buf[:, :features])
         return value[:units], value[units:]
 
-    gate, up = gate_up(m_gate_ref[0], come_ref[2 * PAIR], m_up_ref[0], come_ref[2 * PAIR + 1])
+    first = start_copies([(rows_hbm, row_buf)], sems, 4 * PAIR + 4)
+    first += weights(
+        PAIR, m_gate_hbm.at[0], come_hbm.at[2 * PAIR], m_up_hbm.at[0], come_hbm.at[2 * PAIR + 1]
+    )
+    later = []
+    for m in range(PAIR):
+        own = PAIR * half + m
+        later.append(
+            weights(m, t_gate_hbm.at[own], come_hbm.at[m], t_up_hbm.at[own], come_hbm.at[PAIR + m])
+        )
+    move = by_teacher(count, capacity, 0)
+    wait_copies(first)
+    gate, up = gate_up(PAIR)
     silu, slope = silu_split(gate)
     silu_ref[...] = silu
     slope_ref[...] = up * slope
     hidden = [(silu * up).astype(BF16)]
     for m in range(PAIR):
-        own = PAIR * half + m
-        gate, up = gate_up(t_gate_ref[own], come_ref[m], t_up_ref[own], come_ref[PAIR + m])
+        wait_copies(later[m])
+        gate, up = gate_up(m)
         silu, _ = silu_split(gate)
         hidden.append((silu * up).astype(BF16))
-    move = by_teacher(count, capacity, 0)
     hidden = dot_nn(jnp.concatenate(hidden, axis=0), move).astype(BF16)
-    weight_ref[...] = dot_tn(move, rows_ref[:, features:]).astype(BF16)
+    weight_ref[...] = dot_tn(move, row_buf[:, features:]).astype(BF16)
     for m in range(PAIR):
         lanes = slice(m * span, (m + 1) * span)
         first = (1 + m) * units
@@ -153,21 +189,25 @@
             out_ref[at, 3] = hidden[first + block : first + units, lanes]
 
 
-def share_kernel(down_ref, merged_ref, came_ref, merged_came_ref, *out_refs):
+def share_kernel(down_ref, merged_ref, *out_refs):
     half, at = place()
-    block = merged_ref.shape[1]
     quarter = out_refs[0].shape[2]
     for k, out_ref in enumerate(out_refs):
         there = (at + k) % RING
         m = there // (RING // PAIR)
         span = pl.ds(pl.multiple_of(there % (RING // PAIR) * quarter, SIDE), quarter)
-        out_ref[0, :block] = down_ref[PAIR * half + m, :, span]
-        out_ref[0, block:] = came_ref[m, :, span]
-        out_ref[1, :block] = merged_ref[0, :, span]
-        out_ref[1, block:] = merged_came_ref[0, :, span]
-
-
-def gap_kernel(hidden_ref, weight_ref, *refs):
+        out_ref[0] = down_ref[PAIR * half + m, :, span]
+        out_ref[1] = down_ref[PAIR * (1 - half) + m, :, span]
+        out_ref[2] = merged_ref[0, :, span]
+
+
+def pass_kernel(*refs):
+    out_ref = refs[-1]
+    for k, down_ref in enumerate(refs[:-1]):
+        out_ref[k] = down_ref[1:]
+
+
+def gap_kernel(hidden_ref, weight_ref, came_ref, *refs):
     down_refs = refs[:RING]
     grad_ref, kept_ref, other_ref = refs[RING:]
     block = hidden_ref.shape[2]
@@ -177,8 +217,8 @@
     back = [(at + RING - k) % RING for k in range(RING)]
     student = jnp.concatenate([hidden_ref[i, a] for i in back for a in (0, 1)], axis=0)
     teacher = jnp.concatenate([hidden_ref[i, a] for i in back for a in (2, 3)], axis=0)
-    t_down = jnp.concatenate([down_ref[0] for down_ref in down_refs], axis=0)
-    m_down = jnp.concatenate([down_ref[1] for down_ref in down_refs], axis=0)
+    t_down = jnp.concatenate([x for k in range(RING) for x in (down_refs[k][0], came_ref[k, 0])], axis=0)
+    m_down = jnp.concatenate([x for k in range(RING) for x in (down_refs[k][2], came_ref[k, 1])], axis=0)
     gap = dot_tn(student, m_down) - dot_tn(teacher, t_down)
     start = pl.multiple_of(at // (RING // PAIR) * span, span)
     weight = weight_ref[pl.ds(start, span), SIDE - 1 : SIDE].astype(F32)
@@ -272,8 +312,17 @@
     )
     group = exchange(packets, "dp").reshape(n_dp * capacity, wide)
 
-    came = lax.ppermute(halves(teacher_down, 1 - half), "dp", swap)
-    group, came = lax.optimization_barrier((group, came))
+    down = call(
+        share_kernel,
+        tuple(jax.ShapeDtypeStruct((PAIR + 1, block, quarter), BF16) for _ in range(RING)),
+        (teacher_down, merged_down),
+    )
+    down = [down[k] if k == 0 else lax.ppermute(down[k], "dp", turns[k]) for k in range(RING)]
+    early = [down[k] for k in EARLY]
+    group, early = lax.optimization_barrier((group, early))
+    for k, array in zip(EARLY, early):
+        down[k] = array
+
     (slots,) = call(
         lambda *refs: slots_kernel(ranks, capacity, *refs),
         (jax.ShapeDtypeStruct((rows, wide), BF16),),
@@ -282,19 +331,14 @@
     )
     slots = exchange(slots.reshape(experts, PAIR * capacity, wide), "expert").reshape(rows, wide)
 
-    merged_came = lax.ppermute(merged_down, "dp", swap)
-    down = call(
-        share_kernel,
-        tuple(jax.ShapeDtypeStruct((2, 2 * block, quarter), BF16) for _ in range(RING)),
-        (teacher_down, merged_down, came, merged_came),
-    )
-    down = [down[k] if k == 0 else lax.ppermute(down[k], "dp", turns[k]) for k in range(RING)]
-
-    parts = [halves(teacher_gate, 1 - half), halves(teacher_up, 1 - half), merged_gate, merged_up]
-    come = jnp.concatenate(parts, axis=0)
-    come, down[1] = lax.optimization_barrier((come, down[1]))
-    come = lax.ppermute(come, "dp", swap)
+    sent = [halves(teacher_gate, 1 - half), halves(teacher_up, 1 - half), merged_gate, merged_up]
+    come = lax.ppermute(jnp.concatenate(sent, axis=0), "dp", swap)
     slots, come, down = lax.optimization_barrier((slots, come, down))
+
+    (passed,) = call(
+        pass_kernel, (jax.ShapeDtypeStruct((RING, PAIR, block, quarter), BF16),), tuple(down), mib=60
+    )
+    came = lax.ppermute(passed, "dp", swap)
 
     hidden, silu, slope, weight = call(
         lambda *refs: hidden_kernel(capacity, *refs),
@@ -305,6 +349,12 @@
             jax.ShapeDtypeStruct((rows, SIDE), BF16),
         ),
         (slots, teacher_gate, teacher_up, merged_gate, merged_up, come),
+        far=range(6),
+        scratch=[
+            pltpu.VMEM((rows, wide), BF16),
+            pltpu.VMEM((PAIR + 1, 4 * block, features), BF16),
+            pltpu.SemaphoreType.DMA((4 * PAIR + 5,)),
+        ],
         mib=60,
     )
     hidden = exchange(hidden, "dp", rings)
@@ -315,7 +365,8 @@
             jax.ShapeDtypeStruct((RING, block, quarter), BF16),
             jax.ShapeDtypeStruct((RING, block, quarter), BF16),
         ),
-        (hidden, weight, *down),
+        (hidden, weight, came, *down),
+        mib=60,
     )
     parts = exchange(hidden_grad, "dp", rings)
     other_down = lax.ppermute(other_down, "dp", swap)

time: 231 us -> 222 us (0.961)
  the two profiles are of different devices: /device:TPU:32 before, /device:TPU:6 now
where the time goes in v8:
time: 222 us; the launch traced here: 220 us
  waiting for transfers between devices  108 us (49%)
  starting transfers between devices  77.7 us (35%)
  Pallas kernels  21.3 us (10%)
  local copies, waits for them, and re-layouts  9.22 us (4%)
  other arithmetic  3.31 us (1%)
    ppermute x7, waiting for transfers between devices, body(): lax.ppermute(down[k], 'dp', turns[k])  39.5 us
    all_to_all x5, starting transfers between devices, exchange(): lax.all_to_all(array, axis_name, split_axis=0, concat_axis=0, tiled=True,...  37.5 us
    ppermute x7, starting transfers between devices, body(): lax.ppermute(down[k], 'dp', turns[k])  26.6 us
    ppermute x1, waiting for transfers between devices, body(): came = lax.ppermute(passed, 'dp', swap)  23.7 us
    ppermute x1, waiting for transfers between devices, body(): come = lax.ppermute(jnp.concatenate(sent, axis=0), 'dp', swap)  21.6 us
    pallas_call x8, Pallas kernels, call(): pl.pallas_call(kernel, out_shape=outs, in_specs=[space(i, far) for i in r...  21.3 us
    all_to_all x5, waiting for transfers between devices, exchange(): lax.all_to_all(array, axis_name, split_axis=0, concat_axis=0, tiled=True,...  13.2 us
    unnamed x44, local copies, waits for them, and re-layouts  7.14 us
  transfers between devices with their start and end apart: 16, of which 11 were waited for; matrix products, arithmetic and copies ran while one was open for 2% of the time, Pallas kernels for 1%

profile of v8, /device:TPU:6, one launch (start us, length us, event | category | flops | bytes accessed | tf_op | source)
XLA Modules:
  0.0 220.4 jit_solution(10564463813256532085)
XLA Ops:
  3.9 13.3 %all-to-all-start = ((bf16[16,8,2688]{2,1,0:T(8,128)(2,1)}), bf16[16,8,2688]{2,1,0:T(8,128)(2,1)S(1)}, u32[]{:S(2)}, u32[]{:S(2)}) async-start(bf16[16,8,2688]{2,1,0:T(8,128)(2,1)} %shard_map.112), calls=%async_computation | async-start | bytes 1376256 | tf_op jit(solution)/shard_map/all_to_all | solution.py:301
  18.1 3.4 %collective-permute-start = (bf16[3,48,640]{2,1,0:T(8,128)(2,1)S(1)}, bf16[3,48,640]{2,1,0:T(8,128)(2,1)S(1)}, u32[]{:S(2)}, u32[]{:S(2)}) collective-permute-start(bf16[3,48,640]{2,1,0:T(8,128)(2,1)S(1)} %get-tuple-element.36), channel_id=1, source_target_pairs={{0,32},{32,64},{64,96},{96,128},{128,160},{160,192},{192,224},{224... | collective-permute-start | bytes 552968 | tf_op jit(solution)/shard_map/ppermute | solution.py:320
  21.5 3.7 %collective-permute-start.1 = (bf16[3,48,640]{2,1,0:T(8,128)(2,1)S(1)}, bf16[3,48,640]{2,1,0:T(8,128)(2,1)S(1)}, u32[]{:S(2)}, u32[]{:S(2)}) collective-permute-start(bf16[3,48,640]{2,1,0:T(8,128)(2,1)S(1)} %get-tuple-element.37), channel_id=1, source_target_pairs={{0,224},{32,0},{64,32},{96,64},{128,96},{160,128},{192,160},{224,1... | collective-permute-start | bytes 552968 | tf_op jit(solution)/shard_map/ppermute | solution.py:320
  25.2 3.1 %collective-permute-start.2 = (bf16[3,48,640]{2,1,0:T(8,128)(2,1)S(1)}, bf16[3,48,640]{2,1,0:T(8,128)(2,1)S(1)}, u32[]{:S(2)}, u32[]{:S(2)}) collective-permute-start(bf16[3,48,640]{2,1,0:T(8,128)(2,1)S(1)} %get-tuple-element.38), channel_id=1, source_target_pairs={{0,64},{32,96},{64,128},{96,160},{128,192},{160,224},{192,0},{224,... | collective-permute-start | bytes 552968 | tf_op jit(solution)/shard_map/ppermute | solution.py:320
  28.2 12.5 %collective-permute-done.refs_1_ = bf16[3,48,640]{2,1,0:T(8,128)(2,1)S(1)} collective-permute-done((bf16[3,48,640]{2,1,0:T(8,128)(2,1)S(1)}, bf16[3,48,640]{2,1,0:T(8,128)(2,1)S(1)}, u32[]{:S(2)}, u32[]{:S(2)}) %collective-permute-start) | collective-permute-done | bytes 184352 | tf_op jit(solution)/shard_map/ppermute | solution.py:320
  40.7 5.4 %collective-permute-done.2.refs_2_ = bf16[3,48,640]{2,1,0:T(8,128)(2,1)S(1)} collective-permute-done((bf16[3,48,640]{2,1,0:T(8,128)(2,1)S(1)}, bf16[3,48,640]{2,1,0:T(8,128)(2,1)S(1)}, u32[]{:S(2)}, u32[]{:S(2)}) %collective-permute-start.2) | collective-permute-done | bytes 184352 | tf_op jit(solution)/shard_map/ppermute | solution.py:320
  47.0 3.9 %shard_map.114 = bf16[512,2688]{1,0:T(8,128)(2,1)} custom-call(bf16[128,2688]{1,0:T(8,128)(2,1)} %bitcast.18), custom_call_target="tpu_custom_call" | custom-call | bytes 688128 | tf_op jit(solution)/shard_map/pallas_call | solution.py:33
  50.9 8.7 %all-to-all-start.1 = ((bf16[32,16,2688]{2,1,0:T(8,128)(2,1)}), bf16[32,16,2688]{2,1,0:T(8,128)(2,1)S(1)}, u32[]{:S(2)}, u32[]{:S(2)}) async-start(bf16[32,16,2688]{2,1,0:T(8,128)(2,1)} %bitcast.17), calls=%async_computation.1 | async-start | bytes 5505024 | tf_op jit(solution)/shard_map/all_to_all | solution.py:301
  61.2 2.6 %collective-permute-start.3 = (bf16[6,48,2560]{2,1,0:T(8,128)(2,1)S(1)}, bf16[6,48,2560]{2,1,0:T(8,128)(2,1)}, u32[]{:S(2)}, u32[]{:S(2)}) collective-permute-start(bf16[6,48,2560]{2,1,0:T(8,128)(2,1)S(1)} %pad_maximum_fusion), channel_id=1, source_target_pairs={{0,256},{32,288},{64,320},{96,352},{128,384},{160,416},{192,448},{... | collective-permute-start | bytes 4423688 | tf_op jit(solution)/shard_map/ppermute | solution.py:335
  63.9 3.4 %collective-permute-start.4 = (bf16[3,48,640]{2,1,0:T(8,128)(2,1)S(1)}, bf16[3,48,640]{2,1,0:T(8,128)(2,1)S(1)}, u32[]{:S(2)}, u32[]{:S(2)}) collective-permute-start(bf16[3,48,640]{2,1,0:T(8,128)(2,1)S(1)} %get-tuple-element.43), channel_id=1, source_target_pairs={{0,96},{32,128},{64,160},{96,192},{128,224},{160,0},{192,32},{224,... | collective-permute-start | bytes 552968 | tf_op jit(solution)/shard_map/ppermute | solution.py:320
  67.3 6.4 %collective-permute-start.5 = (bf16[3,48,640]{2,1,0:T(8,128)(2,1)S(1)}, bf16[3,48,640]{2,1,0:T(8,128)(2,1)S(1)}, u32[]{:S(2)}, u32[]{:S(2)}) collective-permute-start(bf16[3,48,640]{2,1,0:T(8,128)(2,1)S(1)} %get-tuple-element.44), channel_id=1, source_target_pairs={{0,128},{32,160},{64,192},{96,224},{128,0},{160,32},{192,64},{224,... | collective-permute-start | bytes 552968 | tf_op jit(solution)/shard_map/ppermute | solution.py:320
  73.7 3.9 %collective-permute-start.6 = (bf16[3,48,640]{2,1,0:T(8,128)(2,1)S(1)}, bf16[3,48,640]{2,1,0:T(8,128)(2,1)S(1)}, u32[]{:S(2)}, u32[]{:S(2)}) collective-permute-start(bf16[3,48,640]{2,1,0:T(8,128)(2,1)S(1)} %get-tuple-element.45), channel_id=1, source_target_pairs={{0,160},{32,192},{64,224},{96,0},{128,32},{160,64},{192,96},{224,1... | collective-permute-start | bytes 552968 | tf_op jit(solution)/shard_map/ppermute | solution.py:320
  77.5 2.9 %collective-permute-start.7 = (bf16[3,48,640]{2,1,0:T(8,128)(2,1)S(1)}, bf16[3,48,640]{2,1,0:T(8,128)(2,1)S(1)}, u32[]{:S(2)}, u32[]{:S(2)}) collective-permute-start(bf16[3,48,640]{2,1,0:T(8,128)(2,1)S(1)} %get-tuple-element.46), channel_id=1, source_target_pairs={{0,192},{32,224},{64,0},{96,32},{128,64},{160,96},{192,128},{224,1... | collective-permute-start | bytes 552968 | tf_op jit(solution)/shard_map/ppermute | solution.py:320
  80.5 6.6 %collective-permute-done.5.refs_4_ = bf16[3,48,640]{2,1,0:T(8,128)(2,1)S(1)} collective-permute-done((bf16[3,48,640]{2,1,0:T(8,128)(2,1)S(1)}, bf16[3,48,640]{2,1,0:T(8,128)(2,1)S(1)}, u32[]{:S(2)}, u32[]{:S(2)}) %collective-permute-start.5) | collective-permute-done | bytes 184352 | tf_op jit(solution)/shard_map/ppermute | solution.py:320
  87.1 7.1 %collective-permute-done.6.refs_5_ = bf16[3,48,640]{2,1,0:T(8,128)(2,1)S(1)} collective-permute-done((bf16[3,48,640]{2,1,0:T(8,128)(2,1)S(1)}, bf16[3,48,640]{2,1,0:T(8,128)(2,1)S(1)}, u32[]{:S(2)}, u32[]{:S(2)}) %collective-permute-start.6) | collective-permute-done | bytes 184352 | tf_op jit(solution)/shard_map/ppermute | solution.py:320
  94.2 7.9 %collective-permute-done.7.refs_6_ = bf16[3,48,640]{2,1,0:T(8,128)(2,1)S(1)} collective-permute-done((bf16[3,48,640]{2,1,0:T(8,128)(2,1)S(1)}, bf16[3,48,640]{2,1,0:T(8,128)(2,1)S(1)}, u32[]{:S(2)}, u32[]{:S(2)}) %collective-permute-start.7) | collective-permute-done | bytes 184352 | tf_op jit(solution)/shard_map/ppermute | solution.py:320
  102.8 21.6 %collective-permute-done.3.refs_5_ = bf16[6,48,2560]{2,1,0:T(8,128)(2,1)} collective-permute-done((bf16[6,48,2560]{2,1,0:T(8,128)(2,1)S(1)}, bf16[6,48,2560]{2,1,0:T(8,128)(2,1)}, u32[]{:S(2)}, u32[]{:S(2)}) %collective-permute-start.3) | collective-permute-done | bytes 1474592 | tf_op jit(solution)/shard_map/ppermute | solution.py:335
  126.0 6.4 %shard_map.115 = (bf16[8,4,48,256]{3,2,1,0:T(8,128)(2,1)}, f32[96,512]{1,0:T(8,128)}, f32[96,512]{1,0:T(8,128)}, bf16[512,128]{1,0:T(8,128)(2,1)}) custom-call(bf16[512,2688]{1,0:T(8,128)(2,1)} %bitcast.12, bf16[4,48,2560]{2,1,0:T(8,128)(2,1)} %refs_1_.1, bf16[4,48,2560]{2,1,0:T(8,128)(2,1)} %refs_2_.1, bf16[1,48,2560]{2,1,0:T(8,128)(2,1)} %refs_3_.1, ...), custom_call_target="tpu_custom_call" | custom-call | bytes 6684672 | tf_op jit(solution)/shard_map/pallas_call | solution.py:33
  132.4 5.1 %all-to-all-start.2 = ((bf16[8,4,48,256]{3,2,1,0:T(8,128)(2,1)}), bf16[8,4,48,256]{3,2,1,0:T(8,128)(2,1)S(1)}, u32[]{:S(2)}, u32[]{:S(2)}) async-start(bf16[8,4,48,256]{3,2,1,0:T(8,128)(2,1)} %get-tuple-element.50), calls=%async_computation.2 | async-start | bytes 1572864 | tf_op jit(solution)/shard_map/all_to_all | solution.py:301
  137.5 2.5 %shard_map.116 = bf16[8,2,48,640]{3,2,1,0:T(8,128)(2,1)} custom-call(bf16[3,48,640]{2,1,0:T(8,128)(2,1)} %copy-done.5, bf16[3,48,640]{2,1,0:T(8,128)(2,1)} %copy-done.15, bf16[3,48,640]{2,1,0:T(8,128)(2,1)} %copy-done.17, bf16[3,48,640]{2,1,0:T(8,128)(2,1)} %copy-done.18, bf16[3,48,640]{2,1,0:T(8,128)(2,1)} %copy-done.19, bf16[3,48,640]{2,1,0:T(8,128)(2,1)} %copy-done.20, ...), custom_call_target="tpu_custom_call" | custom-call | bytes 1474560 | tf_op jit(solution)/shard_map/pallas_call | solution.py:33
  139.9 3.1 %collective-permute-start.8 = (bf16[8,2,48,640]{3,2,1,0:T(8,128)(2,1)}, bf16[8,2,48,640]{3,2,1,0:T(8,128)(2,1)}, u32[]{:S(2)}, u32[]{:S(2)}) collective-permute-start(bf16[8,2,48,640]{3,2,1,0:T(8,128)(2,1)} %shard_map.116), channel_id=1, source_target_pairs={{0,256},{32,288},{64,320},{96,352},{128,384},{160,416},{192,448},{... | collective-permute-start | bytes 2949128 | tf_op jit(solution)/shard_map/ppermute | solution.py:341
  143.1 23.7 %collective-permute-done.8.came_ref = bf16[8,2,48,640]{3,2,1,0:T(8,128)(2,1)} collective-permute-done((bf16[8,2,48,640]{3,2,1,0:T(8,128)(2,1)}, bf16[8,2,48,640]{3,2,1,0:T(8,128)(2,1)}, u32[]{:S(2)}, u32[]{:S(2)}) %collective-permute-start.8) | collective-permute-done | bytes 983072 | tf_op jit(solution)/shard_map/ppermute | solution.py:341
  167.7 4.7 %shard_map.117 = (bf16[8,96,256]{2,1,0:T(8,128)(2,1)}, bf16[8,48,640]{2,1,0:T(8,128)(2,1)}, bf16[8,48,640]{2,1,0:T(8,128)(2,1)}) custom-call(bf16[8,4,48,256]{3,2,1,0:T(8,128)(2,1)} %copy-done.11, bf16[512,128]{1,0:T(8,128)(2,1)} %get-tuple-element.51.weight_ref, bf16[8,2,48,640]{3,2,1,0:T(8,128)(2,1)} %collective-permute-done.8.came_ref, ...), custom_call_target="tpu_custom_call" | custom-call | bytes 3375104 | tf_op jit(solution)/shard_map/pallas_call | solution.py:33
  172.4 3.1 %collective-permute-start.9 = (bf16[8,48,640]{2,1,0:T(8,128)(2,1)}, bf16[8,48,640]{2,1,0:T(8,128)(2,1)}, u32[]{:S(2)}, u32[]{:S(2)}) collective-permute-start(bf16[8,48,640]{2,1,0:T(8,128)(2,1)} %get-tuple-element.66), channel_id=1, source_target_pairs={{0,256},{32,288},{64,320},{96,352},{128,384},{160,416},{192,448},{... | collective-permute-start | bytes 1474568 | tf_op jit(solution)/shard_map/ppermute | solution.py:372
  175.5 6.9 %all-to-all-start.3 = ((bf16[8,96,256]{2,1,0:T(8,128)(2,1)}), bf16[8,96,256]{2,1,0:T(8,128)(2,1)S(1)}, u32[]{:S(2)}, u32[]{:S(2)}) async-start(bf16[8,96,256]{2,1,0:T(8,128)(2,1)} %get-tuple-element.60), calls=%async_computation.3 | async-start | bytes 786432 | tf_op jit(solution)/shard_map/all_to_all | solution.py:301
  182.4 5.5 %collective-permute-done.9 = bf16[8,48,640]{2,1,0:T(8,128)(2,1)} collective-permute-done((bf16[8,48,640]{2,1,0:T(8,128)(2,1)}, bf16[8,48,640]{2,1,0:T(8,128)(2,1)}, u32[]{:S(2)}, u32[]{:S(2)}) %collective-permute-start.9) | collective-permute-done | bytes 491552 | tf_op jit(solution)/shard_map/ppermute | solution.py:372
  187.9 2.1 add_convert_fusion
  190.0 5.1 %all-to-all-done.3.refs_0_ = bf16[8,96,256]{2,1,0:T(8,128)(2,1)S(1)} async-done(((bf16[8,96,256]{2,1,0:T(8,128)(2,1)}), bf16[8,96,256]{2,1,0:T(8,128)(2,1)S(1)}, u32[]{:S(2)}, u32[]{:S(2)}) %all-to-all-start.3) | async-done | bytes 393248 | tf_op jit(solution)/shard_map/all_to_all | solution.py:301
  197.9 4.7 %collective-permute-start.10 = (bf16[2,48,2560]{2,1,0:T(8,128)(2,1)}, bf16[2,48,2560]{2,1,0:T(8,128)(2,1)S(1)}, u32[]{:S(2)}, u32[]{:S(2)}) collective-permute-start(bf16[2,48,2560]{2,1,0:T(8,128)(2,1)} %get-tuple-element.67), channel_id=1, source_target_pairs={{0,256},{32,288},{64,320},{96,352},{128,384},{160,416},{192,448},{... | collective-permute-start | bytes 1474568 | tf_op jit(solution)/shard_map/ppermute | solution.py:384
  202.6 3.5 %all-to-all-start.4 = ((bf16[8,48,640]{2,1,0:T(8,128)(2,1)}), bf16[8,48,640]{2,1,0:T(8,128)(2,1)S(1)}, u32[]{:S(2)}, u32[]{:S(2)}) async-start(bf16[8,48,640]{2,1,0:T(8,128)(2,1)} %add_convert_fusion), calls=%async_computation.4 | async-start | bytes 983040 | tf_op jit(solution)/shard_map/all_to_all | solution.py:301
  206.1 4.4 %collective-permute-done.10 = bf16[2,48,2560]{2,1,0:T(8,128)(2,1)S(1)} collective-permute-done((bf16[2,48,2560]{2,1,0:T(8,128)(2,1)}, bf16[2,48,2560]{2,1,0:T(8,128)(2,1)S(1)}, u32[]{:S(2)}, u32[]{:S(2)}) %collective-permute-start.10) | collective-permute-done | bytes 491552 | tf_op jit(solution)/shard_map/ppermute | solution.py:384
  211.5 8.0 %all-to-all-done.4.parts_ref = bf16[8,48,640]{2,1,0:T(8,128)(2,1)S(1)} async-done(((bf16[8,48,640]{2,1,0:T(8,128)(2,1)}), bf16[8,48,640]{2,1,0:T(8,128)(2,1)S(1)}, u32[]{:S(2)}, u32[]{:S(2)}) %all-to-all-start.4) | async-done | bytes 491552 | tf_op jit(solution)/shard_map/all_to_all | solution.py:301
  (57 shorter events, 14.3 us)
Async XLA Ops:
  0.6 16.6 %copy-start.2 = (bf16[4,48,2560]{2,1,0:T(8,128)(2,1)S(1)}, bf16[4,48,2560]{2,1,0:T(8,128)(2,1)}, u32[]{:S(2)}) copy-start(bf16[4,48,2560]{2,1,0:T(8,128)(2,1)} %down_ref.1) | copy-start | bytes 2949124
  0.6 16.6 %copy-start.6 = (bf16[1,48,2560]{2,1,0:T(8,128)(2,1)S(1)}, bf16[1,48,2560]{2,1,0:T(8,128)(2,1)}, u32[]{:S(2)}) copy-start(bf16[1,48,2560]{2,1,0:T(8,128)(2,1)} %merged_ref.1) | copy-start | bytes 737284
  3.9 42.1 %all-to-all-start = ((bf16[16,8,2688]{2,1,0:T(8,128)(2,1)}), bf16[16,8,2688]{2,1,0:T(8,128)(2,1)S(1)}, u32[]{:S(2)}, u32[]{:S(2)}) async-start(bf16[16,8,2688]{2,1,0:T(8,128)(2,1)} %shard_map.112), calls=%async_computation | async-start | bytes 1376256 | tf_op jit(solution)/shard_map/all_to_all | solution.py:301
  18.1 22.6 %collective-permute-start = (bf16[3,48,640]{2,1,0:T(8,128)(2,1)S(1)}, bf16[3,48,640]{2,1,0:T(8,128)(2,1)S(1)}, u32[]{:S(2)}, u32[]{:S(2)}) collective-permute-start(bf16[3,48,640]{2,1,0:T(8,128)(2,1)S(1)} %get-tuple-element.36), channel_id=1, source_target_pairs={{0,32},{32,64},{64,96},{96,128},{128,160},{160,192},{192,224},{224... | collective-permute-start | bytes 552968 | tf_op jit(solution)/shard_map/ppermute | solution.py:320
  21.5 19.2 %collective-permute-start.1 = (bf16[3,48,640]{2,1,0:T(8,128)(2,1)S(1)}, bf16[3,48,640]{2,1,0:T(8,128)(2,1)S(1)}, u32[]{:S(2)}, u32[]{:S(2)}) collective-permute-start(bf16[3,48,640]{2,1,0:T(8,128)(2,1)S(1)} %get-tuple-element.37), channel_id=1, source_target_pairs={{0,224},{32,0},{64,32},{96,64},{128,96},{160,128},{192,160},{224,1... | collective-permute-start | bytes 552968 | tf_op jit(solution)/shard_map/ppermute | solution.py:320
  25.2 20.9 %collective-permute-start.2 = (bf16[3,48,640]{2,1,0:T(8,128)(2,1)S(1)}, bf16[3,48,640]{2,1,0:T(8,128)(2,1)S(1)}, u32[]{:S(2)}, u32[]{:S(2)}) collective-permute-start(bf16[3,48,640]{2,1,0:T(8,128)(2,1)S(1)} %get-tuple-element.38), channel_id=1, source_target_pairs={{0,64},{32,96},{64,128},{96,160},{128,192},{160,224},{192,0},{224,... | collective-permute-start | bytes 552968 | tf_op jit(solution)/shard_map/ppermute | solution.py:320
  40.7 10.2 %copy-start.15 = (bf16[3,48,640]{2,1,0:T(8,128)(2,1)}, bf16[3,48,640]{2,1,0:T(8,128)(2,1)S(1)}, u32[]{:S(2)}) copy-start(bf16[3,48,640]{2,1,0:T(8,128)(2,1)S(1)} %collective-permute-done.refs_1_) | copy-start | bytes 552964
  40.7 10.2 %copy-start.16 = (bf16[3,48,640]{2,1,0:T(8,128)(2,1)}, bf16[3,48,640]{2,1,0:T(8,128)(2,1)S(1)}, u32[]{:S(2)}) copy-start(bf16[3,48,640]{2,1,0:T(8,128)(2,1)S(1)} %collective-permute-done.1.refs_7_) | copy-start | bytes 552964
  46.1 4.8 %copy-start.17 = (bf16[3,48,640]{2,1,0:T(8,128)(2,1)}, bf16[3,48,640]{2,1,0:T(8,128)(2,1)S(1)}, u32[]{:S(2)}) copy-start(bf16[3,48,640]{2,1,0:T(8,128)(2,1)S(1)} %collective-permute-done.2.refs_2_) | copy-start | bytes 552964
  50.9 73.5 %all-to-all-start.1 = ((bf16[32,16,2688]{2,1,0:T(8,128)(2,1)}), bf16[32,16,2688]{2,1,0:T(8,128)(2,1)S(1)}, u32[]{:S(2)}, u32[]{:S(2)}) async-start(bf16[32,16,2688]{2,1,0:T(8,128)(2,1)} %bitcast.17), calls=%async_computation.1 | async-start | bytes 5505024 | tf_op jit(solution)/shard_map/all_to_all | solution.py:301
  59.7 1.3 copy-start.13
  59.7 1.4 copy-start.14
  61.2 63.2 %collective-permute-start.3 = (bf16[6,48,2560]{2,1,0:T(8,128)(2,1)S(1)}, bf16[6,48,2560]{2,1,0:T(8,128)(2,1)}, u32[]{:S(2)}, u32[]{:S(2)}) collective-permute-start(bf16[6,48,2560]{2,1,0:T(8,128)(2,1)S(1)} %pad_maximum_fusion), channel_id=1, source_target_pairs={{0,256},{32,288},{64,320},{96,352},{128,384},{160,416},{192,448},{... | collective-permute-start | bytes 4423688 | tf_op jit(solution)/shard_map/ppermute | solution.py:335
  63.9 16.6 %collective-permute-start.4 = (bf16[3,48,640]{2,1,0:T(8,128)(2,1)S(1)}, bf16[3,48,640]{2,1,0:T(8,128)(2,1)S(1)}, u32[]{:S(2)}, u32[]{:S(2)}) collective-permute-start(bf16[3,48,640]{2,1,0:T(8,128)(2,1)S(1)} %get-tuple-element.43), channel_id=1, source_target_pairs={{0,96},{32,128},{64,160},{96,192},{128,224},{160,0},{192,32},{224,... | collective-permute-start | bytes 552968 | tf_op jit(solution)/shard_map/ppermute | solution.py:320
  67.3 19.8 %collective-permute-start.5 = (bf16[3,48,640]{2,1,0:T(8,128)(2,1)S(1)}, bf16[3,48,640]{2,1,0:T(8,128)(2,1)S(1)}, u32[]{:S(2)}, u32[]{:S(2)}) collective-permute-start(bf16[3,48,640]{2,1,0:T(8,128)(2,1)S(1)} %get-tuple-element.44), channel_id=1, source_target_pairs={{0,128},{32,160},{64,192},{96,224},{128,0},{160,32},{192,64},{224,... | collective-permute-start | bytes 552968 | tf_op jit(solution)/shard_map/ppermute | solution.py:320
  73.7 20.5 %collective-permute-start.6 = (bf16[3,48,640]{2,1,0:T(8,128)(2,1)S(1)}, bf16[3,48,640]{2,1,0:T(8,128)(2,1)S(1)}, u32[]{:S(2)}, u32[]{:S(2)}) collective-permute-start(bf16[3,48,640]{2,1,0:T(8,128)(2,1)S(1)} %get-tuple-element.45), channel_id=1, source_target_pairs={{0,160},{32,192},{64,224},{96,0},{128,32},{160,64},{192,96},{224,1... | collective-permute-start | bytes 552968 | tf_op jit(solution)/shard_map/ppermute | solution.py:320
  77.5 24.6 %collective-permute-start.7 = (bf16[3,48,640]{2,1,0:T(8,128)(2,1)S(1)}, bf16[3,48,640]{2,1,0:T(8,128)(2,1)S(1)}, u32[]{:S(2)}, u32[]{:S(2)}) collective-permute-start(bf16[3,48,640]{2,1,0:T(8,128)(2,1)S(1)} %get-tuple-element.46), channel_id=1, source_target_pairs={{0,192},{32,224},{64,0},{96,32},{128,64},{160,96},{192,128},{224,1... | collective-permute-start | bytes 552968 | tf_op jit(solution)/shard_map/ppermute | solution.py:320
  80.5 21.7 %copy-start.18 = (bf16[3,48,640]{2,1,0:T(8,128)(2,1)}, bf16[3,48,640]{2,1,0:T(8,128)(2,1)S(1)}, u32[]{:S(2)}) copy-start(bf16[3,48,640]{2,1,0:T(8,128)(2,1)S(1)} %collective-permute-done.4.refs_3_) | copy-start | bytes 552964
  87.1 15.1 %copy-start.19 = (bf16[3,48,640]{2,1,0:T(8,128)(2,1)}, bf16[3,48,640]{2,1,0:T(8,128)(2,1)S(1)}, u32[]{:S(2)}) copy-start(bf16[3,48,640]{2,1,0:T(8,128)(2,1)S(1)} %collective-permute-done.5.refs_4_) | copy-start | bytes 552964
  94.2 8.0 %copy-start.20 = (bf16[3,48,640]{2,1,0:T(8,128)(2,1)}, bf16[3,48,640]{2,1,0:T(8,128)(2,1)S(1)}, u32[]{:S(2)}) copy-start(bf16[3,48,640]{2,1,0:T(8,128)(2,1)S(1)} %collective-permute-done.6.refs_5_) | copy-start | bytes 552964
  124.5 1.5 copy-start
  132.4 34.4 %all-to-all-start.2 = ((bf16[8,4,48,256]{3,2,1,0:T(8,128)(2,1)}), bf16[8,4,48,256]{3,2,1,0:T(8,128)(2,1)S(1)}, u32[]{:S(2)}, u32[]{:S(2)}) async-start(bf16[8,4,48,256]{3,2,1,0:T(8,128)(2,1)} %get-tuple-element.50), calls=%async_computation.2 | async-start | bytes 1572864 | tf_op jit(solution)/shard_map/all_to_all | solution.py:301
  139.9 26.9 %collective-permute-start.8 = (bf16[8,2,48,640]{3,2,1,0:T(8,128)(2,1)}, bf16[8,2,48,640]{3,2,1,0:T(8,128)(2,1)}, u32[]{:S(2)}, u32[]{:S(2)}) collective-permute-start(bf16[8,2,48,640]{3,2,1,0:T(8,128)(2,1)} %shard_map.116), channel_id=1, source_target_pairs={{0,256},{32,288},{64,320},{96,352},{128,384},{160,416},{192,448},{... | collective-permute-start | bytes 2949128 | tf_op jit(solution)/shard_map/ppermute | solution.py:341
  167.7 27.4 %copy-start.1 = (bf16[32,16,2688]{2,1,0:T(8,128)(2,1)S(1)}, bf16[32,16,2688]{2,1,0:T(8,128)(2,1)}, u32[]{:S(2)}) copy-start(bf16[32,16,2688]{2,1,0:T(8,128)(2,1)} %copy-done) | copy-start | bytes 8257540
  172.4 22.8 %copy-start.7 = (f32[96,512]{1,0:T(8,128)S(1)}, f32[96,512]{1,0:T(8,128)}, u32[]{:S(2)}) copy-start(f32[96,512]{1,0:T(8,128)} %get-tuple-element.61.refs_1_) | copy-start | bytes 589828
  172.4 22.8 %copy-start.8 = (f32[96,512]{1,0:T(8,128)S(1)}, f32[96,512]{1,0:T(8,128)}, u32[]{:S(2)}) copy-start(f32[96,512]{1,0:T(8,128)} %get-tuple-element.62.refs_2_) | copy-start | bytes 589828
  172.4 15.5 %collective-permute-start.9 = (bf16[8,48,640]{2,1,0:T(8,128)(2,1)}, bf16[8,48,640]{2,1,0:T(8,128)(2,1)}, u32[]{:S(2)}, u32[]{:S(2)}) collective-permute-start(bf16[8,48,640]{2,1,0:T(8,128)(2,1)} %get-tuple-element.66), channel_id=1, source_target_pairs={{0,256},{32,288},{64,320},{96,352},{128,384},{160,416},{192,448},{... | collective-permute-start | bytes 1474568 | tf_op jit(solution)/shard_map/ppermute | solution.py:372
  175.5 19.6 %all-to-all-start.3 = ((bf16[8,96,256]{2,1,0:T(8,128)(2,1)}), bf16[8,96,256]{2,1,0:T(8,128)(2,1)S(1)}, u32[]{:S(2)}, u32[]{:S(2)}) async-start(bf16[8,96,256]{2,1,0:T(8,128)(2,1)} %get-tuple-element.60), calls=%async_computation.3 | async-start | bytes 786432 | tf_op jit(solution)/shard_map/all_to_all | solution.py:301
  196.9 1.0 copy-start.3
  197.9 12.6 %copy-start.4 = (f32[2,48,2560]{2,1,0:T(8,128)S(1)}, f32[2,48,2560]{2,1,0:T(8,128)}, u32[]{:S(2)}) copy-start(f32[2,48,2560]{2,1,0:T(8,128)} %copy-done.3) | copy-start | bytes 2949124
  197.9 12.6 %collective-permute-start.10 = (bf16[2,48,2560]{2,1,0:T(8,128)(2,1)}, bf16[2,48,2560]{2,1,0:T(8,128)(2,1)S(1)}, u32[]{:S(2)}, u32[]{:S(2)}) collective-permute-start(bf16[2,48,2560]{2,1,0:T(8,128)(2,1)} %get-tuple-element.67), channel_id=1, source_target_pairs={{0,256},{32,288},{64,320},{96,352},{128,384},{160,416},{192,448},{... | collective-permute-start | bytes 1474568 | tf_op jit(solution)/shard_map/ppermute | solution.py:384
  202.6 17.0 %all-to-all-start.4 = ((bf16[8,48,640]{2,1,0:T(8,128)(2,1)}), bf16[8,48,640]{2,1,0:T(8,128)(2,1)S(1)}, u32[]{:S(2)}, u32[]{:S(2)}) async-start(bf16[8,48,640]{2,1,0:T(8,128)(2,1)} %add_convert_fusion), calls=%async_computation.4 | async-start | bytes 983040 | tf_op jit(solution)/shard_map/all_to_all | solution.py:301
  (6 other events, 4.6 us)

commit v9 on v8

--- a/solution.py
+++ b/solution.py
@@ -7,7 +7,7 @@
 
 HALVES = 2
 PAIR = 2
-EARLY = (1, 7, 2)
+EARLY = (1,)
 RING = 8
 SIDE = 128
 BF16 = jnp.bfloat16
@@ -129,7 +129,8 @@
     t_up_hbm,
     m_gate_hbm,
     m_up_hbm,
-    come_hbm,
+    t_come_hbm,
+    m_come_hbm,
     out_ref,
     silu_ref,
     slope_ref,
@@ -156,13 +157,13 @@
 
     first = start_copies([(rows_hbm, row_buf)], sems, 4 * PAIR + 4)
     first += weights(
-        PAIR, m_gate_hbm.at[0], come_hbm.at[2 * PAIR], m_up_hbm.at[0], come_hbm.at[2 * PAIR + 1]
+        PAIR, m_gate_hbm.at[0], m_come_hbm.at[0], m_up_hbm.at[0], m_come_hbm.at[1]
     )
     later = []
     for m in range(PAIR):
         own = PAIR * half + m
         later.append(
-            weights(m, t_gate_hbm.at[own], come_hbm.at[m], t_up_hbm.at[own], come_hbm.at[PAIR + m])
+            weights(m, t_gate_hbm.at[own], t_come_hbm.at[m], t_up_hbm.at[own], t_come_hbm.at[PAIR + m])
         )
     move = by_teacher(count, capacity, 0)
     wait_copies(first)
@@ -309,6 +310,7 @@
         pack_kernel,
         (jax.ShapeDtypeStruct((n_dp, capacity, wide), BF16),),
         (teacher_ids[0].T, tokens[0], route_weight[0]),
+        mib=60,
     )
     group = exchange(packets, "dp").reshape(n_dp * capacity, wide)
 
@@ -319,7 +321,8 @@
     )
     down = [down[k] if k == 0 else lax.ppermute(down[k], "dp", turns[k]) for k in range(RING)]
     early = [down[k] for k in EARLY]
-    group, early = lax.optimization_barrier((group, early))
+    m_come = lax.ppermute(jnp.concatenate([merged_gate, merged_up], axis=0), "dp", swap)
+    group, early, m_come = lax.optimization_barrier((group, early, m_come))
     for k, array in zip(EARLY, early):
         down[k] = array
 
@@ -331,13 +334,12 @@
     )
     slots = exchange(slots.reshape(experts, PAIR * capacity, wide), "expert").reshape(rows, wide)
 
-    sent = [halves(teacher_gate, 1 - half), halves(teacher_up, 1 - half), merged_gate, merged_up]
-    come = lax.ppermute(jnp.concatenate(sent, axis=0), "dp", swap)
-    slots, come, down = lax.optimization_barrier((slots, come, down))
-
+    sent = [halves(teacher_gate, 1 - half), halves(teacher_up, 1 - half)]
+    t_come = lax.ppermute(jnp.concatenate(sent, axis=0), "dp", swap)
     (passed,) = call(
         pass_kernel, (jax.ShapeDtypeStruct((RING, PAIR, block, quarter), BF16),), tuple(down), mib=60
     )
+    slots, t_come, passed = lax.optimization_barrier((slots, t_come, passed))
     came = lax.ppermute(passed, "dp", swap)
 
     hidden, silu, slope, weight = call(
@@ -348,8 +350,8 @@
             jax.ShapeDtypeStruct((2 * block, rows), F32),
             jax.ShapeDtypeStruct((rows, SIDE), BF16),
         ),
-        (slots, teacher_gate, teacher_up, merged_gate, merged_up, come),
-        far=range(6),
+        (slots, teacher_gate, teacher_up, merged_gate, merged_up, t_come, m_come),
+        far=range(7),
         scratch=[
             pltpu.VMEM((rows, wide), BF16),
             pltpu.VMEM((PAIR + 1, 4 * block, features), BF16),
@@ -379,9 +381,8 @@
         ),
         (parts, silu, slope, slots),
     )
-    other, down_grad = lax.optimization_barrier((other, down_grad))
+    other = lax.ppermute(other, "dp", swap)
     down_grad = exchange(down_grad, "dp", rings)
-    other = lax.ppermute(other, "dp", swap)
     (grad_down,) = call(
         down_sum_kernel, (jax.ShapeDtypeStruct((block, features), F32),), (down_grad,)
     )

time: 222 us -> 211 us (0.950)
  waiting for transfers between devices: 108 us -> 88.6 us
  starting transfers between devices: 77.7 us -> 83.8 us
    ppermute x1 -> x2, waiting for transfers between devices: 21.6 us -> 0.4 us  [the longest x1 0.39 us: body(): lax.ppermute(jnp.concatenate([merged_gate, merged_up], axis=0), 'dp', swap)]
    all_to_all x5, waiting for transfers between devices: 13.2 us -> 26.8 us  [exchange(): lax.all_to_all(array, axis_name, split_axis=0, concat_axis=0, tiled=True,...]
    ppermute x7, waiting for transfers between devices: 39.5 us -> 33.2 us  [body(): lax.ppermute(down[k], 'dp', turns[k])]
    ppermute x1, waiting for transfers between devices: 5.5 us -> 0.01 us  [body(): other_down = lax.ppermute(other_down, 'dp', swap)]
    ppermute x7, starting transfers between devices: 26.6 us -> 29.6 us  [body(): lax.ppermute(down[k], 'dp', turns[k])]
    ppermute x1 -> x2, starting transfers between devices: 2.62 us -> 4.87 us  [the longest x1 2.86 us: body(): t_come = lax.ppermute(jnp.concatenate(sent, axis=0), 'dp', swap)]
  transfers between devices with their start and end apart: 16 -> 17, of which waited for: 11 -> 12; matrix products, arithmetic and copies ran while one was open for 2% -> 3% of each run, Pallas kernels for 1% -> 2%
where the time goes in v9:
time: 211 us; the launch traced here: 209 us
  waiting for transfers between devices  88.6 us (42%)
  starting transfers between devices  83.8 us (40%)
  Pallas kernels  21.9 us (10%)
  local copies, waits for them, and re-layouts  8.76 us (4%)
  other arithmetic  5.13 us (2%)
    all_to_all x5, starting transfers between devices, exchange(): lax.all_to_all(array, axis_name, split_axis=0, concat_axis=0, tiled=True,...  38.4 us
    ppermute x7, waiting for transfers between devices, body(): lax.ppermute(down[k], 'dp', turns[k])  33.2 us
    ppermute x7, starting transfers between devices, body(): lax.ppermute(down[k], 'dp', turns[k])  29.6 us
    all_to_all x5, waiting for transfers between devices, exchange(): lax.all_to_all(array, axis_name, split_axis=0, concat_axis=0, tiled=True,...  26.8 us
    ppermute x1, waiting for transfers between devices, body(): came = lax.ppermute(passed, 'dp', swap)  23.5 us
    pallas_call x8, Pallas kernels, call(): pl.pallas_call(kernel, out_shape=outs, in_specs=[space(i, far) for i in r...  21.9 us
    unnamed x44, local copies, waits for them, and re-layouts  6.09 us
    ppermute x1, waiting for transfers between devices, body(): other = lax.ppermute(other, 'dp', swap)  4.69 us
  transfers between devices with their start and end apart: 17, of which 12 were waited for; matrix products, arithmetic and copies ran while one was open for 3% of the time, Pallas kernels for 2%

profile of v9, /device:TPU:6, one launch (start us, length us, event | category | flops | bytes accessed | tf_op | source)
XLA Modules:
  0.0 209.1 jit_solution(2098490975317756929)
XLA Ops:
  3.8 13.3 %all-to-all-start = ((bf16[16,8,2688]{2,1,0:T(8,128)(2,1)}), bf16[16,8,2688]{2,1,0:T(8,128)(2,1)S(1)}, u32[]{:S(2)}, u32[]{:S(2)}) async-start(bf16[16,8,2688]{2,1,0:T(8,128)(2,1)} %shard_map.112), calls=%async_computation | async-start | bytes 1376256 | tf_op jit(solution)/shard_map/all_to_all | solution.py:302
  18.3 2.0 collective-permute-start.1
  22.5 3.8 %collective-permute-start = (bf16[3,48,640]{2,1,0:T(8,128)(2,1)S(1)}, bf16[3,48,640]{2,1,0:T(8,128)(2,1)S(1)}, u32[]{:S(2)}, u32[]{:S(2)}) collective-permute-start(bf16[3,48,640]{2,1,0:T(8,128)(2,1)S(1)} %get-tuple-element.26), channel_id=1, source_target_pairs={{0,32},{32,64},{64,96},{96,128},{128,160},{160,192},{192,224},{224... | collective-permute-start | bytes 552968 | tf_op jit(solution)/shard_map/ppermute | solution.py:322
  26.3 12.5 %collective-permute-done.refs_1_ = bf16[3,48,640]{2,1,0:T(8,128)(2,1)S(1)} collective-permute-done((bf16[3,48,640]{2,1,0:T(8,128)(2,1)S(1)}, bf16[3,48,640]{2,1,0:T(8,128)(2,1)S(1)}, u32[]{:S(2)}, u32[]{:S(2)}) %collective-permute-start) | collective-permute-done | bytes 184352 | tf_op jit(solution)/shard_map/ppermute | solution.py:322
  40.1 3.9 %shard_map.114 = bf16[512,2688]{1,0:T(8,128)(2,1)} custom-call(bf16[128,2688]{1,0:T(8,128)(2,1)} %bitcast.15), custom_call_target="tpu_custom_call" | custom-call | bytes 688128 | tf_op jit(solution)/shard_map/pallas_call | solution.py:33
  44.0 8.7 %all-to-all-start.1 = ((bf16[32,16,2688]{2,1,0:T(8,128)(2,1)}), bf16[32,16,2688]{2,1,0:T(8,128)(2,1)S(1)}, u32[]{:S(2)}, u32[]{:S(2)}) async-start(bf16[32,16,2688]{2,1,0:T(8,128)(2,1)} %bitcast.14), calls=%async_computation.1 | async-start | bytes 5505024 | tf_op jit(solution)/shard_map/all_to_all | solution.py:302
  55.2 2.9 %collective-permute-start.2 = (bf16[4,48,2560]{2,1,0:T(8,128)(2,1)}, bf16[4,48,2560]{2,1,0:T(8,128)(2,1)}, u32[]{:S(2)}, u32[]{:S(2)}) collective-permute-start(bf16[4,48,2560]{2,1,0:T(8,128)(2,1)} %pad_maximum_fusion), channel_id=1, source_target_pairs={{0,256},{32,288},{64,320},{96,352},{128,384},{160,416},{192,448},{... | collective-permute-start | bytes 2949128 | tf_op jit(solution)/shard_map/ppermute | solution.py:338
  58.0 4.7 %collective-permute-start.3 = (bf16[3,48,640]{2,1,0:T(8,128)(2,1)S(1)}, bf16[3,48,640]{2,1,0:T(8,128)(2,1)S(1)}, u32[]{:S(2)}, u32[]{:S(2)}) collective-permute-start(bf16[3,48,640]{2,1,0:T(8,128)(2,1)S(1)} %copy-done.12), channel_id=1, source_target_pairs={{0,64},{32,96},{64,128},{96,160},{128,192},{160,224},{192,0},{224,... | collective-permute-start | bytes 552968 | tf_op jit(solution)/shard_map/ppermute | solution.py:322
  62.8 5.5 %collective-permute-start.4 = (bf16[3,48,640]{2,1,0:T(8,128)(2,1)S(1)}, bf16[3,48,640]{2,1,0:T(8,128)(2,1)S(1)}, u32[]{:S(2)}, u32[]{:S(2)}) collective-permute-start(bf16[3,48,640]{2,1,0:T(8,128)(2,1)S(1)} %copy-done.10), channel_id=1, source_target_pairs={{0,96},{32,128},{64,160},{96,192},{128,224},{160,0},{192,32},{224,... | collective-permute-start | bytes 552968 | tf_op jit(solution)/shard_map/ppermute | solution.py:322
  68.3 3.4 %collective-permute-start.5 = (bf16[3,48,640]{2,1,0:T(8,128)(2,1)S(1)}, bf16[3,48,640]{2,1,0:T(8,128)(2,1)S(1)}, u32[]{:S(2)}, u32[]{:S(2)}) collective-permute-start(bf16[3,48,640]{2,1,0:T(8,128)(2,1)S(1)} %get-tuple-element.32), channel_id=1, source_target_pairs={{0,128},{32,160},{64,192},{96,224},{128,0},{160,32},{192,64},{224,... | collective-permute-start | bytes 552968 | tf_op jit(solution)/shard_map/ppermute | solution.py:322
  71.7 5.2 %collective-permute-start.6 = (bf16[3,48,640]{2,1,0:T(8,128)(2,1)S(1)}, bf16[3,48,640]{2,1,0:T(8,128)(2,1)S(1)}, u32[]{:S(2)}, u32[]{:S(2)}) collective-permute-start(bf16[3,48,640]{2,1,0:T(8,128)(2,1)S(1)} %get-tuple-element.33), channel_id=1, source_target_pairs={{0,160},{32,192},{64,224},{96,0},{128,32},{160,64},{192,96},{224,1... | collective-permute-start | bytes 552968 | tf_op jit(solution)/shard_map/ppermute | solution.py:322
  77.0 5.0 %collective-permute-start.7 = (bf16[3,48,640]{2,1,0:T(8,128)(2,1)S(1)}, bf16[3,48,640]{2,1,0:T(8,128)(2,1)S(1)}, u32[]{:S(2)}, u32[]{:S(2)}) collective-permute-start(bf16[3,48,640]{2,1,0:T(8,128)(2,1)S(1)} %get-tuple-element.34), channel_id=1, source_target_pairs={{0,192},{32,224},{64,0},{96,32},{128,64},{160,96},{192,128},{224,1... | collective-permute-start | bytes 552968 | tf_op jit(solution)/shard_map/ppermute | solution.py:322
  82.0 7.0 %collective-permute-done.4.refs_3_ = bf16[3,48,640]{2,1,0:T(8,128)(2,1)S(1)} collective-permute-done((bf16[3,48,640]{2,1,0:T(8,128)(2,1)S(1)}, bf16[3,48,640]{2,1,0:T(8,128)(2,1)S(1)}, u32[]{:S(2)}, u32[]{:S(2)}) %collective-permute-start.4) | collective-permute-done | bytes 184352 | tf_op jit(solution)/shard_map/ppermute | solution.py:322
  89.0 1.9 collective-permute-start.8
  91.9 5.0 %collective-permute-done.6.refs_5_ = bf16[3,48,640]{2,1,0:T(8,128)(2,1)S(1)} collective-permute-done((bf16[3,48,640]{2,1,0:T(8,128)(2,1)S(1)}, bf16[3,48,640]{2,1,0:T(8,128)(2,1)S(1)}, u32[]{:S(2)}, u32[]{:S(2)}) %collective-permute-start.6) | collective-permute-done | bytes 184352 | tf_op jit(solution)/shard_map/ppermute | solution.py:322
  96.8 5.6 %collective-permute-done.7.refs_6_ = bf16[3,48,640]{2,1,0:T(8,128)(2,1)S(1)} collective-permute-done((bf16[3,48,640]{2,1,0:T(8,128)(2,1)S(1)}, bf16[3,48,640]{2,1,0:T(8,128)(2,1)S(1)}, u32[]{:S(2)}, u32[]{:S(2)}) %collective-permute-start.7) | collective-permute-done | bytes 184352 | tf_op jit(solution)/shard_map/ppermute | solution.py:322
  102.4 2.1 %collective-permute-done.8.refs_7_ = bf16[3,48,640]{2,1,0:T(8,128)(2,1)S(1)} collective-permute-done((bf16[3,48,640]{2,1,0:T(8,128)(2,1)S(1)}, bf16[3,48,640]{2,1,0:T(8,128)(2,1)S(1)}, u32[]{:S(2)}, u32[]{:S(2)}) %collective-permute-start.8) | collective-permute-done | bytes 184352 | tf_op jit(solution)/shard_map/ppermute | solution.py:322
  105.2 2.5 %shard_map.115 = bf16[8,2,48,640]{3,2,1,0:T(8,128)(2,1)} custom-call(bf16[3,48,640]{2,1,0:T(8,128)(2,1)} %copy-done.5, bf16[3,48,640]{2,1,0:T(8,128)(2,1)} %copy-done.14, bf16[3,48,640]{2,1,0:T(8,128)(2,1)} %copy-done.15, bf16[3,48,640]{2,1,0:T(8,128)(2,1)} %copy-done.16, bf16[3,48,640]{2,1,0:T(8,128)(2,1)} %copy-done.17, bf16[3,48,640]{2,1,0:T(8,128)(2,1)} %copy-done.18, ...), custom_call_target="tpu_custom_call" | custom-call | bytes 1474560 | tf_op jit(solution)/shard_map/pallas_call | solution.py:33
  107.7 8.8 %all-to-all-done.1 = bf16[32,16,2688]{2,1,0:T(8,128)(2,1)S(1)} async-done(((bf16[32,16,2688]{2,1,0:T(8,128)(2,1)}), bf16[32,16,2688]{2,1,0:T(8,128)(2,1)S(1)}, u32[]{:S(2)}, u32[]{:S(2)}) %all-to-all-start.1) | async-done | bytes 2752544 | tf_op jit(solution)/shard_map/all_to_all | solution.py:302
  118.1 6.3 %shard_map.116 = (bf16[8,4,48,256]{3,2,1,0:T(8,128)(2,1)}, f32[96,512]{1,0:T(8,128)}, f32[96,512]{1,0:T(8,128)}, bf16[512,128]{1,0:T(8,128)(2,1)}) custom-call(bf16[512,2688]{1,0:T(8,128)(2,1)} %bitcast.12, bf16[4,48,2560]{2,1,0:T(8,128)(2,1)} %refs_1_.1, bf16[4,48,2560]{2,1,0:T(8,128)(2,1)} %refs_2_.1, bf16[1,48,2560]{2,1,0:T(8,128)(2,1)} %refs_3_.1, ...), custom_call_target="tpu_custom_call" | custom-call | bytes 6684672 | tf_op jit(solution)/shard_map/pallas_call | solution.py:33
  124.4 6.0 %all-to-all-start.2 = ((bf16[8,4,48,256]{3,2,1,0:T(8,128)(2,1)}), bf16[8,4,48,256]{3,2,1,0:T(8,128)(2,1)}, u32[]{:S(2)}, u32[]{:S(2)}) async-start(bf16[8,4,48,256]{3,2,1,0:T(8,128)(2,1)} %get-tuple-element.39), calls=%async_computation.2 | async-start | bytes 1572864 | tf_op jit(solution)/shard_map/all_to_all | solution.py:302
  130.4 3.6 %collective-permute-start.9 = (bf16[8,2,48,640]{3,2,1,0:T(8,128)(2,1)}, bf16[8,2,48,640]{3,2,1,0:T(8,128)(2,1)}, u32[]{:S(2)}, u32[]{:S(2)}) collective-permute-start(bf16[8,2,48,640]{3,2,1,0:T(8,128)(2,1)} %shard_map.115), channel_id=1, source_target_pairs={{0,256},{32,288},{64,320},{96,352},{128,384},{160,416},{192,448},{... | collective-permute-start | bytes 2949128 | tf_op jit(solution)/shard_map/ppermute | solution.py:343
  134.0 23.5 %collective-permute-done.9.came_ref = bf16[8,2,48,640]{3,2,1,0:T(8,128)(2,1)} collective-permute-done((bf16[8,2,48,640]{3,2,1,0:T(8,128)(2,1)}, bf16[8,2,48,640]{3,2,1,0:T(8,128)(2,1)}, u32[]{:S(2)}, u32[]{:S(2)}) %collective-permute-start.9) | collective-permute-done | bytes 983072 | tf_op jit(solution)/shard_map/ppermute | solution.py:343
  157.6 4.5 %shard_map.117 = (bf16[8,96,256]{2,1,0:T(8,128)(2,1)}, bf16[8,48,640]{2,1,0:T(8,128)(2,1)}, bf16[8,48,640]{2,1,0:T(8,128)(2,1)}) custom-call(bf16[8,4,48,256]{3,2,1,0:T(8,128)(2,1)} %all-to-all-done.2.hidden_ref, bf16[512,128]{1,0:T(8,128)(2,1)} %get-tuple-element.40.weight_ref, bf16[8,2,48,640]{3,2,1,0:T(8,128)(2,1)} %collective-permute-done.9.came_ref, ...), custom_call_target="tpu_custom_call" | custom-call | bytes 3375104 | tf_op jit(solution)/shard_map/pallas_call | solution.py:33
  162.1 6.9 %all-to-all-start.3 = ((bf16[8,96,256]{2,1,0:T(8,128)(2,1)}), bf16[8,96,256]{2,1,0:T(8,128)(2,1)S(1)}, u32[]{:S(2)}, u32[]{:S(2)}) async-start(bf16[8,96,256]{2,1,0:T(8,128)(2,1)} %get-tuple-element.42), calls=%async_computation.3 | async-start | bytes 786432 | tf_op jit(solution)/shard_map/all_to_all | solution.py:302
  169.0 3.6 %collective-permute-start.11 = (bf16[8,48,640]{2,1,0:T(8,128)(2,1)}, bf16[8,48,640]{2,1,0:T(8,128)(2,1)}, u32[]{:S(2)}, u32[]{:S(2)}) collective-permute-start(bf16[8,48,640]{2,1,0:T(8,128)(2,1)} %get-tuple-element.48), channel_id=1, source_target_pairs={{0,256},{32,288},{64,320},{96,352},{128,384},{160,416},{192,448},{... | collective-permute-start | bytes 1474568 | tf_op jit(solution)/shard_map/ppermute | solution.py:374
  172.6 9.8 %all-to-all-done.3.refs_0_ = bf16[8,96,256]{2,1,0:T(8,128)(2,1)S(1)} async-done(((bf16[8,96,256]{2,1,0:T(8,128)(2,1)}), bf16[8,96,256]{2,1,0:T(8,128)(2,1)S(1)}, u32[]{:S(2)}, u32[]{:S(2)}) %all-to-all-start.3) | async-done | bytes 393248 | tf_op jit(solution)/shard_map/all_to_all | solution.py:302
  185.2 3.7 %collective-permute-start.10 = (bf16[2,48,2560]{2,1,0:T(8,128)(2,1)}, bf16[2,48,2560]{2,1,0:T(8,128)(2,1)S(1)}, u32[]{:S(2)}, u32[]{:S(2)}) collective-permute-start(bf16[2,48,2560]{2,1,0:T(8,128)(2,1)} %get-tuple-element.46), channel_id=1, source_target_pairs={{0,256},{32,288},{64,320},{96,352},{128,384},{160,416},{192,448},{... | collective-permute-start | bytes 1474568 | tf_op jit(solution)/shard_map/ppermute | solution.py:384
  189.0 1.9 add_convert_fusion
  190.9 3.5 %all-to-all-start.4 = ((bf16[8,48,640]{2,1,0:T(8,128)(2,1)}), bf16[8,48,640]{2,1,0:T(8,128)(2,1)S(1)}, u32[]{:S(2)}, u32[]{:S(2)}) async-start(bf16[8,48,640]{2,1,0:T(8,128)(2,1)} %add_convert_fusion), calls=%async_computation.4 | async-start | bytes 983040 | tf_op jit(solution)/shard_map/all_to_all | solution.py:302
  194.4 4.7 %collective-permute-done.10 = bf16[2,48,2560]{2,1,0:T(8,128)(2,1)S(1)} collective-permute-done((bf16[2,48,2560]{2,1,0:T(8,128)(2,1)}, bf16[2,48,2560]{2,1,0:T(8,128)(2,1)S(1)}, u32[]{:S(2)}, u32[]{:S(2)}) %collective-permute-start.10) | collective-permute-done | bytes 491552 | tf_op jit(solution)/shard_map/ppermute | solution.py:384
  200.1 8.2 %all-to-all-done.4.parts_ref = bf16[8,48,640]{2,1,0:T(8,128)(2,1)S(1)} async-done(((bf16[8,48,640]{2,1,0:T(8,128)(2,1)}), bf16[8,48,640]{2,1,0:T(8,128)(2,1)S(1)}, u32[]{:S(2)}, u32[]{:S(2)}) %all-to-all-start.4) | async-done | bytes 491552 | tf_op jit(solution)/shard_map/all_to_all | solution.py:302
  (60 shorter events, 17.9 us)
Async XLA Ops:
  0.6 19.6 %copy-start.2 = (bf16[4,48,2560]{2,1,0:T(8,128)(2,1)S(1)}, bf16[4,48,2560]{2,1,0:T(8,128)(2,1)}, u32[]{:S(2)}) copy-start(bf16[4,48,2560]{2,1,0:T(8,128)(2,1)} %down_ref.1) | copy-start | bytes 2949124
  0.6 19.6 %copy-start.6 = (bf16[1,48,2560]{2,1,0:T(8,128)(2,1)S(1)}, bf16[1,48,2560]{2,1,0:T(8,128)(2,1)}, u32[]{:S(2)}) copy-start(bf16[1,48,2560]{2,1,0:T(8,128)(2,1)} %merged_ref.1) | copy-start | bytes 737284
  3.8 35.4 %all-to-all-start = ((bf16[16,8,2688]{2,1,0:T(8,128)(2,1)}), bf16[16,8,2688]{2,1,0:T(8,128)(2,1)S(1)}, u32[]{:S(2)}, u32[]{:S(2)}) async-start(bf16[16,8,2688]{2,1,0:T(8,128)(2,1)} %shard_map.112), calls=%async_computation | async-start | bytes 1376256 | tf_op jit(solution)/shard_map/all_to_all | solution.py:302
  18.3 21.0 %collective-permute-start.1 = (bf16[2,48,2560]{2,1,0:T(8,128)(2,1)S(1)}, bf16[2,48,2560]{2,1,0:T(8,128)(2,1)}, u32[]{:S(2)}, u32[]{:S(2)}) collective-permute-start(bf16[2,48,2560]{2,1,0:T(8,128)(2,1)S(1)} %pad_maximum_fusion.1), channel_id=1, source_target_pairs={{0,256},{32,288},{64,320},{96,352},{128,384},{160,416},{192,448},{... | collective-permute-start | bytes 1474568 | tf_op jit(solution)/shard_map/ppermute | solution.py:324
  22.5 16.4 %collective-permute-start = (bf16[3,48,640]{2,1,0:T(8,128)(2,1)S(1)}, bf16[3,48,640]{2,1,0:T(8,128)(2,1)S(1)}, u32[]{:S(2)}, u32[]{:S(2)}) collective-permute-start(bf16[3,48,640]{2,1,0:T(8,128)(2,1)S(1)} %get-tuple-element.26), channel_id=1, source_target_pairs={{0,32},{32,64},{64,96},{96,128},{128,160},{160,192},{192,224},{224... | collective-permute-start | bytes 552968 | tf_op jit(solution)/shard_map/ppermute | solution.py:322
  38.8 5.2 %copy-start.14 = (bf16[3,48,640]{2,1,0:T(8,128)(2,1)}, bf16[3,48,640]{2,1,0:T(8,128)(2,1)S(1)}, u32[]{:S(2)}) copy-start(bf16[3,48,640]{2,1,0:T(8,128)(2,1)S(1)} %collective-permute-done.refs_1_) | copy-start | bytes 552964
  44.0 72.5 %all-to-all-start.1 = ((bf16[32,16,2688]{2,1,0:T(8,128)(2,1)}), bf16[32,16,2688]{2,1,0:T(8,128)(2,1)S(1)}, u32[]{:S(2)}, u32[]{:S(2)}) async-start(bf16[32,16,2688]{2,1,0:T(8,128)(2,1)} %bitcast.14), calls=%async_computation.1 | async-start | bytes 5505024 | tf_op jit(solution)/shard_map/all_to_all | solution.py:302
  52.8 5.3 %copy-start.12 = (bf16[3,48,640]{2,1,0:T(8,128)(2,1)S(1)}, bf16[3,48,640]{2,1,0:T(8,128)(2,1)}, u32[]{:S(2)}) copy-start(bf16[3,48,640]{2,1,0:T(8,128)(2,1)} %copy-done.11) | copy-start | bytes 552964
  52.8 10.0 %copy-start.10 = (bf16[3,48,640]{2,1,0:T(8,128)(2,1)S(1)}, bf16[3,48,640]{2,1,0:T(8,128)(2,1)}, u32[]{:S(2)}) copy-start(bf16[3,48,640]{2,1,0:T(8,128)(2,1)} %copy-done.9) | copy-start | bytes 552964
  55.2 52.5 %collective-permute-start.2 = (bf16[4,48,2560]{2,1,0:T(8,128)(2,1)}, bf16[4,48,2560]{2,1,0:T(8,128)(2,1)}, u32[]{:S(2)}, u32[]{:S(2)}) collective-permute-start(bf16[4,48,2560]{2,1,0:T(8,128)(2,1)} %pad_maximum_fusion), channel_id=1, source_target_pairs={{0,256},{32,288},{64,320},{96,352},{128,384},{160,416},{192,448},{... | collective-permute-start | bytes 2949128 | tf_op jit(solution)/shard_map/ppermute | solution.py:338
  58.0 18.9 %collective-permute-start.3 = (bf16[3,48,640]{2,1,0:T(8,128)(2,1)S(1)}, bf16[3,48,640]{2,1,0:T(8,128)(2,1)S(1)}, u32[]{:S(2)}, u32[]{:S(2)}) collective-permute-start(bf16[3,48,640]{2,1,0:T(8,128)(2,1)S(1)} %copy-done.12), channel_id=1, source_target_pairs={{0,64},{32,96},{64,128},{96,160},{128,192},{160,224},{192,0},{224,... | collective-permute-start | bytes 552968 | tf_op jit(solution)/shard_map/ppermute | solution.py:322
  62.8 26.2 %collective-permute-start.4 = (bf16[3,48,640]{2,1,0:T(8,128)(2,1)S(1)}, bf16[3,48,640]{2,1,0:T(8,128)(2,1)S(1)}, u32[]{:S(2)}, u32[]{:S(2)}) collective-permute-start(bf16[3,48,640]{2,1,0:T(8,128)(2,1)S(1)} %copy-done.10), channel_id=1, source_target_pairs={{0,96},{32,128},{64,160},{96,192},{128,224},{160,0},{192,32},{224,... | collective-permute-start | bytes 552968 | tf_op jit(solution)/shard_map/ppermute | solution.py:322
  68.3 23.6 %collective-permute-start.5 = (bf16[3,48,640]{2,1,0:T(8,128)(2,1)S(1)}, bf16[3,48,640]{2,1,0:T(8,128)(2,1)S(1)}, u32[]{:S(2)}, u32[]{:S(2)}) collective-permute-start(bf16[3,48,640]{2,1,0:T(8,128)(2,1)S(1)} %get-tuple-element.32), channel_id=1, source_target_pairs={{0,128},{32,160},{64,192},{96,224},{128,0},{160,32},{192,64},{224,... | collective-permute-start | bytes 552968 | tf_op jit(solution)/shard_map/ppermute | solution.py:322
  71.7 25.1 %collective-permute-start.6 = (bf16[3,48,640]{2,1,0:T(8,128)(2,1)S(1)}, bf16[3,48,640]{2,1,0:T(8,128)(2,1)S(1)}, u32[]{:S(2)}, u32[]{:S(2)}) collective-permute-start(bf16[3,48,640]{2,1,0:T(8,128)(2,1)S(1)} %get-tuple-element.33), channel_id=1, source_target_pairs={{0,160},{32,192},{64,224},{96,0},{128,32},{160,64},{192,96},{224,1... | collective-permute-start | bytes 552968 | tf_op jit(solution)/shard_map/ppermute | solution.py:322
  76.9 28.3 %copy-start.15 = (bf16[3,48,640]{2,1,0:T(8,128)(2,1)}, bf16[3,48,640]{2,1,0:T(8,128)(2,1)S(1)}, u32[]{:S(2)}) copy-start(bf16[3,48,640]{2,1,0:T(8,128)(2,1)S(1)} %collective-permute-done.3.refs_2_) | copy-start | bytes 552964
  77.0 25.5 %collective-permute-start.7 = (bf16[3,48,640]{2,1,0:T(8,128)(2,1)S(1)}, bf16[3,48,640]{2,1,0:T(8,128)(2,1)S(1)}, u32[]{:S(2)}, u32[]{:S(2)}) collective-permute-start(bf16[3,48,640]{2,1,0:T(8,128)(2,1)S(1)} %get-tuple-element.34), channel_id=1, source_target_pairs={{0,192},{32,224},{64,0},{96,32},{128,64},{160,96},{192,128},{224,1... | collective-permute-start | bytes 552968 | tf_op jit(solution)/shard_map/ppermute | solution.py:322
  89.0 16.2 %copy-start.16 = (bf16[3,48,640]{2,1,0:T(8,128)(2,1)}, bf16[3,48,640]{2,1,0:T(8,128)(2,1)S(1)}, u32[]{:S(2)}) copy-start(bf16[3,48,640]{2,1,0:T(8,128)(2,1)S(1)} %collective-permute-done.4.refs_3_) | copy-start | bytes 552964
  89.0 15.5 %collective-permute-start.8 = (bf16[3,48,640]{2,1,0:T(8,128)(2,1)S(1)}, bf16[3,48,640]{2,1,0:T(8,128)(2,1)S(1)}, u32[]{:S(2)}, u32[]{:S(2)}) collective-permute-start(bf16[3,48,640]{2,1,0:T(8,128)(2,1)S(1)} %get-tuple-element.35), channel_id=1, source_target_pairs={{0,224},{32,0},{64,32},{96,64},{128,96},{160,128},{192,160},{224,1... | collective-permute-start | bytes 552968 | tf_op jit(solution)/shard_map/ppermute | solution.py:322
  91.9 13.4 %copy-start.17 = (bf16[3,48,640]{2,1,0:T(8,128)(2,1)}, bf16[3,48,640]{2,1,0:T(8,128)(2,1)S(1)}, u32[]{:S(2)}) copy-start(bf16[3,48,640]{2,1,0:T(8,128)(2,1)S(1)} %collective-permute-done.5.refs_4_) | copy-start | bytes 552964
  96.8 7.7 %copy-start.18 = (bf16[3,48,640]{2,1,0:T(8,128)(2,1)}, bf16[3,48,640]{2,1,0:T(8,128)(2,1)S(1)}, u32[]{:S(2)}) copy-start(bf16[3,48,640]{2,1,0:T(8,128)(2,1)S(1)} %collective-permute-done.6.refs_5_) | copy-start | bytes 552964
  102.4 2.1 %copy-start.19 = (bf16[3,48,640]{2,1,0:T(8,128)(2,1)}, bf16[3,48,640]{2,1,0:T(8,128)(2,1)S(1)}, u32[]{:S(2)}) copy-start(bf16[3,48,640]{2,1,0:T(8,128)(2,1)S(1)} %collective-permute-done.7.refs_6_) | copy-start | bytes 552964
  124.4 58.0 %copy-start.1 = (bf16[32,16,2688]{2,1,0:T(8,128)(2,1)S(1)}, bf16[32,16,2688]{2,1,0:T(8,128)(2,1)}, u32[]{:S(2)}) copy-start(bf16[32,16,2688]{2,1,0:T(8,128)(2,1)} %copy-done) | copy-start | bytes 8257540
  124.4 58.0 %copy-start.7 = (f32[96,512]{1,0:T(8,128)S(1)}, f32[96,512]{1,0:T(8,128)}, u32[]{:S(2)}) copy-start(f32[96,512]{1,0:T(8,128)} %get-tuple-element.43.refs_1_) | copy-start | bytes 589828
  124.4 58.0 %copy-start.8 = (f32[96,512]{1,0:T(8,128)S(1)}, f32[96,512]{1,0:T(8,128)}, u32[]{:S(2)}) copy-start(f32[96,512]{1,0:T(8,128)} %get-tuple-element.44.refs_2_) | copy-start | bytes 589828
  124.4 33.1 %all-to-all-start.2 = ((bf16[8,4,48,256]{3,2,1,0:T(8,128)(2,1)}), bf16[8,4,48,256]{3,2,1,0:T(8,128)(2,1)}, u32[]{:S(2)}, u32[]{:S(2)}) async-start(bf16[8,4,48,256]{3,2,1,0:T(8,128)(2,1)} %get-tuple-element.39), calls=%async_computation.2 | async-start | bytes 1572864 | tf_op jit(solution)/shard_map/all_to_all | solution.py:302
  130.4 27.1 %collective-permute-start.9 = (bf16[8,2,48,640]{3,2,1,0:T(8,128)(2,1)}, bf16[8,2,48,640]{3,2,1,0:T(8,128)(2,1)}, u32[]{:S(2)}, u32[]{:S(2)}) collective-permute-start(bf16[8,2,48,640]{3,2,1,0:T(8,128)(2,1)} %shard_map.115), channel_id=1, source_target_pairs={{0,256},{32,288},{64,320},{96,352},{128,384},{160,416},{192,448},{... | collective-permute-start | bytes 2949128 | tf_op jit(solution)/shard_map/ppermute | solution.py:343
  162.1 20.4 %all-to-all-start.3 = ((bf16[8,96,256]{2,1,0:T(8,128)(2,1)}), bf16[8,96,256]{2,1,0:T(8,128)(2,1)S(1)}, u32[]{:S(2)}, u32[]{:S(2)}) async-start(bf16[8,96,256]{2,1,0:T(8,128)(2,1)} %get-tuple-element.42), calls=%async_computation.3 | async-start | bytes 786432 | tf_op jit(solution)/shard_map/all_to_all | solution.py:302
  169.0 20.0 %collective-permute-start.11 = (bf16[8,48,640]{2,1,0:T(8,128)(2,1)}, bf16[8,48,640]{2,1,0:T(8,128)(2,1)}, u32[]{:S(2)}, u32[]{:S(2)}) collective-permute-start(bf16[8,48,640]{2,1,0:T(8,128)(2,1)} %get-tuple-element.48), channel_id=1, source_target_pairs={{0,256},{32,288},{64,320},{96,352},{128,384},{160,416},{192,448},{... | collective-permute-start | bytes 1474568 | tf_op jit(solution)/shard_map/ppermute | solution.py:374
  182.4 6.5 %copy-start.21 = (bf16[8,48,640]{2,1,0:T(8,128)(2,1)S(1)}, bf16[8,48,640]{2,1,0:T(8,128)(2,1)}, u32[]{:S(2)}) copy-start(bf16[8,48,640]{2,1,0:T(8,128)(2,1)} %get-tuple-element.47) | copy-start | bytes 1474564
  185.2 13.9 %copy-start.4 = (f32[2,48,2560]{2,1,0:T(8,128)S(1)}, f32[2,48,2560]{2,1,0:T(8,128)}, u32[]{:S(2)}) copy-start(f32[2,48,2560]{2,1,0:T(8,128)} %copy-done.3) | copy-start | bytes 2949124
  185.2 13.9 %collective-permute-start.10 = (bf16[2,48,2560]{2,1,0:T(8,128)(2,1)}, bf16[2,48,2560]{2,1,0:T(8,128)(2,1)S(1)}, u32[]{:S(2)}, u32[]{:S(2)}) collective-permute-start(bf16[2,48,2560]{2,1,0:T(8,128)(2,1)} %get-tuple-element.46), channel_id=1, source_target_pairs={{0,256},{32,288},{64,320},{96,352},{128,384},{160,416},{192,448},{... | collective-permute-start | bytes 1474568 | tf_op jit(solution)/shard_map/ppermute | solution.py:384
  190.9 17.4 %all-to-all-start.4 = ((bf16[8,48,640]{2,1,0:T(8,128)(2,1)}), bf16[8,48,640]{2,1,0:T(8,128)(2,1)S(1)}, u32[]{:S(2)}, u32[]{:S(2)}) async-start(bf16[8,48,640]{2,1,0:T(8,128)(2,1)} %add_convert_fusion), calls=%async_computation.4 | async-start | bytes 983040 | tf_op jit(solution)/shard_map/all_to_all | solution.py:302
  (7 other events, 6.0 us)

commit v10 on v9

--- a/solution.py
+++ b/solution.py
@@ -7,7 +7,8 @@
 
 HALVES = 2
 PAIR = 2
-EARLY = (1,)
+EARLY = (1, 7)
+PARTS = ((0, 1, 7), (2, 3, 4, 5, 6))
 RING = 8
 SIDE = 128
 BF16 = jnp.bfloat16
@@ -208,9 +209,12 @@
         out_ref[k] = down_ref[1:]
 
 
-def gap_kernel(hidden_ref, weight_ref, came_ref, *refs):
-    down_refs = refs[:RING]
-    grad_ref, kept_ref, other_ref = refs[RING:]
+def gap_kernel(hidden_ref, weight_ref, *refs):
+    came_refs, down_refs = refs[:2], refs[2 : 2 + RING]
+    grad_ref, kept_ref, other_ref = refs[2 + RING :]
+    came = {
+        k: came_ref.at[i] for came_ref, part in zip(came_refs, PARTS) for i, k in enumerate(part)
+    }
     block = hidden_ref.shape[2]
     units = 2 * block
     span = hidden_ref.shape[3]
@@ -218,8 +222,8 @@
     back = [(at + RING - k) % RING for k in range(RING)]
     student = jnp.concatenate([hidden_ref[i, a] for i in back for a in (0, 1)], axis=0)
     teacher = jnp.concatenate([hidden_ref[i, a] for i in back for a in (2, 3)], axis=0)
-    t_down = jnp.concatenate([x for k in range(RING) for x in (down_refs[k][0], came_ref[k, 0])], axis=0)
-    m_down = jnp.concatenate([x for k in range(RING) for x in (down_refs[k][2], came_ref[k, 1])], axis=0)
+    t_down = jnp.concatenate([x for k in range(RING) for x in (down_refs[k][0], came[k][0])], axis=0)
+    m_down = jnp.concatenate([x for k in range(RING) for x in (down_refs[k][2], came[k][1])], axis=0)
     gap = dot_tn(student, m_down) - dot_tn(teacher, t_down)
     start = pl.multiple_of(at // (RING // PAIR) * span, span)
     weight = weight_ref[pl.ds(start, span), SIDE - 1 : SIDE].astype(F32)
@@ -336,11 +340,18 @@
 
     sent = [halves(teacher_gate, 1 - half), halves(teacher_up, 1 - half)]
     t_come = lax.ppermute(jnp.concatenate(sent, axis=0), "dp", swap)
-    (passed,) = call(
-        pass_kernel, (jax.ShapeDtypeStruct((RING, PAIR, block, quarter), BF16),), tuple(down), mib=60
-    )
-    slots, t_come, passed = lax.optimization_barrier((slots, t_come, passed))
-    came = lax.ppermute(passed, "dp", swap)
+    first, second = [
+        call(
+            pass_kernel,
+            (jax.ShapeDtypeStruct((len(part), PAIR, block, quarter), BF16),),
+            tuple(down[k] for k in part),
+            mib=60,
+        )[0]
+        for part in PARTS
+    ]
+    first = lax.ppermute(first, "dp", swap)
+    slots, t_come, first, second = lax.optimization_barrier((slots, t_come, first, second))
+    second = lax.ppermute(second, "dp", swap)
 
     hidden, silu, slope, weight = call(
         lambda *refs: hidden_kernel(capacity, *refs),
@@ -367,7 +378,7 @@
             jax.ShapeDtypeStruct((RING, block, quarter), BF16),
             jax.ShapeDtypeStruct((RING, block, quarter), BF16),
         ),
-        (hidden, weight, came, *down),
+        (hidden, weight, first, second, *down),
         mib=60,
     )
     parts = exchange(hidden_grad, "dp", rings)

time: 211 us -> 209 us (level)
  waiting for transfers between devices: 88.6 us -> 73.8 us
  starting transfers between devices: 83.8 us -> 95.2 us
    ppermute x7, waiting for transfers between devices: 33.2 us -> 21 us  [body(): lax.ppermute(down[k], 'dp', turns[k])]
    ppermute x7, starting transfers between devices: 29.6 us -> 41.4 us  [body(): lax.ppermute(down[k], 'dp', turns[k])]
    ppermute x1 -> x2, waiting for transfers between devices: 23.5 us -> 20 us  [the longest x1 15.6 us: body(): second = lax.ppermute(second, 'dp', swap)]
    all_to_all x5, starting transfers between devices: 38.4 us -> 34.9 us  [exchange(): lax.all_to_all(array, axis_name, split_axis=0, concat_axis=0, tiled=True,...]
    ppermute x1 -> x2, starting transfers between devices: 3.6 us -> 6.66 us  [the longest x1 3.6 us: body(): second = lax.ppermute(second, 'dp', swap)]
    ppermute x1, waiting for transfers between devices: 4.69 us -> 7.7 us  [body(): other = lax.ppermute(other, 'dp', swap)]
    pallas_call x8 -> x9, Pallas kernels: 21.9 us -> 23.3 us  [call(): pl.pallas_call(kernel, out_shape=outs, in_specs=[space(i, far) for i in r...]
    unnamed x44 -> x40, local copies, waits for them, and re-layouts: 6.09 us -> 5.39 us
  transfers between devices with their start and end apart: 17 -> 18, of which waited for: 12 -> 11; matrix products, arithmetic and copies ran while one was open for 3% -> 3% of each run, Pallas kernels for 2% -> 3%
where the time goes in v10:
time: 209 us; the launch traced here: 207 us
  starting transfers between devices  95.2 us (46%)
  waiting for transfers between devices  73.8 us (35%)
  Pallas kernels  23.3 us (11%)
  local copies, waits for them, and re-layouts  8.05 us (4%)
  other arithmetic  5.12 us (2%)
    ppermute x7, starting transfers between devices, body(): lax.ppermute(down[k], 'dp', turns[k])  41.4 us
    all_to_all x5, starting transfers between devices, exchange(): lax.all_to_all(array, axis_name, split_axis=0, concat_axis=0, tiled=True,...  34.9 us
    all_to_all x5, waiting for transfers between devices, exchange(): lax.all_to_all(array, axis_name, split_axis=0, concat_axis=0, tiled=True,...  24.8 us
    pallas_call x9, Pallas kernels, call(): pl.pallas_call(kernel, out_shape=outs, in_specs=[space(i, far) for i in r...  23.3 us
    ppermute x7, waiting for transfers between devices, body(): lax.ppermute(down[k], 'dp', turns[k])  21 us
    ppermute x1, waiting for transfers between devices, body(): second = lax.ppermute(second, 'dp', swap)  15.6 us
    ppermute x1, waiting for transfers between devices, body(): other = lax.ppermute(other, 'dp', swap)  7.7 us
    unnamed x40, local copies, waits for them, and re-layouts  5.39 us
  transfers between devices with their start and end apart: 18, of which 11 were waited for; matrix products, arithmetic and copies ran while one was open for 3% of the time, Pallas kernels for 3%

profile of v10, /device:TPU:6, one launch (start us, length us, event | category | flops | bytes accessed | tf_op | source)
XLA Modules:
  0.0 206.5 jit_solution(11577948307039038996)
XLA Ops:
  3.9 13.3 %all-to-all-start = ((bf16[16,8,2688]{2,1,0:T(8,128)(2,1)}), bf16[16,8,2688]{2,1,0:T(8,128)(2,1)S(1)}, u32[]{:S(2)}, u32[]{:S(2)}) async-start(bf16[16,8,2688]{2,1,0:T(8,128)(2,1)} %shard_map.112), calls=%async_computation | async-start | bytes 1376256 | tf_op jit(solution)/shard_map/all_to_all | solution.py:306
  18.3 2.0 collective-permute-start.2
  21.8 3.8 %collective-permute-start = (bf16[3,48,640]{2,1,0:T(8,128)(2,1)S(1)}, bf16[3,48,640]{2,1,0:T(8,128)(2,1)S(1)}, u32[]{:S(2)}, u32[]{:S(2)}) collective-permute-start(bf16[3,48,640]{2,1,0:T(8,128)(2,1)S(1)} %get-tuple-element.28), channel_id=1, source_target_pairs={{0,32},{32,64},{64,96},{96,128},{128,160},{160,192},{192,224},{224... | collective-permute-start | bytes 552968 | tf_op jit(solution)/shard_map/ppermute | solution.py:326
  25.6 3.2 %collective-permute-start.1 = (bf16[3,48,640]{2,1,0:T(8,128)(2,1)S(1)}, bf16[3,48,640]{2,1,0:T(8,128)(2,1)S(1)}, u32[]{:S(2)}, u32[]{:S(2)}) collective-permute-start(bf16[3,48,640]{2,1,0:T(8,128)(2,1)S(1)} %get-tuple-element.29), channel_id=1, source_target_pairs={{0,224},{32,0},{64,32},{96,64},{128,96},{160,128},{192,160},{224,1... | collective-permute-start | bytes 552968 | tf_op jit(solution)/shard_map/ppermute | solution.py:326
  28.9 10.0 %collective-permute-done.refs_1_.refs_3_ = bf16[3,48,640]{2,1,0:T(8,128)(2,1)S(1)} collective-permute-done((bf16[3,48,640]{2,1,0:T(8,128)(2,1)S(1)}, bf16[3,48,640]{2,1,0:T(8,128)(2,1)S(1)}, u32[]{:S(2)}, u32[]{:S(2)}) %collective-permute-start) | collective-permute-done | bytes 184352 | tf_op jit(solution)/shard_map/ppermute | solution.py:326
  40.1 3.9 %shard_map.114 = bf16[512,2688]{1,0:T(8,128)(2,1)} custom-call(bf16[128,2688]{1,0:T(8,128)(2,1)} %bitcast.15), custom_call_target="tpu_custom_call" | custom-call | bytes 688128 | tf_op jit(solution)/shard_map/pallas_call | solution.py:34
  44.0 8.7 %all-to-all-start.1 = ((bf16[32,16,2688]{2,1,0:T(8,128)(2,1)}), bf16[32,16,2688]{2,1,0:T(8,128)(2,1)S(1)}, u32[]{:S(2)}, u32[]{:S(2)}) async-start(bf16[32,16,2688]{2,1,0:T(8,128)(2,1)} %bitcast.14), calls=%async_computation.1 | async-start | bytes 5505024 | tf_op jit(solution)/shard_map/all_to_all | solution.py:306
  55.1 2.9 %collective-permute-start.3 = (bf16[4,48,2560]{2,1,0:T(8,128)(2,1)}, bf16[4,48,2560]{2,1,0:T(8,128)(2,1)}, u32[]{:S(2)}, u32[]{:S(2)}) collective-permute-start(bf16[4,48,2560]{2,1,0:T(8,128)(2,1)} %pad_maximum_fusion), channel_id=1, source_target_pairs={{0,256},{32,288},{64,320},{96,352},{128,384},{160,416},{192,448},{... | collective-permute-start | bytes 2949128 | tf_op jit(solution)/shard_map/ppermute | solution.py:342
  58.0 4.7 %collective-permute-start.5 = (bf16[3,48,640]{2,1,0:T(8,128)(2,1)S(1)}, bf16[3,48,640]{2,1,0:T(8,128)(2,1)S(1)}, u32[]{:S(2)}, u32[]{:S(2)}) collective-permute-start(bf16[3,48,640]{2,1,0:T(8,128)(2,1)S(1)} %copy-done.10), channel_id=1, source_target_pairs={{0,64},{32,96},{64,128},{96,160},{128,192},{160,224},{192,0},{224,... | collective-permute-start | bytes 552968 | tf_op jit(solution)/shard_map/ppermute | solution.py:326
  62.7 5.5 %collective-permute-start.6 = (bf16[3,48,640]{2,1,0:T(8,128)(2,1)S(1)}, bf16[3,48,640]{2,1,0:T(8,128)(2,1)S(1)}, u32[]{:S(2)}, u32[]{:S(2)}) collective-permute-start(bf16[3,48,640]{2,1,0:T(8,128)(2,1)S(1)} %get-tuple-element.35), channel_id=1, source_target_pairs={{0,96},{32,128},{64,160},{96,192},{128,224},{160,0},{192,32},{224,... | collective-permute-start | bytes 552968 | tf_op jit(solution)/shard_map/ppermute | solution.py:326
  70.1 3.1 %collective-permute-start.4 = (bf16[3,2,48,640]{3,2,1,0:T(8,128)(2,1)}, bf16[3,2,48,640]{3,2,1,0:T(8,128)(2,1)}, u32[]{:S(2)}, u32[]{:S(2)}) collective-permute-start(bf16[3,2,48,640]{3,2,1,0:T(8,128)(2,1)} %shard_map.115), channel_id=1, source_target_pairs={{0,256},{32,288},{64,320},{96,352},{128,384},{160,416},{192,448},{... | collective-permute-start | bytes 1105928 | tf_op jit(solution)/shard_map/ppermute | solution.py:352
  73.2 4.7 %collective-permute-start.7 = (bf16[3,48,640]{2,1,0:T(8,128)(2,1)S(1)}, bf16[3,48,640]{2,1,0:T(8,128)(2,1)S(1)}, u32[]{:S(2)}, u32[]{:S(2)}) collective-permute-start(bf16[3,48,640]{2,1,0:T(8,128)(2,1)S(1)} %get-tuple-element.36), channel_id=1, source_target_pairs={{0,128},{32,160},{64,192},{96,224},{128,0},{160,32},{192,64},{224,... | collective-permute-start | bytes 552968 | tf_op jit(solution)/shard_map/ppermute | solution.py:326
  77.9 5.4 %collective-permute-start.8 = (bf16[3,48,640]{2,1,0:T(8,128)(2,1)S(1)}, bf16[3,48,640]{2,1,0:T(8,128)(2,1)S(1)}, u32[]{:S(2)}, u32[]{:S(2)}) collective-permute-start(bf16[3,48,640]{2,1,0:T(8,128)(2,1)S(1)} %get-tuple-element.37), channel_id=1, source_target_pairs={{0,160},{32,192},{64,224},{96,0},{128,32},{160,64},{192,96},{224,1... | collective-permute-start | bytes 552968 | tf_op jit(solution)/shard_map/ppermute | solution.py:326
  83.3 14.1 %collective-permute-start.9 = (bf16[3,48,640]{2,1,0:T(8,128)(2,1)S(1)}, bf16[3,48,640]{2,1,0:T(8,128)(2,1)S(1)}, u32[]{:S(2)}, u32[]{:S(2)}) collective-permute-start(bf16[3,48,640]{2,1,0:T(8,128)(2,1)S(1)} %get-tuple-element.38), channel_id=1, source_target_pairs={{0,192},{32,224},{64,0},{96,32},{128,64},{160,96},{192,128},{224,1... | collective-permute-start | bytes 552968 | tf_op jit(solution)/shard_map/ppermute | solution.py:326
  97.4 5.2 %collective-permute-done.8.refs_3_.refs_7_ = bf16[3,48,640]{2,1,0:T(8,128)(2,1)S(1)} collective-permute-done((bf16[3,48,640]{2,1,0:T(8,128)(2,1)S(1)}, bf16[3,48,640]{2,1,0:T(8,128)(2,1)S(1)}, u32[]{:S(2)}, u32[]{:S(2)}) %collective-permute-start.8) | collective-permute-done | bytes 184352 | tf_op jit(solution)/shard_map/ppermute | solution.py:326
  102.6 5.7 %collective-permute-done.9.refs_4_.refs_8_ = bf16[3,48,640]{2,1,0:T(8,128)(2,1)S(1)} collective-permute-done((bf16[3,48,640]{2,1,0:T(8,128)(2,1)S(1)}, bf16[3,48,640]{2,1,0:T(8,128)(2,1)S(1)}, u32[]{:S(2)}, u32[]{:S(2)}) %collective-permute-start.9) | collective-permute-done | bytes 184352 | tf_op jit(solution)/shard_map/ppermute | solution.py:326
  109.0 2.1 %shard_map.116 = bf16[5,2,48,640]{3,2,1,0:T(8,128)(2,1)} custom-call(bf16[3,48,640]{2,1,0:T(8,128)(2,1)} %copy-done.12, bf16[3,48,640]{2,1,0:T(8,128)(2,1)} %copy-done.13, bf16[3,48,640]{2,1,0:T(8,128)(2,1)} %copy-done.14, bf16[3,48,640]{2,1,0:T(8,128)(2,1)} %copy-done.15, bf16[3,48,640]{2,1,0:T(8,128)(2,1)} %copy-done.16), custom_call_target="tpu_custom_call" | custom-call | bytes 921600 | tf_op jit(solution)/shard_map/pallas_call | solution.py:34
  111.2 4.3 %collective-permute-done.4.refs_0_ = bf16[3,2,48,640]{3,2,1,0:T(8,128)(2,1)} collective-permute-done((bf16[3,2,48,640]{3,2,1,0:T(8,128)(2,1)}, bf16[3,2,48,640]{3,2,1,0:T(8,128)(2,1)}, u32[]{:S(2)}, u32[]{:S(2)}) %collective-permute-start.4) | collective-permute-done | bytes 368672 | tf_op jit(solution)/shard_map/ppermute | solution.py:352
  118.1 6.4 %shard_map.117 = (bf16[8,4,48,256]{3,2,1,0:T(8,128)(2,1)}, f32[96,512]{1,0:T(8,128)}, f32[96,512]{1,0:T(8,128)}, bf16[512,128]{1,0:T(8,128)(2,1)}) custom-call(bf16[512,2688]{1,0:T(8,128)(2,1)} %bitcast.12, bf16[4,48,2560]{2,1,0:T(8,128)(2,1)} %refs_1_.1, bf16[4,48,2560]{2,1,0:T(8,128)(2,1)} %refs_2_.1, bf16[1,48,2560]{2,1,0:T(8,128)(2,1)} %refs_3_.1, ...), custom_call_target="tpu_custom_call" | custom-call | bytes 6684672 | tf_op jit(solution)/shard_map/pallas_call | solution.py:34
  124.5 6.0 %all-to-all-start.2 = ((bf16[8,4,48,256]{3,2,1,0:T(8,128)(2,1)}), bf16[8,4,48,256]{3,2,1,0:T(8,128)(2,1)}, u32[]{:S(2)}, u32[]{:S(2)}) async-start(bf16[8,4,48,256]{3,2,1,0:T(8,128)(2,1)} %get-tuple-element.42), calls=%async_computation.2 | async-start | bytes 1572864 | tf_op jit(solution)/shard_map/all_to_all | solution.py:306
  130.4 3.6 %collective-permute-start.10 = (bf16[5,2,48,640]{3,2,1,0:T(8,128)(2,1)}, bf16[5,2,48,640]{3,2,1,0:T(8,128)(2,1)}, u32[]{:S(2)}, u32[]{:S(2)}) collective-permute-start(bf16[5,2,48,640]{3,2,1,0:T(8,128)(2,1)} %shard_map.116), channel_id=1, source_target_pairs={{0,256},{32,288},{64,320},{96,352},{128,384},{160,416},{192,448},{... | collective-permute-start | bytes 1843208 | tf_op jit(solution)/shard_map/ppermute | solution.py:354
  134.1 15.6 %collective-permute-done.10.refs_1_ = bf16[5,2,48,640]{3,2,1,0:T(8,128)(2,1)} collective-permute-done((bf16[5,2,48,640]{3,2,1,0:T(8,128)(2,1)}, bf16[5,2,48,640]{3,2,1,0:T(8,128)(2,1)}, u32[]{:S(2)}, u32[]{:S(2)}) %collective-permute-start.10) | collective-permute-done | bytes 614432 | tf_op jit(solution)/shard_map/ppermute | solution.py:354
  149.7 4.2 %all-to-all-done.2.hidden_ref = bf16[8,4,48,256]{3,2,1,0:T(8,128)(2,1)} async-done(((bf16[8,4,48,256]{3,2,1,0:T(8,128)(2,1)}), bf16[8,4,48,256]{3,2,1,0:T(8,128)(2,1)}, u32[]{:S(2)}, u32[]{:S(2)}) %all-to-all-start.2) | async-done | bytes 786464 | tf_op jit(solution)/shard_map/all_to_all | solution.py:306
  153.9 4.4 %shard_map.118 = (bf16[8,96,256]{2,1,0:T(8,128)(2,1)}, bf16[8,48,640]{2,1,0:T(8,128)(2,1)}, bf16[8,48,640]{2,1,0:T(8,128)(2,1)}) custom-call(bf16[8,4,48,256]{3,2,1,0:T(8,128)(2,1)} %all-to-all-done.2.hidden_ref, bf16[512,128]{1,0:T(8,128)(2,1)} %get-tuple-element.43.weight_ref, bf16[3,2,48,640]{3,2,1,0:T(8,128)(2,1)} %collective-permute-done.4.refs_0_, ...), custom_call_target="tpu_custom_call" | custom-call | bytes 3375104 | tf_op jit(solution)/shard_map/pallas_call | solution.py:34
  158.3 3.5 %all-to-all-start.3 = ((bf16[8,96,256]{2,1,0:T(8,128)(2,1)}), bf16[8,96,256]{2,1,0:T(8,128)(2,1)S(1)}, u32[]{:S(2)}, u32[]{:S(2)}) async-start(bf16[8,96,256]{2,1,0:T(8,128)(2,1)} %get-tuple-element.46), calls=%async_computation.3 | async-start | bytes 786432 | tf_op jit(solution)/shard_map/all_to_all | solution.py:306
  161.8 3.6 %collective-permute-start.12 = (bf16[8,48,640]{2,1,0:T(8,128)(2,1)}, bf16[8,48,640]{2,1,0:T(8,128)(2,1)}, u32[]{:S(2)}, u32[]{:S(2)}) collective-permute-start(bf16[8,48,640]{2,1,0:T(8,128)(2,1)} %get-tuple-element.52), channel_id=1, source_target_pairs={{0,256},{32,288},{64,320},{96,352},{128,384},{160,416},{192,448},{... | collective-permute-start | bytes 1474568 | tf_op jit(solution)/shard_map/ppermute | solution.py:385
  165.4 11.4 %all-to-all-done.3.refs_0_ = bf16[8,96,256]{2,1,0:T(8,128)(2,1)S(1)} async-done(((bf16[8,96,256]{2,1,0:T(8,128)(2,1)}), bf16[8,96,256]{2,1,0:T(8,128)(2,1)S(1)}, u32[]{:S(2)}, u32[]{:S(2)}) %all-to-all-start.3) | async-done | bytes 393248 | tf_op jit(solution)/shard_map/all_to_all | solution.py:306
  179.6 3.7 %collective-permute-start.11 = (bf16[2,48,2560]{2,1,0:T(8,128)(2,1)}, bf16[2,48,2560]{2,1,0:T(8,128)(2,1)S(1)}, u32[]{:S(2)}, u32[]{:S(2)}) collective-permute-start(bf16[2,48,2560]{2,1,0:T(8,128)(2,1)} %get-tuple-element.50), channel_id=1, source_target_pairs={{0,256},{32,288},{64,320},{96,352},{128,384},{160,416},{192,448},{... | collective-permute-start | bytes 1474568 | tf_op jit(solution)/shard_map/ppermute | solution.py:395
  183.4 1.9 add_convert_fusion
  185.3 3.5 %all-to-all-start.4 = ((bf16[8,48,640]{2,1,0:T(8,128)(2,1)}), bf16[8,48,640]{2,1,0:T(8,128)(2,1)S(1)}, u32[]{:S(2)}, u32[]{:S(2)}) async-start(bf16[8,48,640]{2,1,0:T(8,128)(2,1)} %add_convert_fusion), calls=%async_computation.4 | async-start | bytes 983040 | tf_op jit(solution)/shard_map/all_to_all | solution.py:306
  188.8 7.7 %collective-permute-done.11 = bf16[2,48,2560]{2,1,0:T(8,128)(2,1)S(1)} collective-permute-done((bf16[2,48,2560]{2,1,0:T(8,128)(2,1)}, bf16[2,48,2560]{2,1,0:T(8,128)(2,1)S(1)}, u32[]{:S(2)}, u32[]{:S(2)}) %collective-permute-start.11) | collective-permute-done | bytes 491552 | tf_op jit(solution)/shard_map/ppermute | solution.py:395
  197.5 8.2 %all-to-all-done.4.parts_ref = bf16[8,48,640]{2,1,0:T(8,128)(2,1)S(1)} async-done(((bf16[8,48,640]{2,1,0:T(8,128)(2,1)}), bf16[8,48,640]{2,1,0:T(8,128)(2,1)S(1)}, u32[]{:S(2)}, u32[]{:S(2)}) %all-to-all-start.4) | async-done | bytes 491552 | tf_op jit(solution)/shard_map/all_to_all | solution.py:306
  (59 shorter events, 19.2 us)
Async XLA Ops:
  0.6 19.6 %copy-start.2 = (bf16[4,48,2560]{2,1,0:T(8,128)(2,1)S(1)}, bf16[4,48,2560]{2,1,0:T(8,128)(2,1)}, u32[]{:S(2)}) copy-start(bf16[4,48,2560]{2,1,0:T(8,128)(2,1)} %down_ref.1) | copy-start | bytes 2949124
  0.6 19.6 %copy-start.6 = (bf16[1,48,2560]{2,1,0:T(8,128)(2,1)S(1)}, bf16[1,48,2560]{2,1,0:T(8,128)(2,1)}, u32[]{:S(2)}) copy-start(bf16[1,48,2560]{2,1,0:T(8,128)(2,1)} %merged_ref.1) | copy-start | bytes 737284
  3.9 35.4 %all-to-all-start = ((bf16[16,8,2688]{2,1,0:T(8,128)(2,1)}), bf16[16,8,2688]{2,1,0:T(8,128)(2,1)S(1)}, u32[]{:S(2)}, u32[]{:S(2)}) async-start(bf16[16,8,2688]{2,1,0:T(8,128)(2,1)} %shard_map.112), calls=%async_computation | async-start | bytes 1376256 | tf_op jit(solution)/shard_map/all_to_all | solution.py:306
  18.3 21.0 %collective-permute-start.2 = (bf16[2,48,2560]{2,1,0:T(8,128)(2,1)S(1)}, bf16[2,48,2560]{2,1,0:T(8,128)(2,1)}, u32[]{:S(2)}, u32[]{:S(2)}) collective-permute-start(bf16[2,48,2560]{2,1,0:T(8,128)(2,1)S(1)} %pad_maximum_fusion.1), channel_id=1, source_target_pairs={{0,256},{32,288},{64,320},{96,352},{128,384},{160,416},{192,448},{... | collective-permute-start | bytes 1474568 | tf_op jit(solution)/shard_map/ppermute | solution.py:328
  21.8 17.0 %collective-permute-start = (bf16[3,48,640]{2,1,0:T(8,128)(2,1)S(1)}, bf16[3,48,640]{2,1,0:T(8,128)(2,1)S(1)}, u32[]{:S(2)}, u32[]{:S(2)}) collective-permute-start(bf16[3,48,640]{2,1,0:T(8,128)(2,1)S(1)} %get-tuple-element.28), channel_id=1, source_target_pairs={{0,32},{32,64},{64,96},{96,128},{128,160},{160,192},{192,224},{224... | collective-permute-start | bytes 552968 | tf_op jit(solution)/shard_map/ppermute | solution.py:326
  25.6 13.2 %collective-permute-start.1 = (bf16[3,48,640]{2,1,0:T(8,128)(2,1)S(1)}, bf16[3,48,640]{2,1,0:T(8,128)(2,1)S(1)}, u32[]{:S(2)}, u32[]{:S(2)}) collective-permute-start(bf16[3,48,640]{2,1,0:T(8,128)(2,1)S(1)} %get-tuple-element.29), channel_id=1, source_target_pairs={{0,224},{32,0},{64,32},{96,64},{128,96},{160,128},{192,160},{224,1... | collective-permute-start | bytes 552968 | tf_op jit(solution)/shard_map/ppermute | solution.py:326
  38.9 5.2 %copy-start.17 = (bf16[3,48,640]{2,1,0:T(8,128)(2,1)}, bf16[3,48,640]{2,1,0:T(8,128)(2,1)S(1)}, u32[]{:S(2)}) copy-start(bf16[3,48,640]{2,1,0:T(8,128)(2,1)S(1)} %collective-permute-done.refs_1_.refs_3_) | copy-start | bytes 552964
  38.9 5.2 %copy-start.18 = (bf16[3,48,640]{2,1,0:T(8,128)(2,1)}, bf16[3,48,640]{2,1,0:T(8,128)(2,1)S(1)}, u32[]{:S(2)}) copy-start(bf16[3,48,640]{2,1,0:T(8,128)(2,1)S(1)} %collective-permute-done.1.refs_2_.refs_9_) | copy-start | bytes 552964
  44.0 72.5 %all-to-all-start.1 = ((bf16[32,16,2688]{2,1,0:T(8,128)(2,1)}), bf16[32,16,2688]{2,1,0:T(8,128)(2,1)S(1)}, u32[]{:S(2)}, u32[]{:S(2)}) async-start(bf16[32,16,2688]{2,1,0:T(8,128)(2,1)} %bitcast.14), calls=%async_computation.1 | async-start | bytes 5505024 | tf_op jit(solution)/shard_map/all_to_all | solution.py:306
  52.8 5.2 %copy-start.10 = (bf16[3,48,640]{2,1,0:T(8,128)(2,1)S(1)}, bf16[3,48,640]{2,1,0:T(8,128)(2,1)}, u32[]{:S(2)}) copy-start(bf16[3,48,640]{2,1,0:T(8,128)(2,1)} %copy-done.9) | copy-start | bytes 552964
  55.1 56.0 %collective-permute-start.3 = (bf16[4,48,2560]{2,1,0:T(8,128)(2,1)}, bf16[4,48,2560]{2,1,0:T(8,128)(2,1)}, u32[]{:S(2)}, u32[]{:S(2)}) collective-permute-start(bf16[4,48,2560]{2,1,0:T(8,128)(2,1)} %pad_maximum_fusion), channel_id=1, source_target_pairs={{0,256},{32,288},{64,320},{96,352},{128,384},{160,416},{192,448},{... | collective-permute-start | bytes 2949128 | tf_op jit(solution)/shard_map/ppermute | solution.py:342
  58.0 19.9 %collective-permute-start.5 = (bf16[3,48,640]{2,1,0:T(8,128)(2,1)S(1)}, bf16[3,48,640]{2,1,0:T(8,128)(2,1)S(1)}, u32[]{:S(2)}, u32[]{:S(2)}) collective-permute-start(bf16[3,48,640]{2,1,0:T(8,128)(2,1)S(1)} %copy-done.10), channel_id=1, source_target_pairs={{0,64},{32,96},{64,128},{96,160},{128,192},{160,224},{192,0},{224,... | collective-permute-start | bytes 552968 | tf_op jit(solution)/shard_map/ppermute | solution.py:326
  62.7 20.5 %collective-permute-start.6 = (bf16[3,48,640]{2,1,0:T(8,128)(2,1)S(1)}, bf16[3,48,640]{2,1,0:T(8,128)(2,1)S(1)}, u32[]{:S(2)}, u32[]{:S(2)}) collective-permute-start(bf16[3,48,640]{2,1,0:T(8,128)(2,1)S(1)} %get-tuple-element.35), channel_id=1, source_target_pairs={{0,96},{32,128},{64,160},{96,192},{128,224},{160,0},{192,32},{224,... | collective-permute-start | bytes 552968 | tf_op jit(solution)/shard_map/ppermute | solution.py:326
  70.1 45.4 %collective-permute-start.4 = (bf16[3,2,48,640]{3,2,1,0:T(8,128)(2,1)}, bf16[3,2,48,640]{3,2,1,0:T(8,128)(2,1)}, u32[]{:S(2)}, u32[]{:S(2)}) collective-permute-start(bf16[3,2,48,640]{3,2,1,0:T(8,128)(2,1)} %shard_map.115), channel_id=1, source_target_pairs={{0,256},{32,288},{64,320},{96,352},{128,384},{160,416},{192,448},{... | collective-permute-start | bytes 1105928 | tf_op jit(solution)/shard_map/ppermute | solution.py:352
  73.2 24.2 %collective-permute-start.7 = (bf16[3,48,640]{2,1,0:T(8,128)(2,1)S(1)}, bf16[3,48,640]{2,1,0:T(8,128)(2,1)S(1)}, u32[]{:S(2)}, u32[]{:S(2)}) collective-permute-start(bf16[3,48,640]{2,1,0:T(8,128)(2,1)S(1)} %get-tuple-element.36), channel_id=1, source_target_pairs={{0,128},{32,160},{64,192},{96,224},{128,0},{160,32},{192,64},{224,... | collective-permute-start | bytes 552968 | tf_op jit(solution)/shard_map/ppermute | solution.py:326
  77.9 30.5 %copy-start.12 = (bf16[3,48,640]{2,1,0:T(8,128)(2,1)}, bf16[3,48,640]{2,1,0:T(8,128)(2,1)S(1)}, u32[]{:S(2)}) copy-start(bf16[3,48,640]{2,1,0:T(8,128)(2,1)S(1)} %collective-permute-done.5.refs_0_.refs_4_) | copy-start | bytes 552964
  77.9 24.8 %collective-permute-start.8 = (bf16[3,48,640]{2,1,0:T(8,128)(2,1)S(1)}, bf16[3,48,640]{2,1,0:T(8,128)(2,1)S(1)}, u32[]{:S(2)}, u32[]{:S(2)}) collective-permute-start(bf16[3,48,640]{2,1,0:T(8,128)(2,1)S(1)} %get-tuple-element.37), channel_id=1, source_target_pairs={{0,160},{32,192},{64,224},{96,0},{128,32},{160,64},{192,96},{224,1... | collective-permute-start | bytes 552968 | tf_op jit(solution)/shard_map/ppermute | solution.py:326
  83.2 25.1 %copy-start.13 = (bf16[3,48,640]{2,1,0:T(8,128)(2,1)}, bf16[3,48,640]{2,1,0:T(8,128)(2,1)S(1)}, u32[]{:S(2)}) copy-start(bf16[3,48,640]{2,1,0:T(8,128)(2,1)S(1)} %collective-permute-done.6.refs_1_.refs_5_) | copy-start | bytes 552964
  83.3 25.1 %collective-permute-start.9 = (bf16[3,48,640]{2,1,0:T(8,128)(2,1)S(1)}, bf16[3,48,640]{2,1,0:T(8,128)(2,1)S(1)}, u32[]{:S(2)}, u32[]{:S(2)}) collective-permute-start(bf16[3,48,640]{2,1,0:T(8,128)(2,1)S(1)} %get-tuple-element.38), channel_id=1, source_target_pairs={{0,192},{32,224},{64,0},{96,32},{128,64},{160,96},{192,128},{224,1... | collective-permute-start | bytes 552968 | tf_op jit(solution)/shard_map/ppermute | solution.py:326
  97.4 5.3 %copy-start.14 = (bf16[3,48,640]{2,1,0:T(8,128)(2,1)}, bf16[3,48,640]{2,1,0:T(8,128)(2,1)S(1)}, u32[]{:S(2)}) copy-start(bf16[3,48,640]{2,1,0:T(8,128)(2,1)S(1)} %collective-permute-done.7.refs_2_.refs_6_) | copy-start | bytes 552964
  102.6 5.7 %copy-start.15 = (bf16[3,48,640]{2,1,0:T(8,128)(2,1)}, bf16[3,48,640]{2,1,0:T(8,128)(2,1)S(1)}, u32[]{:S(2)}) copy-start(bf16[3,48,640]{2,1,0:T(8,128)(2,1)S(1)} %collective-permute-done.8.refs_3_.refs_7_) | copy-start | bytes 552964
  124.4 52.4 %copy-start.1 = (bf16[32,16,2688]{2,1,0:T(8,128)(2,1)S(1)}, bf16[32,16,2688]{2,1,0:T(8,128)(2,1)}, u32[]{:S(2)}) copy-start(bf16[32,16,2688]{2,1,0:T(8,128)(2,1)} %copy-done) | copy-start | bytes 8257540
  124.4 52.4 %copy-start.7 = (f32[96,512]{1,0:T(8,128)S(1)}, f32[96,512]{1,0:T(8,128)}, u32[]{:S(2)}) copy-start(f32[96,512]{1,0:T(8,128)} %get-tuple-element.47.refs_1_) | copy-start | bytes 589828
  124.5 52.4 %copy-start.8 = (f32[96,512]{1,0:T(8,128)S(1)}, f32[96,512]{1,0:T(8,128)}, u32[]{:S(2)}) copy-start(f32[96,512]{1,0:T(8,128)} %get-tuple-element.48.refs_2_) | copy-start | bytes 589828
  124.5 29.4 %all-to-all-start.2 = ((bf16[8,4,48,256]{3,2,1,0:T(8,128)(2,1)}), bf16[8,4,48,256]{3,2,1,0:T(8,128)(2,1)}, u32[]{:S(2)}, u32[]{:S(2)}) async-start(bf16[8,4,48,256]{3,2,1,0:T(8,128)(2,1)} %get-tuple-element.42), calls=%async_computation.2 | async-start | bytes 1572864 | tf_op jit(solution)/shard_map/all_to_all | solution.py:306
  130.4 19.2 %collective-permute-start.10 = (bf16[5,2,48,640]{3,2,1,0:T(8,128)(2,1)}, bf16[5,2,48,640]{3,2,1,0:T(8,128)(2,1)}, u32[]{:S(2)}, u32[]{:S(2)}) collective-permute-start(bf16[5,2,48,640]{3,2,1,0:T(8,128)(2,1)} %shard_map.116), channel_id=1, source_target_pairs={{0,256},{32,288},{64,320},{96,352},{128,384},{160,416},{192,448},{... | collective-permute-start | bytes 1843208 | tf_op jit(solution)/shard_map/ppermute | solution.py:354
  158.3 18.5 %all-to-all-start.3 = ((bf16[8,96,256]{2,1,0:T(8,128)(2,1)}), bf16[8,96,256]{2,1,0:T(8,128)(2,1)S(1)}, u32[]{:S(2)}, u32[]{:S(2)}) async-start(bf16[8,96,256]{2,1,0:T(8,128)(2,1)} %get-tuple-element.46), calls=%async_computation.3 | async-start | bytes 786432 | tf_op jit(solution)/shard_map/all_to_all | solution.py:306
  161.8 21.6 %collective-permute-start.12 = (bf16[8,48,640]{2,1,0:T(8,128)(2,1)}, bf16[8,48,640]{2,1,0:T(8,128)(2,1)}, u32[]{:S(2)}, u32[]{:S(2)}) collective-permute-start(bf16[8,48,640]{2,1,0:T(8,128)(2,1)} %get-tuple-element.52), channel_id=1, source_target_pairs={{0,256},{32,288},{64,320},{96,352},{128,384},{160,416},{192,448},{... | collective-permute-start | bytes 1474568 | tf_op jit(solution)/shard_map/ppermute | solution.py:385
  176.8 6.5 %copy-start.19 = (bf16[8,48,640]{2,1,0:T(8,128)(2,1)S(1)}, bf16[8,48,640]{2,1,0:T(8,128)(2,1)}, u32[]{:S(2)}) copy-start(bf16[8,48,640]{2,1,0:T(8,128)(2,1)} %get-tuple-element.51) | copy-start | bytes 1474564
  179.6 16.9 %copy-start.4 = (f32[2,48,2560]{2,1,0:T(8,128)S(1)}, f32[2,48,2560]{2,1,0:T(8,128)}, u32[]{:S(2)}) copy-start(f32[2,48,2560]{2,1,0:T(8,128)} %copy-done.3) | copy-start | bytes 2949124
  179.6 16.9 %collective-permute-start.11 = (bf16[2,48,2560]{2,1,0:T(8,128)(2,1)}, bf16[2,48,2560]{2,1,0:T(8,128)(2,1)S(1)}, u32[]{:S(2)}, u32[]{:S(2)}) collective-permute-start(bf16[2,48,2560]{2,1,0:T(8,128)(2,1)} %get-tuple-element.50), channel_id=1, source_target_pairs={{0,256},{32,288},{64,320},{96,352},{128,384},{160,416},{192,448},{... | collective-permute-start | bytes 1474568 | tf_op jit(solution)/shard_map/ppermute | solution.py:395
  185.3 20.4 %all-to-all-start.4 = ((bf16[8,48,640]{2,1,0:T(8,128)(2,1)}), bf16[8,48,640]{2,1,0:T(8,128)(2,1)S(1)}, u32[]{:S(2)}, u32[]{:S(2)}) async-start(bf16[8,48,640]{2,1,0:T(8,128)(2,1)} %add_convert_fusion), calls=%async_computation.4 | async-start | bytes 983040 | tf_op jit(solution)/shard_map/all_to_all | solution.py:306
  (6 other events, 5.3 us)

commit v11 on v10

--- a/solution.py
+++ b/solution.py
@@ -27,7 +27,7 @@
     return lax.dot_general(a, b, (((0,), (0,)), ((), ())), preferred_element_type=F32)
 
 
-def call(kernel, outs, args, far=(), scratch=(), mib=16):
+def call(kernel, outs, args, far=(), far_outs=(), scratch=(), mib=16):
     def space(i, alone):
         return pl.BlockSpec(memory_space=pltpu.HBM if i in alone else pltpu.VMEM)
 
@@ -35,7 +35,7 @@
         kernel,
         out_shape=outs,
         in_specs=[space(i, far) for i in range(len(args))],
-        out_specs=[space(i, ()) for i in range(len(outs))],
+        out_specs=[space(i, far_outs) for i in range(len(outs))],
         scratch_shapes=scratch,
         compiler_params=pltpu.CompilerParams(vmem_limit_bytes=mib * 1024 * 1024),
         cost_estimate=pl.CostEstimate(
@@ -67,12 +67,13 @@
 
 
 def pack_kernel(ids_ref, token_ref, weight_ref, out_ref):
-    ranks, count = ids_ref.shape
+    ranks, _, count = ids_ref.shape
     features = token_ref.shape[1]
     lane = lax.broadcasted_iota(jnp.int32, (ranks, SIDE), 1)
     rank = lax.broadcasted_iota(jnp.int32, (ranks, SIDE), 0)
     spread = jnp.where(lane == rank, 1.0, 0.0).astype(BF16)
-    side = dot_tn(ids_ref[...].astype(F32).astype(BF16), spread)
+    ids = jnp.concatenate([ids_ref[k] for k in range(ranks)], axis=0)
+    side = dot_tn(ids.astype(F32).astype(BF16), spread)
     lane = lax.broadcasted_iota(jnp.int32, (count, SIDE), 1)
     weight = weight_ref[...].astype(F32)
     for k in range(ranks):
@@ -84,7 +85,7 @@
         out_ref[i, :, features:] = side
 
 
-def slots_kernel(ranks, capacity, group_ref, out_ref):
+def slots_kernel(ranks, capacity, group_ref, out_hbm, out_ref, sems):
     half, _ = place()
     wide = group_ref.shape[1] - SIDE
     count = group_ref.shape[0]
@@ -105,9 +106,17 @@
     below = jnp.where(earlier < later, 1.0, 0.0).astype(BF16)
     before = dot_nn(below, hits.astype(BF16))
     chosen = jnp.where((hits > 0.0) & (before == position), 1.0, 0.0)
-    out_ref[:, :wide] = dot_tn(chosen.astype(BF16), group_ref[:, :wide]).astype(BF16)
+    pick = chosen.astype(BF16)
     weights = dot_tn((chosen * weight).astype(BF16), jnp.ones((count, SIDE), BF16))
     out_ref[:, wide:] = weights.astype(BF16)
+    tile = 7 * SIDE
+    copies = []
+    for n, start in enumerate(range(0, wide + SIDE, tile)):
+        stop = min(start + tile, wide)
+        out_ref[:, start:stop] = dot_tn(pick, group_ref[:, start:stop]).astype(BF16)
+        span = (slice(None), pl.ds(start, tile))
+        copies += start_copies([(out_ref.at[span], out_hbm.at[span])], sems, n)
+    wait_copies(copies)
 
 
 def by_teacher(count, capacity, source_axis):
@@ -236,8 +245,8 @@
         other_ref[i] = down_grad[k * units + block : (k + 1) * units]
 
 
-def grads_kernel(capacity, parts_ref, silu_ref, slope_ref, rows_ref, own_ref, other_ref):
-    block = own_ref.shape[1]
+def other_kernel(capacity, parts_ref, silu_ref, slope_ref, rows_ref, other_ref, stack_ref):
+    block = other_ref.shape[1]
     places = parts_ref.shape[0] // PAIR
     units = parts_ref.shape[1]
     count = rows_ref.shape[0]
@@ -254,12 +263,18 @@
         total += parts[i * units : (i + 1) * units]
     gate = (total * slope_ref[...]).astype(BF16)
     up = (total * silu_ref[...]).astype(BF16)
-    stack = jnp.concatenate([gate[:block], up[:block], gate[block:], up[block:]], axis=0)
-    grads = dot_nn(stack, rows_ref[:, : own_ref.shape[2]])
+    stack_ref[...] = jnp.concatenate([gate[:block], up[:block]], axis=0)
+    stack = jnp.concatenate([gate[block:], up[block:]], axis=0)
+    grads = dot_nn(stack, rows_ref[:, : other_ref.shape[2]])
+    other_ref[0] = grads[:block].astype(BF16)
+    other_ref[1] = grads[block:].astype(BF16)
+
+
+def own_kernel(stack_ref, rows_ref, own_ref):
+    block = own_ref.shape[1]
+    grads = dot_nn(stack_ref[...], rows_ref[:, : own_ref.shape[2]])
     own_ref[0] = grads[:block]
-    own_ref[1] = grads[block : 2 * block]
-    other_ref[0] = grads[2 * block : 3 * block].astype(BF16)
-    other_ref[1] = grads[3 * block :].astype(BF16)
+    own_ref[1] = grads[block:]
 
 
 def down_sum_kernel(parts_ref, out_ref):
@@ -313,7 +328,7 @@
     (packets,) = call(
         pack_kernel,
         (jax.ShapeDtypeStruct((n_dp, capacity, wide), BF16),),
-        (teacher_ids[0].T, tokens[0], route_weight[0]),
+        (teacher_ids.transpose(2, 0, 1), tokens[0], route_weight[0]),
         mib=60,
     )
     group = exchange(packets, "dp").reshape(n_dp * capacity, wide)
@@ -334,6 +349,8 @@
         lambda *refs: slots_kernel(ranks, capacity, *refs),
         (jax.ShapeDtypeStruct((rows, wide), BF16),),
         (group,),
+        far_outs=(0,),
+        scratch=[pltpu.VMEM((rows, wide), BF16), pltpu.SemaphoreType.DMA((8,))],
         mib=60,
     )
     slots = exchange(slots.reshape(experts, PAIR * capacity, wide), "expert").reshape(rows, wide)
@@ -384,13 +401,16 @@
     parts = exchange(hidden_grad, "dp", rings)
     other_down = lax.ppermute(other_down, "dp", swap)
     down_grad = (kept_down.astype(F32) + other_down.astype(F32)).astype(BF16)
-    own, other = call(
-        lambda *refs: grads_kernel(capacity, *refs),
+    other, stack = call(
+        lambda *refs: other_kernel(capacity, *refs),
         (
-            jax.ShapeDtypeStruct((2, block, features), F32),
             jax.ShapeDtypeStruct((2, block, features), BF16),
+            jax.ShapeDtypeStruct((2 * block, rows), BF16),
         ),
         (parts, silu, slope, slots),
+    )
+    (own,) = call(
+        own_kernel, (jax.ShapeDtypeStruct((2, block, features), F32),), (stack, slots)
     )
     other = lax.ppermute(other, "dp", swap)
     down_grad = exchange(down_grad, "dp", rings)

time: 209 us -> 207 us (level)
  waiting for transfers between devices: 73.8 us -> 70.7 us
    pallas_call x9 -> x10, Pallas kernels: 23.3 us -> 23.5 us  [call(): pl.pallas_call(kernel, out_shape=outs, in_specs=[space(i, far) for i in r...]
  transfers between devices with their start and end apart: 18 -> 18, of which waited for: 11 -> 11; matrix products, arithmetic and copies ran while one was open for 3% -> 4% of each run, Pallas kernels for 3% -> 3%
where the time goes in v11:
time: 207 us; the launch traced here: 204 us
  starting transfers between devices  94.4 us (46%)
  waiting for transfers between devices  70.7 us (34%)
  Pallas kernels  23.5 us (11%)
  local copies, waits for them, and re-layouts  8.57 us (4%)
  other arithmetic  6.18 us (3%)
    ppermute x7, starting transfers between devices, body(): lax.ppermute(down[k], 'dp', turns[k])  41.4 us
    all_to_all x5, starting transfers between devices, exchange(): lax.all_to_all(array, axis_name, split_axis=0, concat_axis=0, tiled=True,...  34 us
    all_to_all x5, waiting for transfers between devices, exchange(): lax.all_to_all(array, axis_name, split_axis=0, concat_axis=0, tiled=True,...  23.9 us
    pallas_call x10, Pallas kernels, call(): pl.pallas_call(kernel, out_shape=outs, in_specs=[space(i, far) for i in r...  23.5 us
    ppermute x7, waiting for transfers between devices, body(): lax.ppermute(down[k], 'dp', turns[k])  19.7 us
    ppermute x1, waiting for transfers between devices, body(): second = lax.ppermute(second, 'dp', swap)  15.6 us
    unnamed x40, local copies, waits for them, and re-layouts  7.29 us
    ppermute x1, waiting for transfers between devices, body(): other = lax.ppermute(other, 'dp', swap)  6.36 us
  transfers between devices with their start and end apart: 18, of which 11 were waited for; matrix products, arithmetic and copies ran while one was open for 4% of the time, Pallas kernels for 3%

profile of v11, /device:TPU:6, one launch (start us, length us, event | category | flops | bytes accessed | tf_op | source)
XLA Modules:
  0.0 204.3 jit_solution(7557694412283256492)
XLA Ops:
  2.6 13.3 %all-to-all-start = ((bf16[16,8,2688]{2,1,0:T(8,128)(2,1)}), bf16[16,8,2688]{2,1,0:T(8,128)(2,1)S(1)}, u32[]{:S(2)}, u32[]{:S(2)}) async-start(bf16[16,8,2688]{2,1,0:T(8,128)(2,1)} %shard_map.112), calls=%async_computation | async-start | bytes 1376256 | tf_op jit(solution)/shard_map/all_to_all | solution.py:321
  17.0 2.0 collective-permute-start.2
  20.5 3.8 %collective-permute-start = (bf16[3,48,640]{2,1,0:T(8,128)(2,1)S(1)}, bf16[3,48,640]{2,1,0:T(8,128)(2,1)S(1)}, u32[]{:S(2)}, u32[]{:S(2)}) collective-permute-start(bf16[3,48,640]{2,1,0:T(8,128)(2,1)S(1)} %get-tuple-element.28), channel_id=1, source_target_pairs={{0,32},{32,64},{64,96},{96,128},{128,160},{160,192},{192,224},{224... | collective-permute-start | bytes 552968 | tf_op jit(solution)/shard_map/ppermute | solution.py:341
  24.4 3.2 %collective-permute-start.1 = (bf16[3,48,640]{2,1,0:T(8,128)(2,1)S(1)}, bf16[3,48,640]{2,1,0:T(8,128)(2,1)S(1)}, u32[]{:S(2)}, u32[]{:S(2)}) collective-permute-start(bf16[3,48,640]{2,1,0:T(8,128)(2,1)S(1)} %get-tuple-element.29), channel_id=1, source_target_pairs={{0,224},{32,0},{64,32},{96,64},{128,96},{160,128},{192,160},{224,1... | collective-permute-start | bytes 552968 | tf_op jit(solution)/shard_map/ppermute | solution.py:341
  27.6 10.0 %collective-permute-done.refs_1_.refs_3_ = bf16[3,48,640]{2,1,0:T(8,128)(2,1)S(1)} collective-permute-done((bf16[3,48,640]{2,1,0:T(8,128)(2,1)S(1)}, bf16[3,48,640]{2,1,0:T(8,128)(2,1)S(1)}, u32[]{:S(2)}, u32[]{:S(2)}) %collective-permute-start) | collective-permute-done | bytes 184352 | tf_op jit(solution)/shard_map/ppermute | solution.py:341
  39.8 3.6 %shard_map.114 = bf16[512,2688]{1,0:T(8,128)(2,1)} custom-call(bf16[128,2688]{1,0:T(8,128)(2,1)} %bitcast.11), custom_call_target="tpu_custom_call" | custom-call | bytes 688128 | tf_op jit(solution)/shard_map/pallas_call | solution.py:34
  43.4 8.7 %all-to-all-start.1 = ((bf16[32,16,2688]{2,1,0:T(8,128)(2,1)}), bf16[32,16,2688]{2,1,0:T(8,128)(2,1)S(1)}, u32[]{:S(2)}, u32[]{:S(2)}) async-start(bf16[32,16,2688]{2,1,0:T(8,128)(2,1)} %bitcast.10), calls=%async_computation.1 | async-start | bytes 5505024 | tf_op jit(solution)/shard_map/all_to_all | solution.py:321
  54.5 2.5 %collective-permute-start.3 = (bf16[4,48,2560]{2,1,0:T(8,128)(2,1)}, bf16[4,48,2560]{2,1,0:T(8,128)(2,1)}, u32[]{:S(2)}, u32[]{:S(2)}) collective-permute-start(bf16[4,48,2560]{2,1,0:T(8,128)(2,1)} %pad_maximum_fusion), channel_id=1, source_target_pairs={{0,256},{32,288},{64,320},{96,352},{128,384},{160,416},{192,448},{... | collective-permute-start | bytes 2949128 | tf_op jit(solution)/shard_map/ppermute | solution.py:359
  57.0 4.1 %collective-permute-start.5 = (bf16[3,48,640]{2,1,0:T(8,128)(2,1)S(1)}, bf16[3,48,640]{2,1,0:T(8,128)(2,1)S(1)}, u32[]{:S(2)}, u32[]{:S(2)}) collective-permute-start(bf16[3,48,640]{2,1,0:T(8,128)(2,1)S(1)} %copy-done.10), channel_id=1, source_target_pairs={{0,64},{32,96},{64,128},{96,160},{128,192},{160,224},{192,0},{224,... | collective-permute-start | bytes 552968 | tf_op jit(solution)/shard_map/ppermute | solution.py:341
  61.1 5.5 %collective-permute-start.6 = (bf16[3,48,640]{2,1,0:T(8,128)(2,1)S(1)}, bf16[3,48,640]{2,1,0:T(8,128)(2,1)S(1)}, u32[]{:S(2)}, u32[]{:S(2)}) collective-permute-start(bf16[3,48,640]{2,1,0:T(8,128)(2,1)S(1)} %get-tuple-element.35), channel_id=1, source_target_pairs={{0,96},{32,128},{64,160},{96,192},{128,224},{160,0},{192,32},{224,... | collective-permute-start | bytes 552968 | tf_op jit(solution)/shard_map/ppermute | solution.py:341
  68.5 3.8 %collective-permute-start.4 = (bf16[3,2,48,640]{3,2,1,0:T(8,128)(2,1)}, bf16[3,2,48,640]{3,2,1,0:T(8,128)(2,1)}, u32[]{:S(2)}, u32[]{:S(2)}) collective-permute-start(bf16[3,2,48,640]{3,2,1,0:T(8,128)(2,1)} %shard_map.115), channel_id=1, source_target_pairs={{0,256},{32,288},{64,320},{96,352},{128,384},{160,416},{192,448},{... | collective-permute-start | bytes 1105928 | tf_op jit(solution)/shard_map/ppermute | solution.py:369
  72.3 4.0 %collective-permute-start.7 = (bf16[3,48,640]{2,1,0:T(8,128)(2,1)S(1)}, bf16[3,48,640]{2,1,0:T(8,128)(2,1)S(1)}, u32[]{:S(2)}, u32[]{:S(2)}) collective-permute-start(bf16[3,48,640]{2,1,0:T(8,128)(2,1)S(1)} %get-tuple-element.36), channel_id=1, source_target_pairs={{0,128},{32,160},{64,192},{96,224},{128,0},{160,32},{192,64},{224,... | collective-permute-start | bytes 552968 | tf_op jit(solution)/shard_map/ppermute | solution.py:341
  76.3 5.3 %collective-permute-start.8 = (bf16[3,48,640]{2,1,0:T(8,128)(2,1)S(1)}, bf16[3,48,640]{2,1,0:T(8,128)(2,1)S(1)}, u32[]{:S(2)}, u32[]{:S(2)}) collective-permute-start(bf16[3,48,640]{2,1,0:T(8,128)(2,1)S(1)} %get-tuple-element.37), channel_id=1, source_target_pairs={{0,160},{32,192},{64,224},{96,0},{128,32},{160,64},{192,96},{224,1... | collective-permute-start | bytes 552968 | tf_op jit(solution)/shard_map/ppermute | solution.py:341
  82.0 15.4 %collective-permute-start.9 = (bf16[3,48,640]{2,1,0:T(8,128)(2,1)S(1)}, bf16[3,48,640]{2,1,0:T(8,128)(2,1)S(1)}, u32[]{:S(2)}, u32[]{:S(2)}) collective-permute-start(bf16[3,48,640]{2,1,0:T(8,128)(2,1)S(1)} %get-tuple-element.38), channel_id=1, source_target_pairs={{0,192},{32,224},{64,0},{96,32},{128,64},{160,96},{192,128},{224,1... | collective-permute-start | bytes 552968 | tf_op jit(solution)/shard_map/ppermute | solution.py:341
  97.4 3.2 %collective-permute-done.8.refs_3_.refs_7_ = bf16[3,48,640]{2,1,0:T(8,128)(2,1)S(1)} collective-permute-done((bf16[3,48,640]{2,1,0:T(8,128)(2,1)S(1)}, bf16[3,48,640]{2,1,0:T(8,128)(2,1)S(1)}, u32[]{:S(2)}, u32[]{:S(2)}) %collective-permute-start.8) | collective-permute-done | bytes 184352 | tf_op jit(solution)/shard_map/ppermute | solution.py:341
  100.6 6.2 %collective-permute-done.9.refs_4_.refs_8_ = bf16[3,48,640]{2,1,0:T(8,128)(2,1)S(1)} collective-permute-done((bf16[3,48,640]{2,1,0:T(8,128)(2,1)S(1)}, bf16[3,48,640]{2,1,0:T(8,128)(2,1)S(1)}, u32[]{:S(2)}, u32[]{:S(2)}) %collective-permute-start.9) | collective-permute-done | bytes 184352 | tf_op jit(solution)/shard_map/ppermute | solution.py:341
  107.4 2.1 %shard_map.116 = bf16[5,2,48,640]{3,2,1,0:T(8,128)(2,1)} custom-call(bf16[3,48,640]{2,1,0:T(8,128)(2,1)} %copy-done.12, bf16[3,48,640]{2,1,0:T(8,128)(2,1)} %copy-done.13, bf16[3,48,640]{2,1,0:T(8,128)(2,1)} %copy-done.14, bf16[3,48,640]{2,1,0:T(8,128)(2,1)} %copy-done.15, bf16[3,48,640]{2,1,0:T(8,128)(2,1)} %copy-done.16), custom_call_target="tpu_custom_call" | custom-call | bytes 921600 | tf_op jit(solution)/shard_map/pallas_call | solution.py:34
  109.6 5.1 %collective-permute-done.4.refs_0_ = bf16[3,2,48,640]{3,2,1,0:T(8,128)(2,1)} collective-permute-done((bf16[3,2,48,640]{3,2,1,0:T(8,128)(2,1)}, bf16[3,2,48,640]{3,2,1,0:T(8,128)(2,1)}, u32[]{:S(2)}, u32[]{:S(2)}) %collective-permute-start.4) | collective-permute-done | bytes 368672 | tf_op jit(solution)/shard_map/ppermute | solution.py:369
  117.5 6.4 %shard_map.117 = (bf16[8,4,48,256]{3,2,1,0:T(8,128)(2,1)}, f32[96,512]{1,0:T(8,128)}, f32[96,512]{1,0:T(8,128)}, bf16[512,128]{1,0:T(8,128)(2,1)}) custom-call(bf16[512,2688]{1,0:T(8,128)(2,1)} %bitcast.7, bf16[4,48,2560]{2,1,0:T(8,128)(2,1)} %refs_1_.1, bf16[4,48,2560]{2,1,0:T(8,128)(2,1)} %refs_2_.1, bf16[1,48,2560]{2,1,0:T(8,128)(2,1)} %refs_3_.1, ...), custom_call_target="tpu_custom_call" | custom-call | bytes 6684672 | tf_op jit(solution)/shard_map/pallas_call | solution.py:34
  123.9 5.0 %all-to-all-start.2 = ((bf16[8,4,48,256]{3,2,1,0:T(8,128)(2,1)}), bf16[8,4,48,256]{3,2,1,0:T(8,128)(2,1)}, u32[]{:S(2)}, u32[]{:S(2)}) async-start(bf16[8,4,48,256]{3,2,1,0:T(8,128)(2,1)} %get-tuple-element.42), calls=%async_computation.2 | async-start | bytes 1572864 | tf_op jit(solution)/shard_map/all_to_all | solution.py:321
  128.9 3.6 %collective-permute-start.10 = (bf16[5,2,48,640]{3,2,1,0:T(8,128)(2,1)}, bf16[5,2,48,640]{3,2,1,0:T(8,128)(2,1)}, u32[]{:S(2)}, u32[]{:S(2)}) collective-permute-start(bf16[5,2,48,640]{3,2,1,0:T(8,128)(2,1)} %shard_map.116), channel_id=1, source_target_pairs={{0,256},{32,288},{64,320},{96,352},{128,384},{160,416},{192,448},{... | collective-permute-start | bytes 1843208 | tf_op jit(solution)/shard_map/ppermute | solution.py:371
  132.5 15.6 %collective-permute-done.10.refs_1_ = bf16[5,2,48,640]{3,2,1,0:T(8,128)(2,1)} collective-permute-done((bf16[5,2,48,640]{3,2,1,0:T(8,128)(2,1)}, bf16[5,2,48,640]{3,2,1,0:T(8,128)(2,1)}, u32[]{:S(2)}, u32[]{:S(2)}) %collective-permute-start.10) | collective-permute-done | bytes 614432 | tf_op jit(solution)/shard_map/ppermute | solution.py:371
  148.1 4.2 %all-to-all-done.2.hidden_ref = bf16[8,4,48,256]{3,2,1,0:T(8,128)(2,1)} async-done(((bf16[8,4,48,256]{3,2,1,0:T(8,128)(2,1)}), bf16[8,4,48,256]{3,2,1,0:T(8,128)(2,1)}, u32[]{:S(2)}, u32[]{:S(2)}) %all-to-all-start.2) | async-done | bytes 786464 | tf_op jit(solution)/shard_map/all_to_all | solution.py:321
  152.3 4.4 %shard_map.118 = (bf16[8,96,256]{2,1,0:T(8,128)(2,1)}, bf16[8,48,640]{2,1,0:T(8,128)(2,1)}, bf16[8,48,640]{2,1,0:T(8,128)(2,1)}) custom-call(bf16[8,4,48,256]{3,2,1,0:T(8,128)(2,1)} %all-to-all-done.2.hidden_ref, bf16[512,128]{1,0:T(8,128)(2,1)} %get-tuple-element.43.weight_ref, bf16[3,2,48,640]{3,2,1,0:T(8,128)(2,1)} %collective-permute-done.4.refs_0_, ...), custom_call_target="tpu_custom_call" | custom-call | bytes 3375104 | tf_op jit(solution)/shard_map/pallas_call | solution.py:34
  156.7 3.5 %all-to-all-start.3 = ((bf16[8,96,256]{2,1,0:T(8,128)(2,1)}), bf16[8,96,256]{2,1,0:T(8,128)(2,1)S(1)}, u32[]{:S(2)}, u32[]{:S(2)}) async-start(bf16[8,96,256]{2,1,0:T(8,128)(2,1)} %get-tuple-element.46), calls=%async_computation.3 | async-start | bytes 786432 | tf_op jit(solution)/shard_map/all_to_all | solution.py:321
  160.2 3.6 %collective-permute-start.12 = (bf16[8,48,640]{2,1,0:T(8,128)(2,1)}, bf16[8,48,640]{2,1,0:T(8,128)(2,1)}, u32[]{:S(2)}, u32[]{:S(2)}) collective-permute-start(bf16[8,48,640]{2,1,0:T(8,128)(2,1)} %get-tuple-element.52), channel_id=1, source_target_pairs={{0,256},{32,288},{64,320},{96,352},{128,384},{160,416},{192,448},{... | collective-permute-start | bytes 1474568 | tf_op jit(solution)/shard_map/ppermute | solution.py:402
  163.8 11.4 %all-to-all-done.3.refs_0_ = bf16[8,96,256]{2,1,0:T(8,128)(2,1)S(1)} async-done(((bf16[8,96,256]{2,1,0:T(8,128)(2,1)}), bf16[8,96,256]{2,1,0:T(8,128)(2,1)S(1)}, u32[]{:S(2)}, u32[]{:S(2)}) %all-to-all-start.3) | async-done | bytes 393248 | tf_op jit(solution)/shard_map/all_to_all | solution.py:321
  177.6 3.6 %collective-permute-start.11 = (bf16[2,48,2560]{2,1,0:T(8,128)(2,1)}, bf16[2,48,2560]{2,1,0:T(8,128)(2,1)}, u32[]{:S(2)}, u32[]{:S(2)}) collective-permute-start(bf16[2,48,2560]{2,1,0:T(8,128)(2,1)} %get-tuple-element.50), channel_id=1, source_target_pairs={{0,256},{32,288},{64,320},{96,352},{128,384},{160,416},{192,448},{... | collective-permute-start | bytes 1474568 | tf_op jit(solution)/shard_map/ppermute | solution.py:415
  183.1 3.5 %all-to-all-start.4 = ((bf16[8,48,640]{2,1,0:T(8,128)(2,1)}), bf16[8,48,640]{2,1,0:T(8,128)(2,1)S(1)}, u32[]{:S(2)}, u32[]{:S(2)}) async-start(bf16[8,48,640]{2,1,0:T(8,128)(2,1)} %add_convert_fusion), calls=%async_computation.4 | async-start | bytes 983040 | tf_op jit(solution)/shard_map/all_to_all | solution.py:321
  188.1 6.4 %collective-permute-done.11 = bf16[2,48,2560]{2,1,0:T(8,128)(2,1)} collective-permute-done((bf16[2,48,2560]{2,1,0:T(8,128)(2,1)}, bf16[2,48,2560]{2,1,0:T(8,128)(2,1)}, u32[]{:S(2)}, u32[]{:S(2)}) %collective-permute-start.11) | collective-permute-done | bytes 491552 | tf_op jit(solution)/shard_map/ppermute | solution.py:415
  194.4 2.1 %slice_add_fusion = (f32[1,48,2560]{2,1,0:T(8,128)}, f32[1,48,2560]{2,1,0:T(8,128)}) fusion(f32[2,48,2560]{2,1,0:T(8,128)S(1)} %shard_map.120, bf16[2,48,2560]{2,1,0:T(8,128)(2,1)} %collective-permute-done.11), kind=kLoop, calls=%fused_computation.2 | loop fusion | flops 491520 | bytes 2457600 | tf_op jit(solution)/shard_map/add | solution.py:421
  196.5 7.0 %all-to-all-done.4.parts_ref = bf16[8,48,640]{2,1,0:T(8,128)(2,1)S(1)} async-done(((bf16[8,48,640]{2,1,0:T(8,128)(2,1)}), bf16[8,48,640]{2,1,0:T(8,128)(2,1)S(1)}, u32[]{:S(2)}, u32[]{:S(2)}) %all-to-all-start.4) | async-done | bytes 491552 | tf_op jit(solution)/shard_map/all_to_all | solution.py:321
  (59 shorter events, 21.3 us)
Async XLA Ops:
  0.6 18.4 %copy-start.2 = (bf16[4,48,2560]{2,1,0:T(8,128)(2,1)S(1)}, bf16[4,48,2560]{2,1,0:T(8,128)(2,1)}, u32[]{:S(2)}) copy-start(bf16[4,48,2560]{2,1,0:T(8,128)(2,1)} %down_ref.1) | copy-start | bytes 2949124
  0.6 18.4 %copy-start.4 = (bf16[1,48,2560]{2,1,0:T(8,128)(2,1)S(1)}, bf16[1,48,2560]{2,1,0:T(8,128)(2,1)}, u32[]{:S(2)}) copy-start(bf16[1,48,2560]{2,1,0:T(8,128)(2,1)} %merged_ref.1) | copy-start | bytes 737284
  2.6 36.4 %all-to-all-start = ((bf16[16,8,2688]{2,1,0:T(8,128)(2,1)}), bf16[16,8,2688]{2,1,0:T(8,128)(2,1)S(1)}, u32[]{:S(2)}, u32[]{:S(2)}) async-start(bf16[16,8,2688]{2,1,0:T(8,128)(2,1)} %shard_map.112), calls=%async_computation | async-start | bytes 1376256 | tf_op jit(solution)/shard_map/all_to_all | solution.py:321
  17.0 22.0 %collective-permute-start.2 = (bf16[2,48,2560]{2,1,0:T(8,128)(2,1)S(1)}, bf16[2,48,2560]{2,1,0:T(8,128)(2,1)}, u32[]{:S(2)}, u32[]{:S(2)}) collective-permute-start(bf16[2,48,2560]{2,1,0:T(8,128)(2,1)S(1)} %pad_maximum_fusion.1), channel_id=1, source_target_pairs={{0,256},{32,288},{64,320},{96,352},{128,384},{160,416},{192,448},{... | collective-permute-start | bytes 1474568 | tf_op jit(solution)/shard_map/ppermute | solution.py:343
  20.5 17.0 %collective-permute-start = (bf16[3,48,640]{2,1,0:T(8,128)(2,1)S(1)}, bf16[3,48,640]{2,1,0:T(8,128)(2,1)S(1)}, u32[]{:S(2)}, u32[]{:S(2)}) collective-permute-start(bf16[3,48,640]{2,1,0:T(8,128)(2,1)S(1)} %get-tuple-element.28), channel_id=1, source_target_pairs={{0,32},{32,64},{64,96},{96,128},{128,160},{160,192},{192,224},{224... | collective-permute-start | bytes 552968 | tf_op jit(solution)/shard_map/ppermute | solution.py:341
  24.4 13.2 %collective-permute-start.1 = (bf16[3,48,640]{2,1,0:T(8,128)(2,1)S(1)}, bf16[3,48,640]{2,1,0:T(8,128)(2,1)S(1)}, u32[]{:S(2)}, u32[]{:S(2)}) collective-permute-start(bf16[3,48,640]{2,1,0:T(8,128)(2,1)S(1)} %get-tuple-element.29), channel_id=1, source_target_pairs={{0,224},{32,0},{64,32},{96,64},{128,96},{160,128},{192,160},{224,1... | collective-permute-start | bytes 552968 | tf_op jit(solution)/shard_map/ppermute | solution.py:341
  39.0 0.9 copy-start.11
  43.4 72.5 %all-to-all-start.1 = ((bf16[32,16,2688]{2,1,0:T(8,128)(2,1)}), bf16[32,16,2688]{2,1,0:T(8,128)(2,1)S(1)}, u32[]{:S(2)}, u32[]{:S(2)}) async-start(bf16[32,16,2688]{2,1,0:T(8,128)(2,1)} %bitcast.10), calls=%async_computation.1 | async-start | bytes 5505024 | tf_op jit(solution)/shard_map/all_to_all | solution.py:321
  52.2 4.8 %copy-start.10 = (bf16[3,48,640]{2,1,0:T(8,128)(2,1)S(1)}, bf16[3,48,640]{2,1,0:T(8,128)(2,1)}, u32[]{:S(2)}) copy-start(bf16[3,48,640]{2,1,0:T(8,128)(2,1)} %copy-done.9) | copy-start | bytes 552964
  54.5 55.1 %collective-permute-start.3 = (bf16[4,48,2560]{2,1,0:T(8,128)(2,1)}, bf16[4,48,2560]{2,1,0:T(8,128)(2,1)}, u32[]{:S(2)}, u32[]{:S(2)}) collective-permute-start(bf16[4,48,2560]{2,1,0:T(8,128)(2,1)} %pad_maximum_fusion), channel_id=1, source_target_pairs={{0,256},{32,288},{64,320},{96,352},{128,384},{160,416},{192,448},{... | collective-permute-start | bytes 2949128 | tf_op jit(solution)/shard_map/ppermute | solution.py:359
  57.0 19.3 %collective-permute-start.5 = (bf16[3,48,640]{2,1,0:T(8,128)(2,1)S(1)}, bf16[3,48,640]{2,1,0:T(8,128)(2,1)S(1)}, u32[]{:S(2)}, u32[]{:S(2)}) collective-permute-start(bf16[3,48,640]{2,1,0:T(8,128)(2,1)S(1)} %copy-done.10), channel_id=1, source_target_pairs={{0,64},{32,96},{64,128},{96,160},{128,192},{160,224},{192,0},{224,... | collective-permute-start | bytes 552968 | tf_op jit(solution)/shard_map/ppermute | solution.py:341
  61.1 20.9 %collective-permute-start.6 = (bf16[3,48,640]{2,1,0:T(8,128)(2,1)S(1)}, bf16[3,48,640]{2,1,0:T(8,128)(2,1)S(1)}, u32[]{:S(2)}, u32[]{:S(2)}) collective-permute-start(bf16[3,48,640]{2,1,0:T(8,128)(2,1)S(1)} %get-tuple-element.35), channel_id=1, source_target_pairs={{0,96},{32,128},{64,160},{96,192},{128,224},{160,0},{192,32},{224,... | collective-permute-start | bytes 552968 | tf_op jit(solution)/shard_map/ppermute | solution.py:341
  68.5 46.1 %collective-permute-start.4 = (bf16[3,2,48,640]{3,2,1,0:T(8,128)(2,1)}, bf16[3,2,48,640]{3,2,1,0:T(8,128)(2,1)}, u32[]{:S(2)}, u32[]{:S(2)}) collective-permute-start(bf16[3,2,48,640]{3,2,1,0:T(8,128)(2,1)} %shard_map.115), channel_id=1, source_target_pairs={{0,256},{32,288},{64,320},{96,352},{128,384},{160,416},{192,448},{... | collective-permute-start | bytes 1105928 | tf_op jit(solution)/shard_map/ppermute | solution.py:369
  72.3 25.1 %collective-permute-start.7 = (bf16[3,48,640]{2,1,0:T(8,128)(2,1)S(1)}, bf16[3,48,640]{2,1,0:T(8,128)(2,1)S(1)}, u32[]{:S(2)}, u32[]{:S(2)}) collective-permute-start(bf16[3,48,640]{2,1,0:T(8,128)(2,1)S(1)} %get-tuple-element.36), channel_id=1, source_target_pairs={{0,128},{32,160},{64,192},{96,224},{128,0},{160,32},{192,64},{224,... | collective-permute-start | bytes 552968 | tf_op jit(solution)/shard_map/ppermute | solution.py:341
  76.3 30.5 %copy-start.12 = (bf16[3,48,640]{2,1,0:T(8,128)(2,1)}, bf16[3,48,640]{2,1,0:T(8,128)(2,1)S(1)}, u32[]{:S(2)}) copy-start(bf16[3,48,640]{2,1,0:T(8,128)(2,1)S(1)} %collective-permute-done.5.refs_0_.refs_4_) | copy-start | bytes 552964
  76.3 24.3 %collective-permute-start.8 = (bf16[3,48,640]{2,1,0:T(8,128)(2,1)S(1)}, bf16[3,48,640]{2,1,0:T(8,128)(2,1)S(1)}, u32[]{:S(2)}, u32[]{:S(2)}) collective-permute-start(bf16[3,48,640]{2,1,0:T(8,128)(2,1)S(1)} %get-tuple-element.37), channel_id=1, source_target_pairs={{0,160},{32,192},{64,224},{96,0},{128,32},{160,64},{192,96},{224,1... | collective-permute-start | bytes 552968 | tf_op jit(solution)/shard_map/ppermute | solution.py:341
  82.0 24.7 %copy-start.13 = (bf16[3,48,640]{2,1,0:T(8,128)(2,1)}, bf16[3,48,640]{2,1,0:T(8,128)(2,1)S(1)}, u32[]{:S(2)}) copy-start(bf16[3,48,640]{2,1,0:T(8,128)(2,1)S(1)} %collective-permute-done.6.refs_1_.refs_5_) | copy-start | bytes 552964
  82.0 24.7 %collective-permute-start.9 = (bf16[3,48,640]{2,1,0:T(8,128)(2,1)S(1)}, bf16[3,48,640]{2,1,0:T(8,128)(2,1)S(1)}, u32[]{:S(2)}, u32[]{:S(2)}) collective-permute-start(bf16[3,48,640]{2,1,0:T(8,128)(2,1)S(1)} %get-tuple-element.38), channel_id=1, source_target_pairs={{0,192},{32,224},{64,0},{96,32},{128,64},{160,96},{192,128},{224,1... | collective-permute-start | bytes 552968 | tf_op jit(solution)/shard_map/ppermute | solution.py:341
  97.4 3.2 %copy-start.14 = (bf16[3,48,640]{2,1,0:T(8,128)(2,1)}, bf16[3,48,640]{2,1,0:T(8,128)(2,1)S(1)}, u32[]{:S(2)}) copy-start(bf16[3,48,640]{2,1,0:T(8,128)(2,1)S(1)} %collective-permute-done.7.refs_2_.refs_6_) | copy-start | bytes 552964
  100.6 6.2 %copy-start.15 = (bf16[3,48,640]{2,1,0:T(8,128)(2,1)}, bf16[3,48,640]{2,1,0:T(8,128)(2,1)S(1)}, u32[]{:S(2)}) copy-start(bf16[3,48,640]{2,1,0:T(8,128)(2,1)S(1)} %collective-permute-done.8.refs_3_.refs_7_) | copy-start | bytes 552964
  115.9 1.5 copy-start
  123.8 51.4 %copy-start.1 = (bf16[32,16,2688]{2,1,0:T(8,128)(2,1)S(1)}, bf16[32,16,2688]{2,1,0:T(8,128)(2,1)}, u32[]{:S(2)}) copy-start(bf16[32,16,2688]{2,1,0:T(8,128)(2,1)} %copy-done) | copy-start | bytes 8257540
  123.8 51.4 %copy-start.5 = (f32[96,512]{1,0:T(8,128)S(1)}, f32[96,512]{1,0:T(8,128)}, u32[]{:S(2)}) copy-start(f32[96,512]{1,0:T(8,128)} %get-tuple-element.47.refs_1_) | copy-start | bytes 589828
  123.9 51.4 %copy-start.6 = (f32[96,512]{1,0:T(8,128)S(1)}, f32[96,512]{1,0:T(8,128)}, u32[]{:S(2)}) copy-start(f32[96,512]{1,0:T(8,128)} %get-tuple-element.48.refs_2_) | copy-start | bytes 589828
  123.9 28.4 %all-to-all-start.2 = ((bf16[8,4,48,256]{3,2,1,0:T(8,128)(2,1)}), bf16[8,4,48,256]{3,2,1,0:T(8,128)(2,1)}, u32[]{:S(2)}, u32[]{:S(2)}) async-start(bf16[8,4,48,256]{3,2,1,0:T(8,128)(2,1)} %get-tuple-element.42), calls=%async_computation.2 | async-start | bytes 1572864 | tf_op jit(solution)/shard_map/all_to_all | solution.py:321
  128.9 19.2 %collective-permute-start.10 = (bf16[5,2,48,640]{3,2,1,0:T(8,128)(2,1)}, bf16[5,2,48,640]{3,2,1,0:T(8,128)(2,1)}, u32[]{:S(2)}, u32[]{:S(2)}) collective-permute-start(bf16[5,2,48,640]{3,2,1,0:T(8,128)(2,1)} %shard_map.116), channel_id=1, source_target_pairs={{0,256},{32,288},{64,320},{96,352},{128,384},{160,416},{192,448},{... | collective-permute-start | bytes 1843208 | tf_op jit(solution)/shard_map/ppermute | solution.py:371
  156.7 18.5 %all-to-all-start.3 = ((bf16[8,96,256]{2,1,0:T(8,128)(2,1)}), bf16[8,96,256]{2,1,0:T(8,128)(2,1)S(1)}, u32[]{:S(2)}, u32[]{:S(2)}) async-start(bf16[8,96,256]{2,1,0:T(8,128)(2,1)} %get-tuple-element.46), calls=%async_computation.3 | async-start | bytes 786432 | tf_op jit(solution)/shard_map/all_to_all | solution.py:321
  160.2 21.0 %collective-permute-start.12 = (bf16[8,48,640]{2,1,0:T(8,128)(2,1)}, bf16[8,48,640]{2,1,0:T(8,128)(2,1)}, u32[]{:S(2)}, u32[]{:S(2)}) collective-permute-start(bf16[8,48,640]{2,1,0:T(8,128)(2,1)} %get-tuple-element.52), channel_id=1, source_target_pairs={{0,256},{32,288},{64,320},{96,352},{128,384},{160,416},{192,448},{... | collective-permute-start | bytes 1474568 | tf_op jit(solution)/shard_map/ppermute | solution.py:402
  175.2 6.0 %copy-start.19 = (bf16[8,48,640]{2,1,0:T(8,128)(2,1)S(1)}, bf16[8,48,640]{2,1,0:T(8,128)(2,1)}, u32[]{:S(2)}) copy-start(bf16[8,48,640]{2,1,0:T(8,128)(2,1)} %get-tuple-element.51) | copy-start | bytes 1474564
  177.6 16.9 %collective-permute-start.11 = (bf16[2,48,2560]{2,1,0:T(8,128)(2,1)}, bf16[2,48,2560]{2,1,0:T(8,128)(2,1)}, u32[]{:S(2)}, u32[]{:S(2)}) collective-permute-start(bf16[2,48,2560]{2,1,0:T(8,128)(2,1)} %get-tuple-element.50), channel_id=1, source_target_pairs={{0,256},{32,288},{64,320},{96,352},{128,384},{160,416},{192,448},{... | collective-permute-start | bytes 1474568 | tf_op jit(solution)/shard_map/ppermute | solution.py:415
  183.1 20.4 %all-to-all-start.4 = ((bf16[8,48,640]{2,1,0:T(8,128)(2,1)}), bf16[8,48,640]{2,1,0:T(8,128)(2,1)S(1)}, u32[]{:S(2)}, u32[]{:S(2)}) async-start(bf16[8,48,640]{2,1,0:T(8,128)(2,1)} %add_convert_fusion), calls=%async_computation.4 | async-start | bytes 983040 | tf_op jit(solution)/shard_map/all_to_all | solution.py:321
  186.6 0.9 copy-start.8
  (6 other events, 4.0 us)

commit v12 on v11

--- a/solution.py
+++ b/solution.py
@@ -10,6 +10,7 @@
 EARLY = (1, 7)
 PARTS = ((0, 1, 7), (2, 3, 4, 5, 6))
 RING = 8
+SUM_COST = 2_000_000_000
 SIDE = 128
 BF16 = jnp.bfloat16
 F32 = jnp.float32
@@ -27,7 +28,7 @@
     return lax.dot_general(a, b, (((0,), (0,)), ((), ())), preferred_element_type=F32)
 
 
-def call(kernel, outs, args, far=(), far_outs=(), scratch=(), mib=16):
+def call(kernel, outs, args, far=(), far_outs=(), scratch=(), mib=16, flops=0):
     def space(i, alone):
         return pl.BlockSpec(memory_space=pltpu.HBM if i in alone else pltpu.VMEM)
 
@@ -39,7 +40,7 @@
         scratch_shapes=scratch,
         compiler_params=pltpu.CompilerParams(vmem_limit_bytes=mib * 1024 * 1024),
         cost_estimate=pl.CostEstimate(
-            flops=0,
+            flops=flops,
             bytes_accessed=sum(a.size * a.dtype.itemsize for a in args),
             transcendentals=0,
         ),
@@ -277,6 +278,15 @@
     own_ref[1] = grads[block:]
 
 
+def add_kernel(own_ref, other_ref, gate_ref, up_ref):
+    gate_ref[...] = own_ref[:1] + other_ref[:1].astype(F32)
+    up_ref[...] = own_ref[1:] + other_ref[1:].astype(F32)
+
+
+def down_add_kernel(kept_ref, other_ref, out_ref):
+    out_ref[...] = (kept_ref[...].astype(F32) + other_ref[...].astype(F32)).astype(BF16)
+
+
 def down_sum_kernel(parts_ref, out_ref):
     count, _, piece = parts_ref.shape
     quarters = out_ref.shape[1] // piece
@@ -400,7 +410,13 @@
     )
     parts = exchange(hidden_grad, "dp", rings)
     other_down = lax.ppermute(other_down, "dp", swap)
-    down_grad = (kept_down.astype(F32) + other_down.astype(F32)).astype(BF16)
+    (down_grad,) = call(
+        down_add_kernel,
+        (jax.ShapeDtypeStruct((RING, block, quarter), BF16),),
+        (kept_down, other_down),
+        mib=16,
+        flops=0,
+    )
     other, stack = call(
         lambda *refs: other_kernel(capacity, *refs),
         (
@@ -415,10 +431,10 @@
     other = lax.ppermute(other, "dp", swap)
     down_grad = exchange(down_grad, "dp", rings)
     (grad_down,) = call(
-        down_sum_kernel, (jax.ShapeDtypeStruct((block, features), F32),), (down_grad,)
-    )
-    grad_gate = own[:1] + other[:1].astype(F32)
-    grad_up = own[1:] + other[1:].astype(F32)
+        down_sum_kernel, (jax.ShapeDtypeStruct((block, features), F32),), (down_grad,), flops=SUM_COST
+    )
+    shape = jax.ShapeDtypeStruct((1, block, features), F32)
+    grad_gate, grad_up = call(add_kernel, (shape, shape), (own, other))
     return grad_gate, grad_up, grad_down[None]
 
 

time: 207 us -> 207 us (level)
  other arithmetic: 6.18 us -> 2.23 us
  starting transfers between devices: 94.4 us -> 97.5 us
  Pallas kernels: 23.5 us -> 25.9 us
    all_to_all x5, waiting for transfers between devices: 23.9 us -> 5.33 us  [exchange(): lax.all_to_all(array, axis_name, split_axis=0, concat_axis=0, tiled=True,...]
    ppermute x1, waiting for transfers between devices: 0.01 us -> 13.1 us  [body(): other_down = lax.ppermute(other_down, 'dp', swap)]
    ppermute x1, waiting for transfers between devices: 6.36 us -> 10.9 us  [body(): other = lax.ppermute(other, 'dp', swap)]
    all_to_all x5, starting transfers between devices: 34 us -> 37.1 us  [exchange(): lax.all_to_all(array, axis_name, split_axis=0, concat_axis=0, tiled=True,...]
    pallas_call x10 -> x12, Pallas kernels: 23.5 us -> 25.9 us  [call(): pl.pallas_call(kernel, out_shape=outs, in_specs=[space(i, far) for i in r...]
    add x1 -> x0, other arithmetic: 2.09 us -> none  [body(): grad_up = own[1:] + other[1:].astype(F32)]
    unnamed x40 -> x38, local copies, waits for them, and re-layouts: 7.29 us -> 7.67 us
  transfers between devices with their start and end apart: 18 -> 18, of which waited for: 11 -> 10; matrix products, arithmetic and copies ran while one was open for 4% -> 2% of each run, Pallas kernels for 3% -> 4%
where the time goes in v12:
time: 207 us; the launch traced here: 205 us
  starting transfers between devices  97.5 us (47%)
  waiting for transfers between devices  69.7 us (34%)
  Pallas kernels  25.9 us (13%)
  local copies, waits for them, and re-layouts  8.96 us (4%)
  other arithmetic  2.23 us (1%)
    ppermute x7, starting transfers between devices, body(): lax.ppermute(down[k], 'dp', turns[k])  41.4 us
    all_to_all x5, starting transfers between devices, exchange(): lax.all_to_all(array, axis_name, split_axis=0, concat_axis=0, tiled=True,...  37.1 us
    pallas_call x12, Pallas kernels, call(): pl.pallas_call(kernel, out_shape=outs, in_specs=[space(i, far) for i in r...  25.9 us
    ppermute x7, waiting for transfers between devices, body(): lax.ppermute(down[k], 'dp', turns[k])  19.6 us
    ppermute x1, waiting for transfers between devices, body(): second = lax.ppermute(second, 'dp', swap)  15.6 us
    ppermute x1, waiting for transfers between devices, body(): other_down = lax.ppermute(other_down, 'dp', swap)  13.1 us
    ppermute x1, waiting for transfers between devices, body(): other = lax.ppermute(other, 'dp', swap)  10.9 us
    unnamed x38, local copies, waits for them, and re-layouts  7.67 us
  transfers between devices with their start and end apart: 18, of which 10 were waited for; matrix products, arithmetic and copies ran while one was open for 2% of the time, Pallas kernels for 4%

profile of v12, /device:TPU:6, one launch (start us, length us, event | category | flops | bytes accessed | tf_op | source)
XLA Modules:
  0.0 205.3 jit_solution(14171729571304151913)
XLA Ops:
  0.7 2.0 shard_map.112
  2.6 13.3 %all-to-all-start = ((bf16[16,8,2688]{2,1,0:T(8,128)(2,1)}), bf16[16,8,2688]{2,1,0:T(8,128)(2,1)S(1)}, u32[]{:S(2)}, u32[]{:S(2)}) async-start(bf16[16,8,2688]{2,1,0:T(8,128)(2,1)} %shard_map.112), calls=%async_computation | async-start | bytes 1376256 | tf_op jit(solution)/shard_map/all_to_all | solution.py:331
  17.0 2.0 collective-permute-start.2
  20.6 3.8 %collective-permute-start = (bf16[3,48,640]{2,1,0:T(8,128)(2,1)S(1)}, bf16[3,48,640]{2,1,0:T(8,128)(2,1)S(1)}, u32[]{:S(2)}, u32[]{:S(2)}) collective-permute-start(bf16[3,48,640]{2,1,0:T(8,128)(2,1)S(1)} %get-tuple-element.30), channel_id=1, source_target_pairs={{0,32},{32,64},{64,96},{96,128},{128,160},{160,192},{192,224},{224... | collective-permute-start | bytes 552968 | tf_op jit(solution)/shard_map/ppermute | solution.py:351
  24.4 3.2 %collective-permute-start.1 = (bf16[3,48,640]{2,1,0:T(8,128)(2,1)S(1)}, bf16[3,48,640]{2,1,0:T(8,128)(2,1)S(1)}, u32[]{:S(2)}, u32[]{:S(2)}) collective-permute-start(bf16[3,48,640]{2,1,0:T(8,128)(2,1)S(1)} %get-tuple-element.31), channel_id=1, source_target_pairs={{0,224},{32,0},{64,32},{96,64},{128,96},{160,128},{192,160},{224,1... | collective-permute-start | bytes 552968 | tf_op jit(solution)/shard_map/ppermute | solution.py:351
  27.6 10.0 %collective-permute-done.refs_1_.refs_3_ = bf16[3,48,640]{2,1,0:T(8,128)(2,1)S(1)} collective-permute-done((bf16[3,48,640]{2,1,0:T(8,128)(2,1)S(1)}, bf16[3,48,640]{2,1,0:T(8,128)(2,1)S(1)}, u32[]{:S(2)}, u32[]{:S(2)}) %collective-permute-start) | collective-permute-done | bytes 184352 | tf_op jit(solution)/shard_map/ppermute | solution.py:351
  39.8 3.6 %shard_map.114 = bf16[512,2688]{1,0:T(8,128)(2,1)} custom-call(bf16[128,2688]{1,0:T(8,128)(2,1)} %bitcast.11), custom_call_target="tpu_custom_call" | custom-call | bytes 688128 | tf_op jit(solution)/shard_map/pallas_call | solution.py:35
  43.4 8.7 %all-to-all-start.1 = ((bf16[32,16,2688]{2,1,0:T(8,128)(2,1)}), bf16[32,16,2688]{2,1,0:T(8,128)(2,1)S(1)}, u32[]{:S(2)}, u32[]{:S(2)}) async-start(bf16[32,16,2688]{2,1,0:T(8,128)(2,1)} %bitcast.10), calls=%async_computation.1 | async-start | bytes 5505024 | tf_op jit(solution)/shard_map/all_to_all | solution.py:331
  54.6 2.5 %collective-permute-start.3 = (bf16[4,48,2560]{2,1,0:T(8,128)(2,1)}, bf16[4,48,2560]{2,1,0:T(8,128)(2,1)}, u32[]{:S(2)}, u32[]{:S(2)}) collective-permute-start(bf16[4,48,2560]{2,1,0:T(8,128)(2,1)} %pad_maximum_fusion), channel_id=1, source_target_pairs={{0,256},{32,288},{64,320},{96,352},{128,384},{160,416},{192,448},{... | collective-permute-start | bytes 2949128 | tf_op jit(solution)/shard_map/ppermute | solution.py:369
  57.1 4.2 %collective-permute-start.5 = (bf16[3,48,640]{2,1,0:T(8,128)(2,1)S(1)}, bf16[3,48,640]{2,1,0:T(8,128)(2,1)S(1)}, u32[]{:S(2)}, u32[]{:S(2)}) collective-permute-start(bf16[3,48,640]{2,1,0:T(8,128)(2,1)S(1)} %copy-done.9), channel_id=1, source_target_pairs={{0,64},{32,96},{64,128},{96,160},{128,192},{160,224},{192,0},{224,... | collective-permute-start | bytes 552968 | tf_op jit(solution)/shard_map/ppermute | solution.py:351
  61.3 5.5 %collective-permute-start.6 = (bf16[3,48,640]{2,1,0:T(8,128)(2,1)S(1)}, bf16[3,48,640]{2,1,0:T(8,128)(2,1)S(1)}, u32[]{:S(2)}, u32[]{:S(2)}) collective-permute-start(bf16[3,48,640]{2,1,0:T(8,128)(2,1)S(1)} %get-tuple-element.37), channel_id=1, source_target_pairs={{0,96},{32,128},{64,160},{96,192},{128,224},{160,0},{192,32},{224,... | collective-permute-start | bytes 552968 | tf_op jit(solution)/shard_map/ppermute | solution.py:351
  66.8 1.9 shard_map.115
  68.6 3.7 %collective-permute-start.4 = (bf16[3,2,48,640]{3,2,1,0:T(8,128)(2,1)}, bf16[3,2,48,640]{3,2,1,0:T(8,128)(2,1)}, u32[]{:S(2)}, u32[]{:S(2)}) collective-permute-start(bf16[3,2,48,640]{3,2,1,0:T(8,128)(2,1)} %shard_map.115), channel_id=1, source_target_pairs={{0,256},{32,288},{64,320},{96,352},{128,384},{160,416},{192,448},{... | collective-permute-start | bytes 1105928 | tf_op jit(solution)/shard_map/ppermute | solution.py:379
  72.4 4.0 %collective-permute-start.7 = (bf16[3,48,640]{2,1,0:T(8,128)(2,1)S(1)}, bf16[3,48,640]{2,1,0:T(8,128)(2,1)S(1)}, u32[]{:S(2)}, u32[]{:S(2)}) collective-permute-start(bf16[3,48,640]{2,1,0:T(8,128)(2,1)S(1)} %get-tuple-element.38), channel_id=1, source_target_pairs={{0,128},{32,160},{64,192},{96,224},{128,0},{160,32},{192,64},{224,... | collective-permute-start | bytes 552968 | tf_op jit(solution)/shard_map/ppermute | solution.py:351
  76.4 5.3 %collective-permute-start.8 = (bf16[3,48,640]{2,1,0:T(8,128)(2,1)S(1)}, bf16[3,48,640]{2,1,0:T(8,128)(2,1)S(1)}, u32[]{:S(2)}, u32[]{:S(2)}) collective-permute-start(bf16[3,48,640]{2,1,0:T(8,128)(2,1)S(1)} %get-tuple-element.39), channel_id=1, source_target_pairs={{0,160},{32,192},{64,224},{96,0},{128,32},{160,64},{192,96},{224,1... | collective-permute-start | bytes 552968 | tf_op jit(solution)/shard_map/ppermute | solution.py:351
  82.1 15.4 %collective-permute-start.9 = (bf16[3,48,640]{2,1,0:T(8,128)(2,1)S(1)}, bf16[3,48,640]{2,1,0:T(8,128)(2,1)S(1)}, u32[]{:S(2)}, u32[]{:S(2)}) collective-permute-start(bf16[3,48,640]{2,1,0:T(8,128)(2,1)S(1)} %get-tuple-element.40), channel_id=1, source_target_pairs={{0,192},{32,224},{64,0},{96,32},{128,64},{160,96},{192,128},{224,1... | collective-permute-start | bytes 552968 | tf_op jit(solution)/shard_map/ppermute | solution.py:351
  97.5 3.2 %collective-permute-done.8.refs_3_.refs_7_ = bf16[3,48,640]{2,1,0:T(8,128)(2,1)S(1)} collective-permute-done((bf16[3,48,640]{2,1,0:T(8,128)(2,1)S(1)}, bf16[3,48,640]{2,1,0:T(8,128)(2,1)S(1)}, u32[]{:S(2)}, u32[]{:S(2)}) %collective-permute-start.8) | collective-permute-done | bytes 184352 | tf_op jit(solution)/shard_map/ppermute | solution.py:351
  100.8 6.1 %collective-permute-done.9.refs_4_.refs_8_ = bf16[3,48,640]{2,1,0:T(8,128)(2,1)S(1)} collective-permute-done((bf16[3,48,640]{2,1,0:T(8,128)(2,1)S(1)}, bf16[3,48,640]{2,1,0:T(8,128)(2,1)S(1)}, u32[]{:S(2)}, u32[]{:S(2)}) %collective-permute-start.9) | collective-permute-done | bytes 184352 | tf_op jit(solution)/shard_map/ppermute | solution.py:351
  107.5 2.1 %shard_map.116 = bf16[5,2,48,640]{3,2,1,0:T(8,128)(2,1)} custom-call(bf16[3,48,640]{2,1,0:T(8,128)(2,1)} %copy-done.12, bf16[3,48,640]{2,1,0:T(8,128)(2,1)} %copy-done.13, bf16[3,48,640]{2,1,0:T(8,128)(2,1)} %copy-done.14, bf16[3,48,640]{2,1,0:T(8,128)(2,1)} %copy-done.15, bf16[3,48,640]{2,1,0:T(8,128)(2,1)} %copy-done.16), custom_call_target="tpu_custom_call" | custom-call | bytes 921600 | tf_op jit(solution)/shard_map/pallas_call | solution.py:35
  109.7 5.1 %collective-permute-done.4.refs_0_ = bf16[3,2,48,640]{3,2,1,0:T(8,128)(2,1)} collective-permute-done((bf16[3,2,48,640]{3,2,1,0:T(8,128)(2,1)}, bf16[3,2,48,640]{3,2,1,0:T(8,128)(2,1)}, u32[]{:S(2)}, u32[]{:S(2)}) %collective-permute-start.4) | collective-permute-done | bytes 368672 | tf_op jit(solution)/shard_map/ppermute | solution.py:379
  117.5 6.4 %shard_map.117 = (bf16[8,4,48,256]{3,2,1,0:T(8,128)(2,1)}, f32[96,512]{1,0:T(8,128)}, f32[96,512]{1,0:T(8,128)}, bf16[512,128]{1,0:T(8,128)(2,1)}) custom-call(bf16[512,2688]{1,0:T(8,128)(2,1)} %bitcast.7, bf16[4,48,2560]{2,1,0:T(8,128)(2,1)} %refs_1_.1, bf16[4,48,2560]{2,1,0:T(8,128)(2,1)} %refs_2_.1, bf16[1,48,2560]{2,1,0:T(8,128)(2,1)} %refs_3_.1, ...), custom_call_target="tpu_custom_call" | custom-call | bytes 6684672 | tf_op jit(solution)/shard_map/pallas_call | solution.py:35
  123.9 4.8 %all-to-all-start.2 = ((bf16[8,4,48,256]{3,2,1,0:T(8,128)(2,1)}), bf16[8,4,48,256]{3,2,1,0:T(8,128)(2,1)S(1)}, u32[]{:S(2)}, u32[]{:S(2)}) async-start(bf16[8,4,48,256]{3,2,1,0:T(8,128)(2,1)} %get-tuple-element.44), calls=%async_computation.2 | async-start | bytes 1572864 | tf_op jit(solution)/shard_map/all_to_all | solution.py:331
  128.6 3.6 %collective-permute-start.10 = (bf16[5,2,48,640]{3,2,1,0:T(8,128)(2,1)}, bf16[5,2,48,640]{3,2,1,0:T(8,128)(2,1)}, u32[]{:S(2)}, u32[]{:S(2)}) collective-permute-start(bf16[5,2,48,640]{3,2,1,0:T(8,128)(2,1)} %shard_map.116), channel_id=1, source_target_pairs={{0,256},{32,288},{64,320},{96,352},{128,384},{160,416},{192,448},{... | collective-permute-start | bytes 1843208 | tf_op jit(solution)/shard_map/ppermute | solution.py:381
  132.3 15.6 %collective-permute-done.10.refs_1_ = bf16[5,2,48,640]{3,2,1,0:T(8,128)(2,1)} collective-permute-done((bf16[5,2,48,640]{3,2,1,0:T(8,128)(2,1)}, bf16[5,2,48,640]{3,2,1,0:T(8,128)(2,1)}, u32[]{:S(2)}, u32[]{:S(2)}) %collective-permute-start.10) | collective-permute-done | bytes 614432 | tf_op jit(solution)/shard_map/ppermute | solution.py:381
  147.9 4.1 %all-to-all-done.2.hidden_ref = bf16[8,4,48,256]{3,2,1,0:T(8,128)(2,1)S(1)} async-done(((bf16[8,4,48,256]{3,2,1,0:T(8,128)(2,1)}), bf16[8,4,48,256]{3,2,1,0:T(8,128)(2,1)S(1)}, u32[]{:S(2)}, u32[]{:S(2)}) %all-to-all-start.2) | async-done | bytes 786464 | tf_op jit(solution)/shard_map/all_to_all | solution.py:331
  152.9 4.6 %shard_map.118 = (bf16[8,96,256]{2,1,0:T(8,128)(2,1)}, bf16[8,48,640]{2,1,0:T(8,128)(2,1)}, bf16[8,48,640]{2,1,0:T(8,128)(2,1)}) custom-call(bf16[8,4,48,256]{3,2,1,0:T(8,128)(2,1)} %copy-done.10, bf16[512,128]{1,0:T(8,128)(2,1)} %get-tuple-element.45.weight_ref, bf16[3,2,48,640]{3,2,1,0:T(8,128)(2,1)} %collective-permute-done.4.refs_0_, ...), custom_call_target="tpu_custom_call" | custom-call | bytes 3375104 | tf_op jit(solution)/shard_map/pallas_call | solution.py:35
  157.4 3.5 %all-to-all-start.3 = ((bf16[8,96,256]{2,1,0:T(8,128)(2,1)}), bf16[8,96,256]{2,1,0:T(8,128)(2,1)S(1)}, u32[]{:S(2)}, u32[]{:S(2)}) async-start(bf16[8,96,256]{2,1,0:T(8,128)(2,1)} %get-tuple-element.48), calls=%async_computation.3 | async-start | bytes 786432 | tf_op jit(solution)/shard_map/all_to_all | solution.py:331
  160.9 3.6 %collective-permute-start.12 = (bf16[8,48,640]{2,1,0:T(8,128)(2,1)}, bf16[8,48,640]{2,1,0:T(8,128)(2,1)S(1)}, u32[]{:S(2)}, u32[]{:S(2)}) collective-permute-start(bf16[8,48,640]{2,1,0:T(8,128)(2,1)} %get-tuple-element.56), channel_id=1, source_target_pairs={{0,256},{32,288},{64,320},{96,352},{128,384},{160,416},{192,448},{... | collective-permute-start | bytes 1474568 | tf_op jit(solution)/shard_map/ppermute | solution.py:412
  164.5 13.1 %collective-permute-done.12.other_ref = bf16[8,48,640]{2,1,0:T(8,128)(2,1)S(1)} collective-permute-done((bf16[8,48,640]{2,1,0:T(8,128)(2,1)}, bf16[8,48,640]{2,1,0:T(8,128)(2,1)S(1)}, u32[]{:S(2)}, u32[]{:S(2)}) %collective-permute-start.12) | collective-permute-done | bytes 491552 | tf_op jit(solution)/shard_map/ppermute | solution.py:412
  179.6 6.8 %all-to-all-start.4 = ((bf16[8,48,640]{2,1,0:T(8,128)(2,1)}), bf16[8,48,640]{2,1,0:T(8,128)(2,1)}, u32[]{:S(2)}, u32[]{:S(2)}) async-start(bf16[8,48,640]{2,1,0:T(8,128)(2,1)} %shard_map.122), calls=%async_computation.4 | async-start | bytes 983040 | tf_op jit(solution)/shard_map/all_to_all | solution.py:331
  187.3 3.6 %collective-permute-start.11 = (bf16[2,48,2560]{2,1,0:T(8,128)(2,1)S(1)}, bf16[2,48,2560]{2,1,0:T(8,128)(2,1)S(1)}, u32[]{:S(2)}, u32[]{:S(2)}) collective-permute-start(bf16[2,48,2560]{2,1,0:T(8,128)(2,1)S(1)} %get-tuple-element.52), channel_id=1, source_target_pairs={{0,256},{32,288},{64,320},{96,352},{128,384},{160,416},{192,448},{... | collective-permute-start | bytes 1474568 | tf_op jit(solution)/shard_map/ppermute | solution.py:431
  191.5 10.9 %collective-permute-done.11.other_ref = bf16[2,48,2560]{2,1,0:T(8,128)(2,1)S(1)} collective-permute-done((bf16[2,48,2560]{2,1,0:T(8,128)(2,1)S(1)}, bf16[2,48,2560]{2,1,0:T(8,128)(2,1)S(1)}, u32[]{:S(2)}, u32[]{:S(2)}) %collective-permute-start.11) | collective-permute-done | bytes 491552 | tf_op jit(solution)/shard_map/ppermute | solution.py:431
  (57 shorter events, 18.2 us)
Async XLA Ops:
  0.6 18.4 %copy-start.2 = (bf16[4,48,2560]{2,1,0:T(8,128)(2,1)S(1)}, bf16[4,48,2560]{2,1,0:T(8,128)(2,1)}, u32[]{:S(2)}) copy-start(bf16[4,48,2560]{2,1,0:T(8,128)(2,1)} %down_ref.1) | copy-start | bytes 2949124
  0.6 18.4 %copy-start.5 = (bf16[1,48,2560]{2,1,0:T(8,128)(2,1)S(1)}, bf16[1,48,2560]{2,1,0:T(8,128)(2,1)}, u32[]{:S(2)}) copy-start(bf16[1,48,2560]{2,1,0:T(8,128)(2,1)} %merged_ref.1) | copy-start | bytes 737284
  2.6 36.4 %all-to-all-start = ((bf16[16,8,2688]{2,1,0:T(8,128)(2,1)}), bf16[16,8,2688]{2,1,0:T(8,128)(2,1)S(1)}, u32[]{:S(2)}, u32[]{:S(2)}) async-start(bf16[16,8,2688]{2,1,0:T(8,128)(2,1)} %shard_map.112), calls=%async_computation | async-start | bytes 1376256 | tf_op jit(solution)/shard_map/all_to_all | solution.py:331
  17.0 21.9 %collective-permute-start.2 = (bf16[2,48,2560]{2,1,0:T(8,128)(2,1)S(1)}, bf16[2,48,2560]{2,1,0:T(8,128)(2,1)}, u32[]{:S(2)}, u32[]{:S(2)}) collective-permute-start(bf16[2,48,2560]{2,1,0:T(8,128)(2,1)S(1)} %pad_maximum_fusion.1), channel_id=1, source_target_pairs={{0,256},{32,288},{64,320},{96,352},{128,384},{160,416},{192,448},{... | collective-permute-start | bytes 1474568 | tf_op jit(solution)/shard_map/ppermute | solution.py:353
  20.6 17.0 %collective-permute-start = (bf16[3,48,640]{2,1,0:T(8,128)(2,1)S(1)}, bf16[3,48,640]{2,1,0:T(8,128)(2,1)S(1)}, u32[]{:S(2)}, u32[]{:S(2)}) collective-permute-start(bf16[3,48,640]{2,1,0:T(8,128)(2,1)S(1)} %get-tuple-element.30), channel_id=1, source_target_pairs={{0,32},{32,64},{64,96},{96,128},{128,160},{160,192},{192,224},{224... | collective-permute-start | bytes 552968 | tf_op jit(solution)/shard_map/ppermute | solution.py:351
  24.4 13.2 %collective-permute-start.1 = (bf16[3,48,640]{2,1,0:T(8,128)(2,1)S(1)}, bf16[3,48,640]{2,1,0:T(8,128)(2,1)S(1)}, u32[]{:S(2)}, u32[]{:S(2)}) collective-permute-start(bf16[3,48,640]{2,1,0:T(8,128)(2,1)S(1)} %get-tuple-element.31), channel_id=1, source_target_pairs={{0,224},{32,0},{64,32},{96,64},{128,96},{160,128},{192,160},{224,1... | collective-permute-start | bytes 552968 | tf_op jit(solution)/shard_map/ppermute | solution.py:351
  39.0 0.9 copy-start.11
  43.4 72.5 %all-to-all-start.1 = ((bf16[32,16,2688]{2,1,0:T(8,128)(2,1)}), bf16[32,16,2688]{2,1,0:T(8,128)(2,1)S(1)}, u32[]{:S(2)}, u32[]{:S(2)}) async-start(bf16[32,16,2688]{2,1,0:T(8,128)(2,1)} %bitcast.10), calls=%async_computation.1 | async-start | bytes 5505024 | tf_op jit(solution)/shard_map/all_to_all | solution.py:331
  52.2 4.9 %copy-start.9 = (bf16[3,48,640]{2,1,0:T(8,128)(2,1)S(1)}, bf16[3,48,640]{2,1,0:T(8,128)(2,1)}, u32[]{:S(2)}) copy-start(bf16[3,48,640]{2,1,0:T(8,128)(2,1)} %copy-done.8) | copy-start | bytes 552964
  54.6 55.0 %collective-permute-start.3 = (bf16[4,48,2560]{2,1,0:T(8,128)(2,1)}, bf16[4,48,2560]{2,1,0:T(8,128)(2,1)}, u32[]{:S(2)}, u32[]{:S(2)}) collective-permute-start(bf16[4,48,2560]{2,1,0:T(8,128)(2,1)} %pad_maximum_fusion), channel_id=1, source_target_pairs={{0,256},{32,288},{64,320},{96,352},{128,384},{160,416},{192,448},{... | collective-permute-start | bytes 2949128 | tf_op jit(solution)/shard_map/ppermute | solution.py:369
  57.1 19.3 %collective-permute-start.5 = (bf16[3,48,640]{2,1,0:T(8,128)(2,1)S(1)}, bf16[3,48,640]{2,1,0:T(8,128)(2,1)S(1)}, u32[]{:S(2)}, u32[]{:S(2)}) collective-permute-start(bf16[3,48,640]{2,1,0:T(8,128)(2,1)S(1)} %copy-done.9), channel_id=1, source_target_pairs={{0,64},{32,96},{64,128},{96,160},{128,192},{160,224},{192,0},{224,... | collective-permute-start | bytes 552968 | tf_op jit(solution)/shard_map/ppermute | solution.py:351
  61.3 20.9 %collective-permute-start.6 = (bf16[3,48,640]{2,1,0:T(8,128)(2,1)S(1)}, bf16[3,48,640]{2,1,0:T(8,128)(2,1)S(1)}, u32[]{:S(2)}, u32[]{:S(2)}) collective-permute-start(bf16[3,48,640]{2,1,0:T(8,128)(2,1)S(1)} %get-tuple-element.37), channel_id=1, source_target_pairs={{0,96},{32,128},{64,160},{96,192},{128,224},{160,0},{192,32},{224,... | collective-permute-start | bytes 552968 | tf_op jit(solution)/shard_map/ppermute | solution.py:351
  68.6 46.1 %collective-permute-start.4 = (bf16[3,2,48,640]{3,2,1,0:T(8,128)(2,1)}, bf16[3,2,48,640]{3,2,1,0:T(8,128)(2,1)}, u32[]{:S(2)}, u32[]{:S(2)}) collective-permute-start(bf16[3,2,48,640]{3,2,1,0:T(8,128)(2,1)} %shard_map.115), channel_id=1, source_target_pairs={{0,256},{32,288},{64,320},{96,352},{128,384},{160,416},{192,448},{... | collective-permute-start | bytes 1105928 | tf_op jit(solution)/shard_map/ppermute | solution.py:379
  72.4 25.1 %collective-permute-start.7 = (bf16[3,48,640]{2,1,0:T(8,128)(2,1)S(1)}, bf16[3,48,640]{2,1,0:T(8,128)(2,1)S(1)}, u32[]{:S(2)}, u32[]{:S(2)}) collective-permute-start(bf16[3,48,640]{2,1,0:T(8,128)(2,1)S(1)} %get-tuple-element.38), channel_id=1, source_target_pairs={{0,128},{32,160},{64,192},{96,224},{128,0},{160,32},{192,64},{224,... | collective-permute-start | bytes 552968 | tf_op jit(solution)/shard_map/ppermute | solution.py:351
  76.4 30.4 %copy-start.12 = (bf16[3,48,640]{2,1,0:T(8,128)(2,1)}, bf16[3,48,640]{2,1,0:T(8,128)(2,1)S(1)}, u32[]{:S(2)}) copy-start(bf16[3,48,640]{2,1,0:T(8,128)(2,1)S(1)} %collective-permute-done.5.refs_0_.refs_4_) | copy-start | bytes 552964
  76.4 24.4 %collective-permute-start.8 = (bf16[3,48,640]{2,1,0:T(8,128)(2,1)S(1)}, bf16[3,48,640]{2,1,0:T(8,128)(2,1)S(1)}, u32[]{:S(2)}, u32[]{:S(2)}) collective-permute-start(bf16[3,48,640]{2,1,0:T(8,128)(2,1)S(1)} %get-tuple-element.39), channel_id=1, source_target_pairs={{0,160},{32,192},{64,224},{96,0},{128,32},{160,64},{192,96},{224,1... | collective-permute-start | bytes 552968 | tf_op jit(solution)/shard_map/ppermute | solution.py:351
  82.1 24.7 %copy-start.13 = (bf16[3,48,640]{2,1,0:T(8,128)(2,1)}, bf16[3,48,640]{2,1,0:T(8,128)(2,1)S(1)}, u32[]{:S(2)}) copy-start(bf16[3,48,640]{2,1,0:T(8,128)(2,1)S(1)} %collective-permute-done.6.refs_1_.refs_5_) | copy-start | bytes 552964
  82.1 24.7 %collective-permute-start.9 = (bf16[3,48,640]{2,1,0:T(8,128)(2,1)S(1)}, bf16[3,48,640]{2,1,0:T(8,128)(2,1)S(1)}, u32[]{:S(2)}, u32[]{:S(2)}) collective-permute-start(bf16[3,48,640]{2,1,0:T(8,128)(2,1)S(1)} %get-tuple-element.40), channel_id=1, source_target_pairs={{0,192},{32,224},{64,0},{96,32},{128,64},{160,96},{192,128},{224,1... | collective-permute-start | bytes 552968 | tf_op jit(solution)/shard_map/ppermute | solution.py:351
  97.5 3.3 %copy-start.14 = (bf16[3,48,640]{2,1,0:T(8,128)(2,1)}, bf16[3,48,640]{2,1,0:T(8,128)(2,1)S(1)}, u32[]{:S(2)}) copy-start(bf16[3,48,640]{2,1,0:T(8,128)(2,1)S(1)} %collective-permute-done.7.refs_2_.refs_6_) | copy-start | bytes 552964
  100.8 6.1 %copy-start.15 = (bf16[3,48,640]{2,1,0:T(8,128)(2,1)}, bf16[3,48,640]{2,1,0:T(8,128)(2,1)S(1)}, u32[]{:S(2)}) copy-start(bf16[3,48,640]{2,1,0:T(8,128)(2,1)S(1)} %collective-permute-done.8.refs_3_.refs_7_) | copy-start | bytes 552964
  116.0 1.5 copy-start
  123.9 28.1 %all-to-all-start.2 = ((bf16[8,4,48,256]{3,2,1,0:T(8,128)(2,1)}), bf16[8,4,48,256]{3,2,1,0:T(8,128)(2,1)S(1)}, u32[]{:S(2)}, u32[]{:S(2)}) async-start(bf16[8,4,48,256]{3,2,1,0:T(8,128)(2,1)} %get-tuple-element.44), calls=%async_computation.2 | async-start | bytes 1572864 | tf_op jit(solution)/shard_map/all_to_all | solution.py:331
  128.6 19.2 %collective-permute-start.10 = (bf16[5,2,48,640]{3,2,1,0:T(8,128)(2,1)}, bf16[5,2,48,640]{3,2,1,0:T(8,128)(2,1)}, u32[]{:S(2)}, u32[]{:S(2)}) collective-permute-start(bf16[5,2,48,640]{3,2,1,0:T(8,128)(2,1)} %shard_map.116), channel_id=1, source_target_pairs={{0,256},{32,288},{64,320},{96,352},{128,384},{160,416},{192,448},{... | collective-permute-start | bytes 1843208 | tf_op jit(solution)/shard_map/ppermute | solution.py:381
  152.0 0.9 copy-start.10
  152.9 33.5 %copy-start.1 = (bf16[32,16,2688]{2,1,0:T(8,128)(2,1)S(1)}, bf16[32,16,2688]{2,1,0:T(8,128)(2,1)}, u32[]{:S(2)}) copy-start(bf16[32,16,2688]{2,1,0:T(8,128)(2,1)} %copy-done) | copy-start | bytes 8257540
  152.9 33.5 %copy-start.6 = (f32[96,512]{1,0:T(8,128)S(1)}, f32[96,512]{1,0:T(8,128)}, u32[]{:S(2)}) copy-start(f32[96,512]{1,0:T(8,128)} %get-tuple-element.49.refs_1_) | copy-start | bytes 589828
  152.9 33.6 %copy-start.7 = (f32[96,512]{1,0:T(8,128)S(1)}, f32[96,512]{1,0:T(8,128)}, u32[]{:S(2)}) copy-start(f32[96,512]{1,0:T(8,128)} %get-tuple-element.50.refs_2_) | copy-start | bytes 589828
  157.4 22.1 %all-to-all-start.3 = ((bf16[8,96,256]{2,1,0:T(8,128)(2,1)}), bf16[8,96,256]{2,1,0:T(8,128)(2,1)S(1)}, u32[]{:S(2)}, u32[]{:S(2)}) async-start(bf16[8,96,256]{2,1,0:T(8,128)(2,1)} %get-tuple-element.48), calls=%async_computation.3 | async-start | bytes 786432 | tf_op jit(solution)/shard_map/all_to_all | solution.py:331
  160.9 16.8 %collective-permute-start.12 = (bf16[8,48,640]{2,1,0:T(8,128)(2,1)}, bf16[8,48,640]{2,1,0:T(8,128)(2,1)S(1)}, u32[]{:S(2)}, u32[]{:S(2)}) collective-permute-start(bf16[8,48,640]{2,1,0:T(8,128)(2,1)} %get-tuple-element.56), channel_id=1, source_target_pairs={{0,256},{32,288},{64,320},{96,352},{128,384},{160,416},{192,448},{... | collective-permute-start | bytes 1474568 | tf_op jit(solution)/shard_map/ppermute | solution.py:412
  177.6 1.0 copy-start.4
  179.6 23.9 %all-to-all-start.4 = ((bf16[8,48,640]{2,1,0:T(8,128)(2,1)}), bf16[8,48,640]{2,1,0:T(8,128)(2,1)}, u32[]{:S(2)}, u32[]{:S(2)}) async-start(bf16[8,48,640]{2,1,0:T(8,128)(2,1)} %shard_map.122), calls=%async_computation.4 | async-start | bytes 983040 | tf_op jit(solution)/shard_map/all_to_all | solution.py:331
  187.3 15.1 %collective-permute-start.11 = (bf16[2,48,2560]{2,1,0:T(8,128)(2,1)S(1)}, bf16[2,48,2560]{2,1,0:T(8,128)(2,1)S(1)}, u32[]{:S(2)}, u32[]{:S(2)}) collective-permute-start(bf16[2,48,2560]{2,1,0:T(8,128)(2,1)S(1)} %get-tuple-element.52), channel_id=1, source_target_pairs={{0,256},{32,288},{64,320},{96,352},{128,384},{160,416},{192,448},{... | collective-permute-start | bytes 1474568 | tf_op jit(solution)/shard_map/ppermute | solution.py:431
  (5 other events, 3.4 us)

commit v13 on v11

--- a/solution.py
+++ b/solution.py
@@ -132,72 +132,50 @@
     return value * logistic, logistic * (1.0 + value * (1.0 - logistic))
 
 
-def hidden_kernel(
-    capacity,
-    rows_hbm,
-    t_gate_hbm,
-    t_up_hbm,
-    m_gate_hbm,
-    m_up_hbm,
-    t_come_hbm,
-    m_come_hbm,
-    out_ref,
-    silu_ref,
-    slope_ref,
-    weight_ref,
-    row_buf,
-    weight_buf,
-    sems,
-):
+def weights_kernel(t_gate_ref, t_up_ref, m_gate_ref, m_up_ref, t_come_ref, m_come_ref, out_ref):
     half, _ = place()
-    block = m_gate_hbm.shape[1]
-    units = 2 * block
-    count, wide = row_buf.shape
+    block = m_gate_ref.shape[1]
+
+    def put(at, *parts):
+        for i, part in enumerate(parts):
+            out_ref[at, i * block : (i + 1) * block] = part
+
+    for m in range(PAIR):
+        own = PAIR * half + m
+        put(m, t_gate_ref[own], t_come_ref[m], t_up_ref[own], t_come_ref[PAIR + m])
+    put(PAIR, m_gate_ref[0], m_come_ref[0], m_up_ref[0], m_come_ref[1])
+
+
+def hidden_kernel(capacity, rows_ref, weights_ref, out_ref, slopes_ref, weight_ref):
+    units = weights_ref.shape[1] // 2
+    block = units // 2
+    count, wide = rows_ref.shape
     features = wide - SIDE
     span = count // PAIR
     places = out_ref.shape[0] // PAIR
-
-    def weights(at, *parts):
-        pairs = [(part, weight_buf.at[at, pl.ds(i * block, block)]) for i, part in enumerate(parts)]
-        return start_copies(pairs, sems, 4 * at)
-
-    def gate_up(at):
-        value = dot_nt(weight_buf[at], row_buf[:, :features])
-        return value[:units], value[units:]
-
-    first = start_copies([(rows_hbm, row_buf)], sems, 4 * PAIR + 4)
-    first += weights(
-        PAIR, m_gate_hbm.at[0], m_come_hbm.at[0], m_up_hbm.at[0], m_come_hbm.at[1]
-    )
-    later = []
-    for m in range(PAIR):
-        own = PAIR * half + m
-        later.append(
-            weights(m, t_gate_hbm.at[own], t_come_hbm.at[m], t_up_hbm.at[own], t_come_hbm.at[PAIR + m])
-        )
+    rows = rows_ref[:, :features]
     move = by_teacher(count, capacity, 0)
-    wait_copies(first)
-    gate, up = gate_up(PAIR)
-    silu, slope = silu_split(gate)
-    silu_ref[...] = silu
-    slope_ref[...] = up * slope
-    hidden = [(silu * up).astype(BF16)]
-    for m in range(PAIR):
-        wait_copies(later[m])
-        gate, up = gate_up(m)
-        silu, _ = silu_split(gate)
+    hidden = []
+    for at in range(PAIR + 1):
+        value = dot_nt(weights_ref[at], rows)
+        gate, up = value[:units], value[units:]
+        silu, slope = silu_split(gate)
         hidden.append((silu * up).astype(BF16))
+        if at == PAIR:
+            slopes_ref[0] = silu
+            slopes_ref[1] = up * slope
     hidden = dot_nn(jnp.concatenate(hidden, axis=0), move).astype(BF16)
-    weight_ref[...] = dot_tn(move, row_buf[:, features:]).astype(BF16)
+    weight_ref[...] = dot_tn(move, rows_ref[:, features:]).astype(BF16)
+    student = hidden[PAIR * units :]
     for m in range(PAIR):
         lanes = slice(m * span, (m + 1) * span)
-        first = (1 + m) * units
+        teacher = hidden[m * units : (m + 1) * units]
         for i in range(places):
             at = m * places + i
-            out_ref[at, 0] = hidden[:block, lanes]
-            out_ref[at, 1] = hidden[block:units, lanes]
-            out_ref[at, 2] = hidden[first : first + block, lanes]
-            out_ref[at, 3] = hidden[first + block : first + units, lanes]
+            out_ref[at, 0] = student[:block, lanes]
+            out_ref[at, 1] = student[block:, lanes]
+            out_ref[at, 2] = teacher[:block, lanes]
+            out_ref[at, 3] = teacher[block:, lanes]
 
 
 def share_kernel(down_ref, merged_ref, *out_refs):
@@ -245,7 +223,7 @@
         other_ref[i] = down_grad[k * units + block : (k + 1) * units]
 
 
-def other_kernel(capacity, parts_ref, silu_ref, slope_ref, rows_ref, other_ref, stack_ref):
+def other_kernel(capacity, parts_ref, slopes_ref, rows_ref, other_ref, stack_ref):
     block = other_ref.shape[1]
     places = parts_ref.shape[0] // PAIR
     units = parts_ref.shape[1]
@@ -261,8 +239,8 @@
     total = parts[:units]
     for i in range(1, places):
         total += parts[i * units : (i + 1) * units]
-    gate = (total * slope_ref[...]).astype(BF16)
-    up = (total * silu_ref[...]).astype(BF16)
+    gate = (total * slopes_ref[1]).astype(BF16)
+    up = (total * slopes_ref[0]).astype(BF16)
     stack_ref[...] = jnp.concatenate([gate[:block], up[:block]], axis=0)
     stack = jnp.concatenate([gate[block:], up[block:]], axis=0)
     grads = dot_nn(stack, rows_ref[:, : other_ref.shape[2]])
@@ -351,7 +329,7 @@
         (group,),
         far_outs=(0,),
         scratch=[pltpu.VMEM((rows, wide), BF16), pltpu.SemaphoreType.DMA((8,))],
-        mib=60,
+        mib=52,
     )
     slots = exchange(slots.reshape(experts, PAIR * capacity, wide), "expert").reshape(rows, wide)
 
@@ -367,25 +345,24 @@
         for part in PARTS
     ]
     first = lax.ppermute(first, "dp", swap)
-    slots, t_come, first, second = lax.optimization_barrier((slots, t_come, first, second))
+    (weights,) = call(
+        weights_kernel,
+        (jax.ShapeDtypeStruct((PAIR + 1, 4 * block, features), BF16),),
+        (teacher_gate, teacher_up, merged_gate, merged_up, t_come, m_come),
+        mib=60,
+    )
+    slots, weights, first, second = lax.optimization_barrier((slots, weights, first, second))
     second = lax.ppermute(second, "dp", swap)
 
-    hidden, silu, slope, weight = call(
+    hidden, slopes, weight = call(
         lambda *refs: hidden_kernel(capacity, *refs),
         (
             jax.ShapeDtypeStruct((RING, 4, block, span), BF16),
-            jax.ShapeDtypeStruct((2 * block, rows), F32),
-            jax.ShapeDtypeStruct((2 * block, rows), F32),
+            jax.ShapeDtypeStruct((2, 2 * block, rows), F32),
             jax.ShapeDtypeStruct((rows, SIDE), BF16),
         ),
-        (slots, teacher_gate, teacher_up, merged_gate, merged_up, t_come, m_come),
-        far=range(7),
-        scratch=[
-            pltpu.VMEM((rows, wide), BF16),
-            pltpu.VMEM((PAIR + 1, 4 * block, features), BF16),
-            pltpu.SemaphoreType.DMA((4 * PAIR + 5,)),
-        ],
-        mib=60,
+        (slots, weights),
+        mib=32,
     )
     hidden = exchange(hidden, "dp", rings)
     hidden_grad, kept_down, other_down = call(
@@ -407,7 +384,7 @@
             jax.ShapeDtypeStruct((2, block, features), BF16),
             jax.ShapeDtypeStruct((2 * block, rows), BF16),
         ),
-        (parts, silu, slope, slots),
+        (parts, slopes, slots),
     )
     (own,) = call(
         own_kernel, (jax.ShapeDtypeStruct((2, block, features), F32),), (stack, slots)

time: 207 us -> 203 us (0.981)
  local copies, waits for them, and re-layouts: 8.57 us -> 6.03 us
  waiting for transfers between devices: 70.7 us -> 68.2 us
    ppermute x1, waiting for transfers between devices: 5.1 us -> 0.53 us  [body(): first = lax.ppermute(first, 'dp', swap)]
    unnamed x40 -> x34, local copies, waits for them, and re-layouts: 7.29 us -> 4.75 us
    pallas_call x10 -> x11, Pallas kernels: 23.5 us -> 23.8 us  [call(): pl.pallas_call(kernel, out_shape=outs, in_specs=[space(i, far) for i in r...]
  transfers between devices with their start and end apart: 18 -> 18, of which waited for: 11 -> 11; matrix products, arithmetic and copies ran while one was open for 4% -> 4% of each run, Pallas kernels for 3% -> 5%
where the time goes in v13:
time: 203 us; the launch traced here: 200 us
  starting transfers between devices  94.8 us (47%)
  waiting for transfers between devices  68.2 us (34%)
  Pallas kernels  23.8 us (12%)
  other arithmetic  6.18 us (3%)
  local copies, waits for them, and re-layouts  6.03 us (3%)
    ppermute x7, starting transfers between devices, body(): lax.ppermute(down[k], 'dp', turns[k])  41.4 us
    all_to_all x5, starting transfers between devices, exchange(): lax.all_to_all(array, axis_name, split_axis=0, concat_axis=0, tiled=True,...  34.7 us
    pallas_call x11, Pallas kernels, call(): pl.pallas_call(kernel, out_shape=outs, in_specs=[space(i, far) for i in r...  23.8 us
    all_to_all x5, waiting for transfers between devices, exchange(): lax.all_to_all(array, axis_name, split_axis=0, concat_axis=0, tiled=True,...  23.7 us
    ppermute x7, waiting for transfers between devices, body(): lax.ppermute(down[k], 'dp', turns[k])  21.6 us
    ppermute x1, waiting for transfers between devices, body(): second = lax.ppermute(second, 'dp', swap)  15.6 us
    ppermute x1, waiting for transfers between devices, body(): other = lax.ppermute(other, 'dp', swap)  6.36 us
    unnamed x34, local copies, waits for them, and re-layouts  4.75 us
  transfers between devices with their start and end apart: 18, of which 11 were waited for; matrix products, arithmetic and copies ran while one was open for 4% of the time, Pallas kernels for 5%

profile of v13, /device:TPU:6, one launch (start us, length us, event | category | flops | bytes accessed | tf_op | source)
XLA Modules:
  0.0 199.9 jit_solution(981221788135123954)
XLA Ops:
  2.6 13.3 %all-to-all-start = ((bf16[16,8,2688]{2,1,0:T(8,128)(2,1)}), bf16[16,8,2688]{2,1,0:T(8,128)(2,1)S(1)}, u32[]{:S(2)}, u32[]{:S(2)}) async-start(bf16[16,8,2688]{2,1,0:T(8,128)(2,1)} %shard_map.112), calls=%async_computation | async-start | bytes 1376256 | tf_op jit(solution)/shard_map/all_to_all | solution.py:299
  17.0 2.0 %collective-permute-start.2 = (bf16[2,48,2560]{2,1,0:T(8,128)(2,1)S(1)}, bf16[2,48,2560]{2,1,0:T(8,128)(2,1)}, u32[]{:S(2)}, u32[]{:S(2)}) collective-permute-start(bf16[2,48,2560]{2,1,0:T(8,128)(2,1)S(1)} %pad_maximum_fusion.1), channel_id=1, source_target_pairs={{0,256},{32,288},{64,320},{96,352},{128,384},{160,416},{192,448},{... | collective-permute-start | bytes 1474568 | tf_op jit(solution)/shard_map/ppermute | solution.py:321
  19.9 3.8 %collective-permute-start = (bf16[3,48,640]{2,1,0:T(8,128)(2,1)S(1)}, bf16[3,48,640]{2,1,0:T(8,128)(2,1)S(1)}, u32[]{:S(2)}, u32[]{:S(2)}) collective-permute-start(bf16[3,48,640]{2,1,0:T(8,128)(2,1)S(1)} %get-tuple-element.27), channel_id=1, source_target_pairs={{0,32},{32,64},{64,96},{96,128},{128,160},{160,192},{192,224},{224... | collective-permute-start | bytes 552968 | tf_op jit(solution)/shard_map/ppermute | solution.py:319
  23.7 3.2 %collective-permute-start.1 = (bf16[3,48,640]{2,1,0:T(8,128)(2,1)S(1)}, bf16[3,48,640]{2,1,0:T(8,128)(2,1)S(1)}, u32[]{:S(2)}, u32[]{:S(2)}) collective-permute-start(bf16[3,48,640]{2,1,0:T(8,128)(2,1)S(1)} %get-tuple-element.28), channel_id=1, source_target_pairs={{0,224},{32,0},{64,32},{96,64},{128,96},{160,128},{192,160},{224,1... | collective-permute-start | bytes 552968 | tf_op jit(solution)/shard_map/ppermute | solution.py:319
  26.9 10.6 %collective-permute-done.refs_1_.refs_3_ = bf16[3,48,640]{2,1,0:T(8,128)(2,1)S(1)} collective-permute-done((bf16[3,48,640]{2,1,0:T(8,128)(2,1)S(1)}, bf16[3,48,640]{2,1,0:T(8,128)(2,1)S(1)}, u32[]{:S(2)}, u32[]{:S(2)}) %collective-permute-start) | collective-permute-done | bytes 184352 | tf_op jit(solution)/shard_map/ppermute | solution.py:319
  38.0 2.5 %shard_map.114 = bf16[512,2688]{1,0:T(8,128)(2,1)} custom-call(bf16[128,2688]{1,0:T(8,128)(2,1)S(1)} %bitcast.10), custom_call_target="tpu_custom_call" | custom-call | bytes 688128 | tf_op jit(solution)/shard_map/pallas_call | solution.py:34
  40.5 8.7 %all-to-all-start.1 = ((bf16[32,16,2688]{2,1,0:T(8,128)(2,1)}), bf16[32,16,2688]{2,1,0:T(8,128)(2,1)S(1)}, u32[]{:S(2)}, u32[]{:S(2)}) async-start(bf16[32,16,2688]{2,1,0:T(8,128)(2,1)} %bitcast.11), calls=%async_computation.1 | async-start | bytes 5505024 | tf_op jit(solution)/shard_map/all_to_all | solution.py:299
  51.6 2.9 %collective-permute-start.3 = (bf16[4,48,2560]{2,1,0:T(8,128)(2,1)}, bf16[4,48,2560]{2,1,0:T(8,128)(2,1)}, u32[]{:S(2)}, u32[]{:S(2)}) collective-permute-start(bf16[4,48,2560]{2,1,0:T(8,128)(2,1)} %pad_maximum_fusion), channel_id=1, source_target_pairs={{0,256},{32,288},{64,320},{96,352},{128,384},{160,416},{192,448},{... | collective-permute-start | bytes 2949128 | tf_op jit(solution)/shard_map/ppermute | solution.py:337
  54.5 4.7 %collective-permute-start.5 = (bf16[3,48,640]{2,1,0:T(8,128)(2,1)S(1)}, bf16[3,48,640]{2,1,0:T(8,128)(2,1)S(1)}, u32[]{:S(2)}, u32[]{:S(2)}) collective-permute-start(bf16[3,48,640]{2,1,0:T(8,128)(2,1)S(1)} %copy-done.8), channel_id=1, source_target_pairs={{0,64},{32,96},{64,128},{96,160},{128,192},{160,224},{192,0},{224,... | collective-permute-start | bytes 552968 | tf_op jit(solution)/shard_map/ppermute | solution.py:319
  59.2 5.5 %collective-permute-start.6 = (bf16[3,48,640]{2,1,0:T(8,128)(2,1)S(1)}, bf16[3,48,640]{2,1,0:T(8,128)(2,1)S(1)}, u32[]{:S(2)}, u32[]{:S(2)}) collective-permute-start(bf16[3,48,640]{2,1,0:T(8,128)(2,1)S(1)} %get-tuple-element.35), channel_id=1, source_target_pairs={{0,96},{32,128},{64,160},{96,192},{128,224},{160,0},{192,32},{224,... | collective-permute-start | bytes 552968 | tf_op jit(solution)/shard_map/ppermute | solution.py:319
  66.6 3.1 %collective-permute-start.4 = (bf16[3,2,48,640]{3,2,1,0:T(8,128)(2,1)}, bf16[3,2,48,640]{3,2,1,0:T(8,128)(2,1)}, u32[]{:S(2)}, u32[]{:S(2)}) collective-permute-start(bf16[3,2,48,640]{3,2,1,0:T(8,128)(2,1)} %shard_map.116), channel_id=1, source_target_pairs={{0,256},{32,288},{64,320},{96,352},{128,384},{160,416},{192,448},{... | collective-permute-start | bytes 1105928 | tf_op jit(solution)/shard_map/ppermute | solution.py:347
  69.7 4.7 %collective-permute-start.7 = (bf16[3,48,640]{2,1,0:T(8,128)(2,1)S(1)}, bf16[3,48,640]{2,1,0:T(8,128)(2,1)S(1)}, u32[]{:S(2)}, u32[]{:S(2)}) collective-permute-start(bf16[3,48,640]{2,1,0:T(8,128)(2,1)S(1)} %get-tuple-element.36), channel_id=1, source_target_pairs={{0,128},{32,160},{64,192},{96,224},{128,0},{160,32},{192,64},{224,... | collective-permute-start | bytes 552968 | tf_op jit(solution)/shard_map/ppermute | solution.py:319
  74.4 5.3 %collective-permute-start.8 = (bf16[3,48,640]{2,1,0:T(8,128)(2,1)S(1)}, bf16[3,48,640]{2,1,0:T(8,128)(2,1)S(1)}, u32[]{:S(2)}, u32[]{:S(2)}) collective-permute-start(bf16[3,48,640]{2,1,0:T(8,128)(2,1)S(1)} %get-tuple-element.37), channel_id=1, source_target_pairs={{0,160},{32,192},{64,224},{96,0},{128,32},{160,64},{192,96},{224,1... | collective-permute-start | bytes 552968 | tf_op jit(solution)/shard_map/ppermute | solution.py:319
  79.7 14.1 %collective-permute-start.9 = (bf16[3,48,640]{2,1,0:T(8,128)(2,1)S(1)}, bf16[3,48,640]{2,1,0:T(8,128)(2,1)S(1)}, u32[]{:S(2)}, u32[]{:S(2)}) collective-permute-start(bf16[3,48,640]{2,1,0:T(8,128)(2,1)S(1)} %get-tuple-element.38), channel_id=1, source_target_pairs={{0,192},{32,224},{64,0},{96,32},{128,64},{160,96},{192,128},{224,1... | collective-permute-start | bytes 552968 | tf_op jit(solution)/shard_map/ppermute | solution.py:319
  93.9 5.3 %collective-permute-done.8.refs_3_.refs_7_ = bf16[3,48,640]{2,1,0:T(8,128)(2,1)S(1)} collective-permute-done((bf16[3,48,640]{2,1,0:T(8,128)(2,1)S(1)}, bf16[3,48,640]{2,1,0:T(8,128)(2,1)S(1)}, u32[]{:S(2)}, u32[]{:S(2)}) %collective-permute-start.8) | collective-permute-done | bytes 184352 | tf_op jit(solution)/shard_map/ppermute | solution.py:319
  99.1 5.7 %collective-permute-done.9.refs_4_.refs_8_ = bf16[3,48,640]{2,1,0:T(8,128)(2,1)S(1)} collective-permute-done((bf16[3,48,640]{2,1,0:T(8,128)(2,1)S(1)}, bf16[3,48,640]{2,1,0:T(8,128)(2,1)S(1)}, u32[]{:S(2)}, u32[]{:S(2)}) %collective-permute-start.9) | collective-permute-done | bytes 184352 | tf_op jit(solution)/shard_map/ppermute | solution.py:319
  105.5 2.1 %shard_map.117 = bf16[5,2,48,640]{3,2,1,0:T(8,128)(2,1)} custom-call(bf16[3,48,640]{2,1,0:T(8,128)(2,1)} %copy-done.9, bf16[3,48,640]{2,1,0:T(8,128)(2,1)} %copy-done.10, bf16[3,48,640]{2,1,0:T(8,128)(2,1)} %copy-done.11, bf16[3,48,640]{2,1,0:T(8,128)(2,1)} %copy-done.12, bf16[3,48,640]{2,1,0:T(8,128)(2,1)} %copy-done.13), custom_call_target="tpu_custom_call" | custom-call | bytes 921600 | tf_op jit(solution)/shard_map/pallas_call | solution.py:34
  107.6 3.8 %shard_map.115.refs_1_ = bf16[3,192,2560]{2,1,0:T(8,128)(2,1)} custom-call(bf16[4,48,2560]{2,1,0:T(8,128)(2,1)} %t_gate_ref.1, bf16[4,48,2560]{2,1,0:T(8,128)(2,1)} %t_up_ref.1, bf16[1,48,2560]{2,1,0:T(8,128)(2,1)} %m_gate_ref.1, bf16[1,48,2560]{2,1,0:T(8,128)(2,1)} %m_up_ref.1, bf16[4,48,2560]{2,1,0:T(8,128)(2,1)} %collective-permute-done.3.t_come_ref, ...), custom_call_target="tpu_custom_call" | custom-call | bytes 3932160 | tf_op jit(solution)/shard_map/pallas_call | solution.py:34
  114.9 3.9 %shard_map.118 = (bf16[8,4,48,256]{3,2,1,0:T(8,128)(2,1)}, f32[2,96,512]{2,1,0:T(8,128)S(1)}, bf16[512,128]{1,0:T(8,128)(2,1)S(1)}) custom-call(bf16[512,2688]{1,0:T(8,128)(2,1)S(1)} %bitcast.7, bf16[3,192,2560]{2,1,0:T(8,128)(2,1)S(1)} %copy-done), custom_call_target="tpu_custom_call" | custom-call | bytes 5701632 | tf_op jit(solution)/shard_map/pallas_call | solution.py:34
  118.8 5.7 %all-to-all-start.2 = ((bf16[8,4,48,256]{3,2,1,0:T(8,128)(2,1)}), bf16[8,4,48,256]{3,2,1,0:T(8,128)(2,1)}, u32[]{:S(2)}, u32[]{:S(2)}) async-start(bf16[8,4,48,256]{3,2,1,0:T(8,128)(2,1)} %get-tuple-element.41), calls=%async_computation.2 | async-start | bytes 1572864 | tf_op jit(solution)/shard_map/all_to_all | solution.py:299
  124.5 3.6 %collective-permute-start.10 = (bf16[5,2,48,640]{3,2,1,0:T(8,128)(2,1)}, bf16[5,2,48,640]{3,2,1,0:T(8,128)(2,1)}, u32[]{:S(2)}, u32[]{:S(2)}) collective-permute-start(bf16[5,2,48,640]{3,2,1,0:T(8,128)(2,1)} %shard_map.117), channel_id=1, source_target_pairs={{0,256},{32,288},{64,320},{96,352},{128,384},{160,416},{192,448},{... | collective-permute-start | bytes 1843208 | tf_op jit(solution)/shard_map/ppermute | solution.py:355
  128.1 15.6 %collective-permute-done.10.refs_1_ = bf16[5,2,48,640]{3,2,1,0:T(8,128)(2,1)} collective-permute-done((bf16[5,2,48,640]{3,2,1,0:T(8,128)(2,1)}, bf16[5,2,48,640]{3,2,1,0:T(8,128)(2,1)}, u32[]{:S(2)}, u32[]{:S(2)}) %collective-permute-start.10) | collective-permute-done | bytes 614432 | tf_op jit(solution)/shard_map/ppermute | solution.py:355
  143.7 4.2 %all-to-all-done.2.hidden_ref = bf16[8,4,48,256]{3,2,1,0:T(8,128)(2,1)} async-done(((bf16[8,4,48,256]{3,2,1,0:T(8,128)(2,1)}), bf16[8,4,48,256]{3,2,1,0:T(8,128)(2,1)}, u32[]{:S(2)}, u32[]{:S(2)}) %all-to-all-start.2) | async-done | bytes 786464 | tf_op jit(solution)/shard_map/all_to_all | solution.py:299
  147.9 4.4 %shard_map.119 = (bf16[8,96,256]{2,1,0:T(8,128)(2,1)}, bf16[8,48,640]{2,1,0:T(8,128)(2,1)}, bf16[8,48,640]{2,1,0:T(8,128)(2,1)}) custom-call(bf16[8,4,48,256]{3,2,1,0:T(8,128)(2,1)} %all-to-all-done.2.hidden_ref, bf16[512,128]{1,0:T(8,128)(2,1)} %copy-done.4, bf16[3,2,48,640]{3,2,1,0:T(8,128)(2,1)} %collective-permute-done.4.refs_0_, ...), custom_call_target="tpu_custom_call" | custom-call | bytes 3375104 | tf_op jit(solution)/shard_map/pallas_call | solution.py:34
  152.3 3.5 %all-to-all-start.3 = ((bf16[8,96,256]{2,1,0:T(8,128)(2,1)}), bf16[8,96,256]{2,1,0:T(8,128)(2,1)S(1)}, u32[]{:S(2)}, u32[]{:S(2)}) async-start(bf16[8,96,256]{2,1,0:T(8,128)(2,1)} %get-tuple-element.45), calls=%async_computation.3 | async-start | bytes 786432 | tf_op jit(solution)/shard_map/all_to_all | solution.py:299
  155.8 3.6 %collective-permute-start.12 = (bf16[8,48,640]{2,1,0:T(8,128)(2,1)}, bf16[8,48,640]{2,1,0:T(8,128)(2,1)}, u32[]{:S(2)}, u32[]{:S(2)}) collective-permute-start(bf16[8,48,640]{2,1,0:T(8,128)(2,1)} %get-tuple-element.50), channel_id=1, source_target_pairs={{0,256},{32,288},{64,320},{96,352},{128,384},{160,416},{192,448},{... | collective-permute-start | bytes 1474568 | tf_op jit(solution)/shard_map/ppermute | solution.py:379
  159.4 11.4 %all-to-all-done.3.refs_0_ = bf16[8,96,256]{2,1,0:T(8,128)(2,1)S(1)} async-done(((bf16[8,96,256]{2,1,0:T(8,128)(2,1)}), bf16[8,96,256]{2,1,0:T(8,128)(2,1)S(1)}, u32[]{:S(2)}, u32[]{:S(2)}) %all-to-all-start.3) | async-done | bytes 393248 | tf_op jit(solution)/shard_map/all_to_all | solution.py:299
  173.2 3.6 %collective-permute-start.11 = (bf16[2,48,2560]{2,1,0:T(8,128)(2,1)}, bf16[2,48,2560]{2,1,0:T(8,128)(2,1)}, u32[]{:S(2)}, u32[]{:S(2)}) collective-permute-start(bf16[2,48,2560]{2,1,0:T(8,128)(2,1)} %get-tuple-element.48), channel_id=1, source_target_pairs={{0,256},{32,288},{64,320},{96,352},{128,384},{160,416},{192,448},{... | collective-permute-start | bytes 1474568 | tf_op jit(solution)/shard_map/ppermute | solution.py:392
  178.7 3.5 %all-to-all-start.4 = ((bf16[8,48,640]{2,1,0:T(8,128)(2,1)}), bf16[8,48,640]{2,1,0:T(8,128)(2,1)S(1)}, u32[]{:S(2)}, u32[]{:S(2)}) async-start(bf16[8,48,640]{2,1,0:T(8,128)(2,1)} %add_convert_fusion), calls=%async_computation.4 | async-start | bytes 983040 | tf_op jit(solution)/shard_map/all_to_all | solution.py:299
  183.7 6.4 %collective-permute-done.11 = bf16[2,48,2560]{2,1,0:T(8,128)(2,1)} collective-permute-done((bf16[2,48,2560]{2,1,0:T(8,128)(2,1)}, bf16[2,48,2560]{2,1,0:T(8,128)(2,1)}, u32[]{:S(2)}, u32[]{:S(2)}) %collective-permute-start.11) | collective-permute-done | bytes 491552 | tf_op jit(solution)/shard_map/ppermute | solution.py:392
  190.0 2.1 %slice_add_fusion = (f32[1,48,2560]{2,1,0:T(8,128)}, f32[1,48,2560]{2,1,0:T(8,128)}) fusion(f32[2,48,2560]{2,1,0:T(8,128)S(1)} %shard_map.121, bf16[2,48,2560]{2,1,0:T(8,128)(2,1)} %collective-permute-done.11), kind=kLoop, calls=%fused_computation.2 | loop fusion | flops 491520 | bytes 2457600 | tf_op jit(solution)/shard_map/add | solution.py:398
  192.1 7.0 %all-to-all-done.4.parts_ref = bf16[8,48,640]{2,1,0:T(8,128)(2,1)S(1)} async-done(((bf16[8,48,640]{2,1,0:T(8,128)(2,1)}), bf16[8,48,640]{2,1,0:T(8,128)(2,1)S(1)}, u32[]{:S(2)}, u32[]{:S(2)}) %all-to-all-start.4) | async-done | bytes 491552 | tf_op jit(solution)/shard_map/all_to_all | solution.py:299
  (54 shorter events, 19.1 us)
Async XLA Ops:
  0.6 18.4 %copy-start.1 = (bf16[4,48,2560]{2,1,0:T(8,128)(2,1)S(1)}, bf16[4,48,2560]{2,1,0:T(8,128)(2,1)}, u32[]{:S(2)}) copy-start(bf16[4,48,2560]{2,1,0:T(8,128)(2,1)} %down_ref.1) | copy-start | bytes 2949124
  0.6 18.4 %copy-start.3 = (bf16[1,48,2560]{2,1,0:T(8,128)(2,1)S(1)}, bf16[1,48,2560]{2,1,0:T(8,128)(2,1)}, u32[]{:S(2)}) copy-start(bf16[1,48,2560]{2,1,0:T(8,128)(2,1)} %merged_ref.1) | copy-start | bytes 737284
  2.6 35.4 %all-to-all-start = ((bf16[16,8,2688]{2,1,0:T(8,128)(2,1)}), bf16[16,8,2688]{2,1,0:T(8,128)(2,1)S(1)}, u32[]{:S(2)}, u32[]{:S(2)}) async-start(bf16[16,8,2688]{2,1,0:T(8,128)(2,1)} %shard_map.112), calls=%async_computation | async-start | bytes 1376256 | tf_op jit(solution)/shard_map/all_to_all | solution.py:299
  17.0 21.0 %collective-permute-start.2 = (bf16[2,48,2560]{2,1,0:T(8,128)(2,1)S(1)}, bf16[2,48,2560]{2,1,0:T(8,128)(2,1)}, u32[]{:S(2)}, u32[]{:S(2)}) collective-permute-start(bf16[2,48,2560]{2,1,0:T(8,128)(2,1)S(1)} %pad_maximum_fusion.1), channel_id=1, source_target_pairs={{0,256},{32,288},{64,320},{96,352},{128,384},{160,416},{192,448},{... | collective-permute-start | bytes 1474568 | tf_op jit(solution)/shard_map/ppermute | solution.py:321
  19.9 20.6 %copy-start.7 = (bf16[3,48,640]{2,1,0:T(8,128)(2,1)}, bf16[3,48,640]{2,1,0:T(8,128)(2,1)S(1)}, u32[]{:S(2)}) copy-start(bf16[3,48,640]{2,1,0:T(8,128)(2,1)S(1)} %get-tuple-element.34) | copy-start | bytes 552964
  19.9 17.7 %collective-permute-start = (bf16[3,48,640]{2,1,0:T(8,128)(2,1)S(1)}, bf16[3,48,640]{2,1,0:T(8,128)(2,1)S(1)}, u32[]{:S(2)}, u32[]{:S(2)}) collective-permute-start(bf16[3,48,640]{2,1,0:T(8,128)(2,1)S(1)} %get-tuple-element.27), channel_id=1, source_target_pairs={{0,32},{32,64},{64,96},{96,128},{128,160},{160,192},{192,224},{224... | collective-permute-start | bytes 552968 | tf_op jit(solution)/shard_map/ppermute | solution.py:319
  23.7 13.9 %collective-permute-start.1 = (bf16[3,48,640]{2,1,0:T(8,128)(2,1)S(1)}, bf16[3,48,640]{2,1,0:T(8,128)(2,1)S(1)}, u32[]{:S(2)}, u32[]{:S(2)}) collective-permute-start(bf16[3,48,640]{2,1,0:T(8,128)(2,1)S(1)} %get-tuple-element.28), channel_id=1, source_target_pairs={{0,224},{32,0},{64,32},{96,64},{128,96},{160,128},{192,160},{224,1... | collective-permute-start | bytes 552968 | tf_op jit(solution)/shard_map/ppermute | solution.py:319
  37.6 2.9 %copy-start.14 = (bf16[3,48,640]{2,1,0:T(8,128)(2,1)}, bf16[3,48,640]{2,1,0:T(8,128)(2,1)S(1)}, u32[]{:S(2)}) copy-start(bf16[3,48,640]{2,1,0:T(8,128)(2,1)S(1)} %collective-permute-done.refs_1_.refs_3_) | copy-start | bytes 552964
  37.6 2.9 %copy-start.15 = (bf16[3,48,640]{2,1,0:T(8,128)(2,1)}, bf16[3,48,640]{2,1,0:T(8,128)(2,1)S(1)}, u32[]{:S(2)}) copy-start(bf16[3,48,640]{2,1,0:T(8,128)(2,1)S(1)} %collective-permute-done.1.refs_2_.refs_9_) | copy-start | bytes 552964
  40.5 72.5 %all-to-all-start.1 = ((bf16[32,16,2688]{2,1,0:T(8,128)(2,1)}), bf16[32,16,2688]{2,1,0:T(8,128)(2,1)S(1)}, u32[]{:S(2)}, u32[]{:S(2)}) async-start(bf16[32,16,2688]{2,1,0:T(8,128)(2,1)} %bitcast.11), calls=%async_computation.1 | async-start | bytes 5505024 | tf_op jit(solution)/shard_map/all_to_all | solution.py:299
  49.3 5.2 %copy-start.8 = (bf16[3,48,640]{2,1,0:T(8,128)(2,1)S(1)}, bf16[3,48,640]{2,1,0:T(8,128)(2,1)}, u32[]{:S(2)}) copy-start(bf16[3,48,640]{2,1,0:T(8,128)(2,1)} %copy-done.7) | copy-start | bytes 552964
  51.6 56.0 %collective-permute-start.3 = (bf16[4,48,2560]{2,1,0:T(8,128)(2,1)}, bf16[4,48,2560]{2,1,0:T(8,128)(2,1)}, u32[]{:S(2)}, u32[]{:S(2)}) collective-permute-start(bf16[4,48,2560]{2,1,0:T(8,128)(2,1)} %pad_maximum_fusion), channel_id=1, source_target_pairs={{0,256},{32,288},{64,320},{96,352},{128,384},{160,416},{192,448},{... | collective-permute-start | bytes 2949128 | tf_op jit(solution)/shard_map/ppermute | solution.py:337
  54.5 19.9 %collective-permute-start.5 = (bf16[3,48,640]{2,1,0:T(8,128)(2,1)S(1)}, bf16[3,48,640]{2,1,0:T(8,128)(2,1)S(1)}, u32[]{:S(2)}, u32[]{:S(2)}) collective-permute-start(bf16[3,48,640]{2,1,0:T(8,128)(2,1)S(1)} %copy-done.8), channel_id=1, source_target_pairs={{0,64},{32,96},{64,128},{96,160},{128,192},{160,224},{192,0},{224,... | collective-permute-start | bytes 552968 | tf_op jit(solution)/shard_map/ppermute | solution.py:319
  59.2 20.5 %collective-permute-start.6 = (bf16[3,48,640]{2,1,0:T(8,128)(2,1)S(1)}, bf16[3,48,640]{2,1,0:T(8,128)(2,1)S(1)}, u32[]{:S(2)}, u32[]{:S(2)}) collective-permute-start(bf16[3,48,640]{2,1,0:T(8,128)(2,1)S(1)} %get-tuple-element.35), channel_id=1, source_target_pairs={{0,96},{32,128},{64,160},{96,192},{128,224},{160,0},{192,32},{224,... | collective-permute-start | bytes 552968 | tf_op jit(solution)/shard_map/ppermute | solution.py:319
  66.6 45.4 %collective-permute-start.4 = (bf16[3,2,48,640]{3,2,1,0:T(8,128)(2,1)}, bf16[3,2,48,640]{3,2,1,0:T(8,128)(2,1)}, u32[]{:S(2)}, u32[]{:S(2)}) collective-permute-start(bf16[3,2,48,640]{3,2,1,0:T(8,128)(2,1)} %shard_map.116), channel_id=1, source_target_pairs={{0,256},{32,288},{64,320},{96,352},{128,384},{160,416},{192,448},{... | collective-permute-start | bytes 1105928 | tf_op jit(solution)/shard_map/ppermute | solution.py:347
  69.7 24.2 %collective-permute-start.7 = (bf16[3,48,640]{2,1,0:T(8,128)(2,1)S(1)}, bf16[3,48,640]{2,1,0:T(8,128)(2,1)S(1)}, u32[]{:S(2)}, u32[]{:S(2)}) collective-permute-start(bf16[3,48,640]{2,1,0:T(8,128)(2,1)S(1)} %get-tuple-element.36), channel_id=1, source_target_pairs={{0,128},{32,160},{64,192},{96,224},{128,0},{160,32},{192,64},{224,... | collective-permute-start | bytes 552968 | tf_op jit(solution)/shard_map/ppermute | solution.py:319
  74.4 30.5 %copy-start.9 = (bf16[3,48,640]{2,1,0:T(8,128)(2,1)}, bf16[3,48,640]{2,1,0:T(8,128)(2,1)S(1)}, u32[]{:S(2)}) copy-start(bf16[3,48,640]{2,1,0:T(8,128)(2,1)S(1)} %collective-permute-done.5.refs_0_.refs_4_) | copy-start | bytes 552964
  74.4 24.7 %collective-permute-start.8 = (bf16[3,48,640]{2,1,0:T(8,128)(2,1)S(1)}, bf16[3,48,640]{2,1,0:T(8,128)(2,1)S(1)}, u32[]{:S(2)}, u32[]{:S(2)}) collective-permute-start(bf16[3,48,640]{2,1,0:T(8,128)(2,1)S(1)} %get-tuple-element.37), channel_id=1, source_target_pairs={{0,160},{32,192},{64,224},{96,0},{128,32},{160,64},{192,96},{224,1... | collective-permute-start | bytes 552968 | tf_op jit(solution)/shard_map/ppermute | solution.py:319
  79.7 25.1 %copy-start.10 = (bf16[3,48,640]{2,1,0:T(8,128)(2,1)}, bf16[3,48,640]{2,1,0:T(8,128)(2,1)S(1)}, u32[]{:S(2)}) copy-start(bf16[3,48,640]{2,1,0:T(8,128)(2,1)S(1)} %collective-permute-done.6.refs_1_.refs_5_) | copy-start | bytes 552964
  79.7 25.1 %collective-permute-start.9 = (bf16[3,48,640]{2,1,0:T(8,128)(2,1)S(1)}, bf16[3,48,640]{2,1,0:T(8,128)(2,1)S(1)}, u32[]{:S(2)}, u32[]{:S(2)}) collective-permute-start(bf16[3,48,640]{2,1,0:T(8,128)(2,1)S(1)} %get-tuple-element.38), channel_id=1, source_target_pairs={{0,192},{32,224},{64,0},{96,32},{128,64},{160,96},{192,128},{224,1... | collective-permute-start | bytes 552968 | tf_op jit(solution)/shard_map/ppermute | solution.py:319
  93.8 5.3 %copy-start.11 = (bf16[3,48,640]{2,1,0:T(8,128)(2,1)}, bf16[3,48,640]{2,1,0:T(8,128)(2,1)S(1)}, u32[]{:S(2)}) copy-start(bf16[3,48,640]{2,1,0:T(8,128)(2,1)S(1)} %collective-permute-done.7.refs_2_.refs_6_) | copy-start | bytes 552964
  99.1 5.7 %copy-start.12 = (bf16[3,48,640]{2,1,0:T(8,128)(2,1)}, bf16[3,48,640]{2,1,0:T(8,128)(2,1)S(1)}, u32[]{:S(2)}) copy-start(bf16[3,48,640]{2,1,0:T(8,128)(2,1)S(1)} %collective-permute-done.8.refs_3_.refs_7_) | copy-start | bytes 552964
  113.0 1.8 copy-start
  118.8 29.1 %copy-start.4 = (bf16[512,128]{1,0:T(8,128)(2,1)}, bf16[512,128]{1,0:T(8,128)(2,1)S(1)}, u32[]{:S(2)}) copy-start(bf16[512,128]{1,0:T(8,128)(2,1)S(1)} %get-tuple-element.42.weight_ref) | copy-start | bytes 393220
  118.8 29.1 %all-to-all-start.2 = ((bf16[8,4,48,256]{3,2,1,0:T(8,128)(2,1)}), bf16[8,4,48,256]{3,2,1,0:T(8,128)(2,1)}, u32[]{:S(2)}, u32[]{:S(2)}) async-start(bf16[8,4,48,256]{3,2,1,0:T(8,128)(2,1)} %get-tuple-element.41), calls=%async_computation.2 | async-start | bytes 1572864 | tf_op jit(solution)/shard_map/all_to_all | solution.py:299
  124.5 19.2 %collective-permute-start.10 = (bf16[5,2,48,640]{3,2,1,0:T(8,128)(2,1)}, bf16[5,2,48,640]{3,2,1,0:T(8,128)(2,1)}, u32[]{:S(2)}, u32[]{:S(2)}) collective-permute-start(bf16[5,2,48,640]{3,2,1,0:T(8,128)(2,1)} %shard_map.117), channel_id=1, source_target_pairs={{0,256},{32,288},{64,320},{96,352},{128,384},{160,416},{192,448},{... | collective-permute-start | bytes 1843208 | tf_op jit(solution)/shard_map/ppermute | solution.py:355
  152.3 18.5 %all-to-all-start.3 = ((bf16[8,96,256]{2,1,0:T(8,128)(2,1)}), bf16[8,96,256]{2,1,0:T(8,128)(2,1)S(1)}, u32[]{:S(2)}, u32[]{:S(2)}) async-start(bf16[8,96,256]{2,1,0:T(8,128)(2,1)} %get-tuple-element.45), calls=%async_computation.3 | async-start | bytes 786432 | tf_op jit(solution)/shard_map/all_to_all | solution.py:299
  155.8 21.0 %collective-permute-start.12 = (bf16[8,48,640]{2,1,0:T(8,128)(2,1)}, bf16[8,48,640]{2,1,0:T(8,128)(2,1)}, u32[]{:S(2)}, u32[]{:S(2)}) collective-permute-start(bf16[8,48,640]{2,1,0:T(8,128)(2,1)} %get-tuple-element.50), channel_id=1, source_target_pairs={{0,256},{32,288},{64,320},{96,352},{128,384},{160,416},{192,448},{... | collective-permute-start | bytes 1474568 | tf_op jit(solution)/shard_map/ppermute | solution.py:379
  170.9 5.9 %copy-start.16 = (bf16[8,48,640]{2,1,0:T(8,128)(2,1)S(1)}, bf16[8,48,640]{2,1,0:T(8,128)(2,1)}, u32[]{:S(2)}) copy-start(bf16[8,48,640]{2,1,0:T(8,128)(2,1)} %get-tuple-element.49) | copy-start | bytes 1474564
  173.2 16.9 %collective-permute-start.11 = (bf16[2,48,2560]{2,1,0:T(8,128)(2,1)}, bf16[2,48,2560]{2,1,0:T(8,128)(2,1)}, u32[]{:S(2)}, u32[]{:S(2)}) collective-permute-start(bf16[2,48,2560]{2,1,0:T(8,128)(2,1)} %get-tuple-element.48), channel_id=1, source_target_pairs={{0,256},{32,288},{64,320},{96,352},{128,384},{160,416},{192,448},{... | collective-permute-start | bytes 1474568 | tf_op jit(solution)/shard_map/ppermute | solution.py:392
  178.7 20.4 %all-to-all-start.4 = ((bf16[8,48,640]{2,1,0:T(8,128)(2,1)}), bf16[8,48,640]{2,1,0:T(8,128)(2,1)S(1)}, u32[]{:S(2)}, u32[]{:S(2)}) async-start(bf16[8,48,640]{2,1,0:T(8,128)(2,1)} %add_convert_fusion), calls=%async_computation.4 | async-start | bytes 983040 | tf_op jit(solution)/shard_map/all_to_all | solution.py:299
  182.2 0.9 copy-start.6
  (3 other events, 2.0 us)

commit v14 on v13

--- a/solution.py
+++ b/solution.py
@@ -146,7 +146,12 @@
     put(PAIR, m_gate_ref[0], m_come_ref[0], m_up_ref[0], m_come_ref[1])
 
 
-def hidden_kernel(capacity, rows_ref, weights_ref, out_ref, slopes_ref, weight_ref):
+def hidden_kernel(
+    capacity, rows_ref, weights_hbm, out_ref, slopes_ref, weight_ref, weights_ref, sems
+):
+    copies = start_copies(
+        [(weights_hbm.at[at], weights_ref.at[at]) for at in (2, 0, 1)], sems
+    )
     units = weights_ref.shape[1] // 2
     block = units // 2
     count, wide = rows_ref.shape
@@ -155,12 +160,13 @@
     places = out_ref.shape[0] // PAIR
     rows = rows_ref[:, :features]
     move = by_teacher(count, capacity, 0)
-    hidden = []
-    for at in range(PAIR + 1):
+    hidden = [None] * (PAIR + 1)
+    for at, copy in zip((2, 0, 1), copies):
+        copy.wait()
         value = dot_nt(weights_ref[at], rows)
         gate, up = value[:units], value[units:]
         silu, slope = silu_split(gate)
-        hidden.append((silu * up).astype(BF16))
+        hidden[at] = (silu * up).astype(BF16)
         if at == PAIR:
             slopes_ref[0] = silu
             slopes_ref[1] = up * slope
@@ -362,7 +368,12 @@
             jax.ShapeDtypeStruct((rows, SIDE), BF16),
         ),
         (slots, weights),
-        mib=32,
+        far=(1,),
+        scratch=[
+            pltpu.VMEM((PAIR + 1, 4 * block, features), BF16),
+            pltpu.SemaphoreType.DMA((PAIR + 1,)),
+        ],
+        mib=48,
     )
     hidden = exchange(hidden, "dp", rings)
     hidden_grad, kept_down, other_down = call(

time: 203 us -> 203 us (level)
    unnamed x34 -> x32, local copies, waits for them, and re-layouts: 4.75 us -> 2.93 us
where the time goes in v14:
time: 203 us; the launch traced here: 200 us
  starting transfers between devices  94.8 us (47%)
  waiting for transfers between devices  68.2 us (34%)
  Pallas kernels  25.3 us (12%)
  other arithmetic  6.17 us (3%)
  local copies, waits for them, and re-layouts  4.21 us (2%)
    ppermute x7, starting transfers between devices, body(): lax.ppermute(down[k], 'dp', turns[k])  41.4 us
    all_to_all x5, starting transfers between devices, exchange(): lax.all_to_all(array, axis_name, split_axis=0, concat_axis=0, tiled=True,...  34.7 us
    pallas_call x11, Pallas kernels, call(): pl.pallas_call(kernel, out_shape=outs, in_specs=[space(i, far) for i in r...  25.3 us
    all_to_all x5, waiting for transfers between devices, exchange(): lax.all_to_all(array, axis_name, split_axis=0, concat_axis=0, tiled=True,...  23.7 us
    ppermute x7, waiting for transfers between devices, body(): lax.ppermute(down[k], 'dp', turns[k])  21.6 us
    ppermute x1, waiting for transfers between devices, body(): second = lax.ppermute(second, 'dp', swap)  15.6 us
    ppermute x1, waiting for transfers between devices, body(): other = lax.ppermute(other, 'dp', swap)  6.36 us
  transfers between devices with their start and end apart: 18, of which 11 were waited for; matrix products, arithmetic and copies ran while one was open for 4% of the time, Pallas kernels for 5%

profile of v14, /device:TPU:6, one launch (start us, length us, event | category | flops | bytes accessed | tf_op | source)
XLA Modules:
  0.0 199.7 jit_solution(7530502745727410868)
XLA Ops:
  2.6 13.3 %all-to-all-start = ((bf16[16,8,2688]{2,1,0:T(8,128)(2,1)}), bf16[16,8,2688]{2,1,0:T(8,128)(2,1)S(1)}, u32[]{:S(2)}, u32[]{:S(2)}) async-start(bf16[16,8,2688]{2,1,0:T(8,128)(2,1)} %shard_map.112), calls=%async_computation | async-start | bytes 1376256 | tf_op jit(solution)/shard_map/all_to_all | solution.py:305
  17.0 2.0 %collective-permute-start.2 = (bf16[2,48,2560]{2,1,0:T(8,128)(2,1)S(1)}, bf16[2,48,2560]{2,1,0:T(8,128)(2,1)}, u32[]{:S(2)}, u32[]{:S(2)}) collective-permute-start(bf16[2,48,2560]{2,1,0:T(8,128)(2,1)S(1)} %pad_maximum_fusion.1), channel_id=1, source_target_pairs={{0,256},{32,288},{64,320},{96,352},{128,384},{160,416},{192,448},{... | collective-permute-start | bytes 1474568 | tf_op jit(solution)/shard_map/ppermute | solution.py:327
  19.9 3.8 %collective-permute-start = (bf16[3,48,640]{2,1,0:T(8,128)(2,1)S(1)}, bf16[3,48,640]{2,1,0:T(8,128)(2,1)S(1)}, u32[]{:S(2)}, u32[]{:S(2)}) collective-permute-start(bf16[3,48,640]{2,1,0:T(8,128)(2,1)S(1)} %get-tuple-element.27), channel_id=1, source_target_pairs={{0,32},{32,64},{64,96},{96,128},{128,160},{160,192},{192,224},{224... | collective-permute-start | bytes 552968 | tf_op jit(solution)/shard_map/ppermute | solution.py:325
  23.7 3.2 %collective-permute-start.1 = (bf16[3,48,640]{2,1,0:T(8,128)(2,1)S(1)}, bf16[3,48,640]{2,1,0:T(8,128)(2,1)S(1)}, u32[]{:S(2)}, u32[]{:S(2)}) collective-permute-start(bf16[3,48,640]{2,1,0:T(8,128)(2,1)S(1)} %get-tuple-element.28), channel_id=1, source_target_pairs={{0,224},{32,0},{64,32},{96,64},{128,96},{160,128},{192,160},{224,1... | collective-permute-start | bytes 552968 | tf_op jit(solution)/shard_map/ppermute | solution.py:325
  26.9 10.7 %collective-permute-done.refs_1_.refs_3_ = bf16[3,48,640]{2,1,0:T(8,128)(2,1)S(1)} collective-permute-done((bf16[3,48,640]{2,1,0:T(8,128)(2,1)S(1)}, bf16[3,48,640]{2,1,0:T(8,128)(2,1)S(1)}, u32[]{:S(2)}, u32[]{:S(2)}) %collective-permute-start) | collective-permute-done | bytes 184352 | tf_op jit(solution)/shard_map/ppermute | solution.py:325
  38.0 2.6 %shard_map.114 = bf16[512,2688]{1,0:T(8,128)(2,1)} custom-call(bf16[128,2688]{1,0:T(8,128)(2,1)S(1)} %bitcast.10), custom_call_target="tpu_custom_call" | custom-call | bytes 688128 | tf_op jit(solution)/shard_map/pallas_call | solution.py:34
  40.6 8.7 %all-to-all-start.1 = ((bf16[32,16,2688]{2,1,0:T(8,128)(2,1)}), bf16[32,16,2688]{2,1,0:T(8,128)(2,1)S(1)}, u32[]{:S(2)}, u32[]{:S(2)}) async-start(bf16[32,16,2688]{2,1,0:T(8,128)(2,1)} %bitcast.11), calls=%async_computation.1 | async-start | bytes 5505024 | tf_op jit(solution)/shard_map/all_to_all | solution.py:305
  51.7 2.9 %collective-permute-start.3 = (bf16[4,48,2560]{2,1,0:T(8,128)(2,1)}, bf16[4,48,2560]{2,1,0:T(8,128)(2,1)}, u32[]{:S(2)}, u32[]{:S(2)}) collective-permute-start(bf16[4,48,2560]{2,1,0:T(8,128)(2,1)} %pad_maximum_fusion), channel_id=1, source_target_pairs={{0,256},{32,288},{64,320},{96,352},{128,384},{160,416},{192,448},{... | collective-permute-start | bytes 2949128 | tf_op jit(solution)/shard_map/ppermute | solution.py:343
  54.6 4.7 %collective-permute-start.5 = (bf16[3,48,640]{2,1,0:T(8,128)(2,1)S(1)}, bf16[3,48,640]{2,1,0:T(8,128)(2,1)S(1)}, u32[]{:S(2)}, u32[]{:S(2)}) collective-permute-start(bf16[3,48,640]{2,1,0:T(8,128)(2,1)S(1)} %copy-done.7), channel_id=1, source_target_pairs={{0,64},{32,96},{64,128},{96,160},{128,192},{160,224},{192,0},{224,... | collective-permute-start | bytes 552968 | tf_op jit(solution)/shard_map/ppermute | solution.py:325
  59.3 5.5 %collective-permute-start.6 = (bf16[3,48,640]{2,1,0:T(8,128)(2,1)S(1)}, bf16[3,48,640]{2,1,0:T(8,128)(2,1)S(1)}, u32[]{:S(2)}, u32[]{:S(2)}) collective-permute-start(bf16[3,48,640]{2,1,0:T(8,128)(2,1)S(1)} %get-tuple-element.35), channel_id=1, source_target_pairs={{0,96},{32,128},{64,160},{96,192},{128,224},{160,0},{192,32},{224,... | collective-permute-start | bytes 552968 | tf_op jit(solution)/shard_map/ppermute | solution.py:325
  66.7 3.1 %collective-permute-start.4 = (bf16[3,2,48,640]{3,2,1,0:T(8,128)(2,1)}, bf16[3,2,48,640]{3,2,1,0:T(8,128)(2,1)}, u32[]{:S(2)}, u32[]{:S(2)}) collective-permute-start(bf16[3,2,48,640]{3,2,1,0:T(8,128)(2,1)} %shard_map.116), channel_id=1, source_target_pairs={{0,256},{32,288},{64,320},{96,352},{128,384},{160,416},{192,448},{... | collective-permute-start | bytes 1105928 | tf_op jit(solution)/shard_map/ppermute | solution.py:353
  69.7 4.7 %collective-permute-start.7 = (bf16[3,48,640]{2,1,0:T(8,128)(2,1)S(1)}, bf16[3,48,640]{2,1,0:T(8,128)(2,1)S(1)}, u32[]{:S(2)}, u32[]{:S(2)}) collective-permute-start(bf16[3,48,640]{2,1,0:T(8,128)(2,1)S(1)} %get-tuple-element.36), channel_id=1, source_target_pairs={{0,128},{32,160},{64,192},{96,224},{128,0},{160,32},{192,64},{224,... | collective-permute-start | bytes 552968 | tf_op jit(solution)/shard_map/ppermute | solution.py:325
  74.4 5.3 %collective-permute-start.8 = (bf16[3,48,640]{2,1,0:T(8,128)(2,1)S(1)}, bf16[3,48,640]{2,1,0:T(8,128)(2,1)S(1)}, u32[]{:S(2)}, u32[]{:S(2)}) collective-permute-start(bf16[3,48,640]{2,1,0:T(8,128)(2,1)S(1)} %get-tuple-element.37), channel_id=1, source_target_pairs={{0,160},{32,192},{64,224},{96,0},{128,32},{160,64},{192,96},{224,1... | collective-permute-start | bytes 552968 | tf_op jit(solution)/shard_map/ppermute | solution.py:325
  79.8 14.1 %collective-permute-start.9 = (bf16[3,48,640]{2,1,0:T(8,128)(2,1)S(1)}, bf16[3,48,640]{2,1,0:T(8,128)(2,1)S(1)}, u32[]{:S(2)}, u32[]{:S(2)}) collective-permute-start(bf16[3,48,640]{2,1,0:T(8,128)(2,1)S(1)} %get-tuple-element.38), channel_id=1, source_target_pairs={{0,192},{32,224},{64,0},{96,32},{128,64},{160,96},{192,128},{224,1... | collective-permute-start | bytes 552968 | tf_op jit(solution)/shard_map/ppermute | solution.py:325
  93.9 5.2 %collective-permute-done.8.refs_3_.refs_7_ = bf16[3,48,640]{2,1,0:T(8,128)(2,1)S(1)} collective-permute-done((bf16[3,48,640]{2,1,0:T(8,128)(2,1)S(1)}, bf16[3,48,640]{2,1,0:T(8,128)(2,1)S(1)}, u32[]{:S(2)}, u32[]{:S(2)}) %collective-permute-start.8) | collective-permute-done | bytes 184352 | tf_op jit(solution)/shard_map/ppermute | solution.py:325
  99.2 5.7 %collective-permute-done.9.refs_4_.refs_8_ = bf16[3,48,640]{2,1,0:T(8,128)(2,1)S(1)} collective-permute-done((bf16[3,48,640]{2,1,0:T(8,128)(2,1)S(1)}, bf16[3,48,640]{2,1,0:T(8,128)(2,1)S(1)}, u32[]{:S(2)}, u32[]{:S(2)}) %collective-permute-start.9) | collective-permute-done | bytes 184352 | tf_op jit(solution)/shard_map/ppermute | solution.py:325
  105.6 2.1 %shard_map.117 = bf16[5,2,48,640]{3,2,1,0:T(8,128)(2,1)} custom-call(bf16[3,48,640]{2,1,0:T(8,128)(2,1)} %copy-done.8, bf16[3,48,640]{2,1,0:T(8,128)(2,1)} %copy-done.9, bf16[3,48,640]{2,1,0:T(8,128)(2,1)} %copy-done.10, bf16[3,48,640]{2,1,0:T(8,128)(2,1)} %copy-done.11, bf16[3,48,640]{2,1,0:T(8,128)(2,1)} %copy-done.12), custom_call_target="tpu_custom_call" | custom-call | bytes 921600 | tf_op jit(solution)/shard_map/pallas_call | solution.py:34
  107.7 3.8 %shard_map.115.refs_1_ = bf16[3,192,2560]{2,1,0:T(8,128)(2,1)} custom-call(bf16[4,48,2560]{2,1,0:T(8,128)(2,1)} %t_gate_ref.1, bf16[4,48,2560]{2,1,0:T(8,128)(2,1)} %t_up_ref.1, bf16[1,48,2560]{2,1,0:T(8,128)(2,1)} %m_gate_ref.1, bf16[1,48,2560]{2,1,0:T(8,128)(2,1)} %m_up_ref.1, bf16[4,48,2560]{2,1,0:T(8,128)(2,1)} %collective-permute-done.3.t_come_ref, ...), custom_call_target="tpu_custom_call" | custom-call | bytes 3932160 | tf_op jit(solution)/shard_map/pallas_call | solution.py:34
  113.1 5.4 %shard_map.118 = (bf16[8,4,48,256]{3,2,1,0:T(8,128)(2,1)}, f32[2,96,512]{2,1,0:T(8,128)S(1)}, bf16[512,128]{1,0:T(8,128)(2,1)S(1)}) custom-call(bf16[512,2688]{1,0:T(8,128)(2,1)S(1)} %bitcast.7, bf16[3,192,2560]{2,1,0:T(8,128)(2,1)} %shard_map.115.refs_1_), custom_call_target="tpu_custom_call" | custom-call | bytes 5701632 | tf_op jit(solution)/shard_map/pallas_call | solution.py:34
  118.5 5.7 %all-to-all-start.2 = ((bf16[8,4,48,256]{3,2,1,0:T(8,128)(2,1)}), bf16[8,4,48,256]{3,2,1,0:T(8,128)(2,1)}, u32[]{:S(2)}, u32[]{:S(2)}) async-start(bf16[8,4,48,256]{3,2,1,0:T(8,128)(2,1)} %get-tuple-element.41), calls=%async_computation.2 | async-start | bytes 1572864 | tf_op jit(solution)/shard_map/all_to_all | solution.py:305
  124.2 3.6 %collective-permute-start.10 = (bf16[5,2,48,640]{3,2,1,0:T(8,128)(2,1)}, bf16[5,2,48,640]{3,2,1,0:T(8,128)(2,1)}, u32[]{:S(2)}, u32[]{:S(2)}) collective-permute-start(bf16[5,2,48,640]{3,2,1,0:T(8,128)(2,1)} %shard_map.117), channel_id=1, source_target_pairs={{0,256},{32,288},{64,320},{96,352},{128,384},{160,416},{192,448},{... | collective-permute-start | bytes 1843208 | tf_op jit(solution)/shard_map/ppermute | solution.py:361
  127.8 15.6 %collective-permute-done.10.refs_1_ = bf16[5,2,48,640]{3,2,1,0:T(8,128)(2,1)} collective-permute-done((bf16[5,2,48,640]{3,2,1,0:T(8,128)(2,1)}, bf16[5,2,48,640]{3,2,1,0:T(8,128)(2,1)}, u32[]{:S(2)}, u32[]{:S(2)}) %collective-permute-start.10) | collective-permute-done | bytes 614432 | tf_op jit(solution)/shard_map/ppermute | solution.py:361
  143.5 4.2 %all-to-all-done.2.hidden_ref = bf16[8,4,48,256]{3,2,1,0:T(8,128)(2,1)} async-done(((bf16[8,4,48,256]{3,2,1,0:T(8,128)(2,1)}), bf16[8,4,48,256]{3,2,1,0:T(8,128)(2,1)}, u32[]{:S(2)}, u32[]{:S(2)}) %all-to-all-start.2) | async-done | bytes 786464 | tf_op jit(solution)/shard_map/all_to_all | solution.py:305
  147.7 4.4 %shard_map.119 = (bf16[8,96,256]{2,1,0:T(8,128)(2,1)}, bf16[8,48,640]{2,1,0:T(8,128)(2,1)}, bf16[8,48,640]{2,1,0:T(8,128)(2,1)}) custom-call(bf16[8,4,48,256]{3,2,1,0:T(8,128)(2,1)} %all-to-all-done.2.hidden_ref, bf16[512,128]{1,0:T(8,128)(2,1)} %copy-done.3, bf16[3,2,48,640]{3,2,1,0:T(8,128)(2,1)} %collective-permute-done.4.refs_0_, ...), custom_call_target="tpu_custom_call" | custom-call | bytes 3375104 | tf_op jit(solution)/shard_map/pallas_call | solution.py:34
  152.1 3.5 %all-to-all-start.3 = ((bf16[8,96,256]{2,1,0:T(8,128)(2,1)}), bf16[8,96,256]{2,1,0:T(8,128)(2,1)S(1)}, u32[]{:S(2)}, u32[]{:S(2)}) async-start(bf16[8,96,256]{2,1,0:T(8,128)(2,1)} %get-tuple-element.45), calls=%async_computation.3 | async-start | bytes 786432 | tf_op jit(solution)/shard_map/all_to_all | solution.py:305
  155.6 3.6 %collective-permute-start.12 = (bf16[8,48,640]{2,1,0:T(8,128)(2,1)}, bf16[8,48,640]{2,1,0:T(8,128)(2,1)}, u32[]{:S(2)}, u32[]{:S(2)}) collective-permute-start(bf16[8,48,640]{2,1,0:T(8,128)(2,1)} %get-tuple-element.50), channel_id=1, source_target_pairs={{0,256},{32,288},{64,320},{96,352},{128,384},{160,416},{192,448},{... | collective-permute-start | bytes 1474568 | tf_op jit(solution)/shard_map/ppermute | solution.py:390
  159.2 11.4 %all-to-all-done.3.refs_0_ = bf16[8,96,256]{2,1,0:T(8,128)(2,1)S(1)} async-done(((bf16[8,96,256]{2,1,0:T(8,128)(2,1)}), bf16[8,96,256]{2,1,0:T(8,128)(2,1)S(1)}, u32[]{:S(2)}, u32[]{:S(2)}) %all-to-all-start.3) | async-done | bytes 393248 | tf_op jit(solution)/shard_map/all_to_all | solution.py:305
  173.0 3.6 %collective-permute-start.11 = (bf16[2,48,2560]{2,1,0:T(8,128)(2,1)}, bf16[2,48,2560]{2,1,0:T(8,128)(2,1)}, u32[]{:S(2)}, u32[]{:S(2)}) collective-permute-start(bf16[2,48,2560]{2,1,0:T(8,128)(2,1)} %get-tuple-element.48), channel_id=1, source_target_pairs={{0,256},{32,288},{64,320},{96,352},{128,384},{160,416},{192,448},{... | collective-permute-start | bytes 1474568 | tf_op jit(solution)/shard_map/ppermute | solution.py:403
  178.5 3.5 %all-to-all-start.4 = ((bf16[8,48,640]{2,1,0:T(8,128)(2,1)}), bf16[8,48,640]{2,1,0:T(8,128)(2,1)S(1)}, u32[]{:S(2)}, u32[]{:S(2)}) async-start(bf16[8,48,640]{2,1,0:T(8,128)(2,1)} %add_convert_fusion), calls=%async_computation.4 | async-start | bytes 983040 | tf_op jit(solution)/shard_map/all_to_all | solution.py:305
  183.4 6.4 %collective-permute-done.11 = bf16[2,48,2560]{2,1,0:T(8,128)(2,1)} collective-permute-done((bf16[2,48,2560]{2,1,0:T(8,128)(2,1)}, bf16[2,48,2560]{2,1,0:T(8,128)(2,1)}, u32[]{:S(2)}, u32[]{:S(2)}) %collective-permute-start.11) | collective-permute-done | bytes 491552 | tf_op jit(solution)/shard_map/ppermute | solution.py:403
  189.8 2.1 %slice_add_fusion = (f32[1,48,2560]{2,1,0:T(8,128)}, f32[1,48,2560]{2,1,0:T(8,128)}) fusion(f32[2,48,2560]{2,1,0:T(8,128)S(1)} %shard_map.121, bf16[2,48,2560]{2,1,0:T(8,128)(2,1)} %collective-permute-done.11), kind=kLoop, calls=%fused_computation.2 | loop fusion | flops 491520 | bytes 2457600 | tf_op jit(solution)/shard_map/add | solution.py:409
  191.9 7.0 %all-to-all-done.4.parts_ref = bf16[8,48,640]{2,1,0:T(8,128)(2,1)S(1)} async-done(((bf16[8,48,640]{2,1,0:T(8,128)(2,1)}), bf16[8,48,640]{2,1,0:T(8,128)(2,1)S(1)}, u32[]{:S(2)}, u32[]{:S(2)}) %all-to-all-start.4) | async-done | bytes 491552 | tf_op jit(solution)/shard_map/all_to_all | solution.py:305
  (52 shorter events, 17.3 us)
Async XLA Ops:
  0.6 18.4 %copy-start = (bf16[4,48,2560]{2,1,0:T(8,128)(2,1)S(1)}, bf16[4,48,2560]{2,1,0:T(8,128)(2,1)}, u32[]{:S(2)}) copy-start(bf16[4,48,2560]{2,1,0:T(8,128)(2,1)} %down_ref.1) | copy-start | bytes 2949124
  0.6 18.4 %copy-start.2 = (bf16[1,48,2560]{2,1,0:T(8,128)(2,1)S(1)}, bf16[1,48,2560]{2,1,0:T(8,128)(2,1)}, u32[]{:S(2)}) copy-start(bf16[1,48,2560]{2,1,0:T(8,128)(2,1)} %merged_ref.1) | copy-start | bytes 737284
  2.6 35.4 %all-to-all-start = ((bf16[16,8,2688]{2,1,0:T(8,128)(2,1)}), bf16[16,8,2688]{2,1,0:T(8,128)(2,1)S(1)}, u32[]{:S(2)}, u32[]{:S(2)}) async-start(bf16[16,8,2688]{2,1,0:T(8,128)(2,1)} %shard_map.112), calls=%async_computation | async-start | bytes 1376256 | tf_op jit(solution)/shard_map/all_to_all | solution.py:305
  17.0 21.0 %collective-permute-start.2 = (bf16[2,48,2560]{2,1,0:T(8,128)(2,1)S(1)}, bf16[2,48,2560]{2,1,0:T(8,128)(2,1)}, u32[]{:S(2)}, u32[]{:S(2)}) collective-permute-start(bf16[2,48,2560]{2,1,0:T(8,128)(2,1)S(1)} %pad_maximum_fusion.1), channel_id=1, source_target_pairs={{0,256},{32,288},{64,320},{96,352},{128,384},{160,416},{192,448},{... | collective-permute-start | bytes 1474568 | tf_op jit(solution)/shard_map/ppermute | solution.py:327
  19.8 20.7 %copy-start.6 = (bf16[3,48,640]{2,1,0:T(8,128)(2,1)}, bf16[3,48,640]{2,1,0:T(8,128)(2,1)S(1)}, u32[]{:S(2)}) copy-start(bf16[3,48,640]{2,1,0:T(8,128)(2,1)S(1)} %get-tuple-element.34) | copy-start | bytes 552964
  19.9 17.7 %collective-permute-start = (bf16[3,48,640]{2,1,0:T(8,128)(2,1)S(1)}, bf16[3,48,640]{2,1,0:T(8,128)(2,1)S(1)}, u32[]{:S(2)}, u32[]{:S(2)}) collective-permute-start(bf16[3,48,640]{2,1,0:T(8,128)(2,1)S(1)} %get-tuple-element.27), channel_id=1, source_target_pairs={{0,32},{32,64},{64,96},{96,128},{128,160},{160,192},{192,224},{224... | collective-permute-start | bytes 552968 | tf_op jit(solution)/shard_map/ppermute | solution.py:325
  23.7 13.9 %collective-permute-start.1 = (bf16[3,48,640]{2,1,0:T(8,128)(2,1)S(1)}, bf16[3,48,640]{2,1,0:T(8,128)(2,1)S(1)}, u32[]{:S(2)}, u32[]{:S(2)}) collective-permute-start(bf16[3,48,640]{2,1,0:T(8,128)(2,1)S(1)} %get-tuple-element.28), channel_id=1, source_target_pairs={{0,224},{32,0},{64,32},{96,64},{128,96},{160,128},{192,160},{224,1... | collective-permute-start | bytes 552968 | tf_op jit(solution)/shard_map/ppermute | solution.py:325
  37.6 3.0 %copy-start.13 = (bf16[3,48,640]{2,1,0:T(8,128)(2,1)}, bf16[3,48,640]{2,1,0:T(8,128)(2,1)S(1)}, u32[]{:S(2)}) copy-start(bf16[3,48,640]{2,1,0:T(8,128)(2,1)S(1)} %collective-permute-done.refs_1_.refs_3_) | copy-start | bytes 552964
  37.6 3.0 %copy-start.14 = (bf16[3,48,640]{2,1,0:T(8,128)(2,1)}, bf16[3,48,640]{2,1,0:T(8,128)(2,1)S(1)}, u32[]{:S(2)}) copy-start(bf16[3,48,640]{2,1,0:T(8,128)(2,1)S(1)} %collective-permute-done.1.refs_2_.refs_9_) | copy-start | bytes 552964
  40.6 72.5 %all-to-all-start.1 = ((bf16[32,16,2688]{2,1,0:T(8,128)(2,1)}), bf16[32,16,2688]{2,1,0:T(8,128)(2,1)S(1)}, u32[]{:S(2)}, u32[]{:S(2)}) async-start(bf16[32,16,2688]{2,1,0:T(8,128)(2,1)} %bitcast.11), calls=%async_computation.1 | async-start | bytes 5505024 | tf_op jit(solution)/shard_map/all_to_all | solution.py:305
  49.3 5.2 %copy-start.7 = (bf16[3,48,640]{2,1,0:T(8,128)(2,1)S(1)}, bf16[3,48,640]{2,1,0:T(8,128)(2,1)}, u32[]{:S(2)}) copy-start(bf16[3,48,640]{2,1,0:T(8,128)(2,1)} %copy-done.6) | copy-start | bytes 552964
  51.7 56.0 %collective-permute-start.3 = (bf16[4,48,2560]{2,1,0:T(8,128)(2,1)}, bf16[4,48,2560]{2,1,0:T(8,128)(2,1)}, u32[]{:S(2)}, u32[]{:S(2)}) collective-permute-start(bf16[4,48,2560]{2,1,0:T(8,128)(2,1)} %pad_maximum_fusion), channel_id=1, source_target_pairs={{0,256},{32,288},{64,320},{96,352},{128,384},{160,416},{192,448},{... | collective-permute-start | bytes 2949128 | tf_op jit(solution)/shard_map/ppermute | solution.py:343
  54.6 19.9 %collective-permute-start.5 = (bf16[3,48,640]{2,1,0:T(8,128)(2,1)S(1)}, bf16[3,48,640]{2,1,0:T(8,128)(2,1)S(1)}, u32[]{:S(2)}, u32[]{:S(2)}) collective-permute-start(bf16[3,48,640]{2,1,0:T(8,128)(2,1)S(1)} %copy-done.7), channel_id=1, source_target_pairs={{0,64},{32,96},{64,128},{96,160},{128,192},{160,224},{192,0},{224,... | collective-permute-start | bytes 552968 | tf_op jit(solution)/shard_map/ppermute | solution.py:325
  59.3 20.5 %collective-permute-start.6 = (bf16[3,48,640]{2,1,0:T(8,128)(2,1)S(1)}, bf16[3,48,640]{2,1,0:T(8,128)(2,1)S(1)}, u32[]{:S(2)}, u32[]{:S(2)}) collective-permute-start(bf16[3,48,640]{2,1,0:T(8,128)(2,1)S(1)} %get-tuple-element.35), channel_id=1, source_target_pairs={{0,96},{32,128},{64,160},{96,192},{128,224},{160,0},{192,32},{224,... | collective-permute-start | bytes 552968 | tf_op jit(solution)/shard_map/ppermute | solution.py:325
  66.7 45.4 %collective-permute-start.4 = (bf16[3,2,48,640]{3,2,1,0:T(8,128)(2,1)}, bf16[3,2,48,640]{3,2,1,0:T(8,128)(2,1)}, u32[]{:S(2)}, u32[]{:S(2)}) collective-permute-start(bf16[3,2,48,640]{3,2,1,0:T(8,128)(2,1)} %shard_map.116), channel_id=1, source_target_pairs={{0,256},{32,288},{64,320},{96,352},{128,384},{160,416},{192,448},{... | collective-permute-start | bytes 1105928 | tf_op jit(solution)/shard_map/ppermute | solution.py:353
  69.7 24.2 %collective-permute-start.7 = (bf16[3,48,640]{2,1,0:T(8,128)(2,1)S(1)}, bf16[3,48,640]{2,1,0:T(8,128)(2,1)S(1)}, u32[]{:S(2)}, u32[]{:S(2)}) collective-permute-start(bf16[3,48,640]{2,1,0:T(8,128)(2,1)S(1)} %get-tuple-element.36), channel_id=1, source_target_pairs={{0,128},{32,160},{64,192},{96,224},{128,0},{160,32},{192,64},{224,... | collective-permute-start | bytes 552968 | tf_op jit(solution)/shard_map/ppermute | solution.py:325
  74.4 30.5 %copy-start.8 = (bf16[3,48,640]{2,1,0:T(8,128)(2,1)}, bf16[3,48,640]{2,1,0:T(8,128)(2,1)S(1)}, u32[]{:S(2)}) copy-start(bf16[3,48,640]{2,1,0:T(8,128)(2,1)S(1)} %collective-permute-done.5.refs_0_.refs_4_) | copy-start | bytes 552964
  74.4 24.7 %collective-permute-start.8 = (bf16[3,48,640]{2,1,0:T(8,128)(2,1)S(1)}, bf16[3,48,640]{2,1,0:T(8,128)(2,1)S(1)}, u32[]{:S(2)}, u32[]{:S(2)}) collective-permute-start(bf16[3,48,640]{2,1,0:T(8,128)(2,1)S(1)} %get-tuple-element.37), channel_id=1, source_target_pairs={{0,160},{32,192},{64,224},{96,0},{128,32},{160,64},{192,96},{224,1... | collective-permute-start | bytes 552968 | tf_op jit(solution)/shard_map/ppermute | solution.py:325
  79.8 25.1 %copy-start.9 = (bf16[3,48,640]{2,1,0:T(8,128)(2,1)}, bf16[3,48,640]{2,1,0:T(8,128)(2,1)S(1)}, u32[]{:S(2)}) copy-start(bf16[3,48,640]{2,1,0:T(8,128)(2,1)S(1)} %collective-permute-done.6.refs_1_.refs_5_) | copy-start | bytes 552964
  79.8 25.1 %collective-permute-start.9 = (bf16[3,48,640]{2,1,0:T(8,128)(2,1)S(1)}, bf16[3,48,640]{2,1,0:T(8,128)(2,1)S(1)}, u32[]{:S(2)}, u32[]{:S(2)}) collective-permute-start(bf16[3,48,640]{2,1,0:T(8,128)(2,1)S(1)} %get-tuple-element.38), channel_id=1, source_target_pairs={{0,192},{32,224},{64,0},{96,32},{128,64},{160,96},{192,128},{224,1... | collective-permute-start | bytes 552968 | tf_op jit(solution)/shard_map/ppermute | solution.py:325
  93.9 5.3 %copy-start.10 = (bf16[3,48,640]{2,1,0:T(8,128)(2,1)}, bf16[3,48,640]{2,1,0:T(8,128)(2,1)S(1)}, u32[]{:S(2)}) copy-start(bf16[3,48,640]{2,1,0:T(8,128)(2,1)S(1)} %collective-permute-done.7.refs_2_.refs_6_) | copy-start | bytes 552964
  99.2 5.7 %copy-start.11 = (bf16[3,48,640]{2,1,0:T(8,128)(2,1)}, bf16[3,48,640]{2,1,0:T(8,128)(2,1)S(1)}, u32[]{:S(2)}) copy-start(bf16[3,48,640]{2,1,0:T(8,128)(2,1)S(1)} %collective-permute-done.8.refs_3_.refs_7_) | copy-start | bytes 552964
  104.9 0.7 copy-start.12
  118.5 29.2 %copy-start.3 = (bf16[512,128]{1,0:T(8,128)(2,1)}, bf16[512,128]{1,0:T(8,128)(2,1)S(1)}, u32[]{:S(2)}) copy-start(bf16[512,128]{1,0:T(8,128)(2,1)S(1)} %get-tuple-element.42.weight_ref) | copy-start | bytes 393220
  118.5 29.2 %all-to-all-start.2 = ((bf16[8,4,48,256]{3,2,1,0:T(8,128)(2,1)}), bf16[8,4,48,256]{3,2,1,0:T(8,128)(2,1)}, u32[]{:S(2)}, u32[]{:S(2)}) async-start(bf16[8,4,48,256]{3,2,1,0:T(8,128)(2,1)} %get-tuple-element.41), calls=%async_computation.2 | async-start | bytes 1572864 | tf_op jit(solution)/shard_map/all_to_all | solution.py:305
  124.2 19.2 %collective-permute-start.10 = (bf16[5,2,48,640]{3,2,1,0:T(8,128)(2,1)}, bf16[5,2,48,640]{3,2,1,0:T(8,128)(2,1)}, u32[]{:S(2)}, u32[]{:S(2)}) collective-permute-start(bf16[5,2,48,640]{3,2,1,0:T(8,128)(2,1)} %shard_map.117), channel_id=1, source_target_pairs={{0,256},{32,288},{64,320},{96,352},{128,384},{160,416},{192,448},{... | collective-permute-start | bytes 1843208 | tf_op jit(solution)/shard_map/ppermute | solution.py:361
  152.1 18.5 %all-to-all-start.3 = ((bf16[8,96,256]{2,1,0:T(8,128)(2,1)}), bf16[8,96,256]{2,1,0:T(8,128)(2,1)S(1)}, u32[]{:S(2)}, u32[]{:S(2)}) async-start(bf16[8,96,256]{2,1,0:T(8,128)(2,1)} %get-tuple-element.45), calls=%async_computation.3 | async-start | bytes 786432 | tf_op jit(solution)/shard_map/all_to_all | solution.py:305
  155.6 21.0 %collective-permute-start.12 = (bf16[8,48,640]{2,1,0:T(8,128)(2,1)}, bf16[8,48,640]{2,1,0:T(8,128)(2,1)}, u32[]{:S(2)}, u32[]{:S(2)}) collective-permute-start(bf16[8,48,640]{2,1,0:T(8,128)(2,1)} %get-tuple-element.50), channel_id=1, source_target_pairs={{0,256},{32,288},{64,320},{96,352},{128,384},{160,416},{192,448},{... | collective-permute-start | bytes 1474568 | tf_op jit(solution)/shard_map/ppermute | solution.py:390
  170.6 6.0 %copy-start.15 = (bf16[8,48,640]{2,1,0:T(8,128)(2,1)S(1)}, bf16[8,48,640]{2,1,0:T(8,128)(2,1)}, u32[]{:S(2)}) copy-start(bf16[8,48,640]{2,1,0:T(8,128)(2,1)} %get-tuple-element.49) | copy-start | bytes 1474564
  173.0 16.8 %collective-permute-start.11 = (bf16[2,48,2560]{2,1,0:T(8,128)(2,1)}, bf16[2,48,2560]{2,1,0:T(8,128)(2,1)}, u32[]{:S(2)}, u32[]{:S(2)}) collective-permute-start(bf16[2,48,2560]{2,1,0:T(8,128)(2,1)} %get-tuple-element.48), channel_id=1, source_target_pairs={{0,256},{32,288},{64,320},{96,352},{128,384},{160,416},{192,448},{... | collective-permute-start | bytes 1474568 | tf_op jit(solution)/shard_map/ppermute | solution.py:403
  178.5 20.4 %all-to-all-start.4 = ((bf16[8,48,640]{2,1,0:T(8,128)(2,1)}), bf16[8,48,640]{2,1,0:T(8,128)(2,1)S(1)}, u32[]{:S(2)}, u32[]{:S(2)}) async-start(bf16[8,48,640]{2,1,0:T(8,128)(2,1)} %add_convert_fusion), calls=%async_computation.4 | async-start | bytes 983040 | tf_op jit(solution)/shard_map/all_to_all | solution.py:305
  182.0 0.9 copy-start.5
  (2 other events, 1.3 us)
